TPU v7x, 32 devices: a whole 2x2x4 slice. The times are simulated.
32 devices in a mesh: tm: 8 (over z, y), gy: 4 (over x, core).
Axes of the slice: x: 2, y: 2, z: 4, core: 2. Of those that a mesh axis runs over, the one named last changes fastest.
Arguments:
- residual: float32 [8, 8, 256, 1024], P('tm', None, 'gy'), may hold values from -0.4 to 0.4
Outputs:
- correction: float32 [8, 8, 256, 1024], P('tm', None, 'gy')
All inputs are finite; a program needn't handle non-finite values.
Results may differ from a plain program's by a relative error of at most 0.00019.
Values sent between devices are 32-bit elements; how exact they have to be, the bound alone decides.
No kernel may reach another device: no remote copies, remote signals or barrier semaphores. Data moves between devices by JAX's collectives and lax.ppermute only.
A program may use at most 64 MiB of HBM per device.

v0:
```python
import math

import jax
import jax.numpy as jnp
from jax import lax
from jax.sharding import PartitionSpec as P

ALPHA_RATIO = 0.95
STEP_SCALE = 0.26


def sine_table(count):
    indices = jnp.arange(count, dtype=jnp.int32) + 1
    product = indices[:, None] * indices[None, :] % (2 * (count + 1))
    return math.sqrt(2.0 / (count + 1)) * jnp.sin(
        jnp.pi * product.astype(jnp.float32) / (count + 1)
    )


def spectrum_of(count):
    indices = jnp.arange(count, dtype=jnp.float32) + 1.0
    return 2.0 - 2.0 * jnp.cos(jnp.pi * indices / (count + 1))


def symbol_of(freq, count, weight_mu):
    radius = ALPHA_RATIO ** (1.0 / count)
    theta = 2.0 * jnp.pi * freq / count
    zreal = radius * jnp.cos(theta)
    zimag = -radius * jnp.sin(theta)
    first = 1.0 - zreal
    second = -zimag
    lam_re = first * first - second * second + STEP_SCALE * weight_mu * zreal
    lam_im = 2.0 * first * second + STEP_SCALE * weight_mu * zimag
    return (lam_re, lam_im)


def divide_by(top_re, top_im, lam_re, lam_im):
    denom = lam_re * lam_re + lam_im * lam_im
    return (
        (top_re * lam_re + top_im * lam_im) / denom,
        (top_im * lam_re - top_re * lam_im) / denom,
    )


def on_device(residual):
    highest = lax.Precision.HIGHEST
    steps = lax.axis_size("tm")
    groups = lax.axis_size("gy")
    moment = lax.axis_index("tm")
    group = lax.axis_index("gy")
    depth = residual.shape[1]
    rows_dev = residual.shape[2]
    width = residual.shape[3]
    sine_z = sine_table(depth)
    sine_x = sine_table(width)
    sine_y = sine_table(rows_dev * groups)
    mu_z = spectrum_of(depth)
    mu_y = spectrum_of(rows_dev * groups)
    mu_all = spectrum_of(width)
    columns = width // groups
    planes = jnp.einsum("cz,zyx->cyx", sine_z, residual[0], precision=highest)
    across = jnp.einsum("ax,cyx->cay", sine_x, planes, precision=highest)
    slab = lax.all_to_all(across, "gy", split_axis=1, concat_axis=2, tiled=True)
    hatted = jnp.einsum("by,cay->cab", sine_y, slab, precision=highest)
    piece = columns // steps
    moved = lax.all_to_all(hatted[None], "tm", split_axis=2, concat_axis=0, tiled=True)
    mu_x = lax.dynamic_slice_in_dim(mu_all, group * columns + moment * piece, piece)
    weight_mu = mu_z[:, None, None] + mu_x[None, :, None] + mu_y[None, None, :]
    counter = jnp.arange(steps, dtype=jnp.int32)
    angle = 2.0 * jnp.pi * (counter[:, None] * counter[None, :] % steps).astype(jnp.float32) / steps
    decay = ALPHA_RATIO ** (counter.astype(jnp.float32) / steps)
    fwd_cos = jnp.cos(angle) * decay[None, :]
    fwd_sin = -jnp.sin(angle) * decay[None, :]
    spec_re = jnp.einsum("kn,nzab->kzab", fwd_cos, moved, precision=highest)
    spec_im = jnp.einsum("kn,nzab->kzab", fwd_sin, moved, precision=highest)
    freq = counter.astype(jnp.float32)[:, None, None, None]
    lam_re, lam_im = symbol_of(freq, steps, weight_mu[None])
    solved_re, solved_im = divide_by(spec_re, spec_im, lam_re, lam_im)
    inv_cos = jnp.cos(angle) / decay[:, None] / steps
    inv_sin = -jnp.sin(angle) / decay[:, None] / steps
    timed = jnp.einsum("nk,kzab->nzab", inv_cos, solved_re, precision=highest)
    timed = timed + jnp.einsum("nk,kzab->nzab", inv_sin, solved_im, precision=highest)
    solved = lax.all_to_all(timed, "tm", split_axis=0, concat_axis=2, tiled=True)[0]
    inverse_y = jnp.einsum("by,cab->cay", sine_y, solved, precision=highest)
    gathered = lax.all_to_all(inverse_y, "gy", split_axis=2, concat_axis=1, tiled=True)
    rows_field = jnp.einsum("ax,cay->cyx", sine_x, gathered, precision=highest)
    result = jnp.einsum("cz,cyx->zyx", sine_z, rows_field, precision=highest)
    return result[None]


def solution(mesh):
    in_specs = (P("tm", None, "gy", None),)
    out_specs = P("tm", None, "gy", None)
    return jax.shard_map(
        on_device, mesh=mesh, in_specs=in_specs, out_specs=out_specs, check_vma=False
    )
```

profile of v0, /device:TPU:0, one launch (start us, length us, event | category | flops | bytes accessed | tf_op | source)
XLA Modules:
  0.0 286.2 jit_solution(13713882660918540891)
XLA Ops:
  0.0 1.6 copy-done
  1.6 3.0 %fusion.17 = f32[8,64,1024]{2,0,1:T(8,128)S(1)} fusion(f32[8,64,1024]{2,1,0:T(8,128)S(1)} %bitcast.61, s32[8]{0:T(128)S(1)} %iota_add_fusion.2), kind=kOutput, calls=%fused_computation.17 | convolution fusion | flops 50332288 | bytes 4194336 | tf_op jit(solution)/shard_map/cz,zyx->cyx/dot_general | solution.py:61
  4.6 26.4 %fusion.43 = f32[8,1024,64]{1,2,0:T(8,128)} fusion(s32[1024]{0:T(1024)S(1)} %iota_add_fusion, f32[8,64,1024]{2,0,1:T(8,128)S(1)} %fusion.17), kind=kOutput, calls=%fused_computation.46 | convolution fusion | flops 6452936704 | bytes 4198400 | tf_op jit(solution)/shard_map/ax,cyx->cay/dot_general | solution.py:62
  31.0 3.8 %copy.40 = f32[8,1024,64]{2,0,1:T(8,128)} copy(f32[8,1024,64]{1,2,0:T(8,128)} %fusion.43) | data formatting | bytes 4194304 | tf_op jit(solution)/shard_map/ax,cyx->cay/transpose | solution.py:62
  34.8 5.5 %reshape.130 = f32[4,1,131072]{2,1,0:T(1,128)} reshape(f32[1024,8,64]{2,1,0:T(8,128)} %bitcast.62) | data formatting | bytes 4194304
  40.3 4.5 %all-to-all-start = ((f32[4,1,131072]{2,1,0:T(1,128)}), f32[4,1,131072]{2,1,0:T(1,128)}, u32[]{:S(2)}, u32[]{:S(2)}) async-start(f32[4,1,131072]{2,1,0:T(1,128)} %reshape.130), calls=%async_computation | async-start | bytes 4194304 | tf_op jit(solution)/shard_map/all_to_all | solution.py:63
  44.7 26.3 %all-to-all-done = f32[4,1,131072]{2,1,0:T(1,128)} async-done(((f32[4,1,131072]{2,1,0:T(1,128)}), f32[4,1,131072]{2,1,0:T(1,128)}, u32[]{:S(2)}, u32[]{:S(2)}) %all-to-all-start) | async-done | bytes 2097184 | tf_op jit(solution)/shard_map/all_to_all | solution.py:63
  71.1 0.5 broadcast.265
  71.6 9.0 %reduce = f32[4,131072]{1,0:T(4,128)} reduce(f32[4,1,131072]{2,1,0:T(1,128)} %all-to-all-done, f32[]{:T(128)} %broadcast.265), dimensions={1}, to_apply=%all_to_all.50.reduce_sub_computation | reduce | bytes 4194308 | tf_op jit(solution)/shard_map/all_to_all | solution.py:63
  80.6 5.5 %reshape.131 = f32[1024,8,64]{2,1,0:T(8,128)} reshape(f32[4,131072]{1,0:T(4,128)} %reduce) | data formatting | bytes 4194304
  86.1 3.8 %copy.67 = f32[8,4,256,64]{2,1,3,0:T(4,128)} copy(f32[8,4,256,64]{3,0,2,1:T(8,128)} %bitcast.63) | data formatting | bytes 4194304 | tf_op jit(solution)/shard_map/all_to_all | solution.py:63
  89.9 2.0 copy.42
  91.9 4.5 %convolution_bitcast_fusion.1 = f32[1,8,256,256]{3,2,1,0:T(8,128)S(1)} fusion(f32[8,256,256]{1,2,0:T(8,128)S(1)} %bitcast.66, s32[256]{0:T(256)S(1)} %iota_add_fusion.1), kind=kOutput, calls=%fused_computation.48 | convolution fusion | flops 1611268096 | bytes 4195328 | tf_op jit(solution)/shard_map/by,cay->cab/dot_general | solution.py:64
  96.4 2.5 copy.44
  98.9 6.8 %all-to-all-start.1 = ((f32[1,8,256,256]{3,1,0,2:T(8,128)}), f32[1,8,256,256]{3,1,0,2:T(8,128)}, u32[]{:S(2)}, u32[]{:S(2)}) async-start(f32[1,8,256,256]{3,1,0,2:T(8,128)} %copy.44), calls=%async_computation.1 | async-start | bytes 4194304 | tf_op jit(solution)/shard_map/all_to_all | solution.py:66
  105.8 0.1 dynamic_slice.3
  106.2 0.1 add_multiply_fusion
  106.3 47.5 %all-to-all-done.1 = f32[1,8,256,256]{3,1,0,2:T(8,128)} async-done(((f32[1,8,256,256]{3,1,0,2:T(8,128)}), f32[1,8,256,256]{3,1,0,2:T(8,128)}, u32[]{:S(2)}, u32[]{:S(2)}) %all-to-all-start.1) | async-done | bytes 2097184 | tf_op jit(solution)/shard_map/all_to_all | solution.py:66
  153.7 4.5 %fusion.12 = f32[8,8,32,256]{3,0,2,1:T(8,128)S(1)} fusion(f32[1,8,8,32,256]{4,1,3,2,0:T(8,128)} %bitcast.12, f32[8]{0:T(128)S(1)} %multiply_power_fusion), kind=kOutput, calls=%fused_computation.12 | convolution fusion | flops 50332672 | bytes 4194336 | tf_op jit(solution)/shard_map/kn,nzab->kzab/dot_general | solution.py:75
  158.2 4.5 %fusion.14 = f32[8,8,32,256]{3,0,2,1:T(8,128)S(1)} fusion(f32[1,8,8,32,256]{4,1,3,2,0:T(8,128)} %bitcast.12, f32[8]{0:T(128)S(1)} %multiply_power_fusion), kind=kOutput, calls=%fused_computation.14 | convolution fusion | flops 50332608 | bytes 4194336 | tf_op jit(solution)/shard_map/kn,nzab->kzab/dot_general | solution.py:74
  162.7 2.6 fusion.19
  165.3 2.6 fusion.48
  167.9 0.9 copy.51
  168.8 51.8 %all_to_all.69 = f32[8,8,32,256]{3,2,1,0:T(8,128)S(1)} all-to-all(f32[8,8,32,256]{3,2,1,0:T(8,128)S(1)} %copy.51), channel_id=1, replica_groups=mesh['tm'=8,'gy'=4] {'tm'}, dimensions={0} | all-to-all | bytes 4194304 | tf_op jit(solution)/shard_map/all_to_all | solution.py:83
  220.6 0.2 copy.52
  220.9 4.2 %fusion.69 = f32[8,256,256]{2,1,0:T(8,128)} fusion(f32[8,256,256]{2,1,0:T(8,128)S(1)} %bitcast.65, s32[256]{0:T(256)S(1)} %iota_add_fusion.1), kind=kOutput, calls=%fused_computation.71 | convolution fusion | flops 1611268096 | bytes 4195328 | tf_op jit(solution)/shard_map/by,cab->cay/dot_general | solution.py:84
  225.1 3.1 %copy.53 = f32[8,256,256]{1,0,2:T(8,128)} copy(f32[8,256,256]{2,1,0:T(8,128)} %fusion.69) | data formatting | bytes 4194304 | tf_op jit(solution)/shard_map/by,cab->cay/dot_general | solution.py:84
  228.2 29.3 %all_to_all.70 = f32[8,256,256]{1,0,2:T(8,128)S(1)} all-to-all(f32[8,256,256]{1,0,2:T(8,128)} %copy.53), channel_id=1, replica_groups=mesh['tm'=8,'gy'=4] {'gy'}, dimensions={2} | all-to-all | bytes 4194304 | tf_op jit(solution)/shard_map/all_to_all | solution.py:85
  257.4 0.3 copy.75
  257.7 23.7 %fusion.8 = f32[8,64,1024]{2,0,1:T(8,128)S(1)} fusion(f32[8,1024,64]{1,0,2:T(8,128)S(1)} %bitcast.68, s32[1024]{0:T(1024)S(1)} %iota_add_fusion), kind=kOutput, calls=%fused_computation.10 | convolution fusion | flops 6452936704 | bytes 4198400 | tf_op jit(solution)/shard_map/ax,cay->cyx/dot_general | solution.py:86
  281.4 2.0 convolution_bitcast_fusion
  283.4 2.5 copy.57
  (11 shorter events, 0.3 us)
Async XLA Ops:
  0.0 1.6 copy-start
  40.3 30.8 %all-to-all-start = ((f32[4,1,131072]{2,1,0:T(1,128)}), f32[4,1,131072]{2,1,0:T(1,128)}, u32[]{:S(2)}, u32[]{:S(2)}) async-start(f32[4,1,131072]{2,1,0:T(1,128)} %reshape.130), calls=%async_computation | async-start | bytes 4194304 | tf_op jit(solution)/shard_map/all_to_all | solution.py:63
  98.9 54.8 %all-to-all-start.1 = ((f32[1,8,256,256]{3,1,0,2:T(8,128)}), f32[1,8,256,256]{3,1,0,2:T(8,128)}, u32[]{:S(2)}, u32[]{:S(2)}) async-start(f32[1,8,256,256]{3,1,0,2:T(8,128)} %copy.44), calls=%async_computation.1 | async-start | bytes 4194304 | tf_op jit(solution)/shard_map/all_to_all | solution.py:66
where the time goes:
time: 290 us; the launch traced here: 286 us
  blocking collectives  81.1 us (28%)
  matrix products  77.9 us (27%)
  waiting for transfers between devices  73.8 us (25%)
  local copies, waits for them, and re-layouts  32.3 us (11%)
  starting transfers between devices  11.3 us (4%)
  other arithmetic  9.44 us (3%)
    all_to_all x1, blocking collectives, on_device(): lax.all_to_all(timed, 'tm', split_axis=0, concat_axis=2, tiled=True)[0]  51.8 us
    all_to_all x1, waiting for transfers between devices, on_device(): lax.all_to_all(hatted[None], 'tm', split_axis=2, concat_axis=0, tiled=True)  47.5 us
    all_to_all x1, blocking collectives, on_device(): lax.all_to_all(inverse_y, 'gy', split_axis=2, concat_axis=1, tiled=True)  29.3 us
    dot_general x1, matrix products, on_device(): across = jnp.einsum('ax,cyx->cay', sine_x, planes, precision=highest)  26.4 us
    all_to_all x1, waiting for transfers between devices, on_device(): slab = lax.all_to_all(across, 'gy', split_axis=1, concat_axis=2, tiled=True)  26.3 us
    dot_general x1, matrix products, on_device(): rows_field = jnp.einsum('ax,cay->cyx', sine_x, gathered, precision=highest)  23.7 us
    unnamed x4, local copies, waits for them, and re-layouts  12.6 us
    all_to_all x1, other arithmetic, on_device(): slab = lax.all_to_all(across, 'gy', split_axis=1, concat_axis=2, tiled=True)  9.01 us
  transfers between devices with their start and end apart: 2, of which 2 were waited for; matrix products, arithmetic and copies ran while one was open for 0% of the time, Pallas kernels for 0%

commit v1 on v0

v1 whole, which is shorter than its diff:
```python
import functools
import math

import jax
import jax.numpy as jnp
import numpy as np
from jax import lax
from jax.experimental import pallas as pl
from jax.experimental.pallas import tpu as pltpu
from jax.sharding import PartitionSpec as P

ALPHA_RATIO = 0.95
STEP_SCALE = 0.26
CHUNKS = 4
LANES = 128
VMEM_BYTES = 40 * 1024 * 1024


def sine_table(count):
    indices = np.arange(count, dtype=np.int64) + 1
    product = indices[:, None] * indices[None, :] % (2 * (count + 1))
    return math.sqrt(2.0 / (count + 1)) * np.sin(np.pi * product / (count + 1))


def spectrum_of(count):
    indices = np.arange(count, dtype=np.float64) + 1.0
    return 2.0 - 2.0 * np.cos(np.pi * indices / (count + 1))


def table_parts(count):
    table = sine_table(count).astype(np.float32)
    high = table.astype(jnp.bfloat16)
    low = (table - high.astype(np.float32)).astype(jnp.bfloat16)
    return jnp.asarray(high), jnp.asarray(low)


def parts_of(values):
    high = values.astype(jnp.bfloat16)
    return high, (values - high.astype(jnp.float32)).astype(jnp.bfloat16)


def dot(left, right):
    return jnp.dot(left, right, preferred_element_type=jnp.float32)


def call(kernel, out_shape, flops, moved, scratch=(), in_smem=1, n_in=1):
    specs = [pl.BlockSpec(memory_space=pltpu.SMEM)] * in_smem
    specs += [pl.BlockSpec(memory_space=pltpu.VMEM)] * (n_in - in_smem)
    return pl.pallas_call(
        kernel,
        out_shape=out_shape,
        in_specs=specs,
        out_specs=jax.tree.map(
            lambda _: pl.BlockSpec(memory_space=pltpu.VMEM), out_shape
        ),
        scratch_shapes=scratch,
        compiler_params=pltpu.CompilerParams(vmem_limit_bytes=VMEM_BYTES),
        cost_estimate=pl.CostEstimate(
            flops=flops, bytes_accessed=moved, transcendentals=0
        ),
    )


class Plan:
    def __init__(self, mesh, shape):
        self.steps = mesh.shape["tm"]
        self.groups = mesh.shape["gy"]
        self.depth, self.rows, self.width = shape[1], shape[2], shape[3]
        self.height = self.rows
        self.half = self.steps // 2
        self.across = min(self.groups, self.width // LANES)
        self.deep = self.groups // self.across
        self.block = self.width // self.across
        self.chunks = min(CHUNKS, self.depth // self.deep)
        self.planes = self.depth // self.deep // self.chunks
        self.rows_dev = self.height // self.groups
        self.piece = self.height // self.half
        self.sine_z = sine_table(self.depth)


def forward_x(plan, chunk, ids, x, sxh, sxl, *refs):
    outs, (high, low) = refs[: plan.groups], refs[plan.groups :]
    rows = plan.rows_dev
    strip = 16
    per = plan.depth // plan.deep

    def planes(index, carry):
        at = pl.multiple_of(index * strip, strip)
        total = [None] * (plan.deep * plan.planes)
        for z in range(plan.depth):
            value = x[z, pl.ds(at, strip), :]
            for jc in range(plan.deep):
                for u in range(plan.planes):
                    c = jc * per + chunk * plan.planes + u
                    term = value * np.float32(plan.sine_z[c, z])
                    slot = jc * plan.planes + u
                    total[slot] = term if z == 0 else total[slot] + term
        for slot, value in enumerate(total):
            top, rest = parts_of(value)
            high[slot, pl.ds(at, strip), :] = top
            low[slot, pl.ds(at, strip), :] = rest
        return carry

    lax.fori_loop(0, rows // strip, planes, 0)
    me = ids[1]
    for k in range(plan.groups):
        owner = me ^ k
        first = (owner // plan.across) * plan.planes
        columns = pl.ds(
            pl.multiple_of(owner % plan.across * plan.block, LANES), plan.block
        )
        top = high[pl.ds(first, plan.planes)].reshape(-1, plan.width)
        rest = low[pl.ds(first, plan.planes)].reshape(-1, plan.width)
        right = sxh[:, columns]
        value = dot(top, right) + dot(rest, right) + dot(top, sxl[:, columns])
        outs[k][...] = value.reshape(plan.planes, rows, plan.block)


def transform_y(plan, axis_in, axis_out, ids, *refs):
    size = (plan.groups, plan.half)
    rows = (plan.rows_dev, plan.piece)
    n_in, n_out = size[axis_in], size[axis_out]
    r_in, r_out = rows[axis_in], rows[axis_out]
    where = (ids[1], lax.rem(ids[0], plan.half))
    pieces = refs[:n_in]
    syh, syl = refs[n_in : n_in + 2]
    outs = refs[n_in + 2 : n_in + 2 + n_out]
    high, low, full = refs[n_in + 2 + n_out :]
    for k in range(n_in):
        at = pl.ds(pl.multiple_of((where[axis_in] ^ k) * r_in, r_in), r_in)
        for u in range(plan.planes):
            top, rest = parts_of(pieces[k][u])
            high[u, at, :] = top
            low[u, at, :] = rest
    for u in range(plan.planes):
        right = high[u]
        full[u] = dot(syh[...], right) + dot(syl[...], right) + dot(syh[...], low[u])
    for k in range(n_out):
        at = pl.ds(pl.multiple_of((where[axis_out] ^ k) * r_out, r_out), r_out)
        for u in range(plan.planes):
            outs[k][u] = full[u, at, :]


STRIP = 16


def per_strip(plan, chunk, ids, smu_z, smu_y, smu_x, body):
    me, group = ids[0], ids[1]
    first = (group // plan.across) * (plan.depth // plan.deep) + chunk * plan.planes
    columns = pl.ds(
        pl.multiple_of(group % plan.across * plan.block, LANES), plan.block
    )
    across = smu_x[:, columns]
    base = lax.rem(me, plan.half) * plan.piece

    def step(index, carry):
        at = pl.multiple_of(index * STRIP, STRIP)
        down = smu_y[pl.ds(pl.multiple_of(base + at, STRIP), STRIP), :]
        plane = across + down
        for u in range(plan.planes):
            body(u, pl.ds(at, STRIP), plane + smu_z[first + u])
        return carry

    lax.fori_loop(0, plan.piece // STRIP, step, 0)


def chebyshev(smu, count):
    kappa = 2.0 - smu
    values = [jnp.zeros_like(kappa), jnp.ones_like(kappa)]
    for _ in range(count):
        values.append(kappa * values[-1] - values[-2])
    return kappa, values


def half_end(plan, chunk, ids, smu_z, smu_y, smu_x, *refs):
    pieces, out = refs[: plan.half], refs[plan.half]
    place = lax.rem(ids[0], plan.half)
    for case in range(plan.half):

        @pl.when(place == case)
        def _():
            def body(u, rows, smu):
                kappa = 2.0 - smu
                before = pieces[case][u, rows, :]
                last = kappa * before + pieces[case ^ 1][u, rows, :]
                for j in range(2, plan.half):
                    value = pieces[case ^ j][u, rows, :]
                    before, last = last, kappa * last - before + value
                out[0, u, rows, :] = before
                out[1, u, rows, :] = last

            per_strip(plan, chunk, ids, smu_z, smu_y, smu_x, body)


def half_solve(plan, chunk, ids, smu_z, smu_y, smu_x, *refs):
    pieces = refs[: plan.half]
    mine, other = refs[plan.half : plan.half + 2]
    outs = refs[plan.half + 2 :]
    place = lax.rem(ids[0], plan.half)
    entering = jnp.where(ids[0] < plan.half, ALPHA_RATIO, 1.0).astype(jnp.float32)
    for case in range(plan.half):

        @pl.when(place == case)
        def _():
            def body(u, rows, smu):
                kappa, cheb = chebyshev(smu, plan.half)
                u_up, u_at, u_down = cheb[-1], cheb[-2], cheb[-3]
                turn = 0.5 * (u_up - u_down)
                det = (1.0 - ALPHA_RATIO) ** 2 + ALPHA_RATIO * (
                    smu * (4.0 - smu) * (u_at * u_at)
                )
                inverse = 1.0 / det
                far0 = entering * other[0, u, rows, :]
                far1 = entering * other[1, u, rows, :]
                near0 = ALPHA_RATIO * mine[0, u, rows, :]
                near1 = ALPHA_RATIO * mine[1, u, rows, :]
                p0 = u_up * far0 - u_at * far1 + near0
                p1 = u_at * far0 - u_down * far1 + near1
                even = (1.0 - ALPHA_RATIO) * turn * inverse
                odd = 0.5 * (1.0 + ALPHA_RATIO) * u_at * inverse
                before = even * p0 + odd * (2.0 * p1 - kappa * p0)
                last = even * p1 + odd * (kappa * p1 - 2.0 * p0)
                for j in range(plan.half):
                    value = pieces[case ^ j][u, rows, :]
                    before, last = last, kappa * last - before + value
                    outs[case ^ j][u, rows, :] = last

            per_strip(plan, chunk, ids, smu_z, smu_y, smu_x, body)


def rows_of(plan, ids, pieces, sxh, sxl, write):
    me = ids[1]
    for jc in range(plan.deep):
        total = None
        for ja in range(plan.across):
            k = jc * plan.across + ja
            owner = me ^ k
            at = pl.ds(
                pl.multiple_of(owner % plan.across * plan.block, LANES), plan.block
            )
            top, rest = parts_of(
                pieces[k][...].reshape(plan.planes * plan.rows_dev, plan.block)
            )
            right = sxh[at, :]
            value = dot(top, right) + dot(rest, right) + dot(top, sxl[at, :])
            total = value if total is None else total + value
        owner = (me // plan.across) ^ jc
        write(owner, total.reshape(plan.planes, plan.rows_dev, plan.width))


def backward_x(plan, ids, *refs):
    pieces = refs[: plan.groups]
    sxh, sxl, out = refs[plan.groups :]

    def write(owner, value):
        out[pl.ds(owner * plan.planes, plan.planes)] = value

    rows_of(plan, ids, pieces, sxh, sxl, write)


def backward_last(plan, ids, *refs):
    pieces = refs[: plan.groups]
    sxh, sxl = refs[plan.groups : plan.groups + 2]
    ready = refs[plan.groups + 2 : plan.groups + 1 + plan.chunks]
    out, last = refs[plan.groups + 1 + plan.chunks :]

    def write(owner, value):
        last[pl.ds(owner * plan.planes, plan.planes)] = value

    rows_of(plan, ids, pieces, sxh, sxl, write)
    strip = 8
    per = plan.depth // plan.deep
    sources = list(ready) + [last]

    def planes(index, carry):
        at = pl.ds(pl.multiple_of(index * strip, strip), strip)
        total = [None] * plan.depth
        for chunk, source in enumerate(sources):
            for jc in range(plan.deep):
                for u in range(plan.planes):
                    c = jc * per + chunk * plan.planes + u
                    value = source[jc * plan.planes + u, at, :]
                    for z in range(plan.depth):
                        term = value * np.float32(plan.sine_z[z, c])
                        total[z] = term if total[z] is None else total[z] + term
        for z in range(plan.depth):
            out[z, at, :] = total[z]
        return carry

    lax.fori_loop(0, plan.rows_dev // strip, planes, 0)


def swap(values, axis, count, distance):
    if distance == 0:
        return values
    return lax.ppermute(values, axis, [(i, i ^ distance) for i in range(count)])


def on_device(plan, residual):
    steps, groups, half = plan.steps, plan.groups, plan.half
    ids = jnp.stack([lax.axis_index("tm"), lax.axis_index("gy")]).astype(jnp.int32)
    sxh, sxl = table_parts(plan.width)
    syh, syl = table_parts(plan.height)
    smu_z = jnp.asarray(STEP_SCALE * spectrum_of(plan.depth), jnp.float32)
    smu_y = jnp.asarray(STEP_SCALE * spectrum_of(plan.height)[:, None], jnp.float32)
    smu_x = jnp.asarray(STEP_SCALE * spectrum_of(plan.width)[None, :], jnp.float32)
    field = residual[0]
    f32 = functools.partial(jax.ShapeDtypeStruct, dtype=jnp.float32)
    bf16 = jnp.bfloat16
    rows_in = f32((plan.planes, plan.rows_dev, plan.block))
    modes = f32((plan.planes, plan.piece, plan.block))
    ends = f32((2,) + modes.shape)
    count = plan.planes * plan.height * plan.block
    table_x = 4 * plan.width * plan.width
    table_y = 4 * plan.height * plan.height
    y_scratch = [
        pltpu.VMEM((plan.planes, plan.height, plan.block), bf16),
        pltpu.VMEM((plan.planes, plan.height, plan.block), bf16),
        pltpu.VMEM((plan.planes, plan.height, plan.block), jnp.float32),
    ]
    whole_planes = plan.deep * plan.planes
    ready = []
    for chunk in range(plan.chunks):
        pieces = call(
            functools.partial(forward_x, plan, chunk),
            [rows_in] * groups,
            6 * count * plan.width,
            4 * field.size + table_x + 4 * count,
            [pltpu.VMEM((whole_planes, plan.rows_dev, plan.width), bf16)] * 2,
            1,
            4,
        )(ids, field, sxh, sxl)
        pieces = [swap(v, "gy", groups, k) for k, v in enumerate(pieces)]
        pieces = call(
            functools.partial(transform_y, plan, 0, 1),
            [modes] * half,
            6 * count * plan.height,
            8 * count + table_y,
            y_scratch,
            1,
            3 + groups,
        )(ids, *pieces, syh, syl)
        pieces = [swap(v, "tm", steps, k) for k, v in enumerate(pieces)]
        mine = call(
            functools.partial(half_end, plan, chunk),
            ends,
            8 * count,
            6 * count,
            (),
            2,
            4 + half,
        )(ids, smu_z, smu_y, smu_x, *pieces)
        other = swap(mine, "tm", steps, half)
        pieces = call(
            functools.partial(half_solve, plan, chunk),
            [modes] * half,
            40 * count,
            12 * count,
            (),
            2,
            6 + half,
        )(ids, smu_z, smu_y, smu_x, *pieces, mine, other)
        pieces = [swap(v, "tm", steps, k) for k, v in enumerate(pieces)]
        pieces = call(
            functools.partial(transform_y, plan, 1, 0),
            [rows_in] * groups,
            6 * count * plan.height,
            8 * count + table_y,
            y_scratch,
            1,
            3 + half,
        )(ids, *pieces, syh, syl)
        pieces = [swap(v, "gy", groups, k) for k, v in enumerate(pieces)]
        planes = f32((whole_planes, plan.rows_dev, plan.width))
        if chunk < plan.chunks - 1:
            ready.append(
                call(
                    functools.partial(backward_x, plan),
                    planes,
                    6 * count * plan.width,
                    8 * count + table_x,
                    (),
                    1,
                    3 + groups,
                )(ids, *pieces, sxh, sxl)
            )
    result = call(
        functools.partial(backward_last, plan),
        f32(field.shape),
        6 * count * plan.width,
        8 * field.size + table_x,
        [pltpu.VMEM(planes.shape, jnp.float32)],
        1,
        2 + groups + plan.chunks,
    )(ids, *pieces, sxh, sxl, *ready)
    return result[None]


def solution(mesh):
    spec = P("tm", None, "gy", None)

    def whole(residual):
        plan = Plan(mesh, residual.shape)
        plan.height = residual.shape[2]
        return jax.shard_map(
            functools.partial(on_device, plan),
            mesh=mesh,
            in_specs=(spec,),
            out_specs=spec,
            check_vma=False,
        )(residual)

    return whole
```

time: 290 us -> 136 us (0.47); the launches traced: 286 us -> 136 us
  blocking collectives: 81.1 us -> 0 us
  matrix products: 77.9 us -> 0 us
  starting transfers between devices: 11.3 us -> 53.6 us
  Pallas kernels: 0 us -> 33 us
  waiting for transfers between devices: 73.8 us -> 44.3 us
  local copies, waits for them, and re-layouts: 32.3 us -> 4.81 us
  other arithmetic: 9.44 us -> 0.07 us
    all_to_all x2 -> x0, blocking collectives: 81.1 us -> none  [the longest x1 51.8 us: on_device(): lax.all_to_all(timed, 'tm', split_axis=0, concat_axis=2, tiled=True)[0]]
    dot_general x10 -> x0, matrix products: 77.9 us -> none  [the longest x1 26.4 us: on_device(): across = jnp.einsum('ax,cyx->cay', sine_x, planes, precision=highest)]
    all_to_all x2 -> x0, waiting for transfers between devices: 73.8 us -> none  [the longest x1 47.5 us: on_device(): lax.all_to_all(hatted[None], 'tm', split_axis=2, concat_axis=0, tiled=True)]
    ppermute x0 -> x52, starting transfers between devices: none -> 53.6 us  [swap(): return lax.ppermute(values, axis, [(i, i ^ distance) for i in range(count)])]
    ppermute x0 -> x52, waiting for transfers between devices: none -> 44.3 us  [swap(): return lax.ppermute(values, axis, [(i, i ^ distance) for i in range(count)])]
    pallas_call x0 -> x24, Pallas kernels: none -> 33 us  [the longest x4 7.9 us: on_device(): call(functools.partial(forward_x, plan, chunk), [rows_in] * groups, 6 * c...]
    all_to_all x2 -> x0, starting transfers between devices: 11.3 us -> none  [the longest x1 6.84 us: on_device(): lax.all_to_all(hatted[None], 'tm', split_axis=2, concat_axis=0, tiled=True)]
    all_to_all x1 -> x0, other arithmetic: 9.01 us -> none  [on_device(): slab = lax.all_to_all(across, 'gy', split_axis=1, concat_axis=2, tiled=True)]
  transfers between devices with their start and end apart: 2 -> 52, of which waited for: 2 -> 20; matrix products, arithmetic and copies ran while one was open for 0% -> 0% of each run, Pallas kernels for 0% -> 20%
where the time goes in v1:
time: 136 us
  starting transfers between devices  53.6 us (39%)
  waiting for transfers between devices  44.3 us (33%)
  Pallas kernels  33 us (24%)
  local copies, waits for them, and re-layouts  4.81 us (4%)
    ppermute x52, starting transfers between devices, swap(): return lax.ppermute(values, axis, [(i, i ^ distance) for i in range(count)])  53.6 us
    ppermute x52, waiting for transfers between devices, swap(): return lax.ppermute(values, axis, [(i, i ^ distance) for i in range(count)])  44.3 us
    pallas_call x4, Pallas kernels, on_device(): call(functools.partial(forward_x, plan, chunk), [rows_in] * groups, 6 * c...  7.9 us
    unnamed x18, local copies, waits for them, and re-layouts  4.81 us
    pallas_call x4, Pallas kernels, on_device(): call(functools.partial(half_solve, plan, chunk), [modes] * half, 40 * cou...  4.71 us
    pallas_call x3, Pallas kernels, on_device(): call(functools.partial(backward_x, plan), planes, 6 * count * plan.width,...  4.59 us
    pallas_call x4, Pallas kernels, on_device(): call(functools.partial(transform_y, plan, 0, 1), [modes] * half, 6 * coun...  4.1 us
    pallas_call x1, Pallas kernels, on_device(): call(functools.partial(backward_last, plan), f32(field.shape), 6 * count...  4.02 us
  transfers between devices with their start and end apart: 52, of which 20 were waited for; matrix products, arithmetic and copies ran while one was open for 0% of the time, Pallas kernels for 20%

profile of v1, /device:TPU:0, one launch (start us, length us, event | category | flops | bytes accessed | tf_op | source)
XLA Modules:
  0.0 136.2 jit_solution(11923487667666842160)
XLA Ops:
  0.1 1.6 %copy-done = bf16[1024,1024]{1,0:T(8,128)(2,1)S(1)} copy-done((bf16[1024,1024]{1,0:T(8,128)(2,1)S(1)}, bf16[1024,1024]{1,0:T(8,128)(2,1)}, u32[]{:S(2)}) %copy-start) | copy-done | bytes 2097176
  1.7 1.6 %copy-done.2 = bf16[1024,1024]{1,0:T(8,128)(2,1)S(1)} copy-done((bf16[1024,1024]{1,0:T(8,128)(2,1)S(1)}, bf16[1024,1024]{1,0:T(8,128)(2,1)}, u32[]{:S(2)}) %copy-start.2) | copy-done | bytes 2097176
  3.3 1.6 %copy-done.3 = f32[1,8,64,1024]{3,2,1,0:T(8,128)S(1)} copy-done((f32[1,8,64,1024]{3,2,1,0:T(8,128)S(1)}, f32[1,8,64,1024]{3,2,1,0:T(8,128)}, u32[]{:S(2)}) %copy-start.3) | copy-done | bytes 2097176
  4.9 2.0 %shard_map.99 = (f32[2,64,256]{2,1,0:T(8,128)S(1)}, f32[2,64,256]{2,1,0:T(8,128)S(1)}, f32[2,64,256]{2,1,0:T(8,128)S(1)}, f32[2,64,256]{2,1,0:T(8,128)S(1)}) custom-call(s32[2]{0:T(128)S(1)} %pad_add_fusion.ids, f32[8,64,1024]{2,1,0:T(8,128)S(1)} %bitcast.4, bf16[1024,1024]{1,0:T(8,128)(2,1)S(1)} %copy-done.2, bf16[1024,1024]{1,0:T(8,128)(2,1)S(1)} %copy-done), custom_call_target="tpu_custom_call" | custom-call | flops 805306368 | bytes 6815744 | tf_op jit(solution)/shard_map/pallas_call | solution.py:324
  7.4 2.6 %collective-permute-start.40 = (f32[2,64,256]{2,1,0:T(8,128)S(1)}, f32[2,64,256]{2,1,0:T(8,128)S(1)}, u32[]{:S(2)}, u32[]{:S(2)}) collective-permute-start(f32[2,64,256]{2,1,0:T(8,128)S(1)} %get-tuple-element.119), channel_id=1, source_target_pairs={{0,2},{1,3},{2,0},{3,1},{4,6},{5,7},{6,4},{7,5},{8,10},{9,11},{10,... | collective-permute-start | bytes 393224 | tf_op jit(solution)/shard_map/ppermute | solution.py:296
  10.0 2.0 %shard_map.93 = (f32[2,64,256]{2,1,0:T(8,128)S(1)}, f32[2,64,256]{2,1,0:T(8,128)S(1)}, f32[2,64,256]{2,1,0:T(8,128)S(1)}, f32[2,64,256]{2,1,0:T(8,128)S(1)}) custom-call(s32[2]{0:T(128)S(1)} %pad_add_fusion.ids, f32[8,64,1024]{2,1,0:T(8,128)S(1)} %bitcast.5, bf16[1024,1024]{1,0:T(8,128)(2,1)S(1)} %copy-done.2, bf16[1024,1024]{1,0:T(8,128)(2,1)S(1)} %copy-done), custom_call_target="tpu_custom_call" | custom-call | flops 805306368 | bytes 6815744 | tf_op jit(solution)/shard_map/pallas_call | solution.py:324
  12.2 1.9 %collective-permute-start.27 = (f32[2,64,256]{2,1,0:T(8,128)S(1)}, f32[2,64,256]{2,1,0:T(8,128)S(1)}, u32[]{:S(2)}, u32[]{:S(2)}) collective-permute-start(f32[2,64,256]{2,1,0:T(8,128)S(1)} %get-tuple-element.103), channel_id=1, source_target_pairs={{0,2},{1,3},{2,0},{3,1},{4,6},{5,7},{6,4},{7,5},{8,10},{9,11},{10,... | collective-permute-start | bytes 393224 | tf_op jit(solution)/shard_map/ppermute | solution.py:296
  14.1 2.0 %shard_map.87 = (f32[2,64,256]{2,1,0:T(8,128)S(1)}, f32[2,64,256]{2,1,0:T(8,128)S(1)}, f32[2,64,256]{2,1,0:T(8,128)S(1)}, f32[2,64,256]{2,1,0:T(8,128)S(1)}) custom-call(s32[2]{0:T(128)S(1)} %pad_add_fusion.ids, f32[8,64,1024]{2,1,0:T(8,128)S(1)} %bitcast.6, bf16[1024,1024]{1,0:T(8,128)(2,1)S(1)} %copy-done.2, bf16[1024,1024]{1,0:T(8,128)(2,1)S(1)} %copy-done), custom_call_target="tpu_custom_call" | custom-call | flops 805306368 | bytes 6815744 | tf_op jit(solution)/shard_map/pallas_call | solution.py:324
  16.4 2.0 %shard_map.82 = (f32[2,64,256]{2,1,0:T(8,128)S(1)}, f32[2,64,256]{2,1,0:T(8,128)S(1)}, f32[2,64,256]{2,1,0:T(8,128)S(1)}, f32[2,64,256]{2,1,0:T(8,128)S(1)}) custom-call(s32[2]{0:T(128)S(1)} %pad_add_fusion.ids, f32[8,64,1024]{2,1,0:T(8,128)S(1)} %bitcast.7, bf16[1024,1024]{1,0:T(8,128)(2,1)S(1)} %copy-done.2, bf16[1024,1024]{1,0:T(8,128)(2,1)S(1)} %copy-done), custom_call_target="tpu_custom_call" | custom-call | flops 805306368 | bytes 6815744 | tf_op jit(solution)/shard_map/pallas_call | solution.py:324
  18.4 2.0 %collective-permute-start.14 = (f32[2,64,256]{2,1,0:T(8,128)S(1)}, f32[2,64,256]{2,1,0:T(8,128)S(1)}, u32[]{:S(2)}, u32[]{:S(2)}) collective-permute-start(f32[2,64,256]{2,1,0:T(8,128)S(1)} %get-tuple-element.87), channel_id=1, source_target_pairs={{0,2},{1,3},{2,0},{3,1},{4,6},{5,7},{6,4},{7,5},{8,10},{9,11},{10,... | collective-permute-start | bytes 393224 | tf_op jit(solution)/shard_map/ppermute | solution.py:296
  25.5 2.0 %collective-permute-start.42 = (f32[2,64,256]{2,1,0:T(8,128)S(1)}, f32[2,64,256]{2,1,0:T(8,128)S(1)}, u32[]{:S(2)}, u32[]{:S(2)}) collective-permute-start(f32[2,64,256]{2,1,0:T(8,128)S(1)} %get-tuple-element.122), channel_id=1, source_target_pairs={{0,4},{4,0},{8,12},{12,8},{16,20},{20,16},{24,28},{28,24},{1,5},{5... | collective-permute-start | bytes 393224 | tf_op jit(solution)/shard_map/ppermute | solution.py:296
  27.8 1.6 %collective-permute-start.43 = (f32[2,64,256]{2,1,0:T(8,128)S(1)}, f32[2,64,256]{2,1,0:T(8,128)S(1)}, u32[]{:S(2)}, u32[]{:S(2)}) collective-permute-start(f32[2,64,256]{2,1,0:T(8,128)S(1)} %get-tuple-element.123), channel_id=1, source_target_pairs={{0,8},{4,12},{8,0},{12,4},{16,24},{20,28},{24,16},{28,20},{1,9},{5... | collective-permute-start | bytes 393224 | tf_op jit(solution)/shard_map/ppermute | solution.py:296
  33.4 1.6 %collective-permute-start.30 = (f32[2,64,256]{2,1,0:T(8,128)S(1)}, f32[2,64,256]{2,1,0:T(8,128)S(1)}, u32[]{:S(2)}, u32[]{:S(2)}) collective-permute-start(f32[2,64,256]{2,1,0:T(8,128)S(1)} %get-tuple-element.107), channel_id=1, source_target_pairs={{0,8},{4,12},{8,0},{12,4},{16,24},{20,28},{24,16},{28,20},{1,9},{5... | collective-permute-start | bytes 393224 | tf_op jit(solution)/shard_map/ppermute | solution.py:296
  38.0 1.6 %collective-permute-start.17 = (f32[2,64,256]{2,1,0:T(8,128)S(1)}, f32[2,64,256]{2,1,0:T(8,128)S(1)}, u32[]{:S(2)}, u32[]{:S(2)}) collective-permute-start(f32[2,64,256]{2,1,0:T(8,128)S(1)} %get-tuple-element.91), channel_id=1, source_target_pairs={{0,8},{4,12},{8,0},{12,4},{16,24},{20,28},{24,16},{28,20},{1,9},{5... | collective-permute-start | bytes 393224 | tf_op jit(solution)/shard_map/ppermute | solution.py:296
  43.0 1.6 %collective-permute-start.3 = (f32[2,64,256]{2,1,0:T(8,128)S(1)}, f32[2,64,256]{2,1,0:T(8,128)S(1)}, u32[]{:S(2)}, u32[]{:S(2)}) collective-permute-start(f32[2,64,256]{2,1,0:T(8,128)S(1)} %get-tuple-element.74), channel_id=1, source_target_pairs={{0,4},{4,0},{8,12},{12,8},{16,20},{20,16},{24,28},{28,24},{1,5},{5... | collective-permute-start | bytes 393224 | tf_op jit(solution)/shard_map/ppermute | solution.py:296
  45.5 2.6 %collective-permute-start.45 = (f32[2,2,64,256]{3,2,1,0:T(8,128)S(1)}, f32[2,2,64,256]{3,2,1,0:T(8,128)S(1)}, u32[]{:S(2)}, u32[]{:S(2)}) collective-permute-start(f32[2,2,64,256]{3,2,1,0:T(8,128)S(1)} %shard_map.101.refs_4_), channel_id=1, source_target_pairs={{0,16},{4,20},{8,24},{12,28},{16,0},{20,4},{24,8},{28,12},{1,17},{... | collective-permute-start | bytes 786440 | tf_op jit(solution)/shard_map/ppermute | solution.py:296
  53.3 3.0 %collective-permute-start.19 = (f32[2,2,64,256]{3,2,1,0:T(8,128)S(1)}, f32[2,2,64,256]{3,2,1,0:T(8,128)S(1)}, u32[]{:S(2)}, u32[]{:S(2)}) collective-permute-start(f32[2,2,64,256]{3,2,1,0:T(8,128)S(1)} %shard_map.89.refs_4_), channel_id=1, source_target_pairs={{0,16},{4,20},{8,24},{12,28},{16,0},{20,4},{24,8},{28,12},{1,17},{... | collective-permute-start | bytes 786440 | tf_op jit(solution)/shard_map/ppermute | solution.py:296
  57.7 5.7 %collective-permute-done.5.refs_3_ = f32[2,64,256]{2,1,0:T(8,128)S(1)} collective-permute-done((f32[2,64,256]{2,1,0:T(8,128)S(1)}, f32[2,64,256]{2,1,0:T(8,128)S(1)}, u32[]{:S(2)}, u32[]{:S(2)}) %collective-permute-start.5) | collective-permute-done | bytes 131104 | tf_op jit(solution)/shard_map/ppermute | solution.py:296
  66.7 2.0 %collective-permute-start.47 = (f32[2,64,256]{2,1,0:T(8,128)S(1)}, f32[2,64,256]{2,1,0:T(8,128)S(1)}, u32[]{:S(2)}, u32[]{:S(2)}) collective-permute-start(f32[2,64,256]{2,1,0:T(8,128)S(1)} %get-tuple-element.127), channel_id=1, source_target_pairs={{0,8},{4,12},{8,0},{12,4},{16,24},{20,28},{24,16},{28,20},{1,9},{5... | collective-permute-start | bytes 393224 | tf_op jit(solution)/shard_map/ppermute | solution.py:296
  68.7 15.2 %collective-permute-done.32.refs_5_ = f32[2,2,64,256]{3,2,1,0:T(8,128)S(1)} collective-permute-done((f32[2,2,64,256]{3,2,1,0:T(8,128)S(1)}, f32[2,2,64,256]{3,2,1,0:T(8,128)S(1)}, u32[]{:S(2)}, u32[]{:S(2)}) %collective-permute-start.32) | collective-permute-done | bytes 262176 | tf_op jit(solution)/shard_map/ppermute | solution.py:296
  85.0 4.5 %collective-permute-done.19.refs_5_ = f32[2,2,64,256]{3,2,1,0:T(8,128)S(1)} collective-permute-done((f32[2,2,64,256]{3,2,1,0:T(8,128)S(1)}, f32[2,2,64,256]{3,2,1,0:T(8,128)S(1)}, u32[]{:S(2)}, u32[]{:S(2)}) %collective-permute-start.19) | collective-permute-done | bytes 262176 | tf_op jit(solution)/shard_map/ppermute | solution.py:296
  90.1 3.3 %collective-permute-done.6.refs_5_ = f32[2,2,64,256]{3,2,1,0:T(8,128)S(1)} collective-permute-done((f32[2,2,64,256]{3,2,1,0:T(8,128)S(1)}, f32[2,2,64,256]{3,2,1,0:T(8,128)S(1)}, u32[]{:S(2)}, u32[]{:S(2)}) %collective-permute-start.6) | collective-permute-done | bytes 262176 | tf_op jit(solution)/shard_map/ppermute | solution.py:296
  93.3 2.0 %collective-permute-start.35 = (f32[2,64,256]{2,1,0:T(8,128)S(1)}, f32[2,64,256]{2,1,0:T(8,128)S(1)}, u32[]{:S(2)}, u32[]{:S(2)}) collective-permute-start(f32[2,64,256]{2,1,0:T(8,128)S(1)} %get-tuple-element.112), channel_id=1, source_target_pairs={{0,12},{4,8},{8,4},{12,0},{16,28},{20,24},{24,20},{28,16},{1,13},{... | collective-permute-start | bytes 393224 | tf_op jit(solution)/shard_map/ppermute | solution.py:296
  96.4 1.6 %collective-permute-start.20 = (f32[2,64,256]{2,1,0:T(8,128)S(1)}, f32[2,64,256]{2,1,0:T(8,128)S(1)}, u32[]{:S(2)}, u32[]{:S(2)}) collective-permute-start(f32[2,64,256]{2,1,0:T(8,128)S(1)} %get-tuple-element.94), channel_id=1, source_target_pairs={{0,4},{4,0},{8,12},{12,8},{16,20},{20,16},{24,28},{28,24},{1,5},{5... | collective-permute-start | bytes 393224 | tf_op jit(solution)/shard_map/ppermute | solution.py:296
  98.0 2.0 %collective-permute-start.22 = (f32[2,64,256]{2,1,0:T(8,128)S(1)}, f32[2,64,256]{2,1,0:T(8,128)S(1)}, u32[]{:S(2)}, u32[]{:S(2)}) collective-permute-start(f32[2,64,256]{2,1,0:T(8,128)S(1)} %get-tuple-element.96), channel_id=1, source_target_pairs={{0,12},{4,8},{8,4},{12,0},{16,28},{20,24},{24,20},{28,16},{1,13},{... | collective-permute-start | bytes 393224 | tf_op jit(solution)/shard_map/ppermute | solution.py:296
  101.3 1.6 %collective-permute-start.7 = (f32[2,64,256]{2,1,0:T(8,128)S(1)}, f32[2,64,256]{2,1,0:T(8,128)S(1)}, u32[]{:S(2)}, u32[]{:S(2)}) collective-permute-start(f32[2,64,256]{2,1,0:T(8,128)S(1)} %get-tuple-element.78), channel_id=1, source_target_pairs={{0,4},{4,0},{8,12},{12,8},{16,20},{20,16},{24,28},{28,24},{1,5},{5... | collective-permute-start | bytes 393224 | tf_op jit(solution)/shard_map/ppermute | solution.py:296
  104.0 2.5 %collective-permute-start.9 = (f32[2,64,256]{2,1,0:T(8,128)S(1)}, f32[2,64,256]{2,1,0:T(8,128)S(1)}, u32[]{:S(2)}, u32[]{:S(2)}) collective-permute-start(f32[2,64,256]{2,1,0:T(8,128)S(1)} %get-tuple-element.80), channel_id=1, source_target_pairs={{0,12},{4,8},{8,4},{12,0},{16,28},{20,24},{24,20},{28,16},{1,13},{... | collective-permute-start | bytes 393224 | tf_op jit(solution)/shard_map/ppermute | solution.py:296
  106.6 1.6 %collective-permute-done.22.refs_3_ = f32[2,64,256]{2,1,0:T(8,128)S(1)} collective-permute-done((f32[2,64,256]{2,1,0:T(8,128)S(1)}, f32[2,64,256]{2,1,0:T(8,128)S(1)}, u32[]{:S(2)}, u32[]{:S(2)}) %collective-permute-start.22) | collective-permute-done | bytes 131104 | tf_op jit(solution)/shard_map/ppermute | solution.py:296
  125.0 1.8 %collective-permute-done.25.refs_3_ = f32[2,64,256]{2,1,0:T(8,128)S(1)} collective-permute-done((f32[2,64,256]{2,1,0:T(8,128)S(1)}, f32[2,64,256]{2,1,0:T(8,128)S(1)}, u32[]{:S(2)}, u32[]{:S(2)}) %collective-permute-start.25) | collective-permute-done | bytes 131104 | tf_op jit(solution)/shard_map/ppermute | solution.py:296
  128.3 2.2 %collective-permute-done.11.refs_2_ = f32[2,64,256]{2,1,0:T(8,128)S(1)} collective-permute-done((f32[2,64,256]{2,1,0:T(8,128)S(1)}, f32[2,64,256]{2,1,0:T(8,128)S(1)}, u32[]{:S(2)}, u32[]{:S(2)}) %collective-permute-start.11) | collective-permute-done | bytes 131104 | tf_op jit(solution)/shard_map/ppermute | solution.py:296
  130.6 1.6 %collective-permute-done.12.refs_3_ = f32[2,64,256]{2,1,0:T(8,128)S(1)} collective-permute-done((f32[2,64,256]{2,1,0:T(8,128)S(1)}, f32[2,64,256]{2,1,0:T(8,128)S(1)}, u32[]{:S(2)}, u32[]{:S(2)}) %collective-permute-start.12) | collective-permute-done | bytes 131104 | tf_op jit(solution)/shard_map/ppermute | solution.py:296
  132.2 4.0 %shard_map.105 = f32[8,64,1024]{2,1,0:T(8,128)} custom-call(s32[2]{0:T(128)S(1)} %pad_add_fusion.ids, f32[2,64,256]{2,1,0:T(8,128)S(1)} %get-tuple-element.81.refs_0_, f32[2,64,256]{2,1,0:T(8,128)S(1)} %collective-permute-done.10.refs_1_, f32[2,64,256]{2,1,0:T(8,128)S(1)} %collective-permute-done.11.refs_2_, ...), custom_call_target="tpu_custom_call" | custom-call | flops 805306368 | bytes 8388608 | tf_op jit(solution)/shard_map/pallas_call | solution.py:387
  (115 shorter events, 50.9 us)
Async XLA Ops:
  6.8 9.3 %collective-permute-start.39 = (f32[2,64,256]{2,1,0:T(8,128)S(1)}, f32[2,64,256]{2,1,0:T(8,128)S(1)}, u32[]{:S(2)}, u32[]{:S(2)}) collective-permute-start(f32[2,64,256]{2,1,0:T(8,128)S(1)} %get-tuple-element.118), channel_id=1, source_target_pairs={{0,1},{1,0},{2,3},{3,2},{4,5},{5,4},{6,7},{7,6},{8,9},{9,8},{10,11... | collective-permute-start | bytes 393224 | tf_op jit(solution)/shard_map/ppermute | solution.py:296
  7.4 8.8 %collective-permute-start.40 = (f32[2,64,256]{2,1,0:T(8,128)S(1)}, f32[2,64,256]{2,1,0:T(8,128)S(1)}, u32[]{:S(2)}, u32[]{:S(2)}) collective-permute-start(f32[2,64,256]{2,1,0:T(8,128)S(1)} %get-tuple-element.119), channel_id=1, source_target_pairs={{0,2},{1,3},{2,0},{3,1},{4,6},{5,7},{6,4},{7,5},{8,10},{9,11},{10,... | collective-permute-start | bytes 393224 | tf_op jit(solution)/shard_map/ppermute | solution.py:296
  20.4 9.0 %collective-permute-start = (f32[2,64,256]{2,1,0:T(8,128)S(1)}, f32[2,64,256]{2,1,0:T(8,128)S(1)}, u32[]{:S(2)}, u32[]{:S(2)}) collective-permute-start(f32[2,64,256]{2,1,0:T(8,128)S(1)} %get-tuple-element.70), channel_id=1, source_target_pairs={{0,1},{1,0},{2,3},{3,2},{4,5},{5,4},{6,7},{7,6},{8,9},{9,8},{10,11... | collective-permute-start | bytes 393224 | tf_op jit(solution)/shard_map/ppermute | solution.py:296
  22.2 9.7 %collective-permute-start.1 = (f32[2,64,256]{2,1,0:T(8,128)S(1)}, f32[2,64,256]{2,1,0:T(8,128)S(1)}, u32[]{:S(2)}, u32[]{:S(2)}) collective-permute-start(f32[2,64,256]{2,1,0:T(8,128)S(1)} %get-tuple-element.71), channel_id=1, source_target_pairs={{0,2},{1,3},{2,0},{3,1},{4,6},{5,7},{6,4},{7,5},{8,10},{9,11},{10,... | collective-permute-start | bytes 393224 | tf_op jit(solution)/shard_map/ppermute | solution.py:296
  23.7 9.7 %collective-permute-start.2 = (f32[2,64,256]{2,1,0:T(8,128)S(1)}, f32[2,64,256]{2,1,0:T(8,128)S(1)}, u32[]{:S(2)}, u32[]{:S(2)}) collective-permute-start(f32[2,64,256]{2,1,0:T(8,128)S(1)} %get-tuple-element.72), channel_id=1, source_target_pairs={{0,3},{1,2},{2,1},{3,0},{4,7},{5,6},{6,5},{7,4},{8,11},{9,10},{10,... | collective-permute-start | bytes 393224 | tf_op jit(solution)/shard_map/ppermute | solution.py:296
  25.5 10.6 %collective-permute-start.42 = (f32[2,64,256]{2,1,0:T(8,128)S(1)}, f32[2,64,256]{2,1,0:T(8,128)S(1)}, u32[]{:S(2)}, u32[]{:S(2)}) collective-permute-start(f32[2,64,256]{2,1,0:T(8,128)S(1)} %get-tuple-element.122), channel_id=1, source_target_pairs={{0,4},{4,0},{8,12},{12,8},{16,20},{20,16},{24,28},{28,24},{1,5},{5... | collective-permute-start | bytes 393224 | tf_op jit(solution)/shard_map/ppermute | solution.py:296
  27.8 9.8 %collective-permute-start.43 = (f32[2,64,256]{2,1,0:T(8,128)S(1)}, f32[2,64,256]{2,1,0:T(8,128)S(1)}, u32[]{:S(2)}, u32[]{:S(2)}) collective-permute-start(f32[2,64,256]{2,1,0:T(8,128)S(1)} %get-tuple-element.123), channel_id=1, source_target_pairs={{0,8},{4,12},{8,0},{12,4},{16,24},{20,28},{24,16},{28,20},{1,9},{5... | collective-permute-start | bytes 393224 | tf_op jit(solution)/shard_map/ppermute | solution.py:296
  29.4 8.6 %collective-permute-start.44 = (f32[2,64,256]{2,1,0:T(8,128)S(1)}, f32[2,64,256]{2,1,0:T(8,128)S(1)}, u32[]{:S(2)}, u32[]{:S(2)}) collective-permute-start(f32[2,64,256]{2,1,0:T(8,128)S(1)} %get-tuple-element.124), channel_id=1, source_target_pairs={{0,12},{4,8},{8,4},{12,0},{16,28},{20,24},{24,20},{28,16},{1,13},{... | collective-permute-start | bytes 393224 | tf_op jit(solution)/shard_map/ppermute | solution.py:296
  33.4 9.6 %collective-permute-start.30 = (f32[2,64,256]{2,1,0:T(8,128)S(1)}, f32[2,64,256]{2,1,0:T(8,128)S(1)}, u32[]{:S(2)}, u32[]{:S(2)}) collective-permute-start(f32[2,64,256]{2,1,0:T(8,128)S(1)} %get-tuple-element.107), channel_id=1, source_target_pairs={{0,8},{4,12},{8,0},{12,4},{16,24},{20,28},{24,16},{28,20},{1,9},{5... | collective-permute-start | bytes 393224 | tf_op jit(solution)/shard_map/ppermute | solution.py:296
  36.1 9.4 %collective-permute-start.31 = (f32[2,64,256]{2,1,0:T(8,128)S(1)}, f32[2,64,256]{2,1,0:T(8,128)S(1)}, u32[]{:S(2)}, u32[]{:S(2)}) collective-permute-start(f32[2,64,256]{2,1,0:T(8,128)S(1)} %get-tuple-element.108), channel_id=1, source_target_pairs={{0,12},{4,8},{8,4},{12,0},{16,28},{20,24},{24,20},{28,16},{1,13},{... | collective-permute-start | bytes 393224 | tf_op jit(solution)/shard_map/ppermute | solution.py:296
  37.6 10.6 %collective-permute-start.16 = (f32[2,64,256]{2,1,0:T(8,128)S(1)}, f32[2,64,256]{2,1,0:T(8,128)S(1)}, u32[]{:S(2)}, u32[]{:S(2)}) collective-permute-start(f32[2,64,256]{2,1,0:T(8,128)S(1)} %get-tuple-element.90), channel_id=1, source_target_pairs={{0,4},{4,0},{8,12},{12,8},{16,20},{20,16},{24,28},{28,24},{1,5},{5... | collective-permute-start | bytes 393224 | tf_op jit(solution)/shard_map/ppermute | solution.py:296
  38.0 10.6 %collective-permute-start.17 = (f32[2,64,256]{2,1,0:T(8,128)S(1)}, f32[2,64,256]{2,1,0:T(8,128)S(1)}, u32[]{:S(2)}, u32[]{:S(2)}) collective-permute-start(f32[2,64,256]{2,1,0:T(8,128)S(1)} %get-tuple-element.91), channel_id=1, source_target_pairs={{0,8},{4,12},{8,0},{12,4},{16,24},{20,28},{24,16},{28,20},{1,9},{5... | collective-permute-start | bytes 393224 | tf_op jit(solution)/shard_map/ppermute | solution.py:296
  40.4 12.0 %collective-permute-start.18 = (f32[2,64,256]{2,1,0:T(8,128)S(1)}, f32[2,64,256]{2,1,0:T(8,128)S(1)}, u32[]{:S(2)}, u32[]{:S(2)}) collective-permute-start(f32[2,64,256]{2,1,0:T(8,128)S(1)} %get-tuple-element.92), channel_id=1, source_target_pairs={{0,12},{4,8},{8,4},{12,0},{16,28},{20,24},{24,20},{28,16},{1,13},{... | collective-permute-start | bytes 393224 | tf_op jit(solution)/shard_map/ppermute | solution.py:296
  43.0 10.3 %collective-permute-start.3 = (f32[2,64,256]{2,1,0:T(8,128)S(1)}, f32[2,64,256]{2,1,0:T(8,128)S(1)}, u32[]{:S(2)}, u32[]{:S(2)}) collective-permute-start(f32[2,64,256]{2,1,0:T(8,128)S(1)} %get-tuple-element.74), channel_id=1, source_target_pairs={{0,4},{4,0},{8,12},{12,8},{16,20},{20,16},{24,28},{28,24},{1,5},{5... | collective-permute-start | bytes 393224 | tf_op jit(solution)/shard_map/ppermute | solution.py:296
  45.5 18.9 %collective-permute-start.45 = (f32[2,2,64,256]{3,2,1,0:T(8,128)S(1)}, f32[2,2,64,256]{3,2,1,0:T(8,128)S(1)}, u32[]{:S(2)}, u32[]{:S(2)}) collective-permute-start(f32[2,2,64,256]{3,2,1,0:T(8,128)S(1)} %shard_map.101.refs_4_), channel_id=1, source_target_pairs={{0,16},{4,20},{8,24},{12,28},{16,0},{20,4},{24,8},{28,12},{1,17},{... | collective-permute-start | bytes 786440 | tf_op jit(solution)/shard_map/ppermute | solution.py:296
  48.1 9.6 %collective-permute-start.4 = (f32[2,64,256]{2,1,0:T(8,128)S(1)}, f32[2,64,256]{2,1,0:T(8,128)S(1)}, u32[]{:S(2)}, u32[]{:S(2)}) collective-permute-start(f32[2,64,256]{2,1,0:T(8,128)S(1)} %get-tuple-element.75), channel_id=1, source_target_pairs={{0,8},{4,12},{8,0},{12,4},{16,24},{20,28},{24,16},{28,20},{1,9},{5... | collective-permute-start | bytes 393224 | tf_op jit(solution)/shard_map/ppermute | solution.py:296
  48.6 14.8 %collective-permute-start.5 = (f32[2,64,256]{2,1,0:T(8,128)S(1)}, f32[2,64,256]{2,1,0:T(8,128)S(1)}, u32[]{:S(2)}, u32[]{:S(2)}) collective-permute-start(f32[2,64,256]{2,1,0:T(8,128)S(1)} %get-tuple-element.76), channel_id=1, source_target_pairs={{0,12},{4,8},{8,4},{12,0},{16,28},{20,24},{24,20},{28,16},{1,13},{... | collective-permute-start | bytes 393224 | tf_op jit(solution)/shard_map/ppermute | solution.py:296
  52.4 31.5 %collective-permute-start.32 = (f32[2,2,64,256]{3,2,1,0:T(8,128)S(1)}, f32[2,2,64,256]{3,2,1,0:T(8,128)S(1)}, u32[]{:S(2)}, u32[]{:S(2)}) collective-permute-start(f32[2,2,64,256]{3,2,1,0:T(8,128)S(1)} %shard_map.95.refs_4_), channel_id=1, source_target_pairs={{0,16},{4,20},{8,24},{12,28},{16,0},{20,4},{24,8},{28,12},{1,17},{... | collective-permute-start | bytes 786440 | tf_op jit(solution)/shard_map/ppermute | solution.py:296
  53.3 36.2 %collective-permute-start.19 = (f32[2,2,64,256]{3,2,1,0:T(8,128)S(1)}, f32[2,2,64,256]{3,2,1,0:T(8,128)S(1)}, u32[]{:S(2)}, u32[]{:S(2)}) collective-permute-start(f32[2,2,64,256]{3,2,1,0:T(8,128)S(1)} %shard_map.89.refs_4_), channel_id=1, source_target_pairs={{0,16},{4,20},{8,24},{12,28},{16,0},{20,4},{24,8},{28,12},{1,17},{... | collective-permute-start | bytes 786440 | tf_op jit(solution)/shard_map/ppermute | solution.py:296
  64.3 29.0 %collective-permute-start.6 = (f32[2,2,64,256]{3,2,1,0:T(8,128)S(1)}, f32[2,2,64,256]{3,2,1,0:T(8,128)S(1)}, u32[]{:S(2)}, u32[]{:S(2)}) collective-permute-start(f32[2,2,64,256]{3,2,1,0:T(8,128)S(1)} %shard_map.84.refs_4_), channel_id=1, source_target_pairs={{0,16},{4,20},{8,24},{12,28},{16,0},{20,4},{24,8},{28,12},{1,17},{... | collective-permute-start | bytes 786440 | tf_op jit(solution)/shard_map/ppermute | solution.py:296
  65.6 27.7 %collective-permute-start.46 = (f32[2,64,256]{2,1,0:T(8,128)S(1)}, f32[2,64,256]{2,1,0:T(8,128)S(1)}, u32[]{:S(2)}, u32[]{:S(2)}) collective-permute-start(f32[2,64,256]{2,1,0:T(8,128)S(1)} %get-tuple-element.126), channel_id=1, source_target_pairs={{0,4},{4,0},{8,12},{12,8},{16,20},{20,16},{24,28},{28,24},{1,5},{5... | collective-permute-start | bytes 393224 | tf_op jit(solution)/shard_map/ppermute | solution.py:296
  66.7 29.8 %collective-permute-start.47 = (f32[2,64,256]{2,1,0:T(8,128)S(1)}, f32[2,64,256]{2,1,0:T(8,128)S(1)}, u32[]{:S(2)}, u32[]{:S(2)}) collective-permute-start(f32[2,64,256]{2,1,0:T(8,128)S(1)} %get-tuple-element.127), channel_id=1, source_target_pairs={{0,8},{4,12},{8,0},{12,4},{16,24},{20,28},{24,16},{28,20},{1,9},{5... | collective-permute-start | bytes 393224 | tf_op jit(solution)/shard_map/ppermute | solution.py:296
  83.9 14.1 %collective-permute-start.48 = (f32[2,64,256]{2,1,0:T(8,128)S(1)}, f32[2,64,256]{2,1,0:T(8,128)S(1)}, u32[]{:S(2)}, u32[]{:S(2)}) collective-permute-start(f32[2,64,256]{2,1,0:T(8,128)S(1)} %get-tuple-element.128), channel_id=1, source_target_pairs={{0,12},{4,8},{8,4},{12,0},{16,28},{20,24},{24,20},{28,16},{1,13},{... | collective-permute-start | bytes 393224 | tf_op jit(solution)/shard_map/ppermute | solution.py:296
  93.3 9.6 %collective-permute-start.35 = (f32[2,64,256]{2,1,0:T(8,128)S(1)}, f32[2,64,256]{2,1,0:T(8,128)S(1)}, u32[]{:S(2)}, u32[]{:S(2)}) collective-permute-start(f32[2,64,256]{2,1,0:T(8,128)S(1)} %get-tuple-element.112), channel_id=1, source_target_pairs={{0,12},{4,8},{8,4},{12,0},{16,28},{20,24},{24,20},{28,16},{1,13},{... | collective-permute-start | bytes 393224 | tf_op jit(solution)/shard_map/ppermute | solution.py:296
  98.0 10.1 %collective-permute-start.22 = (f32[2,64,256]{2,1,0:T(8,128)S(1)}, f32[2,64,256]{2,1,0:T(8,128)S(1)}, u32[]{:S(2)}, u32[]{:S(2)}) collective-permute-start(f32[2,64,256]{2,1,0:T(8,128)S(1)} %get-tuple-element.96), channel_id=1, source_target_pairs={{0,12},{4,8},{8,4},{12,0},{16,28},{20,24},{24,20},{28,16},{1,13},{... | collective-permute-start | bytes 393224 | tf_op jit(solution)/shard_map/ppermute | solution.py:296
  101.3 9.3 %collective-permute-start.7 = (f32[2,64,256]{2,1,0:T(8,128)S(1)}, f32[2,64,256]{2,1,0:T(8,128)S(1)}, u32[]{:S(2)}, u32[]{:S(2)}) collective-permute-start(f32[2,64,256]{2,1,0:T(8,128)S(1)} %get-tuple-element.78), channel_id=1, source_target_pairs={{0,4},{4,0},{8,12},{12,8},{16,20},{20,16},{24,28},{28,24},{1,5},{5... | collective-permute-start | bytes 393224 | tf_op jit(solution)/shard_map/ppermute | solution.py:296
  104.0 8.9 %collective-permute-start.9 = (f32[2,64,256]{2,1,0:T(8,128)S(1)}, f32[2,64,256]{2,1,0:T(8,128)S(1)}, u32[]{:S(2)}, u32[]{:S(2)}) collective-permute-start(f32[2,64,256]{2,1,0:T(8,128)S(1)} %get-tuple-element.80), channel_id=1, source_target_pairs={{0,12},{4,8},{8,4},{12,0},{16,28},{20,24},{24,20},{28,16},{1,13},{... | collective-permute-start | bytes 393224 | tf_op jit(solution)/shard_map/ppermute | solution.py:296
  116.1 8.9 %collective-permute-start.24 = (f32[2,64,256]{2,1,0:T(8,128)S(1)}, f32[2,64,256]{2,1,0:T(8,128)S(1)}, u32[]{:S(2)}, u32[]{:S(2)}) collective-permute-start(f32[2,64,256]{2,1,0:T(8,128)S(1)} %get-tuple-element.99), channel_id=1, source_target_pairs={{0,2},{1,3},{2,0},{3,1},{4,6},{5,7},{6,4},{7,5},{8,10},{9,11},{10,... | collective-permute-start | bytes 393224 | tf_op jit(solution)/shard_map/ppermute | solution.py:296
  117.6 9.1 %collective-permute-start.25 = (f32[2,64,256]{2,1,0:T(8,128)S(1)}, f32[2,64,256]{2,1,0:T(8,128)S(1)}, u32[]{:S(2)}, u32[]{:S(2)}) collective-permute-start(f32[2,64,256]{2,1,0:T(8,128)S(1)} %get-tuple-element.100), channel_id=1, source_target_pairs={{0,3},{1,2},{2,1},{3,0},{4,7},{5,6},{6,5},{7,4},{8,11},{9,10},{10,... | collective-permute-start | bytes 393224 | tf_op jit(solution)/shard_map/ppermute | solution.py:296
  119.3 9.0 %collective-permute-start.10 = (f32[2,64,256]{2,1,0:T(8,128)S(1)}, f32[2,64,256]{2,1,0:T(8,128)S(1)}, u32[]{:S(2)}, u32[]{:S(2)}) collective-permute-start(f32[2,64,256]{2,1,0:T(8,128)S(1)} %get-tuple-element.82), channel_id=1, source_target_pairs={{0,1},{1,0},{2,3},{3,2},{4,5},{5,4},{6,7},{7,6},{8,9},{9,8},{10,11... | collective-permute-start | bytes 393224 | tf_op jit(solution)/shard_map/ppermute | solution.py:296
  121.2 9.4 %collective-permute-start.11 = (f32[2,64,256]{2,1,0:T(8,128)S(1)}, f32[2,64,256]{2,1,0:T(8,128)S(1)}, u32[]{:S(2)}, u32[]{:S(2)}) collective-permute-start(f32[2,64,256]{2,1,0:T(8,128)S(1)} %get-tuple-element.83), channel_id=1, source_target_pairs={{0,2},{1,3},{2,0},{3,1},{4,6},{5,7},{6,4},{7,5},{8,10},{9,11},{10,... | collective-permute-start | bytes 393224 | tf_op jit(solution)/shard_map/ppermute | solution.py:296
  122.5 9.7 %collective-permute-start.12 = (f32[2,64,256]{2,1,0:T(8,128)S(1)}, f32[2,64,256]{2,1,0:T(8,128)S(1)}, u32[]{:S(2)}, u32[]{:S(2)}) collective-permute-start(f32[2,64,256]{2,1,0:T(8,128)S(1)} %get-tuple-element.84), channel_id=1, source_target_pairs={{0,3},{1,2},{2,1},{3,0},{4,7},{5,6},{6,5},{7,4},{8,11},{9,10},{10,... | collective-permute-start | bytes 393224 | tf_op jit(solution)/shard_map/ppermute | solution.py:296
  (29 other events, 268.5 us)

commit v2 on v1

--- a/solution.py
+++ b/solution.py
@@ -11,7 +11,7 @@
 
 ALPHA_RATIO = 0.95
 STEP_SCALE = 0.26
-CHUNKS = 4
+CHUNKS = 2
 LANES = 128
 VMEM_BYTES = 40 * 1024 * 1024
 

time: 136 us -> 134 us (0.985)
  waiting for transfers between devices: 44.3 us -> 78 us
  starting transfers between devices: 53.6 us -> 27 us
  Pallas kernels: 33 us -> 23.5 us
    ppermute x52 -> x26, waiting for transfers between devices: 44.3 us -> 78 us  [swap(): return lax.ppermute(values, axis, [(i, i ^ distance) for i in range(count)])]
    ppermute x52 -> x26, starting transfers between devices: 53.6 us -> 27 us  [swap(): return lax.ppermute(values, axis, [(i, i ^ distance) for i in range(count)])]
    pallas_call x3 -> x1, Pallas kernels: 4.59 us -> 2.33 us  [on_device(): call(functools.partial(backward_x, plan), planes, 6 * count * plan.width,...]
    pallas_call x4 -> x2, Pallas kernels: 4.71 us -> 2.91 us  [on_device(): call(functools.partial(half_solve, plan, chunk), [modes] * half, 40 * cou...]
    pallas_call x4 -> x2, Pallas kernels: 3.64 us -> 1.92 us  [on_device(): call(functools.partial(half_end, plan, chunk), ends, 8 * count, 6 * count...]
    pallas_call x4 -> x2, Pallas kernels: 7.9 us -> 6.25 us  [on_device(): call(functools.partial(forward_x, plan, chunk), [rows_in] * groups, 6 * c...]
    pallas_call x4 -> x2, Pallas kernels: 4.1 us -> 2.64 us  [on_device(): call(functools.partial(transform_y, plan, 0, 1), [modes] * half, 6 * coun...]
    pallas_call x4 -> x2, Pallas kernels: 3.99 us -> 2.64 us  [on_device(): call(functools.partial(transform_y, plan, 1, 0), [rows_in] * groups, 6 *...]
  transfers between devices with their start and end apart: 52 -> 26, of which waited for: 20 -> 17; matrix products, arithmetic and copies ran while one was open for 0% -> 0% of each run, Pallas kernels for 20% -> 12%
where the time goes in v2:
time: 134 us; the launch traced here: 133 us
  waiting for transfers between devices  78 us (58%)
  starting transfers between devices  27 us (20%)
  Pallas kernels  23.5 us (18%)
  local copies, waits for them, and re-layouts  4.81 us (4%)
    ppermute x26, waiting for transfers between devices, swap(): return lax.ppermute(values, axis, [(i, i ^ distance) for i in range(count)])  78 us
    ppermute x26, starting transfers between devices, swap(): return lax.ppermute(values, axis, [(i, i ^ distance) for i in range(count)])  27 us
    pallas_call x2, Pallas kernels, on_device(): call(functools.partial(forward_x, plan, chunk), [rows_in] * groups, 6 * c...  6.25 us
    pallas_call x1, Pallas kernels, on_device(): call(functools.partial(backward_last, plan), f32(field.shape), 6 * count...  4.82 us
    unnamed x20, local copies, waits for them, and re-layouts  4.81 us
    pallas_call x2, Pallas kernels, on_device(): call(functools.partial(half_solve, plan, chunk), [modes] * half, 40 * cou...  2.91 us
  transfers between devices with their start and end apart: 26, of which 17 were waited for; matrix products, arithmetic and copies ran while one was open for 0% of the time, Pallas kernels for 12%

profile of v2, /device:TPU:0, one launch (start us, length us, event | category | flops | bytes accessed | tf_op | source)
XLA Modules:
  0.0 133.5 jit_solution(8425622680368117891)
XLA Ops:
  0.1 1.6 %copy-done = bf16[1024,1024]{1,0:T(8,128)(2,1)S(1)} copy-done((bf16[1024,1024]{1,0:T(8,128)(2,1)S(1)}, bf16[1024,1024]{1,0:T(8,128)(2,1)}, u32[]{:S(2)}) %copy-start) | copy-done | bytes 2097176
  1.7 1.6 %copy-done.2 = bf16[1024,1024]{1,0:T(8,128)(2,1)S(1)} copy-done((bf16[1024,1024]{1,0:T(8,128)(2,1)S(1)}, bf16[1024,1024]{1,0:T(8,128)(2,1)}, u32[]{:S(2)}) %copy-start.2) | copy-done | bytes 2097176
  3.3 1.6 %copy-done.4 = f32[1,8,64,1024]{3,2,1,0:T(8,128)S(1)} copy-done((f32[1,8,64,1024]{3,2,1,0:T(8,128)S(1)}, f32[1,8,64,1024]{3,2,1,0:T(8,128)}, u32[]{:S(2)}) %copy-start.4) | copy-done | bytes 2097176
  4.9 3.1 %shard_map.87 = (f32[4,64,256]{2,1,0:T(8,128)S(1)}, f32[4,64,256]{2,1,0:T(8,128)S(1)}, f32[4,64,256]{2,1,0:T(8,128)S(1)}, f32[4,64,256]{2,1,0:T(8,128)S(1)}) custom-call(s32[2]{0:T(128)S(1)} %pad_add_fusion.ids, f32[8,64,1024]{2,1,0:T(8,128)S(1)} %bitcast.4, bf16[1024,1024]{1,0:T(8,128)(2,1)S(1)} %copy-done.2, bf16[1024,1024]{1,0:T(8,128)(2,1)S(1)} %copy-done), custom_call_target="tpu_custom_call" | custom-call | flops 1610612736 | bytes 7340032 | tf_op jit(solution)/shard_map/pallas_call | solution.py:324
  8.5 2.6 %collective-permute-start.14 = (f32[4,64,256]{2,1,0:T(8,128)S(1)}, f32[4,64,256]{2,1,0:T(8,128)S(1)}, u32[]{:S(2)}, u32[]{:S(2)}) collective-permute-start(f32[4,64,256]{2,1,0:T(8,128)S(1)} %get-tuple-element.55), channel_id=1, source_target_pairs={{0,2},{1,3},{2,0},{3,1},{4,6},{5,7},{6,4},{7,5},{8,10},{9,11},{10,... | collective-permute-start | bytes 786440 | tf_op jit(solution)/shard_map/ppermute | solution.py:296
  11.1 3.1 %shard_map.82 = (f32[4,64,256]{2,1,0:T(8,128)S(1)}, f32[4,64,256]{2,1,0:T(8,128)S(1)}, f32[4,64,256]{2,1,0:T(8,128)S(1)}, f32[4,64,256]{2,1,0:T(8,128)S(1)}) custom-call(s32[2]{0:T(128)S(1)} %pad_add_fusion.ids, f32[8,64,1024]{2,1,0:T(8,128)S(1)} %bitcast.5, bf16[1024,1024]{1,0:T(8,128)(2,1)S(1)} %copy-done.2, bf16[1024,1024]{1,0:T(8,128)(2,1)S(1)} %copy-done), custom_call_target="tpu_custom_call" | custom-call | flops 1610612736 | bytes 7340032 | tf_op jit(solution)/shard_map/pallas_call | solution.py:324
  14.5 1.9 %collective-permute-start.1 = (f32[4,64,256]{2,1,0:T(8,128)S(1)}, f32[4,64,256]{2,1,0:T(8,128)S(1)}, u32[]{:S(2)}, u32[]{:S(2)}) collective-permute-start(f32[4,64,256]{2,1,0:T(8,128)S(1)} %get-tuple-element.39), channel_id=1, source_target_pairs={{0,2},{1,3},{2,0},{3,1},{4,6},{5,7},{6,4},{7,5},{8,10},{9,11},{10,... | collective-permute-start | bytes 786440 | tf_op jit(solution)/shard_map/ppermute | solution.py:296
  16.5 1.8 %collective-permute-done.14.refs_2_ = f32[4,64,256]{2,1,0:T(8,128)S(1)} collective-permute-done((f32[4,64,256]{2,1,0:T(8,128)S(1)}, f32[4,64,256]{2,1,0:T(8,128)S(1)}, u32[]{:S(2)}, u32[]{:S(2)}) %collective-permute-start.14) | collective-permute-done | bytes 262176 | tf_op jit(solution)/shard_map/ppermute | solution.py:296
  18.2 5.1 %collective-permute-done.15.refs_3_ = f32[4,64,256]{2,1,0:T(8,128)S(1)} collective-permute-done((f32[4,64,256]{2,1,0:T(8,128)S(1)}, f32[4,64,256]{2,1,0:T(8,128)S(1)}, u32[]{:S(2)}, u32[]{:S(2)}) %collective-permute-start.15) | collective-permute-done | bytes 262176 | tf_op jit(solution)/shard_map/ppermute | solution.py:296
  24.6 1.7 %collective-permute-start.16 = (f32[4,64,256]{2,1,0:T(8,128)S(1)}, f32[4,64,256]{2,1,0:T(8,128)S(1)}, u32[]{:S(2)}, u32[]{:S(2)}) collective-permute-start(f32[4,64,256]{2,1,0:T(8,128)S(1)} %get-tuple-element.58), channel_id=1, source_target_pairs={{0,4},{4,0},{8,12},{12,8},{16,20},{20,16},{24,28},{28,24},{1,5},{5... | collective-permute-start | bytes 786440 | tf_op jit(solution)/shard_map/ppermute | solution.py:296
  26.3 1.6 %collective-permute-start.17 = (f32[4,64,256]{2,1,0:T(8,128)S(1)}, f32[4,64,256]{2,1,0:T(8,128)S(1)}, u32[]{:S(2)}, u32[]{:S(2)}) collective-permute-start(f32[4,64,256]{2,1,0:T(8,128)S(1)} %get-tuple-element.59), channel_id=1, source_target_pairs={{0,8},{4,12},{8,0},{12,4},{16,24},{20,28},{24,16},{28,20},{1,9},{5... | collective-permute-start | bytes 786440 | tf_op jit(solution)/shard_map/ppermute | solution.py:296
  29.4 5.1 %collective-permute-done.2.refs_3_ = f32[4,64,256]{2,1,0:T(8,128)S(1)} collective-permute-done((f32[4,64,256]{2,1,0:T(8,128)S(1)}, f32[4,64,256]{2,1,0:T(8,128)S(1)}, u32[]{:S(2)}, u32[]{:S(2)}) %collective-permute-start.2) | collective-permute-done | bytes 262176 | tf_op jit(solution)/shard_map/ppermute | solution.py:296
  35.9 1.7 %collective-permute-start.3 = (f32[4,64,256]{2,1,0:T(8,128)S(1)}, f32[4,64,256]{2,1,0:T(8,128)S(1)}, u32[]{:S(2)}, u32[]{:S(2)}) collective-permute-start(f32[4,64,256]{2,1,0:T(8,128)S(1)} %get-tuple-element.42), channel_id=1, source_target_pairs={{0,4},{4,0},{8,12},{12,8},{16,20},{20,16},{24,28},{28,24},{1,5},{5... | collective-permute-start | bytes 786440 | tf_op jit(solution)/shard_map/ppermute | solution.py:296
  37.5 1.6 %collective-permute-start.4 = (f32[4,64,256]{2,1,0:T(8,128)S(1)}, f32[4,64,256]{2,1,0:T(8,128)S(1)}, u32[]{:S(2)}, u32[]{:S(2)}) collective-permute-start(f32[4,64,256]{2,1,0:T(8,128)S(1)} %get-tuple-element.43), channel_id=1, source_target_pairs={{0,8},{4,12},{8,0},{12,4},{16,24},{20,28},{24,16},{28,20},{1,9},{5... | collective-permute-start | bytes 786440 | tf_op jit(solution)/shard_map/ppermute | solution.py:296
  41.5 2.8 %collective-permute-start.19 = (f32[2,4,64,256]{3,2,1,0:T(8,128)S(1)}, f32[2,4,64,256]{3,2,1,0:T(8,128)S(1)}, u32[]{:S(2)}, u32[]{:S(2)}) collective-permute-start(f32[2,4,64,256]{3,2,1,0:T(8,128)S(1)} %shard_map.89.refs_4_), channel_id=1, source_target_pairs={{0,16},{4,20},{8,24},{12,28},{16,0},{20,4},{24,8},{28,12},{1,17},{... | collective-permute-start | bytes 1572872 | tf_op jit(solution)/shard_map/ppermute | solution.py:296
  44.3 1.9 %collective-permute-done.3.refs_1_ = f32[4,64,256]{2,1,0:T(8,128)S(1)} collective-permute-done((f32[4,64,256]{2,1,0:T(8,128)S(1)}, f32[4,64,256]{2,1,0:T(8,128)S(1)}, u32[]{:S(2)}, u32[]{:S(2)}) %collective-permute-start.3) | collective-permute-done | bytes 262176 | tf_op jit(solution)/shard_map/ppermute | solution.py:296
  46.2 9.8 %collective-permute-done.4.refs_2_ = f32[4,64,256]{2,1,0:T(8,128)S(1)} collective-permute-done((f32[4,64,256]{2,1,0:T(8,128)S(1)}, f32[4,64,256]{2,1,0:T(8,128)S(1)}, u32[]{:S(2)}, u32[]{:S(2)}) %collective-permute-start.4) | collective-permute-done | bytes 262176 | tf_op jit(solution)/shard_map/ppermute | solution.py:296
  55.9 3.8 %collective-permute-done.5.refs_3_ = f32[4,64,256]{2,1,0:T(8,128)S(1)} collective-permute-done((f32[4,64,256]{2,1,0:T(8,128)S(1)}, f32[4,64,256]{2,1,0:T(8,128)S(1)}, u32[]{:S(2)}, u32[]{:S(2)}) %collective-permute-start.5) | collective-permute-done | bytes 262176 | tf_op jit(solution)/shard_map/ppermute | solution.py:296
  61.5 18.3 %collective-permute-done.19.refs_5_ = f32[2,4,64,256]{3,2,1,0:T(8,128)S(1)} collective-permute-done((f32[2,4,64,256]{3,2,1,0:T(8,128)S(1)}, f32[2,4,64,256]{3,2,1,0:T(8,128)S(1)}, u32[]{:S(2)}, u32[]{:S(2)}) %collective-permute-start.19) | collective-permute-done | bytes 524320 | tf_op jit(solution)/shard_map/ppermute | solution.py:296
  79.7 1.4 %shard_map.90 = (f32[4,64,256]{2,1,0:T(8,128)S(1)}, f32[4,64,256]{2,1,0:T(8,128)S(1)}, f32[4,64,256]{2,1,0:T(8,128)S(1)}, f32[4,64,256]{2,1,0:T(8,128)S(1)}) custom-call(s32[2]{0:T(128)S(1)} %pad_add_fusion.ids, f32[8]{0:T(128)S(1)} %copy-done.7, f32[256,1]{1,0:T(8,128)S(1)} %copy-done.5, f32[1,1024]{1,0:T(1,128)S(1)} %copy-done.6, ...), custom_call_target="tpu_custom_call" | custom-call | flops 10485760 | bytes 3145728 | tf_op jit(solution)/shard_map/pallas_call | solution.py:354
  81.1 2.0 %collective-permute-start.20 = (f32[4,64,256]{2,1,0:T(8,128)S(1)}, f32[4,64,256]{2,1,0:T(8,128)S(1)}, u32[]{:S(2)}, u32[]{:S(2)}) collective-permute-start(f32[4,64,256]{2,1,0:T(8,128)S(1)} %get-tuple-element.62), channel_id=1, source_target_pairs={{0,4},{4,0},{8,12},{12,8},{16,20},{20,16},{24,28},{28,24},{1,5},{5... | collective-permute-start | bytes 786440 | tf_op jit(solution)/shard_map/ppermute | solution.py:296
  84.7 5.1 %collective-permute-done.6.refs_5_ = f32[2,4,64,256]{3,2,1,0:T(8,128)S(1)} collective-permute-done((f32[2,4,64,256]{3,2,1,0:T(8,128)S(1)}, f32[2,4,64,256]{3,2,1,0:T(8,128)S(1)}, u32[]{:S(2)}, u32[]{:S(2)}) %collective-permute-start.6) | collective-permute-done | bytes 524320 | tf_op jit(solution)/shard_map/ppermute | solution.py:296
  89.8 1.5 %shard_map.85 = (f32[4,64,256]{2,1,0:T(8,128)S(1)}, f32[4,64,256]{2,1,0:T(8,128)S(1)}, f32[4,64,256]{2,1,0:T(8,128)S(1)}, f32[4,64,256]{2,1,0:T(8,128)S(1)}) custom-call(s32[2]{0:T(128)S(1)} %pad_add_fusion.ids, f32[8]{0:T(128)S(1)} %copy-done.7, f32[256,1]{1,0:T(8,128)S(1)} %copy-done.5, f32[1,1024]{1,0:T(1,128)S(1)} %copy-done.6, ...), custom_call_target="tpu_custom_call" | custom-call | flops 10485760 | bytes 3145728 | tf_op jit(solution)/shard_map/pallas_call | solution.py:354
  91.3 1.6 %collective-permute-start.7 = (f32[4,64,256]{2,1,0:T(8,128)S(1)}, f32[4,64,256]{2,1,0:T(8,128)S(1)}, u32[]{:S(2)}, u32[]{:S(2)}) collective-permute-start(f32[4,64,256]{2,1,0:T(8,128)S(1)} %get-tuple-element.46), channel_id=1, source_target_pairs={{0,4},{4,0},{8,12},{12,8},{16,20},{20,16},{24,28},{28,24},{1,5},{5... | collective-permute-start | bytes 786440 | tf_op jit(solution)/shard_map/ppermute | solution.py:296
  95.4 6.7 %collective-permute-done.22.refs_3_ = f32[4,64,256]{2,1,0:T(8,128)S(1)} collective-permute-done((f32[4,64,256]{2,1,0:T(8,128)S(1)}, f32[4,64,256]{2,1,0:T(8,128)S(1)}, u32[]{:S(2)}, u32[]{:S(2)}) %collective-permute-start.22) | collective-permute-done | bytes 262176 | tf_op jit(solution)/shard_map/ppermute | solution.py:296
  103.4 1.6 %collective-permute-start.24 = (f32[4,64,256]{2,1,0:T(8,128)S(1)}, f32[4,64,256]{2,1,0:T(8,128)S(1)}, u32[]{:S(2)}, u32[]{:S(2)}) collective-permute-start(f32[4,64,256]{2,1,0:T(8,128)S(1)} %get-tuple-element.67), channel_id=1, source_target_pairs={{0,2},{1,3},{2,0},{3,1},{4,6},{5,7},{6,4},{7,5},{8,10},{9,11},{10,... | collective-permute-start | bytes 786440 | tf_op jit(solution)/shard_map/ppermute | solution.py:296
  106.7 6.5 %collective-permute-done.9.refs_3_ = f32[4,64,256]{2,1,0:T(8,128)S(1)} collective-permute-done((f32[4,64,256]{2,1,0:T(8,128)S(1)}, f32[4,64,256]{2,1,0:T(8,128)S(1)}, u32[]{:S(2)}, u32[]{:S(2)}) %collective-permute-start.9) | collective-permute-done | bytes 262176 | tf_op jit(solution)/shard_map/ppermute | solution.py:296
  114.6 1.5 %collective-permute-start.11 = (f32[4,64,256]{2,1,0:T(8,128)S(1)}, f32[4,64,256]{2,1,0:T(8,128)S(1)}, u32[]{:S(2)}, u32[]{:S(2)}) collective-permute-start(f32[4,64,256]{2,1,0:T(8,128)S(1)} %get-tuple-element.51), channel_id=1, source_target_pairs={{0,2},{1,3},{2,0},{3,1},{4,6},{5,7},{6,4},{7,5},{8,10},{9,11},{10,... | collective-permute-start | bytes 786440 | tf_op jit(solution)/shard_map/ppermute | solution.py:296
  117.3 2.3 %shard_map.92.refs_6_ = f32[4,64,1024]{2,1,0:T(8,128)S(1)} custom-call(s32[2]{0:T(128)S(1)} %pad_add_fusion.ids, f32[4,64,256]{2,1,0:T(8,128)S(1)} %get-tuple-element.65.refs_0_, f32[4,64,256]{2,1,0:T(8,128)S(1)} %collective-permute-done.23.refs_1_, f32[4,64,256]{2,1,0:T(8,128)S(1)} %collective-permute-done.24.refs_2_, ...), custom_call_target="tpu_custom_call" | custom-call | flops 1610612736 | bytes 6291456 | tf_op jit(solution)/shard_map/pallas_call | solution.py:377
  119.7 4.1 %collective-permute-done.11.refs_2_ = f32[4,64,256]{2,1,0:T(8,128)S(1)} collective-permute-done((f32[4,64,256]{2,1,0:T(8,128)S(1)}, f32[4,64,256]{2,1,0:T(8,128)S(1)}, u32[]{:S(2)}, u32[]{:S(2)}) %collective-permute-start.11) | collective-permute-done | bytes 262176 | tf_op jit(solution)/shard_map/ppermute | solution.py:296
  123.8 4.9 %collective-permute-done.12.refs_3_ = f32[4,64,256]{2,1,0:T(8,128)S(1)} collective-permute-done((f32[4,64,256]{2,1,0:T(8,128)S(1)}, f32[4,64,256]{2,1,0:T(8,128)S(1)}, u32[]{:S(2)}, u32[]{:S(2)}) %collective-permute-start.12) | collective-permute-done | bytes 262176 | tf_op jit(solution)/shard_map/ppermute | solution.py:296
  128.7 4.8 %shard_map.93 = f32[8,64,1024]{2,1,0:T(8,128)} custom-call(s32[2]{0:T(128)S(1)} %pad_add_fusion.ids, f32[4,64,256]{2,1,0:T(8,128)S(1)} %get-tuple-element.49.refs_0_, f32[4,64,256]{2,1,0:T(8,128)S(1)} %collective-permute-done.10.refs_1_, f32[4,64,256]{2,1,0:T(8,128)S(1)} %collective-permute-done.11.refs_2_, ...), custom_call_target="tpu_custom_call" | custom-call | flops 1610612736 | bytes 8388608 | tf_op jit(solution)/shard_map/pallas_call | solution.py:387
  (53 shorter events, 18.7 us)
Async XLA Ops:
  8.0 8.5 %collective-permute-start.13 = (f32[4,64,256]{2,1,0:T(8,128)S(1)}, f32[4,64,256]{2,1,0:T(8,128)S(1)}, u32[]{:S(2)}, u32[]{:S(2)}) collective-permute-start(f32[4,64,256]{2,1,0:T(8,128)S(1)} %get-tuple-element.54), channel_id=1, source_target_pairs={{0,1},{1,0},{2,3},{3,2},{4,5},{5,4},{6,7},{7,6},{8,9},{9,8},{10,11... | collective-permute-start | bytes 786440 | tf_op jit(solution)/shard_map/ppermute | solution.py:296
  8.5 9.7 %collective-permute-start.14 = (f32[4,64,256]{2,1,0:T(8,128)S(1)}, f32[4,64,256]{2,1,0:T(8,128)S(1)}, u32[]{:S(2)}, u32[]{:S(2)}) collective-permute-start(f32[4,64,256]{2,1,0:T(8,128)S(1)} %get-tuple-element.55), channel_id=1, source_target_pairs={{0,2},{1,3},{2,0},{3,1},{4,6},{5,7},{6,4},{7,5},{8,10},{9,11},{10,... | collective-permute-start | bytes 786440 | tf_op jit(solution)/shard_map/ppermute | solution.py:296
  11.1 12.3 %copy-start.9 = (bf16[256,256]{1,0:T(8,128)(2,1)S(1)}, bf16[256,256]{1,0:T(8,128)(2,1)}, u32[]{:S(2)}) copy-start(bf16[256,256]{1,0:T(8,128)(2,1)} %constant.25.clone.refs_4_) | copy-start | bytes 393220
  11.1 12.2 %collective-permute-start.15 = (f32[4,64,256]{2,1,0:T(8,128)S(1)}, f32[4,64,256]{2,1,0:T(8,128)S(1)}, u32[]{:S(2)}, u32[]{:S(2)}) collective-permute-start(f32[4,64,256]{2,1,0:T(8,128)S(1)} %get-tuple-element.56), channel_id=1, source_target_pairs={{0,3},{1,2},{2,1},{3,0},{4,7},{5,6},{6,5},{7,4},{8,11},{9,10},{10,... | collective-permute-start | bytes 786440 | tf_op jit(solution)/shard_map/ppermute | solution.py:296
  14.3 26.2 %copy-start.5 = (f32[256,1]{1,0:T(8,128)S(1)}, f32[256,1]{1,0:T(8,128)}, u32[]{:S(2)}) copy-start(f32[256,1]{1,0:T(8,128)} %constant.28.clone.smu_y) | copy-start | bytes 3076
  14.3 26.2 %copy-start.6 = (f32[1,1024]{1,0:T(1,128)S(1)}, f32[1,1024]{1,0:T(1,128)}, u32[]{:S(2)}) copy-start(f32[1,1024]{1,0:T(1,128)} %constant.29.clone.smu_x) | copy-start | bytes 12292
  14.3 26.2 %copy-start.7 = (f32[8]{0:T(128)S(1)}, f32[8]{0:T(128)}, u32[]{:S(2)}) copy-start(f32[8]{0:T(128)} %constant.27.clone.smu_z) | copy-start | bytes 100
  14.3 13.6 %collective-permute-start = (f32[4,64,256]{2,1,0:T(8,128)S(1)}, f32[4,64,256]{2,1,0:T(8,128)S(1)}, u32[]{:S(2)}, u32[]{:S(2)}) collective-permute-start(f32[4,64,256]{2,1,0:T(8,128)S(1)} %get-tuple-element.38), channel_id=1, source_target_pairs={{0,1},{1,0},{2,3},{3,2},{4,5},{5,4},{6,7},{7,6},{8,9},{9,8},{10,11... | collective-permute-start | bytes 786440 | tf_op jit(solution)/shard_map/ppermute | solution.py:296
  14.5 14.9 %collective-permute-start.1 = (f32[4,64,256]{2,1,0:T(8,128)S(1)}, f32[4,64,256]{2,1,0:T(8,128)S(1)}, u32[]{:S(2)}, u32[]{:S(2)}) collective-permute-start(f32[4,64,256]{2,1,0:T(8,128)S(1)} %get-tuple-element.39), channel_id=1, source_target_pairs={{0,2},{1,3},{2,0},{3,1},{4,6},{5,7},{6,4},{7,5},{8,10},{9,11},{10,... | collective-permute-start | bytes 786440 | tf_op jit(solution)/shard_map/ppermute | solution.py:296
  16.5 18.1 %collective-permute-start.2 = (f32[4,64,256]{2,1,0:T(8,128)S(1)}, f32[4,64,256]{2,1,0:T(8,128)S(1)}, u32[]{:S(2)}, u32[]{:S(2)}) collective-permute-start(f32[4,64,256]{2,1,0:T(8,128)S(1)} %get-tuple-element.40), channel_id=1, source_target_pairs={{0,3},{1,2},{2,1},{3,0},{4,7},{5,6},{6,5},{7,4},{8,11},{9,10},{10,... | collective-permute-start | bytes 786440 | tf_op jit(solution)/shard_map/ppermute | solution.py:296
  24.6 14.5 %collective-permute-start.16 = (f32[4,64,256]{2,1,0:T(8,128)S(1)}, f32[4,64,256]{2,1,0:T(8,128)S(1)}, u32[]{:S(2)}, u32[]{:S(2)}) collective-permute-start(f32[4,64,256]{2,1,0:T(8,128)S(1)} %get-tuple-element.58), channel_id=1, source_target_pairs={{0,4},{4,0},{8,12},{12,8},{16,20},{20,16},{24,28},{28,24},{1,5},{5... | collective-permute-start | bytes 786440 | tf_op jit(solution)/shard_map/ppermute | solution.py:296
  26.3 13.1 %collective-permute-start.17 = (f32[4,64,256]{2,1,0:T(8,128)S(1)}, f32[4,64,256]{2,1,0:T(8,128)S(1)}, u32[]{:S(2)}, u32[]{:S(2)}) collective-permute-start(f32[4,64,256]{2,1,0:T(8,128)S(1)} %get-tuple-element.59), channel_id=1, source_target_pairs={{0,8},{4,12},{8,0},{12,4},{16,24},{20,28},{24,16},{28,20},{1,9},{5... | collective-permute-start | bytes 786440 | tf_op jit(solution)/shard_map/ppermute | solution.py:296
  27.9 12.6 %collective-permute-start.18 = (f32[4,64,256]{2,1,0:T(8,128)S(1)}, f32[4,64,256]{2,1,0:T(8,128)S(1)}, u32[]{:S(2)}, u32[]{:S(2)}) collective-permute-start(f32[4,64,256]{2,1,0:T(8,128)S(1)} %get-tuple-element.60), channel_id=1, source_target_pairs={{0,12},{4,8},{8,4},{12,0},{16,28},{20,24},{24,20},{28,16},{1,13},{... | collective-permute-start | bytes 786440 | tf_op jit(solution)/shard_map/ppermute | solution.py:296
  35.9 10.3 %collective-permute-start.3 = (f32[4,64,256]{2,1,0:T(8,128)S(1)}, f32[4,64,256]{2,1,0:T(8,128)S(1)}, u32[]{:S(2)}, u32[]{:S(2)}) collective-permute-start(f32[4,64,256]{2,1,0:T(8,128)S(1)} %get-tuple-element.42), channel_id=1, source_target_pairs={{0,4},{4,0},{8,12},{12,8},{16,20},{20,16},{24,28},{28,24},{1,5},{5... | collective-permute-start | bytes 786440 | tf_op jit(solution)/shard_map/ppermute | solution.py:296
  37.5 18.4 %collective-permute-start.4 = (f32[4,64,256]{2,1,0:T(8,128)S(1)}, f32[4,64,256]{2,1,0:T(8,128)S(1)}, u32[]{:S(2)}, u32[]{:S(2)}) collective-permute-start(f32[4,64,256]{2,1,0:T(8,128)S(1)} %get-tuple-element.43), channel_id=1, source_target_pairs={{0,8},{4,12},{8,0},{12,4},{16,24},{20,28},{24,16},{28,20},{1,9},{5... | collective-permute-start | bytes 786440 | tf_op jit(solution)/shard_map/ppermute | solution.py:296
  39.1 20.6 %collective-permute-start.5 = (f32[4,64,256]{2,1,0:T(8,128)S(1)}, f32[4,64,256]{2,1,0:T(8,128)S(1)}, u32[]{:S(2)}, u32[]{:S(2)}) collective-permute-start(f32[4,64,256]{2,1,0:T(8,128)S(1)} %get-tuple-element.44), channel_id=1, source_target_pairs={{0,12},{4,8},{8,4},{12,0},{16,28},{20,24},{24,20},{28,16},{1,13},{... | collective-permute-start | bytes 786440 | tf_op jit(solution)/shard_map/ppermute | solution.py:296
  41.5 38.3 %collective-permute-start.19 = (f32[2,4,64,256]{3,2,1,0:T(8,128)S(1)}, f32[2,4,64,256]{3,2,1,0:T(8,128)S(1)}, u32[]{:S(2)}, u32[]{:S(2)}) collective-permute-start(f32[2,4,64,256]{3,2,1,0:T(8,128)S(1)} %shard_map.89.refs_4_), channel_id=1, source_target_pairs={{0,16},{4,20},{8,24},{12,28},{16,0},{20,4},{24,8},{28,12},{1,17},{... | collective-permute-start | bytes 1572872 | tf_op jit(solution)/shard_map/ppermute | solution.py:296
  60.7 29.0 %collective-permute-start.6 = (f32[2,4,64,256]{3,2,1,0:T(8,128)S(1)}, f32[2,4,64,256]{3,2,1,0:T(8,128)S(1)}, u32[]{:S(2)}, u32[]{:S(2)}) collective-permute-start(f32[2,4,64,256]{3,2,1,0:T(8,128)S(1)} %shard_map.84.refs_4_), channel_id=1, source_target_pairs={{0,16},{4,20},{8,24},{12,28},{16,0},{20,4},{24,8},{28,12},{1,17},{... | collective-permute-start | bytes 1572872 | tf_op jit(solution)/shard_map/ppermute | solution.py:296
  81.1 12.6 %collective-permute-start.20 = (f32[4,64,256]{2,1,0:T(8,128)S(1)}, f32[4,64,256]{2,1,0:T(8,128)S(1)}, u32[]{:S(2)}, u32[]{:S(2)}) collective-permute-start(f32[4,64,256]{2,1,0:T(8,128)S(1)} %get-tuple-element.62), channel_id=1, source_target_pairs={{0,4},{4,0},{8,12},{12,8},{16,20},{20,16},{24,28},{28,24},{1,5},{5... | collective-permute-start | bytes 786440 | tf_op jit(solution)/shard_map/ppermute | solution.py:296
  83.1 12.2 %collective-permute-start.21 = (f32[4,64,256]{2,1,0:T(8,128)S(1)}, f32[4,64,256]{2,1,0:T(8,128)S(1)}, u32[]{:S(2)}, u32[]{:S(2)}) collective-permute-start(f32[4,64,256]{2,1,0:T(8,128)S(1)} %get-tuple-element.63), channel_id=1, source_target_pairs={{0,8},{4,12},{8,0},{12,4},{16,24},{20,28},{24,16},{28,20},{1,9},{5... | collective-permute-start | bytes 786440 | tf_op jit(solution)/shard_map/ppermute | solution.py:296
  83.9 33.4 %copy-start.1 = (bf16[1024,1024]{1,0:T(8,128)(2,1)S(1)}, bf16[1024,1024]{1,0:T(8,128)(2,1)}, u32[]{:S(2)}) copy-start(bf16[1024,1024]{1,0:T(8,128)(2,1)} %constant.24.clone.sxl.refs_5_) | copy-start | bytes 6291460
  83.9 33.4 %copy-start.3 = (bf16[1024,1024]{1,0:T(8,128)(2,1)S(1)}, bf16[1024,1024]{1,0:T(8,128)(2,1)}, u32[]{:S(2)}) copy-start(bf16[1024,1024]{1,0:T(8,128)(2,1)} %constant.23.clone.sxh.refs_4_) | copy-start | bytes 6291460
  83.9 18.1 %collective-permute-start.22 = (f32[4,64,256]{2,1,0:T(8,128)S(1)}, f32[4,64,256]{2,1,0:T(8,128)S(1)}, u32[]{:S(2)}, u32[]{:S(2)}) collective-permute-start(f32[4,64,256]{2,1,0:T(8,128)S(1)} %get-tuple-element.64), channel_id=1, source_target_pairs={{0,12},{4,8},{8,4},{12,0},{16,28},{20,24},{24,20},{28,16},{1,13},{... | collective-permute-start | bytes 786440 | tf_op jit(solution)/shard_map/ppermute | solution.py:296
  91.3 13.7 %collective-permute-start.7 = (f32[4,64,256]{2,1,0:T(8,128)S(1)}, f32[4,64,256]{2,1,0:T(8,128)S(1)}, u32[]{:S(2)}, u32[]{:S(2)}) collective-permute-start(f32[4,64,256]{2,1,0:T(8,128)S(1)} %get-tuple-element.46), channel_id=1, source_target_pairs={{0,4},{4,0},{8,12},{12,8},{16,20},{20,16},{24,28},{28,24},{1,5},{5... | collective-permute-start | bytes 786440 | tf_op jit(solution)/shard_map/ppermute | solution.py:296
  93.0 13.7 %collective-permute-start.8 = (f32[4,64,256]{2,1,0:T(8,128)S(1)}, f32[4,64,256]{2,1,0:T(8,128)S(1)}, u32[]{:S(2)}, u32[]{:S(2)}) collective-permute-start(f32[4,64,256]{2,1,0:T(8,128)S(1)} %get-tuple-element.47), channel_id=1, source_target_pairs={{0,8},{4,12},{8,0},{12,4},{16,24},{20,28},{24,16},{28,20},{1,9},{5... | collective-permute-start | bytes 786440 | tf_op jit(solution)/shard_map/ppermute | solution.py:296
  93.7 19.5 %collective-permute-start.9 = (f32[4,64,256]{2,1,0:T(8,128)S(1)}, f32[4,64,256]{2,1,0:T(8,128)S(1)}, u32[]{:S(2)}, u32[]{:S(2)}) collective-permute-start(f32[4,64,256]{2,1,0:T(8,128)S(1)} %get-tuple-element.48), channel_id=1, source_target_pairs={{0,12},{4,8},{8,4},{12,0},{16,28},{20,24},{24,20},{28,16},{1,13},{... | collective-permute-start | bytes 786440 | tf_op jit(solution)/shard_map/ppermute | solution.py:296
  103.4 12.8 %collective-permute-start.23 = (f32[4,64,256]{2,1,0:T(8,128)S(1)}, f32[4,64,256]{2,1,0:T(8,128)S(1)}, u32[]{:S(2)}, u32[]{:S(2)}) collective-permute-start(f32[4,64,256]{2,1,0:T(8,128)S(1)} %get-tuple-element.66), channel_id=1, source_target_pairs={{0,1},{1,0},{2,3},{3,2},{4,5},{5,4},{6,7},{7,6},{8,9},{9,8},{10,11... | collective-permute-start | bytes 786440 | tf_op jit(solution)/shard_map/ppermute | solution.py:296
  103.4 13.0 %collective-permute-start.24 = (f32[4,64,256]{2,1,0:T(8,128)S(1)}, f32[4,64,256]{2,1,0:T(8,128)S(1)}, u32[]{:S(2)}, u32[]{:S(2)}) collective-permute-start(f32[4,64,256]{2,1,0:T(8,128)S(1)} %get-tuple-element.67), channel_id=1, source_target_pairs={{0,2},{1,3},{2,0},{3,1},{4,6},{5,7},{6,4},{7,5},{8,10},{9,11},{10,... | collective-permute-start | bytes 786440 | tf_op jit(solution)/shard_map/ppermute | solution.py:296
  105.0 12.3 %collective-permute-start.25 = (f32[4,64,256]{2,1,0:T(8,128)S(1)}, f32[4,64,256]{2,1,0:T(8,128)S(1)}, u32[]{:S(2)}, u32[]{:S(2)}) collective-permute-start(f32[4,64,256]{2,1,0:T(8,128)S(1)} %get-tuple-element.68), channel_id=1, source_target_pairs={{0,3},{1,2},{2,1},{3,0},{4,7},{5,6},{6,5},{7,4},{8,11},{9,10},{10,... | collective-permute-start | bytes 786440 | tf_op jit(solution)/shard_map/ppermute | solution.py:296
  114.5 5.2 %collective-permute-start.10 = (f32[4,64,256]{2,1,0:T(8,128)S(1)}, f32[4,64,256]{2,1,0:T(8,128)S(1)}, u32[]{:S(2)}, u32[]{:S(2)}) collective-permute-start(f32[4,64,256]{2,1,0:T(8,128)S(1)} %get-tuple-element.50), channel_id=1, source_target_pairs={{0,1},{1,0},{2,3},{3,2},{4,5},{5,4},{6,7},{7,6},{8,9},{9,8},{10,11... | collective-permute-start | bytes 786440 | tf_op jit(solution)/shard_map/ppermute | solution.py:296
  114.6 9.2 %collective-permute-start.11 = (f32[4,64,256]{2,1,0:T(8,128)S(1)}, f32[4,64,256]{2,1,0:T(8,128)S(1)}, u32[]{:S(2)}, u32[]{:S(2)}) collective-permute-start(f32[4,64,256]{2,1,0:T(8,128)S(1)} %get-tuple-element.51), channel_id=1, source_target_pairs={{0,2},{1,3},{2,0},{3,1},{4,6},{5,7},{6,4},{7,5},{8,10},{9,11},{10,... | collective-permute-start | bytes 786440 | tf_op jit(solution)/shard_map/ppermute | solution.py:296
  116.1 12.5 %collective-permute-start.12 = (f32[4,64,256]{2,1,0:T(8,128)S(1)}, f32[4,64,256]{2,1,0:T(8,128)S(1)}, u32[]{:S(2)}, u32[]{:S(2)}) collective-permute-start(f32[4,64,256]{2,1,0:T(8,128)S(1)} %get-tuple-element.52), channel_id=1, source_target_pairs={{0,3},{1,2},{2,1},{3,0},{4,7},{5,6},{6,5},{7,4},{8,11},{9,10},{10,... | collective-permute-start | bytes 786440 | tf_op jit(solution)/shard_map/ppermute | solution.py:296
  (4 other events, 17.0 us)

commit v3 on v0

v3 whole, which is shorter than its diff:
```python
import functools
import math

import jax
import jax.numpy as jnp
import numpy as np
from jax import lax
from jax.experimental import pallas as pl
from jax.experimental.pallas import tpu as pltpu
from jax.sharding import PartitionSpec as P

ALPHA_RATIO = 0.95
STEP_SCALE = 0.26
CHUNKS = (4, 4)
LANES = 128
STRIP = 16
VMEM_BYTES = 40 * 1024 * 1024


def sine_table(count):
    indices = np.arange(count, dtype=np.int64) + 1
    product = indices[:, None] * indices[None, :] % (2 * (count + 1))
    return math.sqrt(2.0 / (count + 1)) * np.sin(np.pi * product / (count + 1))


def spectrum_of(count):
    indices = np.arange(count, dtype=np.float64) + 1.0
    return 2.0 - 2.0 * np.cos(np.pi * indices / (count + 1))


def table_parts(table):
    table = table.astype(np.float32)
    high = table.astype(jnp.bfloat16)
    low = (table - high.astype(np.float32)).astype(jnp.bfloat16)
    return jnp.asarray(high), jnp.asarray(low)


def edge_responses(steps, depth, rows, width):
    freq = np.arange(steps // 2 + 1)
    turn = ALPHA_RATIO ** (1.0 / steps) * np.exp(-2j * np.pi * freq / steps)
    turn = turn[:, None, None]
    mu = spectrum_of(depth)[:, None] + spectrum_of(width)[None, :]
    scaled = STEP_SCALE * turn
    middle = ((1.0 - turn) ** 2 + scaled * (mu + 2.0)) / scaled
    root = np.sqrt(middle * middle / 4.0 - 1.0)
    ratio = middle / 2.0 - root
    ratio = np.where(np.abs(ratio) < 1.0, ratio, middle / 2.0 + root)
    bottom = 1.0 - ratio ** (2 * rows + 2)
    near = ratio * (1.0 - ratio ** (2 * rows)) / bottom
    far = ratio**rows * (1.0 - ratio * ratio) / bottom
    parts = np.stack([near.real, near.imag, far.real, far.imag], axis=1)
    return parts.astype(np.float32)


def parts_of(values):
    high = values.astype(jnp.bfloat16)
    return high, (values - high.astype(jnp.float32)).astype(jnp.bfloat16)


def dot(left, right):
    return jnp.dot(left, right, preferred_element_type=jnp.float32)


def dot_parts(left, right):
    return dot(left[0], right[0]) + dot(left[1], right[0]) + dot(left[0], right[1])


def call(kernel, out_shape, flops, args, scratch=()):
    smem = pl.BlockSpec(memory_space=pltpu.SMEM)
    vmem = pl.BlockSpec(memory_space=pltpu.VMEM)
    moved = sum(x.size * x.dtype.itemsize for x in args)
    return pl.pallas_call(
        kernel,
        out_shape=out_shape,
        in_specs=[smem] + [vmem] * (len(args) - 1),
        out_specs=jax.tree.map(lambda _: vmem, out_shape),
        scratch_shapes=scratch,
        compiler_params=pltpu.CompilerParams(vmem_limit_bytes=VMEM_BYTES),
        cost_estimate=pl.CostEstimate(
            flops=flops, bytes_accessed=moved, transcendentals=0
        ),
    )(*args)


class Plan:
    def __init__(self, mesh, shape):
        self.steps = mesh.shape["tm"]
        self.groups = mesh.shape["gy"]
        self.depth, self.width = shape[1], shape[3]
        self.rows = shape[2] // self.groups
        self.half = self.steps // 2
        self.block = self.width // self.half
        self.chunks = []
        first = 0
        for size in CHUNKS:
            size = min(size, self.depth - first)
            if size:
                self.chunks.append((first, size))
            first += size

    def columns(self, owner):
        return pl.ds(pl.multiple_of(owner * self.block, LANES), self.block)


def forward(plan, planes, ids, kzh, kzl, x, sxh, sxl, *outs):
    place = lax.rem(ids[0], plan.half)
    whole = parts_of(x[...].reshape(plan.depth * plan.rows, plan.width))
    left = parts_of(dot_parts((kzh[...], kzl[...]), whole))
    for k in range(plan.half):
        columns = plan.columns(place ^ k)
        value = dot_parts(left, (sxh[:, columns], sxl[:, columns]))
        outs[k][...] = value.reshape(planes, plan.rows, plan.block)


def backward(plan, planes, with_total, ids, kzh, kzl, sxh, sxl, *refs):
    place = lax.rem(ids[0], plan.half)
    pieces, out = refs[: plan.half], refs[-1]
    total = None
    for k in range(plan.half):
        at = plan.columns(place ^ k)
        piece = parts_of(pieces[k][...].reshape(planes * plan.rows, plan.block))
        value = dot_parts(piece, (sxh[at, :], sxl[at, :]))
        total = value if total is None else total + value
    value = dot_parts((kzh[...], kzl[...]), parts_of(total))
    value = value.reshape(plan.depth, plan.rows, plan.width)
    out[...] = refs[plan.half][...] + value if with_total else value


def per_strip(plan, first, planes, place, smu_z, smu_y, smu_x, edges, body):
    across = smu_x[:, plan.columns(place)]

    def step(index, carry):
        rows = pl.ds(pl.multiple_of(index * STRIP, STRIP), STRIP)
        plane = across + smu_y[rows, :]
        weights = edges[rows, 0:1], edges[rows, 1:2]
        for u in range(planes):
            body(u, rows, plane + smu_z[first + u : first + u + 1, :], weights)
        return carry

    lax.fori_loop(0, plan.rows // STRIP, step, 0)


class Cyclic:
    def __init__(self, smu, half):
        self.kappa = kappa = 2.0 - smu
        values = [jnp.zeros_like(kappa), jnp.ones_like(kappa)]
        for _ in range(half):
            values.append(kappa * values[-1] - values[-2])
        self.up, self.at, self.down = values[-1], values[-2], values[-3]
        det = (1.0 - ALPHA_RATIO) ** 2 + ALPHA_RATIO * (
            smu * (4.0 - smu) * (self.at * self.at)
        )
        inverse = 1.0 / det
        self.even = (0.5 * (1.0 - ALPHA_RATIO)) * (self.up - self.down) * inverse
        self.odd = (0.5 * (1.0 + ALPHA_RATIO)) * self.at * inverse

    def run(self, before, last, sources):
        values = []
        for source in sources:
            value = self.kappa * last - before
            before, last = last, value if source is None else value + source
            values.append(last)
        return before, last, values

    def start(self, sources):
        last = sources[0]
        before, last, _ = self.run(last, self.kappa * last + sources[1], sources[2:])
        return before, last

    def entry(self, p0, p1):
        return (
            self.even * p0 + self.odd * (2.0 * p1 - self.kappa * p0),
            self.even * p1 + self.odd * (self.kappa * p1 - 2.0 * p0),
        )

    def back(self, p0, p1):
        return self.up * p0 - self.at * p1, self.at * p0 - self.down * p1


def by_place(plan, place, body):
    for case in range(plan.half):
        pl.when(place == case)(functools.partial(body, case))


def half_end(plan, first, planes, ids, smu_z, smu_y, smu_x, edges, *refs):
    pieces = refs[: plan.half]
    ends, seen, sums = refs[plan.half :]
    steps, half = plan.steps, plan.half
    place = lax.rem(ids[0], half)
    mine = ids[0] // half
    leaving = jnp.where(mine == 0, 1.0, ALPHA_RATIO).astype(jnp.float32)
    sums[...] = jnp.zeros_like(sums)

    def with_place(case):
        def body(u, rows, smu, weights):
            cyclic = Cyclic(smu, half)
            sources = [pieces[case ^ j][u, rows, :] for j in range(half)]
            before, last = cyclic.start(sources)
            ends[0, u, rows, :] = before
            ends[1, u, rows, :] = last
            entry = cyclic.entry(ALPHA_RATIO * before, ALPHA_RATIO * last)
            before, last, own = cyclic.run(*entry, sources)
            _, _, other = cyclic.run(leaving * before, leaving * last, [None] * half)
            for values, window in ((own, mine), (other, 1 - mine)):
                for j, value in enumerate(values):
                    for edge in range(2):
                        term = weights[edge] * value
                        term = sum(term[i : i + 8] for i in range(0, STRIP, 8))
                        sums[2 * (window * half + j) + edge, u] += term

        per_strip(plan, first, planes, place, smu_z, smu_y, smu_x, edges, body)

    by_place(plan, place, with_place)
    seen[...] = jnp.sum(sums[...], axis=2)


def c_mul(a, b):
    return a[0] * b[0] - a[1] * b[1], a[0] * b[1] + a[1] * b[0]


def c_add(a, b):
    return a[0] + b[0], a[1] + b[1]


def c_gap(a, b):
    product = c_mul(a, b)
    real, imag = 1.0 - product[0], -product[1]
    inverse = 1.0 / (real * real + imag * imag)
    return real * inverse, -imag * inverse


def join_rows(plan, first, planes, ids, responses, *refs):
    groups, steps = plan.groups, plan.steps
    views = refs[:groups]
    out, seen, above, below = refs[groups:]
    place = lax.rem(ids[0], plan.half)
    me = ids[1]
    columns = plan.columns(place)
    for k in range(groups):
        seen[me ^ k] = views[k][...]
    radius = ALPHA_RATIO ** (1.0 / steps)
    grow = [radius**n for n in range(steps)]
    nothing = jnp.zeros((planes, plan.block), jnp.float32)
    for freq in range(steps // 2 + 1):
        angle = [2.0 * math.pi * (freq * n % steps) / steps for n in range(steps)]

        def spectrum(block, edge):
            real, imag = nothing, nothing
            for n in range(steps):
                value = seen[block, 2 * n + edge]
                real = real + value * np.float32(grow[n] * math.cos(angle[n]))
                if freq % (steps // 2):
                    imag = imag - value * np.float32(grow[n] * math.sin(angle[n]))
            return real, imag

        head = [spectrum(block, 0) for block in range(groups)]
        tail = [spectrum(block, 1) for block in range(groups)]
        near, far = (
            tuple(
                responses[freq, 2 * kind + part, first : first + planes, columns]
                for part in range(2)
            )
            for kind in range(2)
        )
        square = c_mul(far, far)
        gammas, downs, ups = [near], [tail[0]], [head[groups - 1]]
        for d in range(1, groups - 1):
            gamma = gammas[-1]
            gap = c_gap(gamma, near)
            through = c_mul(far, gap)
            e = groups - 1 - d
            downs.append(
                c_add(
                    tail[d], c_mul(through, c_add(downs[-1], c_mul(gamma, head[d])))
                )
            )
            ups.append(
                c_add(head[e], c_mul(through, c_add(ups[-1], c_mul(gamma, tail[e]))))
            )
            gammas.append(c_add(near, c_mul(square, c_mul(gamma, gap))))
        for d in range(groups - 1):
            down, up = downs[d], ups[groups - 2 - d]
            from_top, from_end = gammas[d], gammas[groups - 2 - d]
            gap = c_gap(from_top, from_end)
            last = c_mul(c_add(down, c_mul(from_top, up)), gap)
            start = c_mul(c_add(up, c_mul(from_end, down)), gap)
            for part in range(2):
                above[d + 1, 2 * freq + part] = last[part]
                below[d, 2 * freq + part] = start[part]
        for part in range(2):
            above[0, 2 * freq + part] = nothing
            below[groups - 1, 2 * freq + part] = nothing
    for edge, side in enumerate((above, below)):
        parts = [side[me, i] for i in range(steps + 2)]
        for n in range(steps):
            total = nothing
            shrink = STEP_SCALE / (steps * grow[n])
            if n == steps - 1:
                shrink *= ALPHA_RATIO
            for freq in range(steps // 2 + 1):
                angle = 2.0 * math.pi * (freq * n % steps) / steps
                single = freq % (steps // 2) == 0
                weight = shrink if single else 2.0 * shrink
                total = total + parts[2 * freq] * np.float32(weight * math.cos(angle))
                if not single:
                    total = total - parts[2 * freq + 1] * np.float32(
                        weight * math.sin(angle)
                    )
            out[2 * ((n + 1) % steps) + edge] = total


def half_solve(plan, first, planes, ids, smu_z, smu_y, smu_x, edges, *refs):
    pieces = refs[: plan.half]
    far, beside, beside_far = refs[plan.half : plan.half + 3]
    outs = refs[plan.half + 3 :]
    half = plan.half
    place = lax.rem(ids[0], half)
    mine = ids[0] // half
    entering = jnp.where(mine == 0, ALPHA_RATIO, 1.0).astype(jnp.float32)

    def with_place(case):
        def body(u, rows, smu, weights):
            cyclic = Cyclic(smu, half)

            def source(window, j):
                total = None
                for edge in range(2):
                    at = 2 * (window * half + j) + edge
                    row = beside[at, u : u + 1, :] + beside_far[at, u : u + 1, :]
                    term = weights[edge] * row
                    total = term if total is None else total + term
                return total

            own = [pieces[case ^ j][u, rows, :] + source(mine, j) for j in range(half)]
            other = [source(1 - mine, j) for j in range(half)]
            before, last = cyclic.start(other)
            before = entering * (before + far[0, u, rows, :])
            last = entering * (last + far[1, u, rows, :])
            before, last = cyclic.back(before, last)
            near = cyclic.start(own)
            entry = cyclic.entry(
                before + ALPHA_RATIO * near[0], last + ALPHA_RATIO * near[1]
            )
            _, _, values = cyclic.run(*entry, own)
            for j, value in enumerate(values):
                outs[case ^ j][u, rows, :] = value

        per_strip(plan, first, planes, place, smu_z, smu_y, smu_x, edges, body)

    by_place(plan, place, with_place)


def swap(values, axis, count, distance):
    if distance == 0:
        return values
    return lax.ppermute(values, axis, [(i, i ^ distance) for i in range(count)])


def on_device(plan, residual):
    steps, groups, half = plan.steps, plan.groups, plan.half
    ids = jnp.stack([lax.axis_index("tm"), lax.axis_index("gy")]).astype(jnp.int32)
    sine_rows = sine_table(plan.rows)
    sxh, sxl = table_parts(sine_table(plan.width))
    both = np.kron(sine_table(plan.depth), sine_rows)
    smu_z, smu_y, smu_x = (
        jnp.asarray(STEP_SCALE * spectrum_of(count).reshape(shape), jnp.float32)
        for count, shape in (
            (plan.depth, (-1, 1)),
            (plan.rows, (-1, 1)),
            (plan.width, (1, -1)),
        )
    )
    edges = jnp.asarray(sine_rows[:, [0, plan.rows - 1]], jnp.float32)
    responses = jnp.asarray(edge_responses(steps, plan.depth, plan.rows, plan.width))
    field = residual[0]
    f32 = functools.partial(jax.ShapeDtypeStruct, dtype=jnp.float32)
    total = None
    for first, planes in plan.chunks:
        modes = f32((planes, plan.rows, plan.block))
        ends = f32((2,) + modes.shape)
        seen = f32((2 * steps, planes, plan.block))
        count = planes * plan.rows * plan.width
        flops = 6 * count * (plan.width + plan.depth * plan.rows)
        span = slice(first * plan.rows, (first + planes) * plan.rows)
        small = (smu_z, smu_y, smu_x, edges)
        pieces = call(
            functools.partial(forward, plan, planes),
            [modes] * half,
            flops,
            (ids, *table_parts(both[span]), field, sxh, sxl),
        )
        pieces = [swap(v, "tm", steps, k) for k, v in enumerate(pieces)]
        mine, view = call(
            functools.partial(half_end, plan, first, planes),
            [ends, seen],
            100 * count,
            (ids, *small, *pieces),
            [pltpu.VMEM((2 * steps, planes, 8, plan.block), jnp.float32)],
        )
        far = swap(mine, "tm", steps, half)
        views = [swap(view, "gy", groups, k) for k in range(groups)]
        sides = pltpu.VMEM((groups, steps + 2, planes, plan.block), jnp.float32)
        beside = call(
            functools.partial(join_rows, plan, first, planes),
            seen,
            100 * count // plan.rows,
            (ids, responses, *views),
            [pltpu.VMEM((groups,) + seen.shape, jnp.float32), sides, sides],
        )
        beside_far = swap(beside, "tm", steps, half)
        pieces = call(
            functools.partial(half_solve, plan, first, planes),
            [modes] * half,
            100 * count,
            (ids, *small, *pieces, far, beside, beside_far),
        )
        pieces = [swap(v, "tm", steps, k) for k, v in enumerate(pieces)]
        ready = () if total is None else (total,)
        total = call(
            functools.partial(backward, plan, planes, total is not None),
            f32(field.shape),
            flops,
            (ids, *table_parts(both[:, span]), sxh, sxl, *pieces, *ready),
        )
    return total[None]


def solution(mesh):
    spec = P("tm", None, "gy", None)

    def whole(residual):
        plan = Plan(mesh, residual.shape)
        return jax.shard_map(
            functools.partial(on_device, plan),
            mesh=mesh,
            in_specs=(spec,),
            out_specs=spec,
            check_vma=False,
        )(residual)

    return whole
```

time: 290 us -> 118 us (0.41); the launches traced: 286 us -> 117 us
  blocking collectives: 81.1 us -> 0 us
  matrix products: 77.9 us -> 0 us
  local copies, waits for them, and re-layouts: 32.3 us -> 6.73 us
  Pallas kernels: 0 us -> 24.2 us
  starting transfers between devices: 11.3 us -> 28 us
  waiting for transfers between devices: 73.8 us -> 58.1 us
  other arithmetic: 9.44 us -> 0.07 us
    all_to_all x2 -> x0, blocking collectives: 81.1 us -> none  [the longest x1 51.8 us: on_device(): lax.all_to_all(timed, 'tm', split_axis=0, concat_axis=2, tiled=True)[0]]
    dot_general x10 -> x0, matrix products: 77.9 us -> none  [the longest x1 26.4 us: on_device(): across = jnp.einsum('ax,cyx->cay', sine_x, planes, precision=highest)]
    all_to_all x2 -> x0, waiting for transfers between devices: 73.8 us -> none  [the longest x1 47.5 us: on_device(): lax.all_to_all(hatted[None], 'tm', split_axis=2, concat_axis=0, tiled=True)]
    ppermute x0 -> x22, waiting for transfers between devices: none -> 58.1 us  [swap(): return lax.ppermute(values, axis, [(i, i ^ distance) for i in range(count)])]
    ppermute x0 -> x22, starting transfers between devices: none -> 28 us  [swap(): return lax.ppermute(values, axis, [(i, i ^ distance) for i in range(count)])]
    pallas_call x0 -> x10, Pallas kernels: none -> 24.2 us  [call(): pl.pallas_call(kernel, out_shape=out_shape, in_specs=[smem] + [vmem] * (l...]
    all_to_all x2 -> x0, starting transfers between devices: 11.3 us -> none  [the longest x1 6.84 us: on_device(): lax.all_to_all(hatted[None], 'tm', split_axis=2, concat_axis=0, tiled=True)]
    all_to_all x1 -> x0, other arithmetic: 9.01 us -> none  [on_device(): slab = lax.all_to_all(across, 'gy', split_axis=1, concat_axis=2, tiled=True)]
  transfers between devices with their start and end apart: 2 -> 22, of which waited for: 2 -> 12; matrix products, arithmetic and copies ran while one was open for 0% -> 0% of each run, Pallas kernels for 0% -> 14%
where the time goes in v3:
time: 118 us; the launch traced here: 117 us
  waiting for transfers between devices  58.1 us (49%)
  starting transfers between devices  28 us (24%)
  Pallas kernels  24.2 us (21%)
  local copies, waits for them, and re-layouts  6.73 us (6%)
    ppermute x22, waiting for transfers between devices, swap(): return lax.ppermute(values, axis, [(i, i ^ distance) for i in range(count)])  58.1 us
    ppermute x22, starting transfers between devices, swap(): return lax.ppermute(values, axis, [(i, i ^ distance) for i in range(count)])  28 us
    pallas_call x10, Pallas kernels, call(): pl.pallas_call(kernel, out_shape=out_shape, in_specs=[smem] + [vmem] * (l...  24.2 us
    unnamed x38, local copies, waits for them, and re-layouts  6.73 us
  transfers between devices with their start and end apart: 22, of which 12 were waited for; matrix products, arithmetic and copies ran while one was open for 0% of the time, Pallas kernels for 14%

profile of v3, /device:TPU:0, one launch (start us, length us, event | category | flops | bytes accessed | tf_op | source)
XLA Modules:
  0.0 117.3 jit_solution(11180833447077650350)
XLA Ops:
  0.1 1.6 %copy-done.1 = bf16[1024,1024]{1,0:T(8,128)(2,1)S(1)} copy-done((bf16[1024,1024]{1,0:T(8,128)(2,1)S(1)}, bf16[1024,1024]{1,0:T(8,128)(2,1)}, u32[]{:S(2)}) %copy-start.1) | copy-done | bytes 2097176
  1.7 1.6 %copy-done.3 = bf16[1024,1024]{1,0:T(8,128)(2,1)S(1)} copy-done((bf16[1024,1024]{1,0:T(8,128)(2,1)S(1)}, bf16[1024,1024]{1,0:T(8,128)(2,1)}, u32[]{:S(2)}) %copy-start.3) | copy-done | bytes 2097176
  3.3 1.6 %copy-done.11 = f32[1,8,64,1024]{3,2,1,0:T(8,128)S(1)} copy-done((f32[1,8,64,1024]{3,2,1,0:T(8,128)S(1)}, f32[1,8,64,1024]{3,2,1,0:T(8,128)}, u32[]{:S(2)}) %copy-start.11) | copy-done | bytes 2097176
  6.8 3.2 %shard_map.158 = (f32[4,64,256]{2,1,0:T(8,128)S(1)}, f32[4,64,256]{2,1,0:T(8,128)S(1)}, f32[4,64,256]{2,1,0:T(8,128)S(1)}, f32[4,64,256]{2,1,0:T(8,128)S(1)}) custom-call(s32[2]{0:T(128)S(1)} %pad_add_fusion.ids, bf16[256,512]{1,0:T(8,128)(2,1)S(1)} %copy-done.18, bf16[256,512]{1,0:T(8,128)(2,1)S(1)} %copy-done.17, f32[8,64,1024]{2,1,0:T(8,128)S(1)} %bitcast.4, ...), custom_call_target="tpu_custom_call" | custom-call | flops 2415919104 | bytes 6815752 | tf_op jit(solution)/shard_map/pallas_call | solution.py:72
  10.0 3.0 %collective-permute-start.11 = (f32[4,64,256]{2,1,0:T(8,128)S(1)}, f32[4,64,256]{2,1,0:T(8,128)S(1)}, u32[]{:S(2)}, u32[]{:S(2)}) collective-permute-start(f32[4,64,256]{2,1,0:T(8,128)S(1)} %get-tuple-element.36), channel_id=1, source_target_pairs={{0,4},{4,0},{8,12},{12,8},{16,20},{20,16},{24,28},{28,24},{1,5},{5... | collective-permute-start | bytes 786440 | tf_op jit(solution)/shard_map/ppermute | solution.py:356
  13.0 1.6 %collective-permute-start.12 = (f32[4,64,256]{2,1,0:T(8,128)S(1)}, f32[4,64,256]{2,1,0:T(8,128)S(1)}, u32[]{:S(2)}, u32[]{:S(2)}) collective-permute-start(f32[4,64,256]{2,1,0:T(8,128)S(1)} %get-tuple-element.37), channel_id=1, source_target_pairs={{0,8},{4,12},{8,0},{12,4},{16,24},{20,28},{24,16},{28,20},{1,9},{5... | collective-permute-start | bytes 786440 | tf_op jit(solution)/shard_map/ppermute | solution.py:356
  14.8 3.2 %shard_map.154 = (f32[4,64,256]{2,1,0:T(8,128)S(1)}, f32[4,64,256]{2,1,0:T(8,128)S(1)}, f32[4,64,256]{2,1,0:T(8,128)S(1)}, f32[4,64,256]{2,1,0:T(8,128)S(1)}) custom-call(s32[2]{0:T(128)S(1)} %pad_add_fusion.ids, bf16[256,512]{1,0:T(8,128)(2,1)S(1)} %copy-done.16, bf16[256,512]{1,0:T(8,128)(2,1)S(1)} %copy-done.15, f32[8,64,1024]{2,1,0:T(8,128)S(1)} %bitcast.5, ...), custom_call_target="tpu_custom_call" | custom-call | flops 2415919104 | bytes 6815752 | tf_op jit(solution)/shard_map/pallas_call | solution.py:72
  18.0 1.9 %collective-permute-start = (f32[4,64,256]{2,1,0:T(8,128)S(1)}, f32[4,64,256]{2,1,0:T(8,128)S(1)}, u32[]{:S(2)}, u32[]{:S(2)}) collective-permute-start(f32[4,64,256]{2,1,0:T(8,128)S(1)} %get-tuple-element.26), channel_id=1, source_target_pairs={{0,4},{4,0},{8,12},{12,8},{16,20},{20,16},{24,28},{28,24},{1,5},{5... | collective-permute-start | bytes 786440 | tf_op jit(solution)/shard_map/ppermute | solution.py:356
  19.9 1.6 %collective-permute-start.1 = (f32[4,64,256]{2,1,0:T(8,128)S(1)}, f32[4,64,256]{2,1,0:T(8,128)S(1)}, u32[]{:S(2)}, u32[]{:S(2)}) collective-permute-start(f32[4,64,256]{2,1,0:T(8,128)S(1)} %get-tuple-element.27), channel_id=1, source_target_pairs={{0,8},{4,12},{8,0},{12,4},{16,24},{20,28},{24,16},{28,20},{1,9},{5... | collective-permute-start | bytes 786440 | tf_op jit(solution)/shard_map/ppermute | solution.py:356
  22.4 5.0 %collective-permute-done.13.refs_3_ = f32[4,64,256]{2,1,0:T(8,128)S(1)} collective-permute-done((f32[4,64,256]{2,1,0:T(8,128)S(1)}, f32[4,64,256]{2,1,0:T(8,128)S(1)}, u32[]{:S(2)}, u32[]{:S(2)}) %collective-permute-start.13) | collective-permute-done | bytes 262176 | tf_op jit(solution)/shard_map/ppermute | solution.py:356
  27.4 1.9 %shard_map.159 = (f32[2,4,64,256]{3,2,1,0:T(8,128)S(1)}, f32[16,4,256]{2,1,0:T(4,128)S(1)}) custom-call(s32[2]{0:T(128)S(1)} %pad_add_fusion.ids, f32[8,1]{1,0:T(8,128)S(1)} %copy-done.10, f32[64,1]{1,0:T(8,128)S(1)} %copy-done.6, f32[1,1024]{1,0:T(1,128)S(1)} %copy-done.9, f32[64,2]{1,0:T(8,128)S(1)} %copy-done.5, ...), custom_call_target="tpu_custom_call" | custom-call | flops 26214400 | bytes 1053480 | tf_op jit(solution)/shard_map/pallas_call | solution.py:72
  29.3 3.1 %collective-permute-start.14 = (f32[2,4,64,256]{3,2,1,0:T(8,128)S(1)}, f32[2,4,64,256]{3,2,1,0:T(8,128)S(1)}, u32[]{:S(2)}, u32[]{:S(2)}) collective-permute-start(f32[2,4,64,256]{3,2,1,0:T(8,128)S(1)} %get-tuple-element.39), channel_id=1, source_target_pairs={{0,16},{4,20},{8,24},{12,28},{16,0},{20,4},{24,8},{28,12},{1,17},{... | collective-permute-start | bytes 1572872 | tf_op jit(solution)/shard_map/ppermute | solution.py:356
  32.5 10.1 %collective-permute-done.1.refs_2_ = f32[4,64,256]{2,1,0:T(8,128)S(1)} collective-permute-done((f32[4,64,256]{2,1,0:T(8,128)S(1)}, f32[4,64,256]{2,1,0:T(8,128)S(1)}, u32[]{:S(2)}, u32[]{:S(2)}) %collective-permute-start.1) | collective-permute-done | bytes 262176 | tf_op jit(solution)/shard_map/ppermute | solution.py:356
  42.6 3.1 %collective-permute-done.2.refs_3_ = f32[4,64,256]{2,1,0:T(8,128)S(1)} collective-permute-done((f32[4,64,256]{2,1,0:T(8,128)S(1)}, f32[4,64,256]{2,1,0:T(8,128)S(1)}, u32[]{:S(2)}, u32[]{:S(2)}) %collective-permute-start.2) | collective-permute-done | bytes 262176 | tf_op jit(solution)/shard_map/ppermute | solution.py:356
  45.7 1.9 %shard_map.155 = (f32[2,4,64,256]{3,2,1,0:T(8,128)S(1)}, f32[16,4,256]{2,1,0:T(4,128)S(1)}) custom-call(s32[2]{0:T(128)S(1)} %pad_add_fusion.ids, f32[8,1]{1,0:T(8,128)S(1)} %copy-done.10, f32[64,1]{1,0:T(8,128)S(1)} %copy-done.6, f32[1,1024]{1,0:T(1,128)S(1)} %copy-done.9, f32[64,2]{1,0:T(8,128)S(1)} %copy-done.5, ...), custom_call_target="tpu_custom_call" | custom-call | flops 26214400 | bytes 1053480 | tf_op jit(solution)/shard_map/pallas_call | solution.py:72
  48.3 1.5 %collective-permute-start.16 = (f32[16,4,256]{2,1,0:T(4,128)S(1)}, f32[16,4,256]{2,1,0:T(4,128)S(1)}, u32[]{:S(2)}, u32[]{:S(2)}) collective-permute-start(f32[16,4,256]{2,1,0:T(4,128)S(1)} %get-tuple-element.40.refs_0_), channel_id=1, source_target_pairs={{0,2},{1,3},{2,0},{3,1},{4,6},{5,7},{6,4},{7,5},{8,10},{9,11},{10,... | collective-permute-start | bytes 196616 | tf_op jit(solution)/shard_map/ppermute | solution.py:356
  50.2 2.5 %collective-permute-done.17.refs_3_ = f32[16,4,256]{2,1,0:T(4,128)S(1)} collective-permute-done((f32[16,4,256]{2,1,0:T(4,128)S(1)}, f32[16,4,256]{2,1,0:T(4,128)S(1)}, u32[]{:S(2)}, u32[]{:S(2)}) %collective-permute-start.17) | collective-permute-done | bytes 65568 | tf_op jit(solution)/shard_map/ppermute | solution.py:356
  52.7 1.5 %collective-permute-done.16.refs_2_ = f32[16,4,256]{2,1,0:T(4,128)S(1)} collective-permute-done((f32[16,4,256]{2,1,0:T(4,128)S(1)}, f32[16,4,256]{2,1,0:T(4,128)S(1)}, u32[]{:S(2)}, u32[]{:S(2)}) %collective-permute-start.16) | collective-permute-done | bytes 65568 | tf_op jit(solution)/shard_map/ppermute | solution.py:356
  55.2 2.3 %collective-permute-start.18 = (f32[16,4,256]{2,1,0:T(4,128)S(1)}, f32[16,4,256]{2,1,0:T(4,128)S(1)}, u32[]{:S(2)}, u32[]{:S(2)}) collective-permute-start(f32[16,4,256]{2,1,0:T(4,128)S(1)} %shard_map.160.refs_5_), channel_id=1, source_target_pairs={{0,16},{4,20},{8,24},{12,28},{16,0},{20,4},{24,8},{28,12},{1,17},{... | collective-permute-start | bytes 196616 | tf_op jit(solution)/shard_map/ppermute | solution.py:356
  57.9 20.6 %collective-permute-done.18.refs_6_ = f32[16,4,256]{2,1,0:T(4,128)S(1)} collective-permute-done((f32[16,4,256]{2,1,0:T(4,128)S(1)}, f32[16,4,256]{2,1,0:T(4,128)S(1)}, u32[]{:S(2)}, u32[]{:S(2)}) %collective-permute-start.18) | collective-permute-done | bytes 65568 | tf_op jit(solution)/shard_map/ppermute | solution.py:356
  78.5 2.0 %shard_map.161 = (f32[4,64,256]{2,1,0:T(8,128)S(1)}, f32[4,64,256]{2,1,0:T(8,128)S(1)}, f32[4,64,256]{2,1,0:T(8,128)S(1)}, f32[4,64,256]{2,1,0:T(8,128)S(1)}) custom-call(s32[2]{0:T(128)S(1)} %pad_add_fusion.ids, f32[8,1]{1,0:T(8,128)S(1)} %copy-done.10, f32[64,1]{1,0:T(8,128)S(1)} %copy-done.6, f32[1,1024]{1,0:T(1,128)S(1)} %copy-done.9, ...), custom_call_target="tpu_custom_call" | custom-call | flops 26214400 | bytes 1708840 | tf_op jit(solution)/shard_map/pallas_call | solution.py:72
  80.5 1.4 %collective-permute-start.19 = (f32[4,64,256]{2,1,0:T(8,128)S(1)}, f32[4,64,256]{2,1,0:T(8,128)S(1)}, u32[]{:S(2)}, u32[]{:S(2)}) collective-permute-start(f32[4,64,256]{2,1,0:T(8,128)S(1)} %get-tuple-element.42), channel_id=1, source_target_pairs={{0,4},{4,0},{8,12},{12,8},{16,20},{20,16},{24,28},{28,24},{1,5},{5... | collective-permute-start | bytes 786440 | tf_op jit(solution)/shard_map/ppermute | solution.py:356
  85.4 3.0 %collective-permute-done.5.refs_2_ = f32[16,4,256]{2,1,0:T(4,128)S(1)} collective-permute-done((f32[16,4,256]{2,1,0:T(4,128)S(1)}, f32[16,4,256]{2,1,0:T(4,128)S(1)}, u32[]{:S(2)}, u32[]{:S(2)}) %collective-permute-start.5) | collective-permute-done | bytes 65568 | tf_op jit(solution)/shard_map/ppermute | solution.py:356
  90.6 2.1 %collective-permute-start.7 = (f32[16,4,256]{2,1,0:T(4,128)S(1)}, f32[16,4,256]{2,1,0:T(4,128)S(1)}, u32[]{:S(2)}, u32[]{:S(2)}) collective-permute-start(f32[16,4,256]{2,1,0:T(4,128)S(1)} %shard_map.156.refs_5_), channel_id=1, source_target_pairs={{0,16},{4,20},{8,24},{12,28},{16,0},{20,4},{24,8},{28,12},{1,17},{... | collective-permute-start | bytes 196616 | tf_op jit(solution)/shard_map/ppermute | solution.py:356
  92.7 4.5 %collective-permute-done.7.refs_6_ = f32[16,4,256]{2,1,0:T(4,128)S(1)} collective-permute-done((f32[16,4,256]{2,1,0:T(4,128)S(1)}, f32[16,4,256]{2,1,0:T(4,128)S(1)}, u32[]{:S(2)}, u32[]{:S(2)}) %collective-permute-start.7) | collective-permute-done | bytes 65568 | tf_op jit(solution)/shard_map/ppermute | solution.py:356
  97.2 2.2 %shard_map.157 = (f32[4,64,256]{2,1,0:T(8,128)S(1)}, f32[4,64,256]{2,1,0:T(8,128)S(1)}, f32[4,64,256]{2,1,0:T(8,128)S(1)}, f32[4,64,256]{2,1,0:T(8,128)S(1)}) custom-call(s32[2]{0:T(128)S(1)} %pad_add_fusion.ids, f32[8,1]{1,0:T(8,128)S(1)} %copy-done.10, f32[64,1]{1,0:T(8,128)S(1)} %copy-done.6, f32[1,1024]{1,0:T(1,128)S(1)} %copy-done.9, ...), custom_call_target="tpu_custom_call" | custom-call | flops 26214400 | bytes 1708840 | tf_op jit(solution)/shard_map/pallas_call | solution.py:72
  99.4 1.4 %collective-permute-start.8 = (f32[4,64,256]{2,1,0:T(8,128)S(1)}, f32[4,64,256]{2,1,0:T(8,128)S(1)}, u32[]{:S(2)}, u32[]{:S(2)}) collective-permute-start(f32[4,64,256]{2,1,0:T(8,128)S(1)} %get-tuple-element.32), channel_id=1, source_target_pairs={{0,4},{4,0},{8,12},{12,8},{16,20},{20,16},{24,28},{28,24},{1,5},{5... | collective-permute-start | bytes 786440 | tf_op jit(solution)/shard_map/ppermute | solution.py:356
  100.9 2.0 %collective-permute-start.10 = (f32[4,64,256]{2,1,0:T(8,128)S(1)}, f32[4,64,256]{2,1,0:T(8,128)S(1)}, u32[]{:S(2)}, u32[]{:S(2)}) collective-permute-start(f32[4,64,256]{2,1,0:T(8,128)S(1)} %get-tuple-element.34), channel_id=1, source_target_pairs={{0,12},{4,8},{8,4},{12,0},{16,28},{20,24},{24,20},{28,16},{1,13},{... | collective-permute-start | bytes 786440 | tf_op jit(solution)/shard_map/ppermute | solution.py:356
  103.0 3.2 %shard_map.162.refs_4_ = f32[8,64,1024]{2,1,0:T(8,128)S(1)} custom-call(s32[2]{0:T(128)S(1)} %pad_add_fusion.ids, bf16[512,256]{1,0:T(8,128)(2,1)S(1)} %copy-done.14, bf16[512,256]{1,0:T(8,128)(2,1)S(1)} %copy-done.13, bf16[1024,1024]{1,0:T(8,128)(2,1)S(1)} %copy-done.4, bf16[1024,1024]{1,0:T(8,128)(2,1)S(1)} %copy-done.2, ...), custom_call_target="tpu_custom_call" | custom-call | flops 2415919104 | bytes 5767176 | tf_op jit(solution)/shard_map/pallas_call | solution.py:72
  107.6 2.3 %collective-permute-done.9.refs_2_ = f32[4,64,256]{2,1,0:T(8,128)S(1)} collective-permute-done((f32[4,64,256]{2,1,0:T(8,128)S(1)}, f32[4,64,256]{2,1,0:T(8,128)S(1)}, u32[]{:S(2)}, u32[]{:S(2)}) %collective-permute-start.9) | collective-permute-done | bytes 262176 | tf_op jit(solution)/shard_map/ppermute | solution.py:356
  109.9 2.8 %collective-permute-done.10.refs_3_ = f32[4,64,256]{2,1,0:T(8,128)S(1)} collective-permute-done((f32[4,64,256]{2,1,0:T(8,128)S(1)}, f32[4,64,256]{2,1,0:T(8,128)S(1)}, u32[]{:S(2)}, u32[]{:S(2)}) %collective-permute-start.10) | collective-permute-done | bytes 262176 | tf_op jit(solution)/shard_map/ppermute | solution.py:356
  112.8 4.5 %shard_map.163 = f32[8,64,1024]{2,1,0:T(8,128)} custom-call(s32[2]{0:T(128)S(1)} %pad_add_fusion.ids, bf16[512,256]{1,0:T(8,128)(2,1)S(1)} %copy-done.8, bf16[512,256]{1,0:T(8,128)(2,1)S(1)} %copy-done.7, bf16[1024,1024]{1,0:T(8,128)(2,1)S(1)} %copy-done.4, bf16[1024,1024]{1,0:T(8,128)(2,1)S(1)} %copy-done.2, f32[4,64,256]{2,1,0:T(8,128)S(1)} %get-tuple-element.31.refs_0_, ...), custom_call_target="tpu_custom_call" | custom-call | flops 2415919104 | bytes 7864328 | tf_op jit(solution)/shard_map/pallas_call | solution.py:72
  (61 shorter events, 12.7 us)
Async XLA Ops:
  6.8 8.0 %copy-start.16 = (bf16[256,512]{1,0:T(8,128)(2,1)S(1)}, bf16[256,512]{1,0:T(8,128)(2,1)}, u32[]{:S(2)}) copy-start(bf16[256,512]{1,0:T(8,128)(2,1)} %constant.50.clone.kzh) | copy-start | bytes 786436
  10.0 11.5 %collective-permute-start.11 = (f32[4,64,256]{2,1,0:T(8,128)S(1)}, f32[4,64,256]{2,1,0:T(8,128)S(1)}, u32[]{:S(2)}, u32[]{:S(2)}) collective-permute-start(f32[4,64,256]{2,1,0:T(8,128)S(1)} %get-tuple-element.36), channel_id=1, source_target_pairs={{0,4},{4,0},{8,12},{12,8},{16,20},{20,16},{24,28},{28,24},{1,5},{5... | collective-permute-start | bytes 786440 | tf_op jit(solution)/shard_map/ppermute | solution.py:356
  13.0 9.3 %collective-permute-start.12 = (f32[4,64,256]{2,1,0:T(8,128)S(1)}, f32[4,64,256]{2,1,0:T(8,128)S(1)}, u32[]{:S(2)}, u32[]{:S(2)}) collective-permute-start(f32[4,64,256]{2,1,0:T(8,128)S(1)} %get-tuple-element.37), channel_id=1, source_target_pairs={{0,8},{4,12},{8,0},{12,4},{16,24},{20,28},{24,16},{28,20},{1,9},{5... | collective-permute-start | bytes 786440 | tf_op jit(solution)/shard_map/ppermute | solution.py:356
  14.6 12.8 %copy-start.5 = (f32[64,2]{1,0:T(8,128)S(1)}, f32[64,2]{1,0:T(8,128)}, u32[]{:S(2)}) copy-start(f32[64,2]{1,0:T(8,128)} %constant.44.clone.edges) | copy-start | bytes 1540
  14.6 12.8 %copy-start.6 = (f32[64,1]{1,0:T(8,128)S(1)}, f32[64,1]{1,0:T(8,128)}, u32[]{:S(2)}) copy-start(f32[64,1]{1,0:T(8,128)} %constant.42.clone.smu_y) | copy-start | bytes 772
  14.6 12.8 %copy-start.9 = (f32[1,1024]{1,0:T(1,128)S(1)}, f32[1,1024]{1,0:T(1,128)}, u32[]{:S(2)}) copy-start(f32[1,1024]{1,0:T(1,128)} %constant.43.clone.smu_x) | copy-start | bytes 12292
  14.6 12.8 %copy-start.10 = (f32[8,1]{1,0:T(8,128)S(1)}, f32[8,1]{1,0:T(8,128)}, u32[]{:S(2)}) copy-start(f32[8,1]{1,0:T(8,128)} %constant.41.clone.smu_z) | copy-start | bytes 100
  14.6 12.8 %collective-permute-start.13 = (f32[4,64,256]{2,1,0:T(8,128)S(1)}, f32[4,64,256]{2,1,0:T(8,128)S(1)}, u32[]{:S(2)}, u32[]{:S(2)}) collective-permute-start(f32[4,64,256]{2,1,0:T(8,128)S(1)} %get-tuple-element.38), channel_id=1, source_target_pairs={{0,12},{4,8},{8,4},{12,0},{16,28},{20,24},{24,20},{28,16},{1,13},{... | collective-permute-start | bytes 786440 | tf_op jit(solution)/shard_map/ppermute | solution.py:356
  18.0 36.2 %copy-start = (f32[5,4,8,1024]{3,2,1,0:T(8,128)S(1)}, f32[5,4,8,1024]{3,2,1,0:T(8,128)}, u32[]{:S(2)}) copy-start(f32[5,4,8,1024]{3,2,1,0:T(8,128)} %constant.45.clone.responses) | copy-start | bytes 1966084
  18.0 14.5 %collective-permute-start = (f32[4,64,256]{2,1,0:T(8,128)S(1)}, f32[4,64,256]{2,1,0:T(8,128)S(1)}, u32[]{:S(2)}, u32[]{:S(2)}) collective-permute-start(f32[4,64,256]{2,1,0:T(8,128)S(1)} %get-tuple-element.26), channel_id=1, source_target_pairs={{0,4},{4,0},{8,12},{12,8},{16,20},{20,16},{24,28},{28,24},{1,5},{5... | collective-permute-start | bytes 786440 | tf_op jit(solution)/shard_map/ppermute | solution.py:356
  19.9 22.7 %collective-permute-start.1 = (f32[4,64,256]{2,1,0:T(8,128)S(1)}, f32[4,64,256]{2,1,0:T(8,128)S(1)}, u32[]{:S(2)}, u32[]{:S(2)}) collective-permute-start(f32[4,64,256]{2,1,0:T(8,128)S(1)} %get-tuple-element.27), channel_id=1, source_target_pairs={{0,8},{4,12},{8,0},{12,4},{16,24},{20,28},{24,16},{28,20},{1,9},{5... | collective-permute-start | bytes 786440 | tf_op jit(solution)/shard_map/ppermute | solution.py:356
  21.5 24.2 %collective-permute-start.2 = (f32[4,64,256]{2,1,0:T(8,128)S(1)}, f32[4,64,256]{2,1,0:T(8,128)S(1)}, u32[]{:S(2)}, u32[]{:S(2)}) collective-permute-start(f32[4,64,256]{2,1,0:T(8,128)S(1)} %get-tuple-element.28), channel_id=1, source_target_pairs={{0,12},{4,8},{8,4},{12,0},{16,28},{20,24},{24,20},{28,16},{1,13},{... | collective-permute-start | bytes 786440 | tf_op jit(solution)/shard_map/ppermute | solution.py:356
  29.3 49.2 %collective-permute-start.14 = (f32[2,4,64,256]{3,2,1,0:T(8,128)S(1)}, f32[2,4,64,256]{3,2,1,0:T(8,128)S(1)}, u32[]{:S(2)}, u32[]{:S(2)}) collective-permute-start(f32[2,4,64,256]{3,2,1,0:T(8,128)S(1)} %get-tuple-element.39), channel_id=1, source_target_pairs={{0,16},{4,20},{8,24},{12,28},{16,0},{20,4},{24,8},{28,12},{1,17},{... | collective-permute-start | bytes 1572872 | tf_op jit(solution)/shard_map/ppermute | solution.py:356
  47.6 49.6 %collective-permute-start.3 = (f32[2,4,64,256]{3,2,1,0:T(8,128)S(1)}, f32[2,4,64,256]{3,2,1,0:T(8,128)S(1)}, u32[]{:S(2)}, u32[]{:S(2)}) collective-permute-start(f32[2,4,64,256]{3,2,1,0:T(8,128)S(1)} %get-tuple-element.29), channel_id=1, source_target_pairs={{0,16},{4,20},{8,24},{12,28},{16,0},{20,4},{24,8},{28,12},{1,17},{... | collective-permute-start | bytes 1572872 | tf_op jit(solution)/shard_map/ppermute | solution.py:356
  48.3 4.3 %collective-permute-start.17 = (f32[16,4,256]{2,1,0:T(4,128)S(1)}, f32[16,4,256]{2,1,0:T(4,128)S(1)}, u32[]{:S(2)}, u32[]{:S(2)}) collective-permute-start(f32[16,4,256]{2,1,0:T(4,128)S(1)} %get-tuple-element.40.refs_0_), channel_id=1, source_target_pairs={{0,3},{1,2},{2,1},{3,0},{4,7},{5,6},{6,5},{7,4},{8,11},{9,10},{10,... | collective-permute-start | bytes 196616 | tf_op jit(solution)/shard_map/ppermute | solution.py:356
  48.3 5.8 %collective-permute-start.16 = (f32[16,4,256]{2,1,0:T(4,128)S(1)}, f32[16,4,256]{2,1,0:T(4,128)S(1)}, u32[]{:S(2)}, u32[]{:S(2)}) collective-permute-start(f32[16,4,256]{2,1,0:T(4,128)S(1)} %get-tuple-element.40.refs_0_), channel_id=1, source_target_pairs={{0,2},{1,3},{2,0},{3,1},{4,6},{5,7},{6,4},{7,5},{8,10},{9,11},{10,... | collective-permute-start | bytes 196616 | tf_op jit(solution)/shard_map/ppermute | solution.py:356
  49.9 4.3 %collective-permute-start.15 = (f32[16,4,256]{2,1,0:T(4,128)S(1)}, f32[16,4,256]{2,1,0:T(4,128)S(1)}, u32[]{:S(2)}, u32[]{:S(2)}) collective-permute-start(f32[16,4,256]{2,1,0:T(4,128)S(1)} %get-tuple-element.40.refs_0_), channel_id=1, source_target_pairs={{0,1},{1,0},{2,3},{3,2},{4,5},{5,4},{6,7},{7,6},{8,9},{9,8},{10,11... | collective-permute-start | bytes 196616 | tf_op jit(solution)/shard_map/ppermute | solution.py:356
  55.2 23.3 %collective-permute-start.18 = (f32[16,4,256]{2,1,0:T(4,128)S(1)}, f32[16,4,256]{2,1,0:T(4,128)S(1)}, u32[]{:S(2)}, u32[]{:S(2)}) collective-permute-start(f32[16,4,256]{2,1,0:T(4,128)S(1)} %shard_map.160.refs_5_), channel_id=1, source_target_pairs={{0,16},{4,20},{8,24},{12,28},{16,0},{20,4},{24,8},{28,12},{1,17},{... | collective-permute-start | bytes 196616 | tf_op jit(solution)/shard_map/ppermute | solution.py:356
  57.5 45.5 %copy-start.13 = (bf16[512,256]{1,0:T(8,128)(2,1)S(1)}, bf16[512,256]{1,0:T(8,128)(2,1)}, u32[]{:S(2)}) copy-start(bf16[512,256]{1,0:T(8,128)(2,1)} %constant.49.clone.kzl) | copy-start | bytes 786436
  57.5 45.5 %copy-start.14 = (bf16[512,256]{1,0:T(8,128)(2,1)S(1)}, bf16[512,256]{1,0:T(8,128)(2,1)}, u32[]{:S(2)}) copy-start(bf16[512,256]{1,0:T(8,128)(2,1)} %constant.48.clone.kzh) | copy-start | bytes 786436
  57.5 26.5 %collective-permute-start.6 = (f32[16,4,256]{2,1,0:T(4,128)S(1)}, f32[16,4,256]{2,1,0:T(4,128)S(1)}, u32[]{:S(2)}, u32[]{:S(2)}) collective-permute-start(f32[16,4,256]{2,1,0:T(4,128)S(1)} %get-tuple-element.30.refs_0_), channel_id=1, source_target_pairs={{0,3},{1,2},{2,1},{3,0},{4,7},{5,6},{6,5},{7,4},{8,11},{9,10},{10,... | collective-permute-start | bytes 196616 | tf_op jit(solution)/shard_map/ppermute | solution.py:356
  80.5 20.4 %collective-permute-start.19 = (f32[4,64,256]{2,1,0:T(8,128)S(1)}, f32[4,64,256]{2,1,0:T(8,128)S(1)}, u32[]{:S(2)}, u32[]{:S(2)}) collective-permute-start(f32[4,64,256]{2,1,0:T(8,128)S(1)} %get-tuple-element.42), channel_id=1, source_target_pairs={{0,4},{4,0},{8,12},{12,8},{16,20},{20,16},{24,28},{28,24},{1,5},{5... | collective-permute-start | bytes 786440 | tf_op jit(solution)/shard_map/ppermute | solution.py:356
  81.9 21.0 %collective-permute-start.20 = (f32[4,64,256]{2,1,0:T(8,128)S(1)}, f32[4,64,256]{2,1,0:T(8,128)S(1)}, u32[]{:S(2)}, u32[]{:S(2)}) collective-permute-start(f32[4,64,256]{2,1,0:T(8,128)S(1)} %get-tuple-element.43), channel_id=1, source_target_pairs={{0,8},{4,12},{8,0},{12,4},{16,24},{20,28},{24,16},{28,20},{1,9},{5... | collective-permute-start | bytes 786440 | tf_op jit(solution)/shard_map/ppermute | solution.py:356
  82.7 20.3 %collective-permute-start.21 = (f32[4,64,256]{2,1,0:T(8,128)S(1)}, f32[4,64,256]{2,1,0:T(8,128)S(1)}, u32[]{:S(2)}, u32[]{:S(2)}) collective-permute-start(f32[4,64,256]{2,1,0:T(8,128)S(1)} %get-tuple-element.44), channel_id=1, source_target_pairs={{0,12},{4,8},{8,4},{12,0},{16,28},{20,24},{24,20},{28,16},{1,13},{... | collective-permute-start | bytes 786440 | tf_op jit(solution)/shard_map/ppermute | solution.py:356
  84.1 4.3 %collective-permute-start.5 = (f32[16,4,256]{2,1,0:T(4,128)S(1)}, f32[16,4,256]{2,1,0:T(4,128)S(1)}, u32[]{:S(2)}, u32[]{:S(2)}) collective-permute-start(f32[16,4,256]{2,1,0:T(4,128)S(1)} %get-tuple-element.30.refs_0_), channel_id=1, source_target_pairs={{0,2},{1,3},{2,0},{3,1},{4,6},{5,7},{6,4},{7,5},{8,10},{9,11},{10,... | collective-permute-start | bytes 196616 | tf_op jit(solution)/shard_map/ppermute | solution.py:356
  88.3 1.3 %collective-permute-start.4 = (f32[16,4,256]{2,1,0:T(4,128)S(1)}, f32[16,4,256]{2,1,0:T(4,128)S(1)}, u32[]{:S(2)}, u32[]{:S(2)}) collective-permute-start(f32[16,4,256]{2,1,0:T(4,128)S(1)} %get-tuple-element.30.refs_0_), channel_id=1, source_target_pairs={{0,1},{1,0},{2,3},{3,2},{4,5},{5,4},{6,7},{7,6},{8,9},{9,8},{10,11... | collective-permute-start | bytes 196616 | tf_op jit(solution)/shard_map/ppermute | solution.py:356
  90.6 6.6 %collective-permute-start.7 = (f32[16,4,256]{2,1,0:T(4,128)S(1)}, f32[16,4,256]{2,1,0:T(4,128)S(1)}, u32[]{:S(2)}, u32[]{:S(2)}) collective-permute-start(f32[16,4,256]{2,1,0:T(4,128)S(1)} %shard_map.156.refs_5_), channel_id=1, source_target_pairs={{0,16},{4,20},{8,24},{12,28},{16,0},{20,4},{24,8},{28,12},{1,17},{... | collective-permute-start | bytes 196616 | tf_op jit(solution)/shard_map/ppermute | solution.py:356
  99.4 8.2 %collective-permute-start.8 = (f32[4,64,256]{2,1,0:T(8,128)S(1)}, f32[4,64,256]{2,1,0:T(8,128)S(1)}, u32[]{:S(2)}, u32[]{:S(2)}) collective-permute-start(f32[4,64,256]{2,1,0:T(8,128)S(1)} %get-tuple-element.32), channel_id=1, source_target_pairs={{0,4},{4,0},{8,12},{12,8},{16,20},{20,16},{24,28},{28,24},{1,5},{5... | collective-permute-start | bytes 786440 | tf_op jit(solution)/shard_map/ppermute | solution.py:356
  100.8 9.1 %collective-permute-start.9 = (f32[4,64,256]{2,1,0:T(8,128)S(1)}, f32[4,64,256]{2,1,0:T(8,128)S(1)}, u32[]{:S(2)}, u32[]{:S(2)}) collective-permute-start(f32[4,64,256]{2,1,0:T(8,128)S(1)} %get-tuple-element.33), channel_id=1, source_target_pairs={{0,8},{4,12},{8,0},{12,4},{16,24},{20,28},{24,16},{28,20},{1,9},{5... | collective-permute-start | bytes 786440 | tf_op jit(solution)/shard_map/ppermute | solution.py:356
  100.9 11.8 %collective-permute-start.10 = (f32[4,64,256]{2,1,0:T(8,128)S(1)}, f32[4,64,256]{2,1,0:T(8,128)S(1)}, u32[]{:S(2)}, u32[]{:S(2)}) collective-permute-start(f32[4,64,256]{2,1,0:T(8,128)S(1)} %get-tuple-element.34), channel_id=1, source_target_pairs={{0,12},{4,8},{8,4},{12,0},{16,28},{20,24},{24,20},{28,16},{1,13},{... | collective-permute-start | bytes 786440 | tf_op jit(solution)/shard_map/ppermute | solution.py:356
  103.0 9.8 %copy-start.7 = (bf16[512,256]{1,0:T(8,128)(2,1)S(1)}, bf16[512,256]{1,0:T(8,128)(2,1)}, u32[]{:S(2)}) copy-start(bf16[512,256]{1,0:T(8,128)(2,1)} %constant.53.clone.kzl) | copy-start | bytes 786436
  103.0 9.8 %copy-start.8 = (bf16[512,256]{1,0:T(8,128)(2,1)S(1)}, bf16[512,256]{1,0:T(8,128)(2,1)}, u32[]{:S(2)}) copy-start(bf16[512,256]{1,0:T(8,128)(2,1)} %constant.52.clone.kzh) | copy-start | bytes 786436
  (9 other events, 38.5 us)

commit v4 on v3

--- a/solution.py
+++ b/solution.py
@@ -11,7 +11,7 @@
 
 ALPHA_RATIO = 0.95
 STEP_SCALE = 0.26
-CHUNKS = (4, 4)
+CHUNKS = (2, 4, 2)
 LANES = 128
 STRIP = 16
 VMEM_BYTES = 40 * 1024 * 1024
@@ -65,14 +65,15 @@
     return dot(left[0], right[0]) + dot(left[1], right[0]) + dot(left[0], right[1])
 
 
-def call(kernel, out_shape, flops, args, scratch=()):
+def call(kernel, out_shape, flops, args, scratch=(), stay=()):
     smem = pl.BlockSpec(memory_space=pltpu.SMEM)
     vmem = pl.BlockSpec(memory_space=pltpu.VMEM)
+    hbm = pl.BlockSpec(memory_space=pl.ANY)
     moved = sum(x.size * x.dtype.itemsize for x in args)
     return pl.pallas_call(
         kernel,
         out_shape=out_shape,
-        in_specs=[smem] + [vmem] * (len(args) - 1),
+        in_specs=[smem] + [hbm if i in stay else vmem for i in range(1, len(args))],
         out_specs=jax.tree.map(lambda _: vmem, out_shape),
         scratch_shapes=scratch,
         compiler_params=pltpu.CompilerParams(vmem_limit_bytes=VMEM_BYTES),
@@ -102,11 +103,32 @@
         return pl.ds(pl.multiple_of(owner * self.block, LANES), self.block)
 
 
-def forward(plan, planes, ids, kzh, kzl, x, sxh, sxl, *outs):
+def forward(plan, planes, ids, kzh, kzl, x, sxh, sxl, *refs):
     place = lax.rem(ids[0], plan.half)
+    outs, fetched = refs[: plan.half], refs[plan.half :]
+    if fetched:
+        x_all, sxh_all, sxl_all, arrived = fetched
+        copies = [pltpu.make_async_copy(x, x_all, arrived.at[0])]
+        for k in range(plan.half):
+            for part, (table, held) in enumerate(((sxh, sxh_all), (sxl, sxl_all))):
+                columns = plan.columns(place ^ k)
+                copies.append(
+                    pltpu.make_async_copy(
+                        table.at[:, columns],
+                        held.at[:, columns],
+                        arrived.at[1 + 2 * k + part],
+                    )
+                )
+        for copy in copies:
+            copy.start()
+        copies[0].wait()
+        x, sxh, sxl = x_all, sxh_all, sxl_all
     whole = parts_of(x[...].reshape(plan.depth * plan.rows, plan.width))
     left = parts_of(dot_parts((kzh[...], kzl[...]), whole))
     for k in range(plan.half):
+        if fetched:
+            copies[1 + 2 * k].wait()
+            copies[2 + 2 * k].wait()
         columns = plan.columns(place ^ k)
         value = dot_parts(left, (sxh[:, columns], sxl[:, columns]))
         outs[k][...] = value.reshape(planes, plan.rows, plan.block)
@@ -374,7 +396,13 @@
     responses = jnp.asarray(edge_responses(steps, plan.depth, plan.rows, plan.width))
     field = residual[0]
     f32 = functools.partial(jax.ShapeDtypeStruct, dtype=jnp.float32)
-    total = None
+    held = [
+        pltpu.VMEM(field.shape, jnp.float32),
+        pltpu.VMEM(sxh.shape, sxh.dtype),
+        pltpu.VMEM(sxl.shape, sxl.dtype),
+        pltpu.SemaphoreType.DMA((1 + 2 * half,)),
+    ]
+    total = beside = None
     for first, planes in plan.chunks:
         modes = f32((planes, plan.rows, plan.block))
         ends = f32((2,) + modes.shape)
@@ -388,8 +416,12 @@
             [modes] * half,
             flops,
             (ids, *table_parts(both[span]), field, sxh, sxl),
+            held if beside is None else (),
+            (3, 4, 5) if beside is None else (),
         )
         pieces = [swap(v, "tm", steps, k) for k, v in enumerate(pieces)]
+        if beside is not None:
+            beside, *pieces = lax.optimization_barrier((beside, *pieces))
         mine, view = call(
             functools.partial(half_end, plan, first, planes),
             [ends, seen],

time: 118 us -> 147 us (1.25)
  starting transfers between devices: 28 us -> 39.4 us
  waiting for transfers between devices: 58.1 us -> 67.9 us
  Pallas kernels: 24.2 us -> 32.1 us
    ppermute x22 -> x33, starting transfers between devices: 28 us -> 39.4 us  [swap(): return lax.ppermute(values, axis, [(i, i ^ distance) for i in range(count)])]
    ppermute x22 -> x33, waiting for transfers between devices: 58.1 us -> 67.9 us  [swap(): return lax.ppermute(values, axis, [(i, i ^ distance) for i in range(count)])]
    pallas_call x10 -> x15, Pallas kernels: 24.2 us -> 32.1 us  [call(): pl.pallas_call(kernel, out_shape=out_shape, in_specs=[smem] + [hbm if i i...]
    unnamed x38 -> x46, local copies, waits for them, and re-layouts: 6.73 us -> 6.68 us
  transfers between devices with their start and end apart: 22 -> 33, of which waited for: 12 -> 11; matrix products, arithmetic and copies ran while one was open for 0% -> 0% of each run, Pallas kernels for 14% -> 15%
where the time goes in v4:
time: 147 us; the launch traced here: 146 us
  waiting for transfers between devices  67.9 us (46%)
  starting transfers between devices  39.4 us (27%)
  Pallas kernels  32.1 us (22%)
  local copies, waits for them, and re-layouts  6.68 us (5%)
    ppermute x33, waiting for transfers between devices, swap(): return lax.ppermute(values, axis, [(i, i ^ distance) for i in range(count)])  67.9 us
    ppermute x33, starting transfers between devices, swap(): return lax.ppermute(values, axis, [(i, i ^ distance) for i in range(count)])  39.4 us
    pallas_call x15, Pallas kernels, call(): pl.pallas_call(kernel, out_shape=out_shape, in_specs=[smem] + [hbm if i i...  32.1 us
    unnamed x46, local copies, waits for them, and re-layouts  6.68 us
  transfers between devices with their start and end apart: 33, of which 11 were waited for; matrix products, arithmetic and copies ran while one was open for 0% of the time, Pallas kernels for 15%

profile of v4, /device:TPU:0, one launch (start us, length us, event | category | flops | bytes accessed | tf_op | source)
XLA Modules:
  0.0 146.5 jit_solution(10801816015815063310)
XLA Ops:
  0.1 1.6 %copy-done = bf16[1024,1024]{1,0:T(8,128)(2,1)S(1)} copy-done((bf16[1024,1024]{1,0:T(8,128)(2,1)S(1)}, bf16[1024,1024]{1,0:T(8,128)(2,1)}, u32[]{:S(2)}) %copy-start) | copy-done | bytes 2097176
  1.7 1.6 %copy-done.2 = bf16[1024,1024]{1,0:T(8,128)(2,1)S(1)} copy-done((bf16[1024,1024]{1,0:T(8,128)(2,1)S(1)}, bf16[1024,1024]{1,0:T(8,128)(2,1)}, u32[]{:S(2)}) %copy-start.2) | copy-done | bytes 2097176
  3.3 1.6 %copy-done.4 = f32[1,8,64,1024]{3,2,1,0:T(8,128)S(1)} copy-done((f32[1,8,64,1024]{3,2,1,0:T(8,128)S(1)}, f32[1,8,64,1024]{3,2,1,0:T(8,128)}, u32[]{:S(2)}) %copy-start.4) | copy-done | bytes 2097176
  6.7 4.2 %shard_map.190 = (f32[2,64,256]{2,1,0:T(8,128)S(1)}, f32[2,64,256]{2,1,0:T(8,128)S(1)}, f32[2,64,256]{2,1,0:T(8,128)S(1)}, f32[2,64,256]{2,1,0:T(8,128)S(1)}) custom-call(s32[2]{0:T(128)S(1)} %pad_add_fusion.ids, bf16[128,512]{1,0:T(8,128)(2,1)S(1)} %copy-done.19, bf16[128,512]{1,0:T(8,128)(2,1)S(1)} %copy-done.20, f32[8,64,1024]{2,1,0:T(8,128)S(1)} %bitcast.4, ...), custom_call_target="tpu_custom_call" | custom-call | flops 1207959552 | bytes 6553608 | tf_op jit(solution)/shard_map/pallas_call | solution.py:73
  11.0 3.0 %collective-permute-start = (f32[2,64,256]{2,1,0:T(8,128)S(1)}, f32[2,64,256]{2,1,0:T(8,128)S(1)}, u32[]{:S(2)}, u32[]{:S(2)}) collective-permute-start(f32[2,64,256]{2,1,0:T(8,128)S(1)} %get-tuple-element.44), channel_id=1, source_target_pairs={{0,4},{4,0},{8,12},{12,8},{16,20},{20,16},{24,28},{28,24},{1,5},{5... | collective-permute-start | bytes 393224 | tf_op jit(solution)/shard_map/ppermute | solution.py:378
  14.0 3.2 %shard_map.193 = (f32[4,64,256]{2,1,0:T(8,128)S(1)}, f32[4,64,256]{2,1,0:T(8,128)S(1)}, f32[4,64,256]{2,1,0:T(8,128)S(1)}, f32[4,64,256]{2,1,0:T(8,128)S(1)}) custom-call(s32[2]{0:T(128)S(1)} %pad_add_fusion.ids, bf16[256,512]{1,0:T(8,128)(2,1)S(1)} %copy-done.21, bf16[256,512]{1,0:T(8,128)(2,1)S(1)} %copy-done.22, f32[8,64,1024]{2,1,0:T(8,128)S(1)} %bitcast.5, ...), custom_call_target="tpu_custom_call" | custom-call | flops 2415919104 | bytes 6815752 | tf_op jit(solution)/shard_map/pallas_call | solution.py:73
  17.4 2.1 %collective-permute-start.7 = (f32[4,64,256]{2,1,0:T(8,128)S(1)}, f32[4,64,256]{2,1,0:T(8,128)S(1)}, u32[]{:S(2)}, u32[]{:S(2)}) collective-permute-start(f32[4,64,256]{2,1,0:T(8,128)S(1)} %get-tuple-element.50), channel_id=1, source_target_pairs={{0,8},{4,12},{8,0},{12,4},{16,24},{20,28},{24,16},{28,20},{1,9},{5... | collective-permute-start | bytes 786440 | tf_op jit(solution)/shard_map/ppermute | solution.py:378
  20.8 1.6 %collective-permute-start.1 = (f32[2,64,256]{2,1,0:T(8,128)S(1)}, f32[2,64,256]{2,1,0:T(8,128)S(1)}, u32[]{:S(2)}, u32[]{:S(2)}) collective-permute-start(f32[2,64,256]{2,1,0:T(8,128)S(1)} %get-tuple-element.45), channel_id=1, source_target_pairs={{0,8},{4,12},{8,0},{12,4},{16,24},{20,28},{24,16},{28,20},{1,9},{5... | collective-permute-start | bytes 393224 | tf_op jit(solution)/shard_map/ppermute | solution.py:378
  22.4 12.6 %collective-permute-done.1.refs_2_ = f32[2,64,256]{2,1,0:T(8,128)S(1)} collective-permute-done((f32[2,64,256]{2,1,0:T(8,128)S(1)}, f32[2,64,256]{2,1,0:T(8,128)S(1)}, u32[]{:S(2)}, u32[]{:S(2)}) %collective-permute-start.1) | collective-permute-done | bytes 131104 | tf_op jit(solution)/shard_map/ppermute | solution.py:378
  35.0 2.5 %collective-permute-done.2.refs_3_ = f32[2,64,256]{2,1,0:T(8,128)S(1)} collective-permute-done((f32[2,64,256]{2,1,0:T(8,128)S(1)}, f32[2,64,256]{2,1,0:T(8,128)S(1)}, u32[]{:S(2)}, u32[]{:S(2)}) %collective-permute-start.2) | collective-permute-done | bytes 131104 | tf_op jit(solution)/shard_map/ppermute | solution.py:378
  39.0 1.6 %collective-permute-start.4 = (f32[16,2,256]{2,1,0:T(2,128)S(1)}, f32[16,2,256]{2,1,0:T(2,128)S(1)}, u32[]{:S(2)}, u32[]{:S(2)}) collective-permute-start(f32[16,2,256]{2,1,0:T(2,128)S(1)} %get-tuple-element.47.refs_0_), channel_id=1, source_target_pairs={{0,2},{1,3},{2,0},{3,1},{4,6},{5,7},{6,4},{7,5},{8,10},{9,11},{10,... | collective-permute-start | bytes 98312 | tf_op jit(solution)/shard_map/ppermute | solution.py:378
  41.5 1.5 %collective-permute-done.4.refs_2_ = f32[16,2,256]{2,1,0:T(2,128)S(1)} collective-permute-done((f32[16,2,256]{2,1,0:T(2,128)S(1)}, f32[16,2,256]{2,1,0:T(2,128)S(1)}, u32[]{:S(2)}, u32[]{:S(2)}) %collective-permute-start.4) | collective-permute-done | bytes 32800 | tf_op jit(solution)/shard_map/ppermute | solution.py:378
  45.0 1.9 %shard_map.194 = (f32[2,4,64,256]{3,2,1,0:T(8,128)S(1)}, f32[16,4,256]{2,1,0:T(4,128)S(1)}) custom-call(s32[2]{0:T(128)S(1)} %pad_add_fusion.ids, f32[8,1]{1,0:T(8,128)S(1)} %copy-done.11, f32[64,1]{1,0:T(8,128)S(1)} %copy-done.7, f32[1,1024]{1,0:T(1,128)S(1)} %copy-done.12, f32[64,2]{1,0:T(8,128)S(1)} %copy-done.8, ...), custom_call_target="tpu_custom_call" | custom-call | flops 26214400 | bytes 1053480 | tf_op jit(solution)/shard_map/pallas_call | solution.py:73
  47.0 2.6 %collective-permute-start.23 = (f32[2,4,64,256]{3,2,1,0:T(8,128)S(1)}, f32[2,4,64,256]{3,2,1,0:T(8,128)S(1)}, u32[]{:S(2)}, u32[]{:S(2)}) collective-permute-start(f32[2,4,64,256]{3,2,1,0:T(8,128)S(1)} %get-tuple-element.71), channel_id=1, source_target_pairs={{0,16},{4,20},{8,24},{12,28},{16,0},{20,4},{24,8},{28,12},{1,17},{... | collective-permute-start | bytes 1572872 | tf_op jit(solution)/shard_map/ppermute | solution.py:378
  50.0 2.1 %shard_map.196 = (f32[2,64,256]{2,1,0:T(8,128)S(1)}, f32[2,64,256]{2,1,0:T(8,128)S(1)}, f32[2,64,256]{2,1,0:T(8,128)S(1)}, f32[2,64,256]{2,1,0:T(8,128)S(1)}) custom-call(s32[2]{0:T(128)S(1)} %pad_add_fusion.ids, bf16[128,512]{1,0:T(8,128)(2,1)S(1)} %copy-done.17, bf16[128,512]{1,0:T(8,128)(2,1)S(1)} %copy-done.18, f32[8,64,1024]{2,1,0:T(8,128)S(1)} %bitcast.6, ...), custom_call_target="tpu_custom_call" | custom-call | flops 1207959552 | bytes 6553608 | tf_op jit(solution)/shard_map/pallas_call | solution.py:73
  53.8 2.6 %collective-permute-start.29 = (f32[16,2,256]{2,1,0:T(2,128)S(1)}, f32[16,2,256]{2,1,0:T(2,128)S(1)}, u32[]{:S(2)}, u32[]{:S(2)}) collective-permute-start(f32[16,2,256]{2,1,0:T(2,128)S(1)} %shard_map.192.refs_5_), channel_id=1, source_target_pairs={{0,16},{4,20},{8,24},{12,28},{16,0},{20,4},{24,8},{28,12},{1,17},{... | collective-permute-start | bytes 98312 | tf_op jit(solution)/shard_map/ppermute | solution.py:378
  57.2 1.6 %collective-permute-start.13 = (f32[2,64,256]{2,1,0:T(8,128)S(1)}, f32[2,64,256]{2,1,0:T(8,128)S(1)}, u32[]{:S(2)}, u32[]{:S(2)}) collective-permute-start(f32[2,64,256]{2,1,0:T(8,128)S(1)} %get-tuple-element.59), channel_id=1, source_target_pairs={{0,8},{4,12},{8,0},{12,4},{16,24},{20,28},{24,16},{28,20},{1,9},{5... | collective-permute-start | bytes 393224 | tf_op jit(solution)/shard_map/ppermute | solution.py:378
  58.8 27.0 %collective-permute-done.29.refs_6_ = f32[16,2,256]{2,1,0:T(2,128)S(1)} collective-permute-done((f32[16,2,256]{2,1,0:T(2,128)S(1)}, f32[16,2,256]{2,1,0:T(2,128)S(1)}, u32[]{:S(2)}, u32[]{:S(2)}) %collective-permute-start.29) | collective-permute-done | bytes 32800 | tf_op jit(solution)/shard_map/ppermute | solution.py:378
  89.1 1.7 %collective-permute-done.11.refs_3_ = f32[16,4,256]{2,1,0:T(4,128)S(1)} collective-permute-done((f32[16,4,256]{2,1,0:T(4,128)S(1)}, f32[16,4,256]{2,1,0:T(4,128)S(1)}, u32[]{:S(2)}, u32[]{:S(2)}) %collective-permute-start.11) | collective-permute-done | bytes 65568 | tf_op jit(solution)/shard_map/ppermute | solution.py:378
  90.7 1.5 %collective-permute-start.30 = (f32[2,64,256]{2,1,0:T(8,128)S(1)}, f32[2,64,256]{2,1,0:T(8,128)S(1)}, u32[]{:S(2)}, u32[]{:S(2)}) collective-permute-start(f32[2,64,256]{2,1,0:T(8,128)S(1)} %get-tuple-element.78), channel_id=1, source_target_pairs={{0,4},{4,0},{8,12},{12,8},{16,20},{20,16},{24,28},{28,24},{1,5},{5... | collective-permute-start | bytes 393224 | tf_op jit(solution)/shard_map/ppermute | solution.py:378
  94.6 2.4 %collective-permute-start.24 = (f32[16,4,256]{2,1,0:T(4,128)S(1)}, f32[16,4,256]{2,1,0:T(4,128)S(1)}, u32[]{:S(2)}, u32[]{:S(2)}) collective-permute-start(f32[16,4,256]{2,1,0:T(4,128)S(1)} %shard_map.195.refs_5_), channel_id=1, source_target_pairs={{0,16},{4,20},{8,24},{12,28},{16,0},{20,4},{24,8},{28,12},{1,17},{... | collective-permute-start | bytes 196616 | tf_op jit(solution)/shard_map/ppermute | solution.py:378
  97.0 1.6 %shard_map.197 = (f32[2,2,64,256]{3,2,1,0:T(8,128)S(1)}, f32[16,2,256]{2,1,0:T(2,128)S(1)}) custom-call(s32[2]{0:T(128)S(1)} %pad_add_fusion.ids, f32[8,1]{1,0:T(8,128)S(1)} %copy-done.11, f32[64,1]{1,0:T(8,128)S(1)} %copy-done.7, f32[1,1024]{1,0:T(1,128)S(1)} %copy-done.12, f32[64,2]{1,0:T(8,128)S(1)} %copy-done.8, ...), custom_call_target="tpu_custom_call" | custom-call | flops 13107200 | bytes 529192 | tf_op jit(solution)/shard_map/pallas_call | solution.py:73
  102.3 2.0 %shard_map.200 = (f32[4,64,256]{2,1,0:T(8,128)S(1)}, f32[4,64,256]{2,1,0:T(8,128)S(1)}, f32[4,64,256]{2,1,0:T(8,128)S(1)}, f32[4,64,256]{2,1,0:T(8,128)S(1)}) custom-call(s32[2]{0:T(128)S(1)} %pad_add_fusion.ids, f32[8,1]{1,0:T(8,128)S(1)} %copy-done.11, f32[64,1]{1,0:T(8,128)S(1)} %copy-done.7, f32[1,1024]{1,0:T(1,128)S(1)} %copy-done.12, ...), custom_call_target="tpu_custom_call" | custom-call | flops 26214400 | bytes 1708840 | tf_op jit(solution)/shard_map/pallas_call | solution.py:73
  104.8 2.4 %collective-permute-start.26 = (f32[4,64,256]{2,1,0:T(8,128)S(1)}, f32[4,64,256]{2,1,0:T(8,128)S(1)}, u32[]{:S(2)}, u32[]{:S(2)}) collective-permute-start(f32[4,64,256]{2,1,0:T(8,128)S(1)} %get-tuple-element.74), channel_id=1, source_target_pairs={{0,8},{4,12},{8,0},{12,4},{16,24},{20,28},{24,16},{28,20},{1,9},{5... | collective-permute-start | bytes 786440 | tf_op jit(solution)/shard_map/ppermute | solution.py:378
  108.3 1.9 %collective-permute-start.32 = (f32[2,64,256]{2,1,0:T(8,128)S(1)}, f32[2,64,256]{2,1,0:T(8,128)S(1)}, u32[]{:S(2)}, u32[]{:S(2)}) collective-permute-start(f32[2,64,256]{2,1,0:T(8,128)S(1)} %get-tuple-element.80), channel_id=1, source_target_pairs={{0,12},{4,8},{8,4},{12,0},{16,28},{20,24},{24,20},{28,16},{1,13},{... | collective-permute-start | bytes 393224 | tf_op jit(solution)/shard_map/ppermute | solution.py:378
  111.3 16.4 %collective-permute-done.32.refs_3_ = f32[2,64,256]{2,1,0:T(8,128)S(1)} collective-permute-done((f32[2,64,256]{2,1,0:T(8,128)S(1)}, f32[2,64,256]{2,1,0:T(8,128)S(1)}, u32[]{:S(2)}, u32[]{:S(2)}) %collective-permute-start.32) | collective-permute-done | bytes 131104 | tf_op jit(solution)/shard_map/ppermute | solution.py:378
  128.7 2.4 %shard_map.202.refs_4_ = f32[8,64,1024]{2,1,0:T(8,128)S(1)} custom-call(s32[2]{0:T(128)S(1)} %pad_add_fusion.ids, bf16[512,128]{1,0:T(8,128)(2,1)S(1)} %copy-done.15, bf16[512,128]{1,0:T(8,128)(2,1)S(1)} %copy-done.16, bf16[1024,1024]{1,0:T(8,128)(2,1)S(1)} %copy-done.1, bf16[1024,1024]{1,0:T(8,128)(2,1)S(1)} %copy-done.3, ...), custom_call_target="tpu_custom_call" | custom-call | flops 1207959552 | bytes 4980744 | tf_op jit(solution)/shard_map/pallas_call | solution.py:73
  132.5 1.4 shard_map.199
  134.5 2.1 %collective-permute-start.21 = (f32[2,64,256]{2,1,0:T(8,128)S(1)}, f32[2,64,256]{2,1,0:T(8,128)S(1)}, u32[]{:S(2)}, u32[]{:S(2)}) collective-permute-start(f32[2,64,256]{2,1,0:T(8,128)S(1)} %get-tuple-element.69), channel_id=1, source_target_pairs={{0,8},{4,12},{8,0},{12,4},{16,24},{20,28},{24,16},{28,20},{1,9},{5... | collective-permute-start | bytes 393224 | tf_op jit(solution)/shard_map/ppermute | solution.py:378
  137.6 3.2 %shard_map.203.refs_4_ = f32[8,64,1024]{2,1,0:T(8,128)S(1)} custom-call(s32[2]{0:T(128)S(1)} %pad_add_fusion.ids, bf16[512,256]{1,0:T(8,128)(2,1)S(1)} %copy-done.9, bf16[512,256]{1,0:T(8,128)(2,1)S(1)} %copy-done.10, bf16[1024,1024]{1,0:T(8,128)(2,1)S(1)} %copy-done.1, bf16[1024,1024]{1,0:T(8,128)(2,1)S(1)} %copy-done.3, ...), custom_call_target="tpu_custom_call" | custom-call | flops 2415919104 | bytes 7864328 | tf_op jit(solution)/shard_map/pallas_call | solution.py:73
  140.8 1.8 %collective-permute-done.22.refs_3_ = f32[2,64,256]{2,1,0:T(8,128)S(1)} collective-permute-done((f32[2,64,256]{2,1,0:T(8,128)S(1)}, f32[2,64,256]{2,1,0:T(8,128)S(1)}, u32[]{:S(2)}, u32[]{:S(2)}) %collective-permute-start.22) | collective-permute-done | bytes 131104 | tf_op jit(solution)/shard_map/ppermute | solution.py:378
  142.7 3.8 %shard_map.204 = f32[8,64,1024]{2,1,0:T(8,128)} custom-call(s32[2]{0:T(128)S(1)} %pad_add_fusion.ids, bf16[512,128]{1,0:T(8,128)(2,1)S(1)} %copy-done.13, bf16[512,128]{1,0:T(8,128)(2,1)S(1)} %copy-done.14, bf16[1024,1024]{1,0:T(8,128)(2,1)S(1)} %copy-done.1, bf16[1024,1024]{1,0:T(8,128)(2,1)S(1)} %copy-done.3, f32[2,64,256]{2,1,0:T(8,128)S(1)} %get-tuple-element.67.refs_0_, ...), custom_call_target="tpu_custom_call" | custom-call | flops 1207959552 | bytes 7077896 | tf_op jit(solution)/shard_map/pallas_call | solution.py:73
  (96 shorter events, 26.6 us)
Async XLA Ops:
  11.0 11.4 %collective-permute-start = (f32[2,64,256]{2,1,0:T(8,128)S(1)}, f32[2,64,256]{2,1,0:T(8,128)S(1)}, u32[]{:S(2)}, u32[]{:S(2)}) collective-permute-start(f32[2,64,256]{2,1,0:T(8,128)S(1)} %get-tuple-element.44), channel_id=1, source_target_pairs={{0,4},{4,0},{8,12},{12,8},{16,20},{20,16},{24,28},{28,24},{1,5},{5... | collective-permute-start | bytes 393224 | tf_op jit(solution)/shard_map/ppermute | solution.py:378
  17.3 27.7 %collective-permute-start.6 = (f32[4,64,256]{2,1,0:T(8,128)S(1)}, f32[4,64,256]{2,1,0:T(8,128)S(1)}, u32[]{:S(2)}, u32[]{:S(2)}) collective-permute-start(f32[4,64,256]{2,1,0:T(8,128)S(1)} %get-tuple-element.49), channel_id=1, source_target_pairs={{0,4},{4,0},{8,12},{12,8},{16,20},{20,16},{24,28},{28,24},{1,5},{5... | collective-permute-start | bytes 786440 | tf_op jit(solution)/shard_map/ppermute | solution.py:378
  17.4 27.6 %collective-permute-start.7 = (f32[4,64,256]{2,1,0:T(8,128)S(1)}, f32[4,64,256]{2,1,0:T(8,128)S(1)}, u32[]{:S(2)}, u32[]{:S(2)}) collective-permute-start(f32[4,64,256]{2,1,0:T(8,128)S(1)} %get-tuple-element.50), channel_id=1, source_target_pairs={{0,8},{4,12},{8,0},{12,4},{16,24},{20,28},{24,16},{28,20},{1,9},{5... | collective-permute-start | bytes 786440 | tf_op jit(solution)/shard_map/ppermute | solution.py:378
  19.4 25.6 %collective-permute-start.8 = (f32[4,64,256]{2,1,0:T(8,128)S(1)}, f32[4,64,256]{2,1,0:T(8,128)S(1)}, u32[]{:S(2)}, u32[]{:S(2)}) collective-permute-start(f32[4,64,256]{2,1,0:T(8,128)S(1)} %get-tuple-element.51), channel_id=1, source_target_pairs={{0,12},{4,8},{8,4},{12,0},{16,28},{20,24},{24,20},{28,16},{1,13},{... | collective-permute-start | bytes 786440 | tf_op jit(solution)/shard_map/ppermute | solution.py:378
  20.8 14.2 %collective-permute-start.1 = (f32[2,64,256]{2,1,0:T(8,128)S(1)}, f32[2,64,256]{2,1,0:T(8,128)S(1)}, u32[]{:S(2)}, u32[]{:S(2)}) collective-permute-start(f32[2,64,256]{2,1,0:T(8,128)S(1)} %get-tuple-element.45), channel_id=1, source_target_pairs={{0,8},{4,12},{8,0},{12,4},{16,24},{20,28},{24,16},{28,20},{1,9},{5... | collective-permute-start | bytes 393224 | tf_op jit(solution)/shard_map/ppermute | solution.py:378
  22.4 15.1 %collective-permute-start.2 = (f32[2,64,256]{2,1,0:T(8,128)S(1)}, f32[2,64,256]{2,1,0:T(8,128)S(1)}, u32[]{:S(2)}, u32[]{:S(2)}) collective-permute-start(f32[2,64,256]{2,1,0:T(8,128)S(1)} %get-tuple-element.46), channel_id=1, source_target_pairs={{0,12},{4,8},{8,4},{12,0},{16,28},{20,24},{24,20},{28,16},{1,13},{... | collective-permute-start | bytes 393224 | tf_op jit(solution)/shard_map/ppermute | solution.py:378
  39.0 1.6 %collective-permute-start.3 = (f32[16,2,256]{2,1,0:T(2,128)S(1)}, f32[16,2,256]{2,1,0:T(2,128)S(1)}, u32[]{:S(2)}, u32[]{:S(2)}) collective-permute-start(f32[16,2,256]{2,1,0:T(2,128)S(1)} %get-tuple-element.47.refs_0_), channel_id=1, source_target_pairs={{0,1},{1,0},{2,3},{3,2},{4,5},{5,4},{6,7},{7,6},{8,9},{9,8},{10,11... | collective-permute-start | bytes 98312 | tf_op jit(solution)/shard_map/ppermute | solution.py:378
  39.0 4.0 %collective-permute-start.4 = (f32[16,2,256]{2,1,0:T(2,128)S(1)}, f32[16,2,256]{2,1,0:T(2,128)S(1)}, u32[]{:S(2)}, u32[]{:S(2)}) collective-permute-start(f32[16,2,256]{2,1,0:T(2,128)S(1)} %get-tuple-element.47.refs_0_), channel_id=1, source_target_pairs={{0,2},{1,3},{2,0},{3,1},{4,6},{5,7},{6,4},{7,5},{8,10},{9,11},{10,... | collective-permute-start | bytes 98312 | tf_op jit(solution)/shard_map/ppermute | solution.py:378
  40.6 3.3 %collective-permute-start.5 = (f32[16,2,256]{2,1,0:T(2,128)S(1)}, f32[16,2,256]{2,1,0:T(2,128)S(1)}, u32[]{:S(2)}, u32[]{:S(2)}) collective-permute-start(f32[16,2,256]{2,1,0:T(2,128)S(1)} %get-tuple-element.47.refs_0_), channel_id=1, source_target_pairs={{0,3},{1,2},{2,1},{3,0},{4,7},{5,6},{6,5},{7,4},{8,11},{9,10},{10,... | collective-permute-start | bytes 98312 | tf_op jit(solution)/shard_map/ppermute | solution.py:378
  47.0 54.4 %collective-permute-start.23 = (f32[2,4,64,256]{3,2,1,0:T(8,128)S(1)}, f32[2,4,64,256]{3,2,1,0:T(8,128)S(1)}, u32[]{:S(2)}, u32[]{:S(2)}) collective-permute-start(f32[2,4,64,256]{3,2,1,0:T(8,128)S(1)} %get-tuple-element.71), channel_id=1, source_target_pairs={{0,16},{4,20},{8,24},{12,28},{16,0},{20,4},{24,8},{28,12},{1,17},{... | collective-permute-start | bytes 1572872 | tf_op jit(solution)/shard_map/ppermute | solution.py:378
  49.6 37.3 %collective-permute-start.28 = (f32[2,2,64,256]{3,2,1,0:T(8,128)S(1)}, f32[2,2,64,256]{3,2,1,0:T(8,128)S(1)}, u32[]{:S(2)}, u32[]{:S(2)}) collective-permute-start(f32[2,2,64,256]{3,2,1,0:T(8,128)S(1)} %get-tuple-element.76), channel_id=1, source_target_pairs={{0,16},{4,20},{8,24},{12,28},{16,0},{20,4},{24,8},{28,12},{1,17},{... | collective-permute-start | bytes 786440 | tf_op jit(solution)/shard_map/ppermute | solution.py:378
  52.1 5.1 %collective-permute-start.12 = (f32[2,64,256]{2,1,0:T(8,128)S(1)}, f32[2,64,256]{2,1,0:T(8,128)S(1)}, u32[]{:S(2)}, u32[]{:S(2)}) collective-permute-start(f32[2,64,256]{2,1,0:T(8,128)S(1)} %get-tuple-element.58), channel_id=1, source_target_pairs={{0,4},{4,0},{8,12},{12,8},{16,20},{20,16},{24,28},{28,24},{1,5},{5... | collective-permute-start | bytes 393224 | tf_op jit(solution)/shard_map/ppermute | solution.py:378
  52.7 33.8 %collective-permute-start.10 = (f32[16,4,256]{2,1,0:T(4,128)S(1)}, f32[16,4,256]{2,1,0:T(4,128)S(1)}, u32[]{:S(2)}, u32[]{:S(2)}) collective-permute-start(f32[16,4,256]{2,1,0:T(4,128)S(1)} %get-tuple-element.56.refs_0_), channel_id=1, source_target_pairs={{0,2},{1,3},{2,0},{3,1},{4,6},{5,7},{6,4},{7,5},{8,10},{9,11},{10,... | collective-permute-start | bytes 196616 | tf_op jit(solution)/shard_map/ppermute | solution.py:378
  53.8 32.0 %collective-permute-start.29 = (f32[16,2,256]{2,1,0:T(2,128)S(1)}, f32[16,2,256]{2,1,0:T(2,128)S(1)}, u32[]{:S(2)}, u32[]{:S(2)}) collective-permute-start(f32[16,2,256]{2,1,0:T(2,128)S(1)} %shard_map.192.refs_5_), channel_id=1, source_target_pairs={{0,16},{4,20},{8,24},{12,28},{16,0},{20,4},{24,8},{28,12},{1,17},{... | collective-permute-start | bytes 98312 | tf_op jit(solution)/shard_map/ppermute | solution.py:378
  57.2 37.4 %collective-permute-start.13 = (f32[2,64,256]{2,1,0:T(8,128)S(1)}, f32[2,64,256]{2,1,0:T(8,128)S(1)}, u32[]{:S(2)}, u32[]{:S(2)}) collective-permute-start(f32[2,64,256]{2,1,0:T(8,128)S(1)} %get-tuple-element.59), channel_id=1, source_target_pairs={{0,8},{4,12},{8,0},{12,4},{16,24},{20,28},{24,16},{28,20},{1,9},{5... | collective-permute-start | bytes 393224 | tf_op jit(solution)/shard_map/ppermute | solution.py:378
  85.8 11.2 %collective-permute-start.14 = (f32[2,64,256]{2,1,0:T(8,128)S(1)}, f32[2,64,256]{2,1,0:T(8,128)S(1)}, u32[]{:S(2)}, u32[]{:S(2)}) collective-permute-start(f32[2,64,256]{2,1,0:T(8,128)S(1)} %get-tuple-element.60), channel_id=1, source_target_pairs={{0,12},{4,8},{8,4},{12,0},{16,28},{20,24},{24,20},{28,16},{1,13},{... | collective-permute-start | bytes 393224 | tf_op jit(solution)/shard_map/ppermute | solution.py:378
  86.4 4.3 %collective-permute-start.11 = (f32[16,4,256]{2,1,0:T(4,128)S(1)}, f32[16,4,256]{2,1,0:T(4,128)S(1)}, u32[]{:S(2)}, u32[]{:S(2)}) collective-permute-start(f32[16,4,256]{2,1,0:T(4,128)S(1)} %get-tuple-element.56.refs_0_), channel_id=1, source_target_pairs={{0,3},{1,2},{2,1},{3,0},{4,7},{5,6},{6,5},{7,4},{8,11},{9,10},{10,... | collective-permute-start | bytes 196616 | tf_op jit(solution)/shard_map/ppermute | solution.py:378
  86.9 5.4 %collective-permute-start.9 = (f32[16,4,256]{2,1,0:T(4,128)S(1)}, f32[16,4,256]{2,1,0:T(4,128)S(1)}, u32[]{:S(2)}, u32[]{:S(2)}) collective-permute-start(f32[16,4,256]{2,1,0:T(4,128)S(1)} %get-tuple-element.56.refs_0_), channel_id=1, source_target_pairs={{0,1},{1,0},{2,3},{3,2},{4,5},{5,4},{6,7},{7,6},{8,9},{9,8},{10,11... | collective-permute-start | bytes 196616 | tf_op jit(solution)/shard_map/ppermute | solution.py:378
  90.7 16.5 %collective-permute-start.30 = (f32[2,64,256]{2,1,0:T(8,128)S(1)}, f32[2,64,256]{2,1,0:T(8,128)S(1)}, u32[]{:S(2)}, u32[]{:S(2)}) collective-permute-start(f32[2,64,256]{2,1,0:T(8,128)S(1)} %get-tuple-element.78), channel_id=1, source_target_pairs={{0,4},{4,0},{8,12},{12,8},{16,20},{20,16},{24,28},{28,24},{1,5},{5... | collective-permute-start | bytes 393224 | tf_op jit(solution)/shard_map/ppermute | solution.py:378
  92.3 16.0 %collective-permute-start.31 = (f32[2,64,256]{2,1,0:T(8,128)S(1)}, f32[2,64,256]{2,1,0:T(8,128)S(1)}, u32[]{:S(2)}, u32[]{:S(2)}) collective-permute-start(f32[2,64,256]{2,1,0:T(8,128)S(1)} %get-tuple-element.79), channel_id=1, source_target_pairs={{0,8},{4,12},{8,0},{12,4},{16,24},{20,28},{24,16},{28,20},{1,9},{5... | collective-permute-start | bytes 393224 | tf_op jit(solution)/shard_map/ppermute | solution.py:378
  94.6 6.4 %collective-permute-start.24 = (f32[16,4,256]{2,1,0:T(4,128)S(1)}, f32[16,4,256]{2,1,0:T(4,128)S(1)}, u32[]{:S(2)}, u32[]{:S(2)}) collective-permute-start(f32[16,4,256]{2,1,0:T(4,128)S(1)} %shard_map.195.refs_5_), channel_id=1, source_target_pairs={{0,16},{4,20},{8,24},{12,28},{16,0},{20,4},{24,8},{28,12},{1,17},{... | collective-permute-start | bytes 196616 | tf_op jit(solution)/shard_map/ppermute | solution.py:378
  99.9 4.4 %collective-permute-start.17 = (f32[16,2,256]{2,1,0:T(2,128)S(1)}, f32[16,2,256]{2,1,0:T(2,128)S(1)}, u32[]{:S(2)}, u32[]{:S(2)}) collective-permute-start(f32[16,2,256]{2,1,0:T(2,128)S(1)} %get-tuple-element.66.refs_0_), channel_id=1, source_target_pairs={{0,2},{1,3},{2,0},{3,1},{4,6},{5,7},{6,4},{7,5},{8,10},{9,11},{10,... | collective-permute-start | bytes 98312 | tf_op jit(solution)/shard_map/ppermute | solution.py:378
  101.0 3.9 %collective-permute-start.18 = (f32[16,2,256]{2,1,0:T(2,128)S(1)}, f32[16,2,256]{2,1,0:T(2,128)S(1)}, u32[]{:S(2)}, u32[]{:S(2)}) collective-permute-start(f32[16,2,256]{2,1,0:T(2,128)S(1)} %get-tuple-element.66.refs_0_), channel_id=1, source_target_pairs={{0,3},{1,2},{2,1},{3,0},{4,7},{5,6},{6,5},{7,4},{8,11},{9,10},{10,... | collective-permute-start | bytes 98312 | tf_op jit(solution)/shard_map/ppermute | solution.py:378
  101.4 31.1 %collective-permute-start.15 = (f32[2,2,64,256]{3,2,1,0:T(8,128)S(1)}, f32[2,2,64,256]{3,2,1,0:T(8,128)S(1)}, u32[]{:S(2)}, u32[]{:S(2)}) collective-permute-start(f32[2,2,64,256]{3,2,1,0:T(8,128)S(1)} %get-tuple-element.65), channel_id=1, source_target_pairs={{0,16},{4,20},{8,24},{12,28},{16,0},{20,4},{24,8},{28,12},{1,17},{... | collective-permute-start | bytes 786440 | tf_op jit(solution)/shard_map/ppermute | solution.py:378
  104.3 32.3 %collective-permute-start.25 = (f32[4,64,256]{2,1,0:T(8,128)S(1)}, f32[4,64,256]{2,1,0:T(8,128)S(1)}, u32[]{:S(2)}, u32[]{:S(2)}) collective-permute-start(f32[4,64,256]{2,1,0:T(8,128)S(1)} %get-tuple-element.73), channel_id=1, source_target_pairs={{0,4},{4,0},{8,12},{12,8},{16,20},{20,16},{24,28},{28,24},{1,5},{5... | collective-permute-start | bytes 786440 | tf_op jit(solution)/shard_map/ppermute | solution.py:378
  104.8 32.7 %collective-permute-start.26 = (f32[4,64,256]{2,1,0:T(8,128)S(1)}, f32[4,64,256]{2,1,0:T(8,128)S(1)}, u32[]{:S(2)}, u32[]{:S(2)}) collective-permute-start(f32[4,64,256]{2,1,0:T(8,128)S(1)} %get-tuple-element.74), channel_id=1, source_target_pairs={{0,8},{4,12},{8,0},{12,4},{16,24},{20,28},{24,16},{28,20},{1,9},{5... | collective-permute-start | bytes 786440 | tf_op jit(solution)/shard_map/ppermute | solution.py:378
  107.3 30.3 %collective-permute-start.27 = (f32[4,64,256]{2,1,0:T(8,128)S(1)}, f32[4,64,256]{2,1,0:T(8,128)S(1)}, u32[]{:S(2)}, u32[]{:S(2)}) collective-permute-start(f32[4,64,256]{2,1,0:T(8,128)S(1)} %get-tuple-element.75), channel_id=1, source_target_pairs={{0,12},{4,8},{8,4},{12,0},{16,28},{20,24},{24,20},{28,16},{1,13},{... | collective-permute-start | bytes 786440 | tf_op jit(solution)/shard_map/ppermute | solution.py:378
  108.3 19.4 %collective-permute-start.32 = (f32[2,64,256]{2,1,0:T(8,128)S(1)}, f32[2,64,256]{2,1,0:T(8,128)S(1)}, u32[]{:S(2)}, u32[]{:S(2)}) collective-permute-start(f32[2,64,256]{2,1,0:T(8,128)S(1)} %get-tuple-element.80), channel_id=1, source_target_pairs={{0,12},{4,8},{8,4},{12,0},{16,28},{20,24},{24,20},{28,16},{1,13},{... | collective-permute-start | bytes 393224 | tf_op jit(solution)/shard_map/ppermute | solution.py:378
  127.7 4.8 %collective-permute-start.19 = (f32[16,2,256]{2,1,0:T(2,128)S(1)}, f32[16,2,256]{2,1,0:T(2,128)S(1)}, u32[]{:S(2)}, u32[]{:S(2)}) collective-permute-start(f32[16,2,256]{2,1,0:T(2,128)S(1)} %shard_map.198.refs_5_), channel_id=1, source_target_pairs={{0,16},{4,20},{8,24},{12,28},{16,0},{20,4},{24,8},{28,12},{1,17},{... | collective-permute-start | bytes 98312 | tf_op jit(solution)/shard_map/ppermute | solution.py:378
  133.9 6.9 %collective-permute-start.20 = (f32[2,64,256]{2,1,0:T(8,128)S(1)}, f32[2,64,256]{2,1,0:T(8,128)S(1)}, u32[]{:S(2)}, u32[]{:S(2)}) collective-permute-start(f32[2,64,256]{2,1,0:T(8,128)S(1)} %get-tuple-element.68), channel_id=1, source_target_pairs={{0,4},{4,0},{8,12},{12,8},{16,20},{20,16},{24,28},{28,24},{1,5},{5... | collective-permute-start | bytes 393224 | tf_op jit(solution)/shard_map/ppermute | solution.py:378
  134.5 6.3 %collective-permute-start.21 = (f32[2,64,256]{2,1,0:T(8,128)S(1)}, f32[2,64,256]{2,1,0:T(8,128)S(1)}, u32[]{:S(2)}, u32[]{:S(2)}) collective-permute-start(f32[2,64,256]{2,1,0:T(8,128)S(1)} %get-tuple-element.69), channel_id=1, source_target_pairs={{0,8},{4,12},{8,0},{12,4},{16,24},{20,28},{24,16},{28,20},{1,9},{5... | collective-permute-start | bytes 393224 | tf_op jit(solution)/shard_map/ppermute | solution.py:378
  136.6 6.1 %collective-permute-start.22 = (f32[2,64,256]{2,1,0:T(8,128)S(1)}, f32[2,64,256]{2,1,0:T(8,128)S(1)}, u32[]{:S(2)}, u32[]{:S(2)}) collective-permute-start(f32[2,64,256]{2,1,0:T(8,128)S(1)} %get-tuple-element.70), channel_id=1, source_target_pairs={{0,12},{4,8},{8,4},{12,0},{16,28},{20,24},{24,20},{28,16},{1,13},{... | collective-permute-start | bytes 393224 | tf_op jit(solution)/shard_map/ppermute | solution.py:378
  (24 other events, 433.1 us)

commit v5 on v3

--- a/solution.py
+++ b/solution.py
@@ -15,6 +15,7 @@
 LANES = 128
 STRIP = 16
 VMEM_BYTES = 40 * 1024 * 1024
+ALL_VMEM = 60 * 1024 * 1024
 
 
 def sine_table(count):
@@ -65,17 +66,21 @@
     return dot(left[0], right[0]) + dot(left[1], right[0]) + dot(left[0], right[1])
 
 
-def call(kernel, out_shape, flops, args, scratch=()):
+def call(
+    kernel, out_shape, flops, args, scratch=(), specs=None, grid=(), out=None, room=None
+):
     smem = pl.BlockSpec(memory_space=pltpu.SMEM)
     vmem = pl.BlockSpec(memory_space=pltpu.VMEM)
+    specs = specs or {}
     moved = sum(x.size * x.dtype.itemsize for x in args)
     return pl.pallas_call(
         kernel,
+        grid=grid,
         out_shape=out_shape,
-        in_specs=[smem] + [vmem] * (len(args) - 1),
-        out_specs=jax.tree.map(lambda _: vmem, out_shape),
+        in_specs=[smem] + [specs.get(i, vmem) for i in range(1, len(args))],
+        out_specs=out or jax.tree.map(lambda _: vmem, out_shape),
         scratch_shapes=scratch,
-        compiler_params=pltpu.CompilerParams(vmem_limit_bytes=VMEM_BYTES),
+        compiler_params=pltpu.CompilerParams(vmem_limit_bytes=room or VMEM_BYTES),
         cost_estimate=pl.CostEstimate(
             flops=flops, bytes_accessed=moved, transcendentals=0
         ),
@@ -102,27 +107,59 @@
         return pl.ds(pl.multiple_of(owner * self.block, LANES), self.block)
 
 
-def forward(plan, planes, ids, kzh, kzl, x, sxh, sxl, *outs):
+def forward(plan, planes, ids, kzh, kzl, x, sxh, sxl, *refs):
     place = lax.rem(ids[0], plan.half)
-    whole = parts_of(x[...].reshape(plan.depth * plan.rows, plan.width))
-    left = parts_of(dot_parts((kzh[...], kzl[...]), whole))
+    outs = refs[: plan.half]
+    x_all, high, low, arrived = refs[plan.half :]
+    parts = x_all.shape[0]
+    deep = plan.depth // parts
+    fields = [
+        pltpu.make_async_copy(x.at[pl.ds(i * deep, deep)], x_all.at[i], arrived.at[i])
+        for i in range(parts)
+    ]
+    tables = []
     for k in range(plan.half):
         columns = plan.columns(place ^ k)
-        value = dot_parts(left, (sxh[:, columns], sxl[:, columns]))
+        tables.append(
+            [
+                pltpu.make_async_copy(
+                    table.at[:, columns], held.at[k], arrived.at[parts + 2 * k + i]
+                )
+                for i, (table, held) in enumerate(((sxh, high), (sxl, low)))
+            ]
+        )
+    for copy in fields + sum(tables, []):
+        copy.start()
+    total = None
+    for i in range(parts):
+        fields[i].wait()
+        field = parts_of(x_all[i].reshape(deep * plan.rows, plan.width))
+        span = slice(i * deep * plan.rows, (i + 1) * deep * plan.rows)
+        value = dot_parts((kzh[:, span], kzl[:, span]), field)
+        total = value if total is None else total + value
+    left = parts_of(total)
+    for k in range(plan.half):
+        for copy in tables[k]:
+            copy.wait()
+        value = dot_parts(left, (high[k], low[k]))
         outs[k][...] = value.reshape(planes, plan.rows, plan.block)
 
 
 def backward(plan, planes, with_total, ids, kzh, kzl, sxh, sxl, *refs):
     place = lax.rem(ids[0], plan.half)
-    pieces, out = refs[: plan.half], refs[-1]
-    total = None
-    for k in range(plan.half):
-        at = plan.columns(place ^ k)
-        piece = parts_of(pieces[k][...].reshape(planes * plan.rows, plan.block))
-        value = dot_parts(piece, (sxh[at, :], sxl[at, :]))
-        total = value if total is None else total + value
+    pieces = refs[: plan.half]
+    out, high, low = refs[-3:]
+
+    @pl.when(pl.program_id(0) == 0)
+    def _():
+        for k in range(plan.half):
+            columns = plan.columns(place ^ k)
+            piece = pieces[k][...].reshape(planes * plan.rows, plan.block)
+            high[:, columns], low[:, columns] = parts_of(piece)
+
+    total = dot_parts((high[...], low[...]), (sxh[...], sxl[...]))
     value = dot_parts((kzh[...], kzl[...]), parts_of(total))
-    value = value.reshape(plan.depth, plan.rows, plan.width)
+    value = value.reshape(out.shape)
     out[...] = refs[plan.half][...] + value if with_total else value
 
 
@@ -374,8 +411,35 @@
     responses = jnp.asarray(edge_responses(steps, plan.depth, plan.rows, plan.width))
     field = residual[0]
     f32 = functools.partial(jax.ShapeDtypeStruct, dtype=jnp.float32)
-    total = None
+    parts = 2
+    table = pltpu.VMEM((half, plan.width, plan.block), sxh.dtype)
+    held = [
+        pltpu.VMEM((parts, plan.depth // parts) + field.shape[1:], jnp.float32),
+        table,
+        table,
+        pltpu.SemaphoreType.DMA((parts + 2 * half,)),
+    ]
+    far_away = dict.fromkeys((3, 4, 5), pl.BlockSpec(memory_space=pltpu.HBM))
+    table = pl.BlockSpec((plan.width, plan.block), lambda j: (0, j))
+    columns = pl.BlockSpec(field.shape[:2] + (plan.block,), lambda j: (0, 0, j))
+    by_columns = {3: table, 4: table, 5 + half: columns}
+    total = far = None
+    sent = []
     for first, planes in plan.chunks:
+        modes = f32((planes, plan.rows, plan.block))
+        span = slice(first * plan.rows, (first + planes) * plan.rows)
+        pieces = call(
+            functools.partial(forward, plan, planes),
+            [modes] * half,
+            6 * planes * plan.rows * plan.width * (plan.width + plan.depth * plan.rows),
+            (ids, *table_parts(both[span]), field, sxh, sxl),
+            held,
+            far_away,
+            room=ALL_VMEM,
+        )
+        sent.append([swap(v, "tm", steps, k) for k, v in enumerate(pieces)])
+    sent[0][0], sent[-1][0] = lax.optimization_barrier((sent[0][0], sent[-1][0]))
+    for (first, planes), pieces in zip(plan.chunks, sent):
         modes = f32((planes, plan.rows, plan.block))
         ends = f32((2,) + modes.shape)
         seen = f32((2 * steps, planes, plan.block))
@@ -383,13 +447,6 @@
         flops = 6 * count * (plan.width + plan.depth * plan.rows)
         span = slice(first * plan.rows, (first + planes) * plan.rows)
         small = (smu_z, smu_y, smu_x, edges)
-        pieces = call(
-            functools.partial(forward, plan, planes),
-            [modes] * half,
-            flops,
-            (ids, *table_parts(both[span]), field, sxh, sxl),
-        )
-        pieces = [swap(v, "tm", steps, k) for k, v in enumerate(pieces)]
         mine, view = call(
             functools.partial(half_end, plan, first, planes),
             [ends, seen],
@@ -397,6 +454,8 @@
             (ids, *small, *pieces),
             [pltpu.VMEM((2 * steps, planes, 8, plan.block), jnp.float32)],
         )
+        if far is not None:
+            mine, far, beside_far = lax.optimization_barrier((mine, far, beside_far))
         far = swap(mine, "tm", steps, half)
         views = [swap(view, "gy", groups, k) for k in range(groups)]
         sides = pltpu.VMEM((groups, steps + 2, planes, plan.block), jnp.float32)
@@ -421,6 +480,10 @@
             f32(field.shape),
             flops,
             (ids, *table_parts(both[:, span]), sxh, sxl, *pieces, *ready),
+            [pltpu.VMEM((planes * plan.rows, plan.width), jnp.bfloat16)] * 2,
+            by_columns,
+            (half,),
+            columns,
         )
     return total[None]
 

time: 118 us -> 105 us (0.89)
  waiting for transfers between devices: 58.1 us -> 38.6 us
  Pallas kernels: 24.2 us -> 39.8 us
  local copies, waits for them, and re-layouts: 6.73 us -> 0.07 us
  starting transfers between devices: 28 us -> 25.5 us
    ppermute x22, waiting for transfers between devices: 58.1 us -> 38.6 us  [swap(): return lax.ppermute(values, axis, [(i, i ^ distance) for i in range(count)])]
    pallas_call x10, Pallas kernels: 24.2 us -> 39.8 us  [call(): pl.pallas_call(kernel, grid=grid, out_shape=out_shape, in_specs=[smem] +...]
    unnamed x38 -> x28, local copies, waits for them, and re-layouts: 6.73 us -> 0.07 us
    ppermute x22, starting transfers between devices: 28 us -> 25.5 us  [swap(): return lax.ppermute(values, axis, [(i, i ^ distance) for i in range(count)])]
  transfers between devices with their start and end apart: 22 -> 22, of which waited for: 12 -> 12; matrix products, arithmetic and copies ran while one was open for 0% -> 0% of each run, Pallas kernels for 14% -> 22%
where the time goes in v5:
time: 105 us
  Pallas kernels  39.8 us (38%)
  waiting for transfers between devices  38.6 us (37%)
  starting transfers between devices  25.5 us (24%)
    pallas_call x10, Pallas kernels, call(): pl.pallas_call(kernel, grid=grid, out_shape=out_shape, in_specs=[smem] +...  39.8 us
    ppermute x22, waiting for transfers between devices, swap(): return lax.ppermute(values, axis, [(i, i ^ distance) for i in range(count)])  38.6 us
    ppermute x22, starting transfers between devices, swap(): return lax.ppermute(values, axis, [(i, i ^ distance) for i in range(count)])  25.5 us
  transfers between devices with their start and end apart: 22, of which 12 were waited for; matrix products, arithmetic and copies ran while one was open for 0% of the time, Pallas kernels for 22%

profile of v5, /device:TPU:0, one launch (start us, length us, event | category | flops | bytes accessed | tf_op | source)
XLA Modules:
  0.0 104.8 jit_solution(6761465330921832052)
XLA Ops:
  0.6 7.9 %shard_map.154 = (f32[4,64,256]{2,1,0:T(8,128)}, f32[4,64,256]{2,1,0:T(8,128)}, f32[4,64,256]{2,1,0:T(8,128)}, f32[4,64,256]{2,1,0:T(8,128)}) custom-call(s32[2]{0:T(128)} %pad_add_fusion.ids, bf16[256,512]{1,0:T(8,128)(2,1)} %constant.46.clone.kzh, bf16[256,512]{1,0:T(8,128)(2,1)} %constant.47.clone.kzl, f32[8,64,1024]{2,1,0:T(8,128)} %bitcast.4, ...), custom_call_target="tpu_custom_call" | custom-call | flops 2415919104 | bytes 6815752 | tf_op jit(solution)/shard_map/pallas_call | solution.py:76
  8.6 3.0 %collective-permute-start.3 = (f32[4,64,256]{2,1,0:T(8,128)}, f32[4,64,256]{2,1,0:T(8,128)S(1)}, u32[]{:S(2)}, u32[]{:S(2)}) collective-permute-start(f32[4,64,256]{2,1,0:T(8,128)} %get-tuple-element.36), channel_id=1, source_target_pairs={{0,4},{4,0},{8,12},{12,8},{16,20},{20,16},{24,28},{28,24},{1,5},{5... | collective-permute-start | bytes 786440 | tf_op jit(solution)/shard_map/ppermute | solution.py:393
  11.6 1.6 %collective-permute-start.4 = (f32[4,64,256]{2,1,0:T(8,128)}, f32[4,64,256]{2,1,0:T(8,128)S(1)}, u32[]{:S(2)}, u32[]{:S(2)}) collective-permute-start(f32[4,64,256]{2,1,0:T(8,128)} %get-tuple-element.37), channel_id=1, source_target_pairs={{0,8},{4,12},{8,0},{12,4},{16,24},{20,28},{24,16},{28,20},{1,9},{5... | collective-permute-start | bytes 786440 | tf_op jit(solution)/shard_map/ppermute | solution.py:393
  13.3 8.1 %shard_map.155 = (f32[4,64,256]{2,1,0:T(8,128)}, f32[4,64,256]{2,1,0:T(8,128)}, f32[4,64,256]{2,1,0:T(8,128)}, f32[4,64,256]{2,1,0:T(8,128)}) custom-call(s32[2]{0:T(128)} %pad_add_fusion.ids, bf16[256,512]{1,0:T(8,128)(2,1)} %constant.48.clone.kzh, bf16[256,512]{1,0:T(8,128)(2,1)} %constant.49.clone.kzl, f32[8,64,1024]{2,1,0:T(8,128)} %bitcast.5, ...), custom_call_target="tpu_custom_call" | custom-call | flops 2415919104 | bytes 6815752 | tf_op jit(solution)/shard_map/pallas_call | solution.py:76
  21.4 3.6 %collective-permute-done.5.refs_3_ = f32[4,64,256]{2,1,0:T(8,128)S(1)} collective-permute-done((f32[4,64,256]{2,1,0:T(8,128)}, f32[4,64,256]{2,1,0:T(8,128)S(1)}, u32[]{:S(2)}, u32[]{:S(2)}) %collective-permute-start.5) | collective-permute-done | bytes 262176 | tf_op jit(solution)/shard_map/ppermute | solution.py:393
  25.0 1.9 %shard_map.157 = (f32[2,4,64,256]{3,2,1,0:T(8,128)S(1)}, f32[16,4,256]{2,1,0:T(4,128)S(1)}) custom-call(s32[2]{0:T(128)S(1)} %copy-done.11, f32[8,1]{1,0:T(8,128)S(1)} %copy-done.10, f32[64,1]{1,0:T(8,128)S(1)} %copy-done.6, f32[1,1024]{1,0:T(1,128)S(1)} %copy-done.9, f32[64,2]{1,0:T(8,128)S(1)} %copy-done.5, f32[4,64,256]{2,1,0:T(8,128)S(1)} %copy-done.4, ...), custom_call_target="tpu_custom_call" | custom-call | flops 26214400 | bytes 1053480 | tf_op jit(solution)/shard_map/pallas_call | solution.py:76
  26.9 2.8 %collective-permute-start.6 = (f32[2,4,64,256]{3,2,1,0:T(8,128)S(1)}, f32[2,4,64,256]{3,2,1,0:T(8,128)S(1)}, u32[]{:S(2)}, u32[]{:S(2)}) collective-permute-start(f32[2,4,64,256]{3,2,1,0:T(8,128)S(1)} %get-tuple-element.39), channel_id=1, source_target_pairs={{0,16},{4,20},{8,24},{12,28},{16,0},{20,4},{24,8},{28,12},{1,17},{... | collective-permute-start | bytes 1572872 | tf_op jit(solution)/shard_map/ppermute | solution.py:393
  29.7 1.5 %collective-permute-start = (f32[4,64,256]{2,1,0:T(8,128)}, f32[4,64,256]{2,1,0:T(8,128)S(1)}, u32[]{:S(2)}, u32[]{:S(2)}) collective-permute-start(f32[4,64,256]{2,1,0:T(8,128)} %get-tuple-element.31), channel_id=1, source_target_pairs={{0,4},{4,0},{8,12},{12,8},{16,20},{20,16},{24,28},{28,24},{1,5},{5... | collective-permute-start | bytes 786440 | tf_op jit(solution)/shard_map/ppermute | solution.py:393
  31.2 1.6 %collective-permute-start.1 = (f32[4,64,256]{2,1,0:T(8,128)}, f32[4,64,256]{2,1,0:T(8,128)S(1)}, u32[]{:S(2)}, u32[]{:S(2)}) collective-permute-start(f32[4,64,256]{2,1,0:T(8,128)} %get-tuple-element.32), channel_id=1, source_target_pairs={{0,8},{4,12},{8,0},{12,4},{16,24},{20,28},{24,16},{28,20},{1,9},{5... | collective-permute-start | bytes 786440 | tf_op jit(solution)/shard_map/ppermute | solution.py:393
  33.2 4.3 %collective-permute-done.9.refs_3_ = f32[16,4,256]{2,1,0:T(4,128)S(1)} collective-permute-done((f32[16,4,256]{2,1,0:T(4,128)S(1)}, f32[16,4,256]{2,1,0:T(4,128)S(1)}, u32[]{:S(2)}, u32[]{:S(2)}) %collective-permute-start.9) | collective-permute-done | bytes 65568 | tf_op jit(solution)/shard_map/ppermute | solution.py:393
  37.5 0.8 collective-permute-start.8
  38.4 3.4 %collective-permute-done.8.refs_2_ = f32[16,4,256]{2,1,0:T(4,128)S(1)} collective-permute-done((f32[16,4,256]{2,1,0:T(4,128)S(1)}, f32[16,4,256]{2,1,0:T(4,128)S(1)}, u32[]{:S(2)}, u32[]{:S(2)}) %collective-permute-start.8) | collective-permute-done | bytes 65568 | tf_op jit(solution)/shard_map/ppermute | solution.py:393
  41.8 1.3 %collective-permute-done.7.refs_1_ = f32[16,4,256]{2,1,0:T(4,128)S(1)} collective-permute-done((f32[16,4,256]{2,1,0:T(4,128)S(1)}, f32[16,4,256]{2,1,0:T(4,128)S(1)}, u32[]{:S(2)}, u32[]{:S(2)}) %collective-permute-start.7) | collective-permute-done | bytes 65568 | tf_op jit(solution)/shard_map/ppermute | solution.py:393
  43.1 1.0 shard_map.158.refs_5_
  44.3 3.6 %collective-permute-done.1.refs_2_ = f32[4,64,256]{2,1,0:T(8,128)S(1)} collective-permute-done((f32[4,64,256]{2,1,0:T(8,128)}, f32[4,64,256]{2,1,0:T(8,128)S(1)}, u32[]{:S(2)}, u32[]{:S(2)}) %collective-permute-start.1) | collective-permute-done | bytes 262176 | tf_op jit(solution)/shard_map/ppermute | solution.py:393
  47.8 4.9 %collective-permute-done.2.refs_3_ = f32[4,64,256]{2,1,0:T(8,128)S(1)} collective-permute-done((f32[4,64,256]{2,1,0:T(8,128)}, f32[4,64,256]{2,1,0:T(8,128)S(1)}, u32[]{:S(2)}, u32[]{:S(2)}) %collective-permute-start.2) | collective-permute-done | bytes 262176 | tf_op jit(solution)/shard_map/ppermute | solution.py:393
  52.8 1.9 %shard_map.156 = (f32[2,4,64,256]{3,2,1,0:T(8,128)S(1)}, f32[16,4,256]{2,1,0:T(4,128)S(1)}) custom-call(s32[2]{0:T(128)S(1)} %copy-done.11, f32[8,1]{1,0:T(8,128)S(1)} %copy-done.10, f32[64,1]{1,0:T(8,128)S(1)} %copy-done.6, f32[1,1024]{1,0:T(1,128)S(1)} %copy-done.9, f32[64,2]{1,0:T(8,128)S(1)} %copy-done.5, f32[4,64,256]{2,1,0:T(8,128)S(1)} %copy-done.3, ...), custom_call_target="tpu_custom_call" | custom-call | flops 26214400 | bytes 1053480 | tf_op jit(solution)/shard_map/pallas_call | solution.py:76
  54.9 2.2 %collective-permute-start.11 = (f32[2,4,64,256]{3,2,1,0:T(8,128)S(1)}, f32[2,4,64,256]{3,2,1,0:T(8,128)S(1)}, u32[]{:S(2)}, u32[]{:S(2)}) collective-permute-start(f32[2,4,64,256]{3,2,1,0:T(8,128)S(1)} %get-tuple-element.41), channel_id=1, source_target_pairs={{0,16},{4,20},{8,24},{12,28},{16,0},{20,4},{24,8},{28,12},{1,17},{... | collective-permute-start | bytes 1572872 | tf_op jit(solution)/shard_map/ppermute | solution.py:393
  57.0 2.0 %shard_map.161 = (f32[4,64,256]{2,1,0:T(8,128)S(1)}, f32[4,64,256]{2,1,0:T(8,128)S(1)}, f32[4,64,256]{2,1,0:T(8,128)S(1)}, f32[4,64,256]{2,1,0:T(8,128)S(1)}) custom-call(s32[2]{0:T(128)S(1)} %copy-done.11, f32[8,1]{1,0:T(8,128)S(1)} %copy-done.10, f32[64,1]{1,0:T(8,128)S(1)} %copy-done.6, f32[1,1024]{1,0:T(1,128)S(1)} %copy-done.9, f32[64,2]{1,0:T(8,128)S(1)} %copy-done.5, ...), custom_call_target="tpu_custom_call" | custom-call | flops 26214400 | bytes 1708840 | tf_op jit(solution)/shard_map/pallas_call | solution.py:76
  59.0 1.7 %collective-permute-start.19 = (f32[4,64,256]{2,1,0:T(8,128)S(1)}, f32[4,64,256]{2,1,0:T(8,128)S(1)}, u32[]{:S(2)}, u32[]{:S(2)}) collective-permute-start(f32[4,64,256]{2,1,0:T(8,128)S(1)} %get-tuple-element.48), channel_id=1, source_target_pairs={{0,4},{4,0},{8,12},{12,8},{16,20},{20,16},{24,28},{28,24},{1,5},{5... | collective-permute-start | bytes 786440 | tf_op jit(solution)/shard_map/ppermute | solution.py:393
  60.7 2.3 %collective-permute-start.20 = (f32[4,64,256]{2,1,0:T(8,128)S(1)}, f32[4,64,256]{2,1,0:T(8,128)S(1)}, u32[]{:S(2)}, u32[]{:S(2)}) collective-permute-start(f32[4,64,256]{2,1,0:T(8,128)S(1)} %get-tuple-element.49), channel_id=1, source_target_pairs={{0,8},{4,12},{8,0},{12,4},{16,24},{20,28},{24,16},{28,20},{1,9},{5... | collective-permute-start | bytes 786440 | tf_op jit(solution)/shard_map/ppermute | solution.py:393
  63.0 1.1 %collective-permute-start.13 = (f32[16,4,256]{2,1,0:T(4,128)S(1)}, f32[16,4,256]{2,1,0:T(4,128)S(1)}, u32[]{:S(2)}, u32[]{:S(2)}) collective-permute-start(f32[16,4,256]{2,1,0:T(4,128)S(1)} %get-tuple-element.42.refs_0_), channel_id=1, source_target_pairs={{0,2},{1,3},{2,0},{3,1},{4,6},{5,7},{6,4},{7,5},{8,10},{9,11},{10,... | collective-permute-start | bytes 196616 | tf_op jit(solution)/shard_map/ppermute | solution.py:393
  64.1 3.3 %collective-permute-done.13.refs_2_ = f32[16,4,256]{2,1,0:T(4,128)S(1)} collective-permute-done((f32[16,4,256]{2,1,0:T(4,128)S(1)}, f32[16,4,256]{2,1,0:T(4,128)S(1)}, u32[]{:S(2)}, u32[]{:S(2)}) %collective-permute-start.13) | collective-permute-done | bytes 65568 | tf_op jit(solution)/shard_map/ppermute | solution.py:393
  67.3 1.3 %collective-permute-done.12.refs_1_ = f32[16,4,256]{2,1,0:T(4,128)S(1)} collective-permute-done((f32[16,4,256]{2,1,0:T(4,128)S(1)}, f32[16,4,256]{2,1,0:T(4,128)S(1)}, u32[]{:S(2)}, u32[]{:S(2)}) %collective-permute-start.12) | collective-permute-done | bytes 65568 | tf_op jit(solution)/shard_map/ppermute | solution.py:393
  68.6 1.0 shard_map.159.refs_5_
  69.6 2.7 %collective-permute-start.15 = (f32[16,4,256]{2,1,0:T(4,128)S(1)}, f32[16,4,256]{2,1,0:T(4,128)S(1)}, u32[]{:S(2)}, u32[]{:S(2)}) collective-permute-start(f32[16,4,256]{2,1,0:T(4,128)S(1)} %shard_map.159.refs_5_), channel_id=1, source_target_pairs={{0,16},{4,20},{8,24},{12,28},{16,0},{20,4},{24,8},{28,12},{1,17},{... | collective-permute-start | bytes 196616 | tf_op jit(solution)/shard_map/ppermute | solution.py:393
  72.3 9.0 %collective-permute-done.15.refs_6_ = f32[16,4,256]{2,1,0:T(4,128)S(1)} collective-permute-done((f32[16,4,256]{2,1,0:T(4,128)S(1)}, f32[16,4,256]{2,1,0:T(4,128)S(1)}, u32[]{:S(2)}, u32[]{:S(2)}) %collective-permute-start.15) | collective-permute-done | bytes 65568 | tf_op jit(solution)/shard_map/ppermute | solution.py:393
  81.3 2.2 %shard_map.160 = (f32[4,64,256]{2,1,0:T(8,128)S(1)}, f32[4,64,256]{2,1,0:T(8,128)S(1)}, f32[4,64,256]{2,1,0:T(8,128)S(1)}, f32[4,64,256]{2,1,0:T(8,128)S(1)}) custom-call(s32[2]{0:T(128)S(1)} %copy-done.11, f32[8,1]{1,0:T(8,128)S(1)} %copy-done.10, f32[64,1]{1,0:T(8,128)S(1)} %copy-done.6, f32[1,1024]{1,0:T(1,128)S(1)} %copy-done.9, f32[64,2]{1,0:T(8,128)S(1)} %copy-done.5, ...), custom_call_target="tpu_custom_call" | custom-call | flops 26214400 | bytes 1708840 | tf_op jit(solution)/shard_map/pallas_call | solution.py:76
  84.0 3.1 %collective-permute-start.17 = (f32[4,64,256]{2,1,0:T(8,128)S(1)}, f32[4,64,256]{2,1,0:T(8,128)S(1)}, u32[]{:S(2)}, u32[]{:S(2)}) collective-permute-start(f32[4,64,256]{2,1,0:T(8,128)S(1)} %get-tuple-element.45), channel_id=1, source_target_pairs={{0,8},{4,12},{8,0},{12,4},{16,24},{20,28},{24,16},{28,20},{1,9},{5... | collective-permute-start | bytes 786440 | tf_op jit(solution)/shard_map/ppermute | solution.py:393
  87.2 6.5 %shard_map.162.refs_4_ = f32[8,64,1024]{2,1,0:T(8,128)S(1)} custom-call(s32[2]{0:T(128)S(1)} %copy-done.11, bf16[512,256]{1,0:T(8,128)(2,1)S(1)} %copy-done.13, bf16[512,256]{1,0:T(8,128)(2,1)S(1)} %copy-done.12, bf16[1024,1024]{1,0:T(8,128)(2,1)S(1)} %copy-done.2, bf16[1024,1024]{1,0:T(8,128)(2,1)S(1)} %copy-done.1, ...), custom_call_target="tpu_custom_call" | custom-call | flops 2415919104 | bytes 5767176 | tf_op jit(solution)/shard_map/pallas_call | solution.py:76
  94.4 3.1 %collective-permute-done.18.refs_3_ = f32[4,64,256]{2,1,0:T(8,128)S(1)} collective-permute-done((f32[4,64,256]{2,1,0:T(8,128)S(1)}, f32[4,64,256]{2,1,0:T(8,128)S(1)}, u32[]{:S(2)}, u32[]{:S(2)}) %collective-permute-start.18) | collective-permute-done | bytes 262176 | tf_op jit(solution)/shard_map/ppermute | solution.py:393
  97.5 7.3 %shard_map.163 = f32[8,64,1024]{2,1,0:T(8,128)} custom-call(s32[2]{0:T(128)S(1)} %copy-done.11, bf16[512,256]{1,0:T(8,128)(2,1)S(1)} %copy-done.8, bf16[512,256]{1,0:T(8,128)(2,1)S(1)} %copy-done.7, bf16[1024,1024]{1,0:T(8,128)(2,1)S(1)} %copy-done.2, bf16[1024,1024]{1,0:T(8,128)(2,1)S(1)} %copy-done.1, f32[4,64,256]{2,1,0:T(8,128)S(1)} %get-tuple-element.43.refs_0_, ...), custom_call_target="tpu_custom_call" | custom-call | flops 2415919104 | bytes 7864328 | tf_op jit(solution)/shard_map/pallas_call | solution.py:76
  (51 shorter events, 2.7 us)
Async XLA Ops:
  8.6 12.8 %collective-permute-start.3 = (f32[4,64,256]{2,1,0:T(8,128)}, f32[4,64,256]{2,1,0:T(8,128)S(1)}, u32[]{:S(2)}, u32[]{:S(2)}) collective-permute-start(f32[4,64,256]{2,1,0:T(8,128)} %get-tuple-element.36), channel_id=1, source_target_pairs={{0,4},{4,0},{8,12},{12,8},{16,20},{20,16},{24,28},{28,24},{1,5},{5... | collective-permute-start | bytes 786440 | tf_op jit(solution)/shard_map/ppermute | solution.py:393
  11.6 9.8 %collective-permute-start.4 = (f32[4,64,256]{2,1,0:T(8,128)}, f32[4,64,256]{2,1,0:T(8,128)S(1)}, u32[]{:S(2)}, u32[]{:S(2)}) collective-permute-start(f32[4,64,256]{2,1,0:T(8,128)} %get-tuple-element.37), channel_id=1, source_target_pairs={{0,8},{4,12},{8,0},{12,4},{16,24},{20,28},{24,16},{28,20},{1,9},{5... | collective-permute-start | bytes 786440 | tf_op jit(solution)/shard_map/ppermute | solution.py:393
  13.2 11.8 %copy-start.6 = (f32[64,1]{1,0:T(8,128)S(1)}, f32[64,1]{1,0:T(8,128)}, u32[]{:S(2)}) copy-start(f32[64,1]{1,0:T(8,128)} %constant.42.clone.smu_y) | copy-start | bytes 772
  13.2 11.8 %copy-start.9 = (f32[1,1024]{1,0:T(1,128)S(1)}, f32[1,1024]{1,0:T(1,128)}, u32[]{:S(2)}) copy-start(f32[1,1024]{1,0:T(1,128)} %constant.43.clone.smu_x) | copy-start | bytes 12292
  13.2 11.8 %copy-start.10 = (f32[8,1]{1,0:T(8,128)S(1)}, f32[8,1]{1,0:T(8,128)}, u32[]{:S(2)}) copy-start(f32[8,1]{1,0:T(8,128)} %constant.41.clone.smu_z) | copy-start | bytes 100
  13.2 11.8 %copy-start.11 = (s32[2]{0:T(128)S(1)}, s32[2]{0:T(128)}, u32[]{:S(2)}) copy-start(s32[2]{0:T(128)} %pad_add_fusion.ids) | copy-start | bytes 28
  13.2 29.9 %copy-start = (f32[5,4,8,1024]{3,2,1,0:T(8,128)S(1)}, f32[5,4,8,1024]{3,2,1,0:T(8,128)}, u32[]{:S(2)}) copy-start(f32[5,4,8,1024]{3,2,1,0:T(8,128)} %constant.45.clone.responses) | copy-start | bytes 1966084
  13.2 11.8 %collective-permute-start.5 = (f32[4,64,256]{2,1,0:T(8,128)}, f32[4,64,256]{2,1,0:T(8,128)S(1)}, u32[]{:S(2)}, u32[]{:S(2)}) collective-permute-start(f32[4,64,256]{2,1,0:T(8,128)} %get-tuple-element.38), channel_id=1, source_target_pairs={{0,12},{4,8},{8,4},{12,0},{16,28},{20,24},{24,20},{28,16},{1,13},{... | collective-permute-start | bytes 786440 | tf_op jit(solution)/shard_map/ppermute | solution.py:393
  21.4 31.4 %copy-start.3 = (f32[4,64,256]{2,1,0:T(8,128)S(1)}, f32[4,64,256]{2,1,0:T(8,128)}, u32[]{:S(2)}) copy-start(f32[4,64,256]{2,1,0:T(8,128)} %get-tuple-element.30.refs_0_) | copy-start | bytes 786436
  26.9 28.0 %collective-permute-start.6 = (f32[2,4,64,256]{3,2,1,0:T(8,128)S(1)}, f32[2,4,64,256]{3,2,1,0:T(8,128)S(1)}, u32[]{:S(2)}, u32[]{:S(2)}) collective-permute-start(f32[2,4,64,256]{3,2,1,0:T(8,128)S(1)} %get-tuple-element.39), channel_id=1, source_target_pairs={{0,16},{4,20},{8,24},{12,28},{16,0},{20,4},{24,8},{28,12},{1,17},{... | collective-permute-start | bytes 1572872 | tf_op jit(solution)/shard_map/ppermute | solution.py:393
  29.7 14.5 %collective-permute-start = (f32[4,64,256]{2,1,0:T(8,128)}, f32[4,64,256]{2,1,0:T(8,128)S(1)}, u32[]{:S(2)}, u32[]{:S(2)}) collective-permute-start(f32[4,64,256]{2,1,0:T(8,128)} %get-tuple-element.31), channel_id=1, source_target_pairs={{0,4},{4,0},{8,12},{12,8},{16,20},{20,16},{24,28},{28,24},{1,5},{5... | collective-permute-start | bytes 786440 | tf_op jit(solution)/shard_map/ppermute | solution.py:393
  31.2 16.6 %collective-permute-start.1 = (f32[4,64,256]{2,1,0:T(8,128)}, f32[4,64,256]{2,1,0:T(8,128)S(1)}, u32[]{:S(2)}, u32[]{:S(2)}) collective-permute-start(f32[4,64,256]{2,1,0:T(8,128)} %get-tuple-element.32), channel_id=1, source_target_pairs={{0,8},{4,12},{8,0},{12,4},{16,24},{20,28},{24,16},{28,20},{1,9},{5... | collective-permute-start | bytes 786440 | tf_op jit(solution)/shard_map/ppermute | solution.py:393
  32.8 20.0 %collective-permute-start.2 = (f32[4,64,256]{2,1,0:T(8,128)}, f32[4,64,256]{2,1,0:T(8,128)S(1)}, u32[]{:S(2)}, u32[]{:S(2)}) collective-permute-start(f32[4,64,256]{2,1,0:T(8,128)} %get-tuple-element.33), channel_id=1, source_target_pairs={{0,12},{4,8},{8,4},{12,0},{16,28},{20,24},{24,20},{28,16},{1,13},{... | collective-permute-start | bytes 786440 | tf_op jit(solution)/shard_map/ppermute | solution.py:393
  33.2 4.3 %collective-permute-start.9 = (f32[16,4,256]{2,1,0:T(4,128)S(1)}, f32[16,4,256]{2,1,0:T(4,128)S(1)}, u32[]{:S(2)}, u32[]{:S(2)}) collective-permute-start(f32[16,4,256]{2,1,0:T(4,128)S(1)} %get-tuple-element.40.refs_0_), channel_id=1, source_target_pairs={{0,3},{1,2},{2,1},{3,0},{4,7},{5,6},{6,5},{7,4},{8,11},{9,10},{10,... | collective-permute-start | bytes 196616 | tf_op jit(solution)/shard_map/ppermute | solution.py:393
  37.5 4.3 %collective-permute-start.8 = (f32[16,4,256]{2,1,0:T(4,128)S(1)}, f32[16,4,256]{2,1,0:T(4,128)S(1)}, u32[]{:S(2)}, u32[]{:S(2)}) collective-permute-start(f32[16,4,256]{2,1,0:T(4,128)S(1)} %get-tuple-element.40.refs_0_), channel_id=1, source_target_pairs={{0,2},{1,3},{2,0},{3,1},{4,6},{5,7},{6,4},{7,5},{8,10},{9,11},{10,... | collective-permute-start | bytes 196616 | tf_op jit(solution)/shard_map/ppermute | solution.py:393
  41.8 1.3 %collective-permute-start.7 = (f32[16,4,256]{2,1,0:T(4,128)S(1)}, f32[16,4,256]{2,1,0:T(4,128)S(1)}, u32[]{:S(2)}, u32[]{:S(2)}) collective-permute-start(f32[16,4,256]{2,1,0:T(4,128)S(1)} %get-tuple-element.40.refs_0_), channel_id=1, source_target_pairs={{0,1},{1,0},{2,3},{3,2},{4,5},{5,4},{6,7},{7,6},{8,9},{9,8},{10,11... | collective-permute-start | bytes 196616 | tf_op jit(solution)/shard_map/ppermute | solution.py:393
  44.1 10.8 %collective-permute-start.10 = (f32[16,4,256]{2,1,0:T(4,128)S(1)}, f32[16,4,256]{2,1,0:T(4,128)S(1)}, u32[]{:S(2)}, u32[]{:S(2)}) collective-permute-start(f32[16,4,256]{2,1,0:T(4,128)S(1)} %shard_map.158.refs_5_), channel_id=1, source_target_pairs={{0,16},{4,20},{8,24},{12,28},{16,0},{20,4},{24,8},{28,12},{1,17},{... | collective-permute-start | bytes 196616 | tf_op jit(solution)/shard_map/ppermute | solution.py:393
  52.8 34.4 %copy-start.13 = (bf16[512,256]{1,0:T(8,128)(2,1)S(1)}, bf16[512,256]{1,0:T(8,128)(2,1)}, u32[]{:S(2)}) copy-start(bf16[512,256]{1,0:T(8,128)(2,1)} %constant.50.clone.kzh) | copy-start | bytes 786436
  54.9 26.4 %collective-permute-start.11 = (f32[2,4,64,256]{3,2,1,0:T(8,128)S(1)}, f32[2,4,64,256]{3,2,1,0:T(8,128)S(1)}, u32[]{:S(2)}, u32[]{:S(2)}) collective-permute-start(f32[2,4,64,256]{3,2,1,0:T(8,128)S(1)} %get-tuple-element.41), channel_id=1, source_target_pairs={{0,16},{4,20},{8,24},{12,28},{16,0},{20,4},{24,8},{28,12},{1,17},{... | collective-permute-start | bytes 1572872 | tf_op jit(solution)/shard_map/ppermute | solution.py:393
  57.0 30.2 %copy-start.1 = (bf16[1024,1024]{1,0:T(8,128)(2,1)S(1)}, bf16[1024,1024]{1,0:T(8,128)(2,1)}, u32[]{:S(2)}) copy-start(bf16[1024,1024]{1,0:T(8,128)(2,1)} %constant.40.clone.sxl) | copy-start | bytes 6291460
  57.0 30.2 %copy-start.2 = (bf16[1024,1024]{1,0:T(8,128)(2,1)S(1)}, bf16[1024,1024]{1,0:T(8,128)(2,1)}, u32[]{:S(2)}) copy-start(bf16[1024,1024]{1,0:T(8,128)(2,1)} %constant.39.clone.sxh) | copy-start | bytes 6291460
  57.0 30.2 %copy-start.12 = (bf16[512,256]{1,0:T(8,128)(2,1)S(1)}, bf16[512,256]{1,0:T(8,128)(2,1)}, u32[]{:S(2)}) copy-start(bf16[512,256]{1,0:T(8,128)(2,1)} %constant.51.clone.kzl) | copy-start | bytes 786436
  57.0 6.0 %collective-permute-start.14 = (f32[16,4,256]{2,1,0:T(4,128)S(1)}, f32[16,4,256]{2,1,0:T(4,128)S(1)}, u32[]{:S(2)}, u32[]{:S(2)}) collective-permute-start(f32[16,4,256]{2,1,0:T(4,128)S(1)} %get-tuple-element.42.refs_0_), channel_id=1, source_target_pairs={{0,3},{1,2},{2,1},{3,0},{4,7},{5,6},{6,5},{7,4},{8,11},{9,10},{10,... | collective-permute-start | bytes 196616 | tf_op jit(solution)/shard_map/ppermute | solution.py:393
  59.0 28.1 %collective-permute-start.19 = (f32[4,64,256]{2,1,0:T(8,128)S(1)}, f32[4,64,256]{2,1,0:T(8,128)S(1)}, u32[]{:S(2)}, u32[]{:S(2)}) collective-permute-start(f32[4,64,256]{2,1,0:T(8,128)S(1)} %get-tuple-element.48), channel_id=1, source_target_pairs={{0,4},{4,0},{8,12},{12,8},{16,20},{20,16},{24,28},{28,24},{1,5},{5... | collective-permute-start | bytes 786440 | tf_op jit(solution)/shard_map/ppermute | solution.py:393
  60.7 26.5 %collective-permute-start.20 = (f32[4,64,256]{2,1,0:T(8,128)S(1)}, f32[4,64,256]{2,1,0:T(8,128)S(1)}, u32[]{:S(2)}, u32[]{:S(2)}) collective-permute-start(f32[4,64,256]{2,1,0:T(8,128)S(1)} %get-tuple-element.49), channel_id=1, source_target_pairs={{0,8},{4,12},{8,0},{12,4},{16,24},{20,28},{24,16},{28,20},{1,9},{5... | collective-permute-start | bytes 786440 | tf_op jit(solution)/shard_map/ppermute | solution.py:393
  63.0 24.2 %collective-permute-start.21 = (f32[4,64,256]{2,1,0:T(8,128)S(1)}, f32[4,64,256]{2,1,0:T(8,128)S(1)}, u32[]{:S(2)}, u32[]{:S(2)}) collective-permute-start(f32[4,64,256]{2,1,0:T(8,128)S(1)} %get-tuple-element.50), channel_id=1, source_target_pairs={{0,12},{4,8},{8,4},{12,0},{16,28},{20,24},{24,20},{28,16},{1,13},{... | collective-permute-start | bytes 786440 | tf_op jit(solution)/shard_map/ppermute | solution.py:393
  63.0 4.3 %collective-permute-start.13 = (f32[16,4,256]{2,1,0:T(4,128)S(1)}, f32[16,4,256]{2,1,0:T(4,128)S(1)}, u32[]{:S(2)}, u32[]{:S(2)}) collective-permute-start(f32[16,4,256]{2,1,0:T(4,128)S(1)} %get-tuple-element.42.refs_0_), channel_id=1, source_target_pairs={{0,2},{1,3},{2,0},{3,1},{4,6},{5,7},{6,4},{7,5},{8,10},{9,11},{10,... | collective-permute-start | bytes 196616 | tf_op jit(solution)/shard_map/ppermute | solution.py:393
  67.3 1.3 %collective-permute-start.12 = (f32[16,4,256]{2,1,0:T(4,128)S(1)}, f32[16,4,256]{2,1,0:T(4,128)S(1)}, u32[]{:S(2)}, u32[]{:S(2)}) collective-permute-start(f32[16,4,256]{2,1,0:T(4,128)S(1)} %get-tuple-element.42.refs_0_), channel_id=1, source_target_pairs={{0,1},{1,0},{2,3},{3,2},{4,5},{5,4},{6,7},{7,6},{8,9},{9,8},{10,11... | collective-permute-start | bytes 196616 | tf_op jit(solution)/shard_map/ppermute | solution.py:393
  69.6 11.7 %collective-permute-start.15 = (f32[16,4,256]{2,1,0:T(4,128)S(1)}, f32[16,4,256]{2,1,0:T(4,128)S(1)}, u32[]{:S(2)}, u32[]{:S(2)}) collective-permute-start(f32[16,4,256]{2,1,0:T(4,128)S(1)} %shard_map.159.refs_5_), channel_id=1, source_target_pairs={{0,16},{4,20},{8,24},{12,28},{16,0},{20,4},{24,8},{28,12},{1,17},{... | collective-permute-start | bytes 196616 | tf_op jit(solution)/shard_map/ppermute | solution.py:393
  83.5 10.3 %collective-permute-start.16 = (f32[4,64,256]{2,1,0:T(8,128)S(1)}, f32[4,64,256]{2,1,0:T(8,128)S(1)}, u32[]{:S(2)}, u32[]{:S(2)}) collective-permute-start(f32[4,64,256]{2,1,0:T(8,128)S(1)} %get-tuple-element.44), channel_id=1, source_target_pairs={{0,4},{4,0},{8,12},{12,8},{16,20},{20,16},{24,28},{28,24},{1,5},{5... | collective-permute-start | bytes 786440 | tf_op jit(solution)/shard_map/ppermute | solution.py:393
  84.0 10.3 %collective-permute-start.17 = (f32[4,64,256]{2,1,0:T(8,128)S(1)}, f32[4,64,256]{2,1,0:T(8,128)S(1)}, u32[]{:S(2)}, u32[]{:S(2)}) collective-permute-start(f32[4,64,256]{2,1,0:T(8,128)S(1)} %get-tuple-element.45), channel_id=1, source_target_pairs={{0,8},{4,12},{8,0},{12,4},{16,24},{20,28},{24,16},{28,20},{1,9},{5... | collective-permute-start | bytes 786440 | tf_op jit(solution)/shard_map/ppermute | solution.py:393
  87.1 10.3 %collective-permute-start.18 = (f32[4,64,256]{2,1,0:T(8,128)S(1)}, f32[4,64,256]{2,1,0:T(8,128)S(1)}, u32[]{:S(2)}, u32[]{:S(2)}) collective-permute-start(f32[4,64,256]{2,1,0:T(8,128)S(1)} %get-tuple-element.46), channel_id=1, source_target_pairs={{0,12},{4,8},{8,4},{12,0},{16,28},{20,24},{24,20},{28,16},{1,13},{... | collective-permute-start | bytes 786440 | tf_op jit(solution)/shard_map/ppermute | solution.py:393
  (4 other events, 44.2 us)

commit v6 on v3

--- a/solution.py
+++ b/solution.py
@@ -11,9 +11,9 @@
 
 ALPHA_RATIO = 0.95
 STEP_SCALE = 0.26
-CHUNKS = (4, 4)
 LANES = 128
 STRIP = 16
+FINE_ROWS = 32
 VMEM_BYTES = 40 * 1024 * 1024
 
 
@@ -65,7 +65,7 @@
     return dot(left[0], right[0]) + dot(left[1], right[0]) + dot(left[0], right[1])
 
 
-def call(kernel, out_shape, flops, args, scratch=()):
+def call(kernel, out_shape, flops, args, scratch=(), out=None):
     smem = pl.BlockSpec(memory_space=pltpu.SMEM)
     vmem = pl.BlockSpec(memory_space=pltpu.VMEM)
     moved = sum(x.size * x.dtype.itemsize for x in args)
@@ -73,7 +73,7 @@
         kernel,
         out_shape=out_shape,
         in_specs=[smem] + [vmem] * (len(args) - 1),
-        out_specs=jax.tree.map(lambda _: vmem, out_shape),
+        out_specs=out or jax.tree.map(lambda _: vmem, out_shape),
         scratch_shapes=scratch,
         compiler_params=pltpu.CompilerParams(vmem_limit_bytes=VMEM_BYTES),
         cost_estimate=pl.CostEstimate(
@@ -90,51 +90,90 @@
         self.rows = shape[2] // self.groups
         self.half = self.steps // 2
         self.block = self.width // self.half
-        self.chunks = []
-        first = 0
-        for size in CHUNKS:
-            size = min(size, self.depth - first)
-            if size:
-                self.chunks.append((first, size))
-            first += size
+        self.planes = self.depth // 2
 
     def columns(self, owner):
         return pl.ds(pl.multiple_of(owner * self.block, LANES), self.block)
 
 
-def forward(plan, planes, ids, kzh, kzl, x, sxh, sxl, *outs):
+def fill_table(plan, ids, coarse_sin, coarse_cos, fine_sin, fine_cos, high, low):
+    fine = fine_sin.shape[0]
+
+    def step(index, carry):
+        rows = pl.ds(pl.multiple_of(index * fine, fine), fine)
+        row = pl.ds(index, 1)
+        value = coarse_sin[row, :] * fine_cos[...] + coarse_cos[row, :] * fine_sin[...]
+        high[rows, :], low[rows, :] = parts_of(value)
+        return carry
+
+    lax.fori_loop(0, plan.width // fine, step, 0)
+
+
+def angle_tables(count, fine):
+    scale = math.sqrt(2.0 / (count + 1))
+    columns = np.arange(count, dtype=np.int64) + 1
+    tables = []
+    for rows, factor in (
+        (np.arange(count // fine, dtype=np.int64) * fine, scale),
+        (np.arange(fine, dtype=np.int64) + 1, 1.0),
+    ):
+        turns = rows[:, None] * columns[None, :] % (2 * (count + 1))
+        angle = np.pi * turns / (count + 1)
+        tables += [factor * np.sin(angle), factor * np.cos(angle)]
+    return [jnp.asarray(table, jnp.float32) for table in tables]
+
+
+def forward(plan, parity, ids, kzh, kzl, x, sxh, sxl, *outs):
     place = lax.rem(ids[0], plan.half)
-    whole = parts_of(x[...].reshape(plan.depth * plan.rows, plan.width))
-    left = parts_of(dot_parts((kzh[...], kzl[...]), whole))
+    planes = plan.planes
+    mirror = jnp.stack([x[plan.depth - 1 - z] for z in range(planes)])
+    folded = x[:planes] - mirror if parity else x[:planes] + mirror
+    folded = parts_of(folded.reshape(planes * plan.rows, plan.width))
+    left = parts_of(dot_parts((kzh[...], kzl[...]), folded))
     for k in range(plan.half):
         columns = plan.columns(place ^ k)
         value = dot_parts(left, (sxh[:, columns], sxl[:, columns]))
         outs[k][...] = value.reshape(planes, plan.rows, plan.block)
 
 
-def backward(plan, planes, with_total, ids, kzh, kzl, sxh, sxl, *refs):
+def backward(plan, ids, kzh, kzl, sxh, sxl, *refs):
     place = lax.rem(ids[0], plan.half)
-    pieces, out = refs[: plan.half], refs[-1]
-    total = None
+    pieces, rest = refs[: plan.half], refs[plan.half :]
+    high, low = rest[-2:]
+    planes = plan.planes
     for k in range(plan.half):
-        at = plan.columns(place ^ k)
-        piece = parts_of(pieces[k][...].reshape(planes * plan.rows, plan.block))
-        value = dot_parts(piece, (sxh[at, :], sxl[at, :]))
-        total = value if total is None else total + value
-    value = dot_parts((kzh[...], kzl[...]), parts_of(total))
-    value = value.reshape(plan.depth, plan.rows, plan.width)
-    out[...] = refs[plan.half][...] + value if with_total else value
-
-
-def per_strip(plan, first, planes, place, smu_z, smu_y, smu_x, edges, body):
+        columns = plan.columns(place ^ k)
+        piece = pieces[k][...].reshape(planes * plan.rows, plan.block)
+        high[:, columns], low[:, columns] = parts_of(piece)
+    for j in range(plan.half):
+        columns = pl.ds(j * plan.block, plan.block)
+        total = dot_parts((high[...], low[...]), (sxh[:, columns], sxl[:, columns]))
+        value = dot_parts((kzh[...], kzl[...]), parts_of(total))
+        value = value.reshape(planes, plan.rows, plan.block)
+        if len(rest) == 3:
+            rest[0][:, :, columns] = value
+            continue
+        even, out, held, sent = rest[:4]
+        other = even[:, :, columns]
+        held[j, :planes] = other + value
+        for z in range(planes):
+            held[j, plan.depth - 1 - z] = other[z] - value[z]
+        pltpu.make_async_copy(held.at[j], out.at[:, :, columns], sent.at[j]).start()
+    if len(rest) > 3:
+        for j in range(plan.half):
+            columns = pl.ds(j * plan.block, plan.block)
+            pltpu.make_async_copy(held.at[j], out.at[:, :, columns], sent.at[j]).wait()
+
+
+def per_strip(plan, place, smu_z, smu_y, smu_x, edges, body):
     across = smu_x[:, plan.columns(place)]
 
     def step(index, carry):
         rows = pl.ds(pl.multiple_of(index * STRIP, STRIP), STRIP)
         plane = across + smu_y[rows, :]
         weights = edges[rows, 0:1], edges[rows, 1:2]
-        for u in range(planes):
-            body(u, rows, plane + smu_z[first + u : first + u + 1, :], weights)
+        for u in range(plan.planes):
+            body(u, rows, plane + smu_z[u : u + 1, :], weights)
         return carry
 
     lax.fori_loop(0, plan.rows // STRIP, step, 0)
@@ -182,9 +221,9 @@
         pl.when(place == case)(functools.partial(body, case))
 
 
-def half_end(plan, first, planes, ids, smu_z, smu_y, smu_x, edges, *refs):
+def half_end(plan, ids, smu_z, smu_y, smu_x, edges, *refs):
     pieces = refs[: plan.half]
-    ends, seen, sums = refs[plan.half :]
+    *before_seen, ends, seen, sums = refs[plan.half :]
     steps, half = plan.steps, plan.half
     place = lax.rem(ids[0], half)
     mine = ids[0] // half
@@ -208,10 +247,15 @@
                         term = sum(term[i : i + 8] for i in range(0, STRIP, 8))
                         sums[2 * (window * half + j) + edge, u] += term
 
-        per_strip(plan, first, planes, place, smu_z, smu_y, smu_x, edges, body)
+        per_strip(plan, place, smu_z, smu_y, smu_x, edges, body)
 
     by_place(plan, place, with_place)
-    seen[...] = jnp.sum(sums[...], axis=2)
+    own = jnp.sum(sums[...], axis=2)
+    if before_seen:
+        seen[:, : plan.planes] = before_seen[0][...]
+        seen[:, plan.planes :] = own
+    else:
+        seen[...] = own
 
 
 def c_mul(a, b):
@@ -229,7 +273,7 @@
     return real * inverse, -imag * inverse
 
 
-def join_rows(plan, first, planes, ids, responses, *refs):
+def join_rows(plan, ids, responses, *refs):
     groups, steps = plan.groups, plan.steps
     views = refs[:groups]
     out, seen, above, below = refs[groups:]
@@ -240,7 +284,7 @@
         seen[me ^ k] = views[k][...]
     radius = ALPHA_RATIO ** (1.0 / steps)
     grow = [radius**n for n in range(steps)]
-    nothing = jnp.zeros((planes, plan.block), jnp.float32)
+    nothing = jnp.zeros((plan.depth, plan.block), jnp.float32)
     for freq in range(steps // 2 + 1):
         angle = [2.0 * math.pi * (freq * n % steps) / steps for n in range(steps)]
 
@@ -257,7 +301,7 @@
         tail = [spectrum(block, 1) for block in range(groups)]
         near, far = (
             tuple(
-                responses[freq, 2 * kind + part, first : first + planes, columns]
+                responses[freq, 2 * kind + part, :, columns]
                 for part in range(2)
             )
             for kind in range(2)
@@ -309,7 +353,7 @@
             out[2 * ((n + 1) % steps) + edge] = total
 
 
-def half_solve(plan, first, planes, ids, smu_z, smu_y, smu_x, edges, *refs):
+def half_solve(plan, parity, ids, smu_z, smu_y, smu_x, edges, *refs):
     pieces = refs[: plan.half]
     far, beside, beside_far = refs[plan.half : plan.half + 3]
     outs = refs[plan.half + 3 :]
@@ -326,7 +370,8 @@
                 total = None
                 for edge in range(2):
                     at = 2 * (window * half + j) + edge
-                    row = beside[at, u : u + 1, :] + beside_far[at, u : u + 1, :]
+                    plane = pl.ds(parity * plan.planes + u, 1)
+                    row = beside[at, plane, :] + beside_far[at, plane, :]
                     term = weights[edge] * row
                     total = term if total is None else total + term
                 return total
@@ -345,7 +390,7 @@
             for j, value in enumerate(values):
                 outs[case ^ j][u, rows, :] = value
 
-        per_strip(plan, first, planes, place, smu_z, smu_y, smu_x, edges, body)
+        per_strip(plan, place, smu_z, smu_y, smu_x, edges, body)
 
     by_place(plan, place, with_place)
 
@@ -357,72 +402,93 @@
 
 
 def on_device(plan, residual):
-    steps, groups, half = plan.steps, plan.groups, plan.half
+    steps, groups, half, planes = plan.steps, plan.groups, plan.half, plan.planes
     ids = jnp.stack([lax.axis_index("tm"), lax.axis_index("gy")]).astype(jnp.int32)
     sine_rows = sine_table(plan.rows)
-    sxh, sxl = table_parts(sine_table(plan.width))
-    both = np.kron(sine_table(plan.depth), sine_rows)
+    sine_depth = sine_table(plan.depth)
     smu_z, smu_y, smu_x = (
-        jnp.asarray(STEP_SCALE * spectrum_of(count).reshape(shape), jnp.float32)
-        for count, shape in (
-            (plan.depth, (-1, 1)),
-            (plan.rows, (-1, 1)),
-            (plan.width, (1, -1)),
-        )
+        STEP_SCALE * spectrum_of(count) for count in (plan.depth, plan.rows, plan.width)
     )
+    smu_y = jnp.asarray(smu_y[:, None], jnp.float32)
+    smu_x = jnp.asarray(smu_x[None, :], jnp.float32)
     edges = jnp.asarray(sine_rows[:, [0, plan.rows - 1]], jnp.float32)
-    responses = jnp.asarray(edge_responses(steps, plan.depth, plan.rows, plan.width))
+    by_parity = np.arange(plan.depth).reshape(planes, 2).T.reshape(-1)
+    responses = edge_responses(steps, plan.depth, plan.rows, plan.width)
+    responses = jnp.asarray(responses[:, :, by_parity])
     field = residual[0]
     f32 = functools.partial(jax.ShapeDtypeStruct, dtype=jnp.float32)
-    total = None
-    for first, planes in plan.chunks:
-        modes = f32((planes, plan.rows, plan.block))
-        ends = f32((2,) + modes.shape)
-        seen = f32((2 * steps, planes, plan.block))
-        count = planes * plan.rows * plan.width
-        flops = 6 * count * (plan.width + plan.depth * plan.rows)
-        span = slice(first * plan.rows, (first + planes) * plan.rows)
-        small = (smu_z, smu_y, smu_x, edges)
+    modes = f32((planes, plan.rows, plan.block))
+    ends = f32((2,) + modes.shape)
+    count = planes * plan.rows * plan.width
+    flops = 6 * count * (plan.width + planes * plan.rows)
+    tables = call(
+        functools.partial(fill_table, plan),
+        [jax.ShapeDtypeStruct((plan.width, plan.width), jnp.bfloat16)] * 2,
+        8 * plan.width * plan.width,
+        (ids, *angle_tables(plan.width, FINE_ROWS)),
+    )
+    sent, small = [], []
+    for parity in range(2):
+        both = np.kron(sine_depth[parity::2, :planes], sine_rows)
         pieces = call(
-            functools.partial(forward, plan, planes),
+            functools.partial(forward, plan, parity),
             [modes] * half,
             flops,
-            (ids, *table_parts(both[span]), field, sxh, sxl),
-        )
-        pieces = [swap(v, "tm", steps, k) for k, v in enumerate(pieces)]
-        mine, view = call(
-            functools.partial(half_end, plan, first, planes),
-            [ends, seen],
+            (ids, *table_parts(both), field, *tables),
+        )
+        sent.append([swap(v, "tm", steps, k) for k, v in enumerate(pieces)])
+        smu_own = jnp.asarray(smu_z[parity::2, None], jnp.float32)
+        small.append((ids, smu_own, smu_y, smu_x, edges))
+    sent[0][0], sent[1][0] = lax.optimization_barrier((sent[0][0], sent[1][0]))
+    mine, seen = [], ()
+    for parity in range(2):
+        end, *seen = call(
+            functools.partial(half_end, plan),
+            [ends, f32((2 * steps, planes * (1 + parity), plan.block))],
             100 * count,
-            (ids, *small, *pieces),
+            (*small[parity], *sent[parity], *seen),
             [pltpu.VMEM((2 * steps, planes, 8, plan.block), jnp.float32)],
         )
-        far = swap(mine, "tm", steps, half)
-        views = [swap(view, "gy", groups, k) for k in range(groups)]
-        sides = pltpu.VMEM((groups, steps + 2, planes, plan.block), jnp.float32)
-        beside = call(
-            functools.partial(join_rows, plan, first, planes),
-            seen,
-            100 * count // plan.rows,
-            (ids, responses, *views),
-            [pltpu.VMEM((groups,) + seen.shape, jnp.float32), sides, sides],
-        )
-        beside_far = swap(beside, "tm", steps, half)
+        mine.append(end)
+    far = swap(mine[0], "tm", steps, half)
+    views = [swap(seen[0], "gy", groups, k) for k in range(groups)]
+    sides = pltpu.VMEM((groups, steps + 2, plan.depth, plan.block), jnp.float32)
+    beside = call(
+        functools.partial(join_rows, plan),
+        f32(seen[0].shape),
+        100 * plan.depth * plan.block * steps,
+        (ids, responses, *views),
+        [pltpu.VMEM((groups,) + seen[0].shape, jnp.float32), sides, sides],
+    )
+    beside_far = swap(beside, "tm", steps, half)
+    second, far, beside_far = lax.optimization_barrier((mine[1], far, beside_far))
+    far = [far, swap(second, "tm", steps, half)]
+    even = ()
+    for parity in range(2):
         pieces = call(
-            functools.partial(half_solve, plan, first, planes),
+            functools.partial(half_solve, plan, parity),
             [modes] * half,
             100 * count,
-            (ids, *small, *pieces, far, beside, beside_far),
+            (*small[parity], *sent[parity], far[parity], beside, beside_far),
         )
         pieces = [swap(v, "tm", steps, k) for k, v in enumerate(pieces)]
-        ready = () if total is None else (total,)
-        total = call(
-            functools.partial(backward, plan, planes, total is not None),
-            f32(field.shape),
+        both = np.kron(sine_depth[:planes, parity::2], sine_rows)
+        hold = [pltpu.VMEM((planes * plan.rows, plan.width), jnp.bfloat16)] * 2
+        if parity:
+            hold = [
+                pltpu.VMEM((half,) + field.shape[:2] + (plan.block,), jnp.float32),
+                pltpu.SemaphoreType.DMA((half,)),
+            ] + hold
+        result = call(
+            functools.partial(backward, plan),
+            f32(field.shape if parity else (planes,) + field.shape[1:]),
             flops,
-            (ids, *table_parts(both[:, span]), sxh, sxl, *pieces, *ready),
-        )
-    return total[None]
+            (ids, *table_parts(both), *tables, *pieces, *even),
+            hold,
+            pl.BlockSpec(memory_space=pltpu.HBM) if parity else None,
+        )
+        even = (result,)
+    return result[None]
 
 
 def solution(mesh):

time: 118 us -> 118 us (level)
  starting transfers between devices: 28 us -> 23.4 us
  Pallas kernels: 24.2 us -> 28.2 us
    ppermute x22 -> x18, starting transfers between devices: 28 us -> 23.4 us  [swap(): return lax.ppermute(values, axis, [(i, i ^ distance) for i in range(count)])]
    pallas_call x10, Pallas kernels: 24.2 us -> 28.2 us  [call(): pl.pallas_call(kernel, out_shape=out_shape, in_specs=[smem] + [vmem] * (l...]
    unnamed x38 -> x36, local copies, waits for them, and re-layouts: 6.73 us -> 7.06 us
    ppermute x22 -> x18, waiting for transfers between devices: 58.1 us -> 58.3 us  [swap(): return lax.ppermute(values, axis, [(i, i ^ distance) for i in range(count)])]
  transfers between devices with their start and end apart: 22 -> 18, of which waited for: 12 -> 9; matrix products, arithmetic and copies ran while one was open for 0% -> 0% of each run, Pallas kernels for 14% -> 15%
where the time goes in v6:
time: 118 us; the launch traced here: 117 us
  waiting for transfers between devices  58.3 us (49%)
  Pallas kernels  28.2 us (24%)
  starting transfers between devices  23.4 us (20%)
  local copies, waits for them, and re-layouts  7.06 us (6%)
    ppermute x18, waiting for transfers between devices, swap(): return lax.ppermute(values, axis, [(i, i ^ distance) for i in range(count)])  58.3 us
    pallas_call x10, Pallas kernels, call(): pl.pallas_call(kernel, out_shape=out_shape, in_specs=[smem] + [vmem] * (l...  28.2 us
    ppermute x18, starting transfers between devices, swap(): return lax.ppermute(values, axis, [(i, i ^ distance) for i in range(count)])  23.4 us
    unnamed x36, local copies, waits for them, and re-layouts  7.06 us
  transfers between devices with their start and end apart: 18, of which 9 were waited for; matrix products, arithmetic and copies ran while one was open for 0% of the time, Pallas kernels for 15%

profile of v6, /device:TPU:0, one launch (start us, length us, event | category | flops | bytes accessed | tf_op | source)
XLA Modules:
  0.0 117.4 jit_solution(9549195616196281357)
XLA Ops:
  1.9 0.9 copy-done.7
  3.7 1.7 %shard_map.181 = (bf16[1024,1024]{1,0:T(8,128)(2,1)S(1)}, bf16[1024,1024]{1,0:T(8,128)(2,1)S(1)}) custom-call(s32[2]{0:T(128)S(1)} %pad_add_fusion.ids, f32[32,1024]{1,0:T(8,128)S(1)} %copy-done.8, f32[32,1024]{1,0:T(8,128)S(1)} %copy-done.7, f32[32,1024]{1,0:T(8,128)S(1)} %copy-done.6, f32[32,1024]{1,0:T(8,128)S(1)} %copy-done.5), custom_call_target="tpu_custom_call" | custom-call | flops 8388608 | bytes 524296 | tf_op jit(solution)/shard_map/pallas_call | solution.py:72
  5.4 1.6 %copy-done.12 = f32[1,8,64,1024]{3,2,1,0:T(8,128)S(1)} copy-done((f32[1,8,64,1024]{3,2,1,0:T(8,128)S(1)}, f32[1,8,64,1024]{3,2,1,0:T(8,128)}, u32[]{:S(2)}) %copy-start.12) | copy-done | bytes 2097176
  8.8 2.8 %shard_map.182 = (f32[4,64,256]{2,1,0:T(8,128)S(1)}, f32[4,64,256]{2,1,0:T(8,128)S(1)}, f32[4,64,256]{2,1,0:T(8,128)S(1)}, f32[4,64,256]{2,1,0:T(8,128)S(1)}) custom-call(s32[2]{0:T(128)S(1)} %pad_add_fusion.ids, bf16[256,256]{1,0:T(8,128)(2,1)S(1)} %copy-done.17, bf16[256,256]{1,0:T(8,128)(2,1)S(1)} %copy-done.16, f32[8,64,1024]{2,1,0:T(8,128)S(1)} %bitcast.4, ...), custom_call_target="tpu_custom_call" | custom-call | flops 2013265920 | bytes 6553608 | tf_op jit(solution)/shard_map/pallas_call | solution.py:72
  11.6 3.0 %collective-permute-start.3 = (f32[4,64,256]{2,1,0:T(8,128)S(1)}, f32[4,64,256]{2,1,0:T(8,128)S(1)}, u32[]{:S(2)}, u32[]{:S(2)}) collective-permute-start(f32[4,64,256]{2,1,0:T(8,128)S(1)} %get-tuple-element.41), channel_id=1, source_target_pairs={{0,4},{4,0},{8,12},{12,8},{16,20},{20,16},{24,28},{28,24},{1,5},{5... | collective-permute-start | bytes 786440 | tf_op jit(solution)/shard_map/ppermute | solution.py:401
  14.7 1.6 %collective-permute-start.4 = (f32[4,64,256]{2,1,0:T(8,128)S(1)}, f32[4,64,256]{2,1,0:T(8,128)S(1)}, u32[]{:S(2)}, u32[]{:S(2)}) collective-permute-start(f32[4,64,256]{2,1,0:T(8,128)S(1)} %get-tuple-element.42), channel_id=1, source_target_pairs={{0,8},{4,12},{8,0},{12,4},{16,24},{20,28},{24,16},{28,20},{1,9},{5... | collective-permute-start | bytes 786440 | tf_op jit(solution)/shard_map/ppermute | solution.py:401
  16.4 2.8 %shard_map.183 = (f32[4,64,256]{2,1,0:T(8,128)S(1)}, f32[4,64,256]{2,1,0:T(8,128)S(1)}, f32[4,64,256]{2,1,0:T(8,128)S(1)}, f32[4,64,256]{2,1,0:T(8,128)S(1)}) custom-call(s32[2]{0:T(128)S(1)} %pad_add_fusion.ids, bf16[256,256]{1,0:T(8,128)(2,1)S(1)} %copy-done.4, bf16[256,256]{1,0:T(8,128)(2,1)S(1)} %copy-done.3, f32[8,64,1024]{2,1,0:T(8,128)S(1)} %bitcast.5, ...), custom_call_target="tpu_custom_call" | custom-call | flops 2013265920 | bytes 6553608 | tf_op jit(solution)/shard_map/pallas_call | solution.py:72
  19.2 1.9 %collective-permute-start = (f32[4,64,256]{2,1,0:T(8,128)S(1)}, f32[4,64,256]{2,1,0:T(8,128)S(1)}, u32[]{:S(2)}, u32[]{:S(2)}) collective-permute-start(f32[4,64,256]{2,1,0:T(8,128)S(1)} %get-tuple-element.37), channel_id=1, source_target_pairs={{0,4},{4,0},{8,12},{12,8},{16,20},{20,16},{24,28},{28,24},{1,5},{5... | collective-permute-start | bytes 786440 | tf_op jit(solution)/shard_map/ppermute | solution.py:401
  21.1 1.6 %collective-permute-start.1 = (f32[4,64,256]{2,1,0:T(8,128)S(1)}, f32[4,64,256]{2,1,0:T(8,128)S(1)}, u32[]{:S(2)}, u32[]{:S(2)}) collective-permute-start(f32[4,64,256]{2,1,0:T(8,128)S(1)} %get-tuple-element.38), channel_id=1, source_target_pairs={{0,8},{4,12},{8,0},{12,4},{16,24},{20,28},{24,16},{28,20},{1,9},{5... | collective-permute-start | bytes 786440 | tf_op jit(solution)/shard_map/ppermute | solution.py:401
  22.7 1.4 %collective-permute-start.2 = (f32[4,64,256]{2,1,0:T(8,128)S(1)}, f32[4,64,256]{2,1,0:T(8,128)S(1)}, u32[]{:S(2)}, u32[]{:S(2)}) collective-permute-start(f32[4,64,256]{2,1,0:T(8,128)S(1)} %get-tuple-element.39), channel_id=1, source_target_pairs={{0,12},{4,8},{8,4},{12,0},{16,28},{20,24},{24,20},{28,16},{1,13},{... | collective-permute-start | bytes 786440 | tf_op jit(solution)/shard_map/ppermute | solution.py:401
  24.1 4.9 %collective-permute-done.5.refs_3_ = f32[4,64,256]{2,1,0:T(8,128)S(1)} collective-permute-done((f32[4,64,256]{2,1,0:T(8,128)S(1)}, f32[4,64,256]{2,1,0:T(8,128)S(1)}, u32[]{:S(2)}, u32[]{:S(2)}) %collective-permute-start.5) | collective-permute-done | bytes 262176 | tf_op jit(solution)/shard_map/ppermute | solution.py:401
  29.1 1.9 %shard_map.184 = (f32[2,4,64,256]{3,2,1,0:T(8,128)S(1)}, f32[16,4,256]{2,1,0:T(4,128)S(1)}) custom-call(s32[2]{0:T(128)S(1)} %pad_add_fusion.ids, f32[4,1]{1,0:T(4,128)S(1)} %copy-done.11, f32[64,1]{1,0:T(8,128)S(1)} %copy-done.2, f32[1,1024]{1,0:T(1,128)S(1)} %copy-done.9, f32[64,2]{1,0:T(8,128)S(1)} %copy-done.1, ...), custom_call_target="tpu_custom_call" | custom-call | flops 26214400 | bytes 1053464 | tf_op jit(solution)/shard_map/pallas_call | solution.py:72
  31.0 3.1 %collective-permute-start.6 = (f32[2,4,64,256]{3,2,1,0:T(8,128)S(1)}, f32[2,4,64,256]{3,2,1,0:T(8,128)S(1)}, u32[]{:S(2)}, u32[]{:S(2)}) collective-permute-start(f32[2,4,64,256]{3,2,1,0:T(8,128)S(1)} %get-tuple-element.46), channel_id=1, source_target_pairs={{0,16},{4,20},{8,24},{12,28},{16,0},{20,4},{24,8},{28,12},{1,17},{... | collective-permute-start | bytes 1572872 | tf_op jit(solution)/shard_map/ppermute | solution.py:401
  34.1 10.1 %collective-permute-done.1.refs_2_ = f32[4,64,256]{2,1,0:T(8,128)S(1)} collective-permute-done((f32[4,64,256]{2,1,0:T(8,128)S(1)}, f32[4,64,256]{2,1,0:T(8,128)S(1)}, u32[]{:S(2)}, u32[]{:S(2)}) %collective-permute-start.1) | collective-permute-done | bytes 262176 | tf_op jit(solution)/shard_map/ppermute | solution.py:401
  44.2 3.1 %collective-permute-done.2.refs_3_ = f32[4,64,256]{2,1,0:T(8,128)S(1)} collective-permute-done((f32[4,64,256]{2,1,0:T(8,128)S(1)}, f32[4,64,256]{2,1,0:T(8,128)S(1)}, u32[]{:S(2)}, u32[]{:S(2)}) %collective-permute-start.2) | collective-permute-done | bytes 262176 | tf_op jit(solution)/shard_map/ppermute | solution.py:401
  47.3 1.9 %shard_map.185 = (f32[2,4,64,256]{3,2,1,0:T(8,128)S(1)}, f32[16,8,256]{2,1,0:T(8,128)S(1)}) custom-call(s32[2]{0:T(128)S(1)} %pad_add_fusion.ids, f32[4,1]{1,0:T(4,128)S(1)} %copy-done.10, f32[64,1]{1,0:T(8,128)S(1)} %copy-done.2, f32[1,1024]{1,0:T(1,128)S(1)} %copy-done.9, f32[64,2]{1,0:T(8,128)S(1)} %copy-done.1, ...), custom_call_target="tpu_custom_call" | custom-call | flops 26214400 | bytes 1119000 | tf_op jit(solution)/shard_map/pallas_call | solution.py:72
  49.3 1.7 %collective-permute-start.8 = (f32[16,8,256]{2,1,0:T(8,128)S(1)}, f32[16,8,256]{2,1,0:T(8,128)S(1)}, u32[]{:S(2)}, u32[]{:S(2)}) collective-permute-start(f32[16,8,256]{2,1,0:T(8,128)S(1)} %get-tuple-element.47.refs_0_), channel_id=1, source_target_pairs={{0,2},{1,3},{2,0},{3,1},{4,6},{5,7},{6,4},{7,5},{8,10},{9,11},{10,... | collective-permute-start | bytes 393224 | tf_op jit(solution)/shard_map/ppermute | solution.py:401
  51.2 3.7 %collective-permute-done.9.refs_3_ = f32[16,8,256]{2,1,0:T(8,128)S(1)} collective-permute-done((f32[16,8,256]{2,1,0:T(8,128)S(1)}, f32[16,8,256]{2,1,0:T(8,128)S(1)}, u32[]{:S(2)}, u32[]{:S(2)}) %collective-permute-start.9) | collective-permute-done | bytes 131104 | tf_op jit(solution)/shard_map/ppermute | solution.py:401
  54.9 3.0 %collective-permute-done.8.refs_2_ = f32[16,8,256]{2,1,0:T(8,128)S(1)} collective-permute-done((f32[16,8,256]{2,1,0:T(8,128)S(1)}, f32[16,8,256]{2,1,0:T(8,128)S(1)}, u32[]{:S(2)}, u32[]{:S(2)}) %collective-permute-start.8) | collective-permute-done | bytes 131104 | tf_op jit(solution)/shard_map/ppermute | solution.py:401
  57.9 1.2 shard_map.186.refs_5_
  59.8 8.4 %collective-permute-done.10.refs_6_ = f32[16,8,256]{2,1,0:T(8,128)S(1)} collective-permute-done((f32[16,8,256]{2,1,0:T(8,128)S(1)}, f32[16,8,256]{2,1,0:T(8,128)S(1)}, u32[]{:S(2)}, u32[]{:S(2)}) %collective-permute-start.10) | collective-permute-done | bytes 131104 | tf_op jit(solution)/shard_map/ppermute | solution.py:401
  68.2 2.0 %shard_map.188 = (f32[4,64,256]{2,1,0:T(8,128)S(1)}, f32[4,64,256]{2,1,0:T(8,128)S(1)}, f32[4,64,256]{2,1,0:T(8,128)S(1)}, f32[4,64,256]{2,1,0:T(8,128)S(1)}) custom-call(s32[2]{0:T(128)S(1)} %pad_add_fusion.ids, f32[4,1]{1,0:T(4,128)S(1)} %copy-done.11, f32[64,1]{1,0:T(8,128)S(1)} %copy-done.2, f32[1,1024]{1,0:T(1,128)S(1)} %copy-done.9, ...), custom_call_target="tpu_custom_call" | custom-call | flops 26214400 | bytes 1839896 | tf_op jit(solution)/shard_map/pallas_call | solution.py:72
  70.3 1.6 %collective-permute-start.15 = (f32[4,64,256]{2,1,0:T(8,128)S(1)}, f32[4,64,256]{2,1,0:T(8,128)S(1)}, u32[]{:S(2)}, u32[]{:S(2)}) collective-permute-start(f32[4,64,256]{2,1,0:T(8,128)S(1)} %get-tuple-element.56), channel_id=1, source_target_pairs={{0,4},{4,0},{8,12},{12,8},{16,20},{20,16},{24,28},{28,24},{1,5},{5... | collective-permute-start | bytes 786440 | tf_op jit(solution)/shard_map/ppermute | solution.py:401
  71.8 2.7 %collective-permute-start.16 = (f32[4,64,256]{2,1,0:T(8,128)S(1)}, f32[4,64,256]{2,1,0:T(8,128)S(1)}, u32[]{:S(2)}, u32[]{:S(2)}) collective-permute-start(f32[4,64,256]{2,1,0:T(8,128)S(1)} %get-tuple-element.57), channel_id=1, source_target_pairs={{0,8},{4,12},{8,0},{12,4},{16,24},{20,28},{24,16},{28,20},{1,9},{5... | collective-permute-start | bytes 786440 | tf_op jit(solution)/shard_map/ppermute | solution.py:401
  74.6 18.7 %collective-permute-done.11.refs_4_ = f32[2,4,64,256]{3,2,1,0:T(8,128)S(1)} collective-permute-done((f32[2,4,64,256]{3,2,1,0:T(8,128)S(1)}, f32[2,4,64,256]{3,2,1,0:T(8,128)S(1)}, u32[]{:S(2)}, u32[]{:S(2)}) %collective-permute-start.11) | collective-permute-done | bytes 524320 | tf_op jit(solution)/shard_map/ppermute | solution.py:401
  93.3 2.2 %shard_map.187 = (f32[4,64,256]{2,1,0:T(8,128)S(1)}, f32[4,64,256]{2,1,0:T(8,128)S(1)}, f32[4,64,256]{2,1,0:T(8,128)S(1)}, f32[4,64,256]{2,1,0:T(8,128)S(1)}) custom-call(s32[2]{0:T(128)S(1)} %pad_add_fusion.ids, f32[4,1]{1,0:T(4,128)S(1)} %copy-done.10, f32[64,1]{1,0:T(8,128)S(1)} %copy-done.2, f32[1,1024]{1,0:T(1,128)S(1)} %copy-done.9, ...), custom_call_target="tpu_custom_call" | custom-call | flops 26214400 | bytes 1839896 | tf_op jit(solution)/shard_map/pallas_call | solution.py:72
  95.5 2.2 %collective-permute-start.12 = (f32[4,64,256]{2,1,0:T(8,128)S(1)}, f32[4,64,256]{2,1,0:T(8,128)S(1)}, u32[]{:S(2)}, u32[]{:S(2)}) collective-permute-start(f32[4,64,256]{2,1,0:T(8,128)S(1)} %get-tuple-element.51), channel_id=1, source_target_pairs={{0,4},{4,0},{8,12},{12,8},{16,20},{20,16},{24,28},{28,24},{1,5},{5... | collective-permute-start | bytes 786440 | tf_op jit(solution)/shard_map/ppermute | solution.py:401
  97.6 1.5 %collective-permute-start.14 = (f32[4,64,256]{2,1,0:T(8,128)S(1)}, f32[4,64,256]{2,1,0:T(8,128)S(1)}, u32[]{:S(2)}, u32[]{:S(2)}) collective-permute-start(f32[4,64,256]{2,1,0:T(8,128)S(1)} %get-tuple-element.53), channel_id=1, source_target_pairs={{0,12},{4,8},{8,4},{12,0},{16,28},{20,24},{24,20},{28,16},{1,13},{... | collective-permute-start | bytes 786440 | tf_op jit(solution)/shard_map/ppermute | solution.py:401
  99.2 5.4 %shard_map.189.refs_4_ = f32[4,64,1024]{2,1,0:T(8,128)S(1)} custom-call(s32[2]{0:T(128)S(1)} %pad_add_fusion.ids, bf16[256,256]{1,0:T(8,128)(2,1)S(1)} %copy-done.15, bf16[256,256]{1,0:T(8,128)(2,1)S(1)} %copy-done.14, bf16[1024,1024]{1,0:T(8,128)(2,1)S(1)} %get-tuple-element.32.sxh, bf16[1024,1024]{1,0:T(8,128)(2,1)S(1)} %get-tuple-element.33.sxl, ...), custom_call_target="tpu_custom_call" | custom-call | flops 2013265920 | bytes 5505032 | tf_op jit(solution)/shard_map/pallas_call | solution.py:72
  104.6 2.2 %collective-permute-done.13.refs_2_ = f32[4,64,256]{2,1,0:T(8,128)S(1)} collective-permute-done((f32[4,64,256]{2,1,0:T(8,128)S(1)}, f32[4,64,256]{2,1,0:T(8,128)S(1)}, u32[]{:S(2)}, u32[]{:S(2)}) %collective-permute-start.13) | collective-permute-done | bytes 262176 | tf_op jit(solution)/shard_map/ppermute | solution.py:401
  106.8 4.1 %collective-permute-done.14.refs_3_ = f32[4,64,256]{2,1,0:T(8,128)S(1)} collective-permute-done((f32[4,64,256]{2,1,0:T(8,128)S(1)}, f32[4,64,256]{2,1,0:T(8,128)S(1)}, u32[]{:S(2)}, u32[]{:S(2)}) %collective-permute-start.14) | collective-permute-done | bytes 262176 | tf_op jit(solution)/shard_map/ppermute | solution.py:401
  110.9 6.3 %shard_map.190 = f32[8,64,1024]{2,1,0:T(8,128)} custom-call(s32[2]{0:T(128)S(1)} %pad_add_fusion.ids, bf16[256,256]{1,0:T(8,128)(2,1)S(1)} %copy-done.4, bf16[256,256]{1,0:T(8,128)(2,1)S(1)} %copy-done.3, bf16[1024,1024]{1,0:T(8,128)(2,1)S(1)} %get-tuple-element.32.sxh, bf16[1024,1024]{1,0:T(8,128)(2,1)S(1)} %get-tuple-element.33.sxl, ...), custom_call_target="tpu_custom_call" | custom-call | flops 2013265920 | bytes 6553608 | tf_op jit(solution)/shard_map/pallas_call | solution.py:72
  (51 shorter events, 5.7 us)
Async XLA Ops:
  0.1 0.9 copy-start.5
  1.0 0.9 copy-start.6
  5.4 1.6 %copy-start.12 = (f32[1,8,64,1024]{3,2,1,0:T(8,128)S(1)}, f32[1,8,64,1024]{3,2,1,0:T(8,128)}, u32[]{:S(2)}) copy-start(f32[1,8,64,1024]{3,2,1,0:T(8,128)} %param.19) | copy-start | bytes 6291460
  8.8 7.5 %copy-start.3 = (bf16[256,256]{1,0:T(8,128)(2,1)S(1)}, bf16[256,256]{1,0:T(8,128)(2,1)}, u32[]{:S(2)}) copy-start(bf16[256,256]{1,0:T(8,128)(2,1)} %constant.53.clone.kzl) | copy-start | bytes 393220
  8.8 7.5 %copy-start.4 = (bf16[256,256]{1,0:T(8,128)(2,1)S(1)}, bf16[256,256]{1,0:T(8,128)(2,1)}, u32[]{:S(2)}) copy-start(bf16[256,256]{1,0:T(8,128)(2,1)} %constant.52.clone.kzh) | copy-start | bytes 393220
  8.8 7.6 %copy-start.13 = (f32[1,8,64,1024]{3,2,1,0:T(8,128)S(1)}, f32[1,8,64,1024]{3,2,1,0:T(8,128)}, u32[]{:S(2)}) copy-start(f32[1,8,64,1024]{3,2,1,0:T(8,128)} %param.19) | copy-start | bytes 6291460
  11.6 11.1 %collective-permute-start.3 = (f32[4,64,256]{2,1,0:T(8,128)S(1)}, f32[4,64,256]{2,1,0:T(8,128)S(1)}, u32[]{:S(2)}, u32[]{:S(2)}) collective-permute-start(f32[4,64,256]{2,1,0:T(8,128)S(1)} %get-tuple-element.41), channel_id=1, source_target_pairs={{0,4},{4,0},{8,12},{12,8},{16,20},{20,16},{24,28},{28,24},{1,5},{5... | collective-permute-start | bytes 786440 | tf_op jit(solution)/shard_map/ppermute | solution.py:401
  14.7 9.5 %collective-permute-start.4 = (f32[4,64,256]{2,1,0:T(8,128)S(1)}, f32[4,64,256]{2,1,0:T(8,128)S(1)}, u32[]{:S(2)}, u32[]{:S(2)}) collective-permute-start(f32[4,64,256]{2,1,0:T(8,128)S(1)} %get-tuple-element.42), channel_id=1, source_target_pairs={{0,8},{4,12},{8,0},{12,4},{16,24},{20,28},{24,16},{28,20},{1,9},{5... | collective-permute-start | bytes 786440 | tf_op jit(solution)/shard_map/ppermute | solution.py:401
  16.2 12.8 %copy-start.1 = (f32[64,2]{1,0:T(8,128)S(1)}, f32[64,2]{1,0:T(8,128)}, u32[]{:S(2)}) copy-start(f32[64,2]{1,0:T(8,128)} %constant.43.clone.edges) | copy-start | bytes 1540
  16.2 12.8 %copy-start.2 = (f32[64,1]{1,0:T(8,128)S(1)}, f32[64,1]{1,0:T(8,128)}, u32[]{:S(2)}) copy-start(f32[64,1]{1,0:T(8,128)} %constant.41.clone.smu_y) | copy-start | bytes 772
  16.2 12.8 %copy-start.9 = (f32[1,1024]{1,0:T(1,128)S(1)}, f32[1,1024]{1,0:T(1,128)}, u32[]{:S(2)}) copy-start(f32[1,1024]{1,0:T(1,128)} %constant.42.clone.smu_x) | copy-start | bytes 12292
  16.2 12.8 %copy-start.11 = (f32[4,1]{1,0:T(4,128)S(1)}, f32[4,1]{1,0:T(4,128)}, u32[]{:S(2)}) copy-start(f32[4,1]{1,0:T(4,128)} %constant.51.clone.smu_z) | copy-start | bytes 52
  16.2 31.1 %copy-start.10 = (f32[4,1]{1,0:T(4,128)S(1)}, f32[4,1]{1,0:T(4,128)}, u32[]{:S(2)}) copy-start(f32[4,1]{1,0:T(4,128)} %constant.54.clone.smu_z) | copy-start | bytes 52
  16.3 12.8 %collective-permute-start.5 = (f32[4,64,256]{2,1,0:T(8,128)S(1)}, f32[4,64,256]{2,1,0:T(8,128)S(1)}, u32[]{:S(2)}, u32[]{:S(2)}) collective-permute-start(f32[4,64,256]{2,1,0:T(8,128)S(1)} %get-tuple-element.43), channel_id=1, source_target_pairs={{0,12},{4,8},{8,4},{12,0},{16,28},{20,24},{24,20},{28,16},{1,13},{... | collective-permute-start | bytes 786440 | tf_op jit(solution)/shard_map/ppermute | solution.py:401
  19.2 38.7 %copy-start = (f32[5,4,8,1024]{3,2,1,0:T(8,128)S(1)}, f32[5,4,8,1024]{3,2,1,0:T(8,128)}, u32[]{:S(2)}) copy-start(f32[5,4,8,1024]{3,2,1,0:T(8,128)} %constant.44.clone.responses) | copy-start | bytes 1966084
  19.2 14.9 %collective-permute-start = (f32[4,64,256]{2,1,0:T(8,128)S(1)}, f32[4,64,256]{2,1,0:T(8,128)S(1)}, u32[]{:S(2)}, u32[]{:S(2)}) collective-permute-start(f32[4,64,256]{2,1,0:T(8,128)S(1)} %get-tuple-element.37), channel_id=1, source_target_pairs={{0,4},{4,0},{8,12},{12,8},{16,20},{20,16},{24,28},{28,24},{1,5},{5... | collective-permute-start | bytes 786440 | tf_op jit(solution)/shard_map/ppermute | solution.py:401
  21.1 23.1 %collective-permute-start.1 = (f32[4,64,256]{2,1,0:T(8,128)S(1)}, f32[4,64,256]{2,1,0:T(8,128)S(1)}, u32[]{:S(2)}, u32[]{:S(2)}) collective-permute-start(f32[4,64,256]{2,1,0:T(8,128)S(1)} %get-tuple-element.38), channel_id=1, source_target_pairs={{0,8},{4,12},{8,0},{12,4},{16,24},{20,28},{24,16},{28,20},{1,9},{5... | collective-permute-start | bytes 786440 | tf_op jit(solution)/shard_map/ppermute | solution.py:401
  22.7 24.6 %collective-permute-start.2 = (f32[4,64,256]{2,1,0:T(8,128)S(1)}, f32[4,64,256]{2,1,0:T(8,128)S(1)}, u32[]{:S(2)}, u32[]{:S(2)}) collective-permute-start(f32[4,64,256]{2,1,0:T(8,128)S(1)} %get-tuple-element.39), channel_id=1, source_target_pairs={{0,12},{4,8},{8,4},{12,0},{16,28},{20,24},{24,20},{28,16},{1,13},{... | collective-permute-start | bytes 786440 | tf_op jit(solution)/shard_map/ppermute | solution.py:401
  31.0 37.3 %collective-permute-start.6 = (f32[2,4,64,256]{3,2,1,0:T(8,128)S(1)}, f32[2,4,64,256]{3,2,1,0:T(8,128)S(1)}, u32[]{:S(2)}, u32[]{:S(2)}) collective-permute-start(f32[2,4,64,256]{3,2,1,0:T(8,128)S(1)} %get-tuple-element.46), channel_id=1, source_target_pairs={{0,16},{4,20},{8,24},{12,28},{16,0},{20,4},{24,8},{28,12},{1,17},{... | collective-permute-start | bytes 1572872 | tf_op jit(solution)/shard_map/ppermute | solution.py:401
  49.3 5.7 %collective-permute-start.9 = (f32[16,8,256]{2,1,0:T(8,128)S(1)}, f32[16,8,256]{2,1,0:T(8,128)S(1)}, u32[]{:S(2)}, u32[]{:S(2)}) collective-permute-start(f32[16,8,256]{2,1,0:T(8,128)S(1)} %get-tuple-element.47.refs_0_), channel_id=1, source_target_pairs={{0,3},{1,2},{2,1},{3,0},{4,7},{5,6},{6,5},{7,4},{8,11},{9,10},{10,... | collective-permute-start | bytes 393224 | tf_op jit(solution)/shard_map/ppermute | solution.py:401
  49.3 8.6 %collective-permute-start.8 = (f32[16,8,256]{2,1,0:T(8,128)S(1)}, f32[16,8,256]{2,1,0:T(8,128)S(1)}, u32[]{:S(2)}, u32[]{:S(2)}) collective-permute-start(f32[16,8,256]{2,1,0:T(8,128)S(1)} %get-tuple-element.47.refs_0_), channel_id=1, source_target_pairs={{0,2},{1,3},{2,0},{3,1},{4,6},{5,7},{6,4},{7,5},{8,10},{9,11},{10,... | collective-permute-start | bytes 393224 | tf_op jit(solution)/shard_map/ppermute | solution.py:401
  51.0 6.9 %collective-permute-start.7 = (f32[16,8,256]{2,1,0:T(8,128)S(1)}, f32[16,8,256]{2,1,0:T(8,128)S(1)}, u32[]{:S(2)}, u32[]{:S(2)}) collective-permute-start(f32[16,8,256]{2,1,0:T(8,128)S(1)} %get-tuple-element.47.refs_0_), channel_id=1, source_target_pairs={{0,1},{1,0},{2,3},{3,2},{4,5},{5,4},{6,7},{7,6},{8,9},{9,8},{10,11... | collective-permute-start | bytes 393224 | tf_op jit(solution)/shard_map/ppermute | solution.py:401
  59.1 40.1 %copy-start.14 = (bf16[256,256]{1,0:T(8,128)(2,1)S(1)}, bf16[256,256]{1,0:T(8,128)(2,1)}, u32[]{:S(2)}) copy-start(bf16[256,256]{1,0:T(8,128)(2,1)} %constant.56.clone.kzl) | copy-start | bytes 393220
  59.1 40.1 %copy-start.15 = (bf16[256,256]{1,0:T(8,128)(2,1)S(1)}, bf16[256,256]{1,0:T(8,128)(2,1)}, u32[]{:S(2)}) copy-start(bf16[256,256]{1,0:T(8,128)(2,1)} %constant.55.clone.kzh) | copy-start | bytes 393220
  59.1 9.1 %collective-permute-start.10 = (f32[16,8,256]{2,1,0:T(8,128)S(1)}, f32[16,8,256]{2,1,0:T(8,128)S(1)}, u32[]{:S(2)}, u32[]{:S(2)}) collective-permute-start(f32[16,8,256]{2,1,0:T(8,128)S(1)} %shard_map.186.refs_5_), channel_id=1, source_target_pairs={{0,16},{4,20},{8,24},{12,28},{16,0},{20,4},{24,8},{28,12},{1,17},{... | collective-permute-start | bytes 393224 | tf_op jit(solution)/shard_map/ppermute | solution.py:401
  68.2 25.0 %collective-permute-start.11 = (f32[2,4,64,256]{3,2,1,0:T(8,128)S(1)}, f32[2,4,64,256]{3,2,1,0:T(8,128)S(1)}, u32[]{:S(2)}, u32[]{:S(2)}) collective-permute-start(f32[2,4,64,256]{3,2,1,0:T(8,128)S(1)} %get-tuple-element.48), channel_id=1, source_target_pairs={{0,16},{4,20},{8,24},{12,28},{16,0},{20,4},{24,8},{28,12},{1,17},{... | collective-permute-start | bytes 1572872 | tf_op jit(solution)/shard_map/ppermute | solution.py:401
  70.3 27.4 %collective-permute-start.15 = (f32[4,64,256]{2,1,0:T(8,128)S(1)}, f32[4,64,256]{2,1,0:T(8,128)S(1)}, u32[]{:S(2)}, u32[]{:S(2)}) collective-permute-start(f32[4,64,256]{2,1,0:T(8,128)S(1)} %get-tuple-element.56), channel_id=1, source_target_pairs={{0,4},{4,0},{8,12},{12,8},{16,20},{20,16},{24,28},{28,24},{1,5},{5... | collective-permute-start | bytes 786440 | tf_op jit(solution)/shard_map/ppermute | solution.py:401
  71.8 27.3 %collective-permute-start.16 = (f32[4,64,256]{2,1,0:T(8,128)S(1)}, f32[4,64,256]{2,1,0:T(8,128)S(1)}, u32[]{:S(2)}, u32[]{:S(2)}) collective-permute-start(f32[4,64,256]{2,1,0:T(8,128)S(1)} %get-tuple-element.57), channel_id=1, source_target_pairs={{0,8},{4,12},{8,0},{12,4},{16,24},{20,28},{24,16},{28,20},{1,9},{5... | collective-permute-start | bytes 786440 | tf_op jit(solution)/shard_map/ppermute | solution.py:401
  74.5 24.6 %collective-permute-start.17 = (f32[4,64,256]{2,1,0:T(8,128)S(1)}, f32[4,64,256]{2,1,0:T(8,128)S(1)}, u32[]{:S(2)}, u32[]{:S(2)}) collective-permute-start(f32[4,64,256]{2,1,0:T(8,128)S(1)} %get-tuple-element.58), channel_id=1, source_target_pairs={{0,12},{4,8},{8,4},{12,0},{16,28},{20,24},{24,20},{28,16},{1,13},{... | collective-permute-start | bytes 786440 | tf_op jit(solution)/shard_map/ppermute | solution.py:401
  95.5 9.2 %collective-permute-start.12 = (f32[4,64,256]{2,1,0:T(8,128)S(1)}, f32[4,64,256]{2,1,0:T(8,128)S(1)}, u32[]{:S(2)}, u32[]{:S(2)}) collective-permute-start(f32[4,64,256]{2,1,0:T(8,128)S(1)} %get-tuple-element.51), channel_id=1, source_target_pairs={{0,4},{4,0},{8,12},{12,8},{16,20},{20,16},{24,28},{28,24},{1,5},{5... | collective-permute-start | bytes 786440 | tf_op jit(solution)/shard_map/ppermute | solution.py:401
  97.6 9.2 %collective-permute-start.13 = (f32[4,64,256]{2,1,0:T(8,128)S(1)}, f32[4,64,256]{2,1,0:T(8,128)S(1)}, u32[]{:S(2)}, u32[]{:S(2)}) collective-permute-start(f32[4,64,256]{2,1,0:T(8,128)S(1)} %get-tuple-element.52), channel_id=1, source_target_pairs={{0,8},{4,12},{8,0},{12,4},{16,24},{20,28},{24,16},{28,20},{1,9},{5... | collective-permute-start | bytes 786440 | tf_op jit(solution)/shard_map/ppermute | solution.py:401
  97.6 13.3 %collective-permute-start.14 = (f32[4,64,256]{2,1,0:T(8,128)S(1)}, f32[4,64,256]{2,1,0:T(8,128)S(1)}, u32[]{:S(2)}, u32[]{:S(2)}) collective-permute-start(f32[4,64,256]{2,1,0:T(8,128)S(1)} %get-tuple-element.53), channel_id=1, source_target_pairs={{0,12},{4,8},{8,4},{12,0},{16,28},{20,24},{24,20},{28,16},{1,13},{... | collective-permute-start | bytes 786440 | tf_op jit(solution)/shard_map/ppermute | solution.py:401
  (4 other events, 3.6 us)

commit v7 on v6

--- a/solution.py
+++ b/solution.py
@@ -14,6 +14,7 @@
 LANES = 128
 STRIP = 16
 FINE_ROWS = 32
+CHUNKS = ((0, 2, 4, 6), (1, 3, 5, 7))
 VMEM_BYTES = 40 * 1024 * 1024
 
 
@@ -90,19 +91,23 @@
         self.rows = shape[2] // self.groups
         self.half = self.steps // 2
         self.block = self.width // self.half
-        self.planes = self.depth // 2
+        self.folds = self.depth // 2
 
     def columns(self, owner):
         return pl.ds(pl.multiple_of(owner * self.block, LANES), self.block)
 
 
-def fill_table(plan, ids, coarse_sin, coarse_cos, fine_sin, fine_cos, high, low):
-    fine = fine_sin.shape[0]
+def fill_table(plan, fine, ids, angles, high, low):
+    coarse = plan.width // fine
+    sine, cosine = (
+        angles[2 * coarse + part * fine : 2 * coarse + (part + 1) * fine]
+        for part in range(2)
+    )
 
     def step(index, carry):
         rows = pl.ds(pl.multiple_of(index * fine, fine), fine)
-        row = pl.ds(index, 1)
-        value = coarse_sin[row, :] * fine_cos[...] + coarse_cos[row, :] * fine_sin[...]
+        value = angles[pl.ds(index, 1), :] * cosine
+        value = value + angles[pl.ds(coarse + index, 1), :] * sine
         high[rows, :], low[rows, :] = parts_of(value)
         return carry
 
@@ -120,46 +125,81 @@
         turns = rows[:, None] * columns[None, :] % (2 * (count + 1))
         angle = np.pi * turns / (count + 1)
         tables += [factor * np.sin(angle), factor * np.cos(angle)]
-    return [jnp.asarray(table, jnp.float32) for table in tables]
-
-
-def forward(plan, parity, ids, kzh, kzl, x, sxh, sxl, *outs):
+    return jnp.asarray(np.concatenate(tables), jnp.float32)
+
+
+def fold_tables(plan):
+    rows, folds = sine_table(plan.rows), plan.folds
+    depth = sine_table(plan.depth)
+    tables = [np.kron(depth[parity::2, :folds], rows) for parity in range(2)]
+    forth = jnp.stack(table_parts(np.stack(tables)))
+    back = jnp.stack(table_parts(np.stack([table.T for table in tables])))
+    return forth, back
+
+
+def by_parity(plan, chunk):
+    start = 0
+    for parity in range(2):
+        places = [c // 2 for c in chunk if c % 2 == parity]
+        if places:
+            assert places == list(range(places[0], places[0] + len(places)))
+            count = len(places) * plan.rows
+            first = places[0] * plan.rows
+            yield parity, slice(start, start + count), slice(first, first + count)
+            start += count
+
+
+def forward(plan, chunk, ids, both, x, sxh, sxl, *outs):
     place = lax.rem(ids[0], plan.half)
-    planes = plan.planes
-    mirror = jnp.stack([x[plan.depth - 1 - z] for z in range(planes)])
-    folded = x[:planes] - mirror if parity else x[:planes] + mirror
-    folded = parts_of(folded.reshape(planes * plan.rows, plan.width))
-    left = parts_of(dot_parts((kzh[...], kzl[...]), folded))
+    folds = plan.folds
+    mirror = jnp.stack([x[plan.depth - 1 - z] for z in range(folds)])
+    left = []
+    for parity, _, at in by_parity(plan, chunk):
+        folded = x[:folds] - mirror if parity else x[:folds] + mirror
+        folded = parts_of(folded.reshape(folds * plan.rows, plan.width))
+        table = both[0, parity, at], both[1, parity, at]
+        left.append(parts_of(dot_parts(table, folded)))
     for k in range(plan.half):
         columns = plan.columns(place ^ k)
-        value = dot_parts(left, (sxh[:, columns], sxl[:, columns]))
-        outs[k][...] = value.reshape(planes, plan.rows, plan.block)
-
-
-def backward(plan, ids, kzh, kzl, sxh, sxl, *refs):
+        right = sxh[:, columns], sxl[:, columns]
+        value = jnp.concatenate([dot_parts(part, right) for part in left])
+        outs[k][...] = value.reshape(len(chunk), plan.rows, plan.block)
+
+
+def backward(plan, chunk, ready, last, ids, both, sxh, sxl, *refs):
     place = lax.rem(ids[0], plan.half)
-    pieces, rest = refs[: plan.half], refs[plan.half :]
-    high, low = rest[-2:]
-    planes = plan.planes
+    pieces, refs = refs[: plan.half], refs[plan.half :]
+    before = dict(zip(ready, refs))
+    outs, (high, low) = refs[len(ready) : -2], refs[-2:]
+    folds = plan.folds
+    shape = folds, plan.rows, plan.block
     for k in range(plan.half):
-        columns = plan.columns(place ^ k)
-        piece = pieces[k][...].reshape(planes * plan.rows, plan.block)
-        high[:, columns], low[:, columns] = parts_of(piece)
+        piece = pieces[k][...].reshape(len(chunk) * plan.rows, plan.block)
+        high[k], low[k] = parts_of(piece)
     for j in range(plan.half):
         columns = pl.ds(j * plan.block, plan.block)
-        total = dot_parts((high[...], low[...]), (sxh[:, columns], sxl[:, columns]))
-        value = dot_parts((kzh[...], kzl[...]), parts_of(total))
-        value = value.reshape(planes, plan.rows, plan.block)
-        if len(rest) == 3:
-            rest[0][:, :, columns] = value
+        total = None
+        for k in range(plan.half):
+            at = plan.columns(place ^ k)
+            value = dot_parts((high[k], low[k]), (sxh[at, columns], sxl[at, columns]))
+            total = value if total is None else total + value
+        total = parts_of(total)
+        sums = {parity: before[parity][:, :, columns] for parity in ready}
+        for parity, rows, at in by_parity(plan, chunk):
+            table = both[0, parity, :, at], both[1, parity, :, at]
+            value = dot_parts(table, (total[0][rows], total[1][rows])).reshape(shape)
+            sums[parity] = sums[parity] + value if parity in sums else value
+        if not last:
+            for parity, out in zip(sorted(sums), outs):
+                out[:, :, columns] = sums[parity]
             continue
-        even, out, held, sent = rest[:4]
-        other = even[:, :, columns]
-        held[j, :planes] = other + value
-        for z in range(planes):
-            held[j, plan.depth - 1 - z] = other[z] - value[z]
+        out, held, sent = outs
+        held[j, :folds] = sums[0] + sums[1]
+        other = sums[0] - sums[1]
+        for z in range(folds):
+            held[j, plan.depth - 1 - z] = other[z]
         pltpu.make_async_copy(held.at[j], out.at[:, :, columns], sent.at[j]).start()
-    if len(rest) > 3:
+    if last:
         for j in range(plan.half):
             columns = pl.ds(j * plan.block, plan.block)
             pltpu.make_async_copy(held.at[j], out.at[:, :, columns], sent.at[j]).wait()
@@ -172,7 +212,7 @@
         rows = pl.ds(pl.multiple_of(index * STRIP, STRIP), STRIP)
         plane = across + smu_y[rows, :]
         weights = edges[rows, 0:1], edges[rows, 1:2]
-        for u in range(plan.planes):
+        for u in range(smu_z.shape[0]):
             body(u, rows, plane + smu_z[u : u + 1, :], weights)
         return carry
 
@@ -223,7 +263,7 @@
 
 def half_end(plan, ids, smu_z, smu_y, smu_x, edges, *refs):
     pieces = refs[: plan.half]
-    *before_seen, ends, seen, sums = refs[plan.half :]
+    ends, seen, sums = refs[plan.half :]
     steps, half = plan.steps, plan.half
     place = lax.rem(ids[0], half)
     mine = ids[0] // half
@@ -250,12 +290,7 @@
         per_strip(plan, place, smu_z, smu_y, smu_x, edges, body)
 
     by_place(plan, place, with_place)
-    own = jnp.sum(sums[...], axis=2)
-    if before_seen:
-        seen[:, : plan.planes] = before_seen[0][...]
-        seen[:, plan.planes :] = own
-    else:
-        seen[...] = own
+    seen[...] = jnp.sum(sums[...], axis=2)
 
 
 def c_mul(a, b):
@@ -284,7 +319,7 @@
         seen[me ^ k] = views[k][...]
     radius = ALPHA_RATIO ** (1.0 / steps)
     grow = [radius**n for n in range(steps)]
-    nothing = jnp.zeros((plan.depth, plan.block), jnp.float32)
+    nothing = jnp.zeros(out.shape[1:], jnp.float32)
     for freq in range(steps // 2 + 1):
         angle = [2.0 * math.pi * (freq * n % steps) / steps for n in range(steps)]
 
@@ -353,7 +388,7 @@
             out[2 * ((n + 1) % steps) + edge] = total
 
 
-def half_solve(plan, parity, ids, smu_z, smu_y, smu_x, edges, *refs):
+def half_solve(plan, ids, smu_z, smu_y, smu_x, edges, *refs):
     pieces = refs[: plan.half]
     far, beside, beside_far = refs[plan.half : plan.half + 3]
     outs = refs[plan.half + 3 :]
@@ -370,8 +405,7 @@
                 total = None
                 for edge in range(2):
                     at = 2 * (window * half + j) + edge
-                    plane = pl.ds(parity * plan.planes + u, 1)
-                    row = beside[at, plane, :] + beside_far[at, plane, :]
+                    row = beside[at, u : u + 1, :] + beside_far[at, u : u + 1, :]
                     term = weights[edge] * row
                     total = term if total is None else total + term
                 return total
@@ -402,92 +436,95 @@
 
 
 def on_device(plan, residual):
-    steps, groups, half, planes = plan.steps, plan.groups, plan.half, plan.planes
+    steps, groups, half = plan.steps, plan.groups, plan.half
     ids = jnp.stack([lax.axis_index("tm"), lax.axis_index("gy")]).astype(jnp.int32)
     sine_rows = sine_table(plan.rows)
-    sine_depth = sine_table(plan.depth)
     smu_z, smu_y, smu_x = (
         STEP_SCALE * spectrum_of(count) for count in (plan.depth, plan.rows, plan.width)
     )
     smu_y = jnp.asarray(smu_y[:, None], jnp.float32)
     smu_x = jnp.asarray(smu_x[None, :], jnp.float32)
     edges = jnp.asarray(sine_rows[:, [0, plan.rows - 1]], jnp.float32)
-    by_parity = np.arange(plan.depth).reshape(planes, 2).T.reshape(-1)
     responses = edge_responses(steps, plan.depth, plan.rows, plan.width)
-    responses = jnp.asarray(responses[:, :, by_parity])
     field = residual[0]
     f32 = functools.partial(jax.ShapeDtypeStruct, dtype=jnp.float32)
-    modes = f32((planes, plan.rows, plan.block))
-    ends = f32((2,) + modes.shape)
-    count = planes * plan.rows * plan.width
-    flops = 6 * count * (plan.width + planes * plan.rows)
+    forth, back = fold_tables(plan)
     tables = call(
-        functools.partial(fill_table, plan),
+        functools.partial(fill_table, plan, FINE_ROWS),
         [jax.ShapeDtypeStruct((plan.width, plan.width), jnp.bfloat16)] * 2,
-        8 * plan.width * plan.width,
-        (ids, *angle_tables(plan.width, FINE_ROWS)),
+        4000 * plan.width * plan.width,
+        (ids, angle_tables(plan.width, FINE_ROWS)),
     )
-    sent, small = [], []
-    for parity in range(2):
-        both = np.kron(sine_depth[parity::2, :planes], sine_rows)
+    work = []
+    for chunk in CHUNKS:
+        modes = f32((len(chunk), plan.rows, plan.block))
+        count = len(chunk) * plan.rows * plan.width
+        flops = 6 * count * (plan.width + plan.folds * plan.rows)
         pieces = call(
-            functools.partial(forward, plan, parity),
+            functools.partial(forward, plan, chunk),
             [modes] * half,
             flops,
-            (ids, *table_parts(both), field, *tables),
-        )
-        sent.append([swap(v, "tm", steps, k) for k, v in enumerate(pieces)])
-        smu_own = jnp.asarray(smu_z[parity::2, None], jnp.float32)
-        small.append((ids, smu_own, smu_y, smu_x, edges))
-    sent[0][0], sent[1][0] = lax.optimization_barrier((sent[0][0], sent[1][0]))
-    mine, seen = [], ()
-    for parity in range(2):
-        end, *seen = call(
+            (ids, forth, field, *tables),
+        )
+        pieces = [swap(v, "tm", steps, k) for k, v in enumerate(pieces)]
+        smu_own = jnp.asarray(smu_z[list(chunk), None], jnp.float32)
+        work.append((chunk, modes, flops, (ids, smu_own, smu_y, smu_x, edges), pieces))
+    first, second = work[0][-1], work[1][-1]
+    first[0], second[0] = lax.optimization_barrier((first[0], second[0]))
+    sums = {}
+    far = None
+    for chunk, modes, flops, small, pieces in work:
+        seen = f32((2 * steps, len(chunk), plan.block))
+        ends, view = call(
             functools.partial(half_end, plan),
-            [ends, f32((2 * steps, planes * (1 + parity), plan.block))],
-            100 * count,
-            (*small[parity], *sent[parity], *seen),
-            [pltpu.VMEM((2 * steps, planes, 8, plan.block), jnp.float32)],
-        )
-        mine.append(end)
-    far = swap(mine[0], "tm", steps, half)
-    views = [swap(seen[0], "gy", groups, k) for k in range(groups)]
-    sides = pltpu.VMEM((groups, steps + 2, plan.depth, plan.block), jnp.float32)
-    beside = call(
-        functools.partial(join_rows, plan),
-        f32(seen[0].shape),
-        100 * plan.depth * plan.block * steps,
-        (ids, responses, *views),
-        [pltpu.VMEM((groups,) + seen[0].shape, jnp.float32), sides, sides],
-    )
-    beside_far = swap(beside, "tm", steps, half)
-    second, far, beside_far = lax.optimization_barrier((mine[1], far, beside_far))
-    far = [far, swap(second, "tm", steps, half)]
-    even = ()
-    for parity in range(2):
+            [f32((2,) + modes.shape), seen],
+            100 * modes.size * half,
+            (*small, *pieces),
+            [pltpu.VMEM((2 * steps, len(chunk), 8, plan.block), jnp.float32)],
+        )
+        if far is not None:
+            ends, far, beside_far = lax.optimization_barrier((ends, far, beside_far))
+        far = swap(ends, "tm", steps, half)
+        views = [swap(view, "gy", groups, k) for k in range(groups)]
+        sides = pltpu.VMEM((groups, steps + 2) + seen.shape[1:], jnp.float32)
+        beside = call(
+            functools.partial(join_rows, plan),
+            seen,
+            100 * seen.size,
+            (ids, jnp.asarray(responses[:, :, list(chunk)]), *views),
+            [pltpu.VMEM((groups,) + seen.shape, jnp.float32), sides, sides],
+        )
+        beside_far = swap(beside, "tm", steps, half)
         pieces = call(
-            functools.partial(half_solve, plan, parity),
+            functools.partial(half_solve, plan),
             [modes] * half,
-            100 * count,
-            (*small[parity], *sent[parity], far[parity], beside, beside_far),
+            100 * modes.size * half,
+            (*small, *pieces, far, beside, beside_far),
         )
         pieces = [swap(v, "tm", steps, k) for k, v in enumerate(pieces)]
-        both = np.kron(sine_depth[:planes, parity::2], sine_rows)
-        hold = [pltpu.VMEM((planes * plan.rows, plan.width), jnp.bfloat16)] * 2
-        if parity:
+        last = chunk == CHUNKS[-1]
+        part = pltpu.VMEM((half, len(chunk) * plan.rows, plan.block), jnp.bfloat16)
+        hold = [part, part]
+        if last:
+            block = field.shape[:2] + (plan.block,)
             hold = [
-                pltpu.VMEM((half,) + field.shape[:2] + (plan.block,), jnp.float32),
+                pltpu.VMEM((half,) + block, jnp.float32),
                 pltpu.SemaphoreType.DMA((half,)),
             ] + hold
+        ready = tuple(sorted(sums))
+        parities = sorted(set(ready) | {c % 2 for c in chunk})
         result = call(
-            functools.partial(backward, plan),
-            f32(field.shape if parity else (planes,) + field.shape[1:]),
+            functools.partial(backward, plan, chunk, ready, last),
+            f32(field.shape)
+            if last
+            else [f32((plan.folds,) + field.shape[1:])] * len(parities),
             flops,
-            (ids, *table_parts(both), *tables, *pieces, *even),
+            (ids, back, *tables, *pieces, *(sums[parity] for parity in ready)),
             hold,
-            pl.BlockSpec(memory_space=pltpu.HBM) if parity else None,
-        )
-        even = (result,)
+            pl.BlockSpec(memory_space=pltpu.HBM) if last else None,
+        )
+        if not last:
+            sums = dict(zip(parities, result))
     return result[None]
 
 

time: 118 us -> 101 us (0.86)
  waiting for transfers between devices: 58.3 us -> 43.9 us
  local copies, waits for them, and re-layouts: 7.06 us -> 1.09 us
  starting transfers between devices: 23.4 us -> 26.9 us
    ppermute x18 -> x22, waiting for transfers between devices: 58.3 us -> 43.9 us  [swap(): return lax.ppermute(values, axis, [(i, i ^ distance) for i in range(count)])]
    unnamed x36 -> x22, local copies, waits for them, and re-layouts: 7.06 us -> 1.09 us
    ppermute x18 -> x22, starting transfers between devices: 23.4 us -> 26.9 us  [swap(): return lax.ppermute(values, axis, [(i, i ^ distance) for i in range(count)])]
    pallas_call x10 -> x11, Pallas kernels: 28.2 us -> 28.3 us  [call(): pl.pallas_call(kernel, out_shape=out_shape, in_specs=[smem] + [vmem] * (l...]
  transfers between devices with their start and end apart: 18 -> 22, of which waited for: 9 -> 15; matrix products, arithmetic and copies ran while one was open for 0% -> 0% of each run, Pallas kernels for 15% -> 16%
where the time goes in v7:
time: 101 us
  waiting for transfers between devices  43.9 us (43%)
  Pallas kernels  28.3 us (28%)
  starting transfers between devices  26.9 us (27%)
  local copies, waits for them, and re-layouts  1.09 us (1%)
    ppermute x22, waiting for transfers between devices, swap(): return lax.ppermute(values, axis, [(i, i ^ distance) for i in range(count)])  43.9 us
    pallas_call x11, Pallas kernels, call(): pl.pallas_call(kernel, out_shape=out_shape, in_specs=[smem] + [vmem] * (l...  28.3 us
    ppermute x22, starting transfers between devices, swap(): return lax.ppermute(values, axis, [(i, i ^ distance) for i in range(count)])  26.9 us
  transfers between devices with their start and end apart: 22, of which 15 were waited for; matrix products, arithmetic and copies ran while one was open for 0% of the time, Pallas kernels for 16%

profile of v7, /device:TPU:0, one launch (start us, length us, event | category | flops | bytes accessed | tf_op | source)
XLA Modules:
  0.0 100.6 jit_solution(5393520021296964215)
XLA Ops:
  1.1 1.7 %shard_map.127 = (bf16[1024,1024]{1,0:T(8,128)(2,1)S(1)}, bf16[1024,1024]{1,0:T(8,128)(2,1)S(1)}) custom-call(s32[2]{0:T(128)S(1)} %pad_add_fusion.ids, f32[128,1024]{1,0:T(8,128)S(1)} %copy-done.10), custom_call_target="tpu_custom_call" | custom-call | flops 4194304000 | bytes 524296 | tf_op jit(solution)/shard_map/pallas_call | solution.py:73
  2.9 2.8 %shard_map.128 = (f32[4,64,256]{2,1,0:T(8,128)S(1)}, f32[4,64,256]{2,1,0:T(8,128)S(1)}, f32[4,64,256]{2,1,0:T(8,128)S(1)}, f32[4,64,256]{2,1,0:T(8,128)S(1)}) custom-call(s32[2]{0:T(128)S(1)} %pad_add_fusion.ids, bf16[2,2,256,256]{3,2,1,0:T(8,128)(2,1)S(1)} %copy-done.9, f32[8,64,1024]{2,1,0:T(8,128)S(1)} %bitcast.4, ...), custom_call_target="tpu_custom_call" | custom-call | flops 2013265920 | bytes 6815752 | tf_op jit(solution)/shard_map/pallas_call | solution.py:73
  5.7 3.0 %collective-permute-start.3 = (f32[4,64,256]{2,1,0:T(8,128)S(1)}, f32[4,64,256]{2,1,0:T(8,128)S(1)}, u32[]{:S(2)}, u32[]{:S(2)}) collective-permute-start(f32[4,64,256]{2,1,0:T(8,128)S(1)} %get-tuple-element.40), channel_id=1, source_target_pairs={{0,4},{4,0},{8,12},{12,8},{16,20},{20,16},{24,28},{28,24},{1,5},{5... | collective-permute-start | bytes 786440 | tf_op jit(solution)/shard_map/ppermute | solution.py:435
  8.7 1.6 %collective-permute-start.4 = (f32[4,64,256]{2,1,0:T(8,128)S(1)}, f32[4,64,256]{2,1,0:T(8,128)S(1)}, u32[]{:S(2)}, u32[]{:S(2)}) collective-permute-start(f32[4,64,256]{2,1,0:T(8,128)S(1)} %get-tuple-element.41), channel_id=1, source_target_pairs={{0,8},{4,12},{8,0},{12,4},{16,24},{20,28},{24,16},{28,20},{1,9},{5... | collective-permute-start | bytes 786440 | tf_op jit(solution)/shard_map/ppermute | solution.py:435
  10.4 2.8 %shard_map.129 = (f32[4,64,256]{2,1,0:T(8,128)S(1)}, f32[4,64,256]{2,1,0:T(8,128)S(1)}, f32[4,64,256]{2,1,0:T(8,128)S(1)}, f32[4,64,256]{2,1,0:T(8,128)S(1)}) custom-call(s32[2]{0:T(128)S(1)} %pad_add_fusion.ids, bf16[2,2,256,256]{3,2,1,0:T(8,128)(2,1)S(1)} %copy-done.9, f32[8,64,1024]{2,1,0:T(8,128)S(1)} %bitcast.5, ...), custom_call_target="tpu_custom_call" | custom-call | flops 2013265920 | bytes 6815752 | tf_op jit(solution)/shard_map/pallas_call | solution.py:73
  13.3 1.8 %collective-permute-done.3.refs_1_ = f32[4,64,256]{2,1,0:T(8,128)S(1)} collective-permute-done((f32[4,64,256]{2,1,0:T(8,128)S(1)}, f32[4,64,256]{2,1,0:T(8,128)S(1)}, u32[]{:S(2)}, u32[]{:S(2)}) %collective-permute-start.3) | collective-permute-done | bytes 262176 | tf_op jit(solution)/shard_map/ppermute | solution.py:435
  15.0 2.9 %collective-permute-done.4.refs_2_ = f32[4,64,256]{2,1,0:T(8,128)S(1)} collective-permute-done((f32[4,64,256]{2,1,0:T(8,128)S(1)}, f32[4,64,256]{2,1,0:T(8,128)S(1)}, u32[]{:S(2)}, u32[]{:S(2)}) %collective-permute-start.4) | collective-permute-done | bytes 262176 | tf_op jit(solution)/shard_map/ppermute | solution.py:435
  18.0 3.9 %collective-permute-done.5.refs_3_ = f32[4,64,256]{2,1,0:T(8,128)S(1)} collective-permute-done((f32[4,64,256]{2,1,0:T(8,128)S(1)}, f32[4,64,256]{2,1,0:T(8,128)S(1)}, u32[]{:S(2)}, u32[]{:S(2)}) %collective-permute-start.5) | collective-permute-done | bytes 262176 | tf_op jit(solution)/shard_map/ppermute | solution.py:435
  21.9 1.9 %shard_map.131 = (f32[2,4,64,256]{3,2,1,0:T(8,128)S(1)}, f32[16,4,256]{2,1,0:T(4,128)S(1)}) custom-call(s32[2]{0:T(128)S(1)} %pad_add_fusion.ids, f32[4,1]{1,0:T(4,128)S(1)} %copy-done.7, f32[64,1]{1,0:T(8,128)S(1)} %copy-done.2, f32[1,1024]{1,0:T(1,128)S(1)} %copy-done.5, f32[64,2]{1,0:T(8,128)S(1)} %copy-done.1, ...), custom_call_target="tpu_custom_call" | custom-call | flops 26214400 | bytes 1053464 | tf_op jit(solution)/shard_map/pallas_call | solution.py:73
  23.9 2.8 %collective-permute-start.6 = (f32[2,4,64,256]{3,2,1,0:T(8,128)S(1)}, f32[2,4,64,256]{3,2,1,0:T(8,128)S(1)}, u32[]{:S(2)}, u32[]{:S(2)}) collective-permute-start(f32[2,4,64,256]{3,2,1,0:T(8,128)S(1)} %get-tuple-element.43), channel_id=1, source_target_pairs={{0,16},{4,20},{8,24},{12,28},{16,0},{20,4},{24,8},{28,12},{1,17},{... | collective-permute-start | bytes 1572872 | tf_op jit(solution)/shard_map/ppermute | solution.py:435
  26.7 1.5 %collective-permute-start = (f32[4,64,256]{2,1,0:T(8,128)S(1)}, f32[4,64,256]{2,1,0:T(8,128)S(1)}, u32[]{:S(2)}, u32[]{:S(2)}) collective-permute-start(f32[4,64,256]{2,1,0:T(8,128)S(1)} %get-tuple-element.35), channel_id=1, source_target_pairs={{0,4},{4,0},{8,12},{12,8},{16,20},{20,16},{24,28},{28,24},{1,5},{5... | collective-permute-start | bytes 786440 | tf_op jit(solution)/shard_map/ppermute | solution.py:435
  28.2 1.6 %collective-permute-start.1 = (f32[4,64,256]{2,1,0:T(8,128)S(1)}, f32[4,64,256]{2,1,0:T(8,128)S(1)}, u32[]{:S(2)}, u32[]{:S(2)}) collective-permute-start(f32[4,64,256]{2,1,0:T(8,128)S(1)} %get-tuple-element.36), channel_id=1, source_target_pairs={{0,8},{4,12},{8,0},{12,4},{16,24},{20,28},{24,16},{28,20},{1,9},{5... | collective-permute-start | bytes 786440 | tf_op jit(solution)/shard_map/ppermute | solution.py:435
  30.1 4.3 %collective-permute-done.9.refs_3_ = f32[16,4,256]{2,1,0:T(4,128)S(1)} collective-permute-done((f32[16,4,256]{2,1,0:T(4,128)S(1)}, f32[16,4,256]{2,1,0:T(4,128)S(1)}, u32[]{:S(2)}, u32[]{:S(2)}) %collective-permute-start.9) | collective-permute-done | bytes 65568 | tf_op jit(solution)/shard_map/ppermute | solution.py:435
  35.3 3.4 %collective-permute-done.8.refs_2_ = f32[16,4,256]{2,1,0:T(4,128)S(1)} collective-permute-done((f32[16,4,256]{2,1,0:T(4,128)S(1)}, f32[16,4,256]{2,1,0:T(4,128)S(1)}, u32[]{:S(2)}, u32[]{:S(2)}) %collective-permute-start.8) | collective-permute-done | bytes 65568 | tf_op jit(solution)/shard_map/ppermute | solution.py:435
  38.8 1.3 %collective-permute-done.7.refs_1_ = f32[16,4,256]{2,1,0:T(4,128)S(1)} collective-permute-done((f32[16,4,256]{2,1,0:T(4,128)S(1)}, f32[16,4,256]{2,1,0:T(4,128)S(1)}, u32[]{:S(2)}, u32[]{:S(2)}) %collective-permute-start.7) | collective-permute-done | bytes 65568 | tf_op jit(solution)/shard_map/ppermute | solution.py:435
  41.0 3.6 %collective-permute-done.1.refs_2_ = f32[4,64,256]{2,1,0:T(8,128)S(1)} collective-permute-done((f32[4,64,256]{2,1,0:T(8,128)S(1)}, f32[4,64,256]{2,1,0:T(8,128)S(1)}, u32[]{:S(2)}, u32[]{:S(2)}) %collective-permute-start.1) | collective-permute-done | bytes 262176 | tf_op jit(solution)/shard_map/ppermute | solution.py:435
  44.6 4.6 %collective-permute-done.2.refs_3_ = f32[4,64,256]{2,1,0:T(8,128)S(1)} collective-permute-done((f32[4,64,256]{2,1,0:T(8,128)S(1)}, f32[4,64,256]{2,1,0:T(8,128)S(1)}, u32[]{:S(2)}, u32[]{:S(2)}) %collective-permute-start.2) | collective-permute-done | bytes 262176 | tf_op jit(solution)/shard_map/ppermute | solution.py:435
  49.3 1.9 %shard_map.130 = (f32[2,4,64,256]{3,2,1,0:T(8,128)S(1)}, f32[16,4,256]{2,1,0:T(4,128)S(1)}) custom-call(s32[2]{0:T(128)S(1)} %pad_add_fusion.ids, f32[4,1]{1,0:T(4,128)S(1)} %copy-done.6, f32[64,1]{1,0:T(8,128)S(1)} %copy-done.2, f32[1,1024]{1,0:T(1,128)S(1)} %copy-done.5, f32[64,2]{1,0:T(8,128)S(1)} %copy-done.1, ...), custom_call_target="tpu_custom_call" | custom-call | flops 26214400 | bytes 1053464 | tf_op jit(solution)/shard_map/pallas_call | solution.py:73
  51.8 2.2 %collective-permute-start.11 = (f32[2,4,64,256]{3,2,1,0:T(8,128)S(1)}, f32[2,4,64,256]{3,2,1,0:T(8,128)S(1)}, u32[]{:S(2)}, u32[]{:S(2)}) collective-permute-start(f32[2,4,64,256]{3,2,1,0:T(8,128)S(1)} %get-tuple-element.45), channel_id=1, source_target_pairs={{0,16},{4,20},{8,24},{12,28},{16,0},{20,4},{24,8},{28,12},{1,17},{... | collective-permute-start | bytes 1572872 | tf_op jit(solution)/shard_map/ppermute | solution.py:435
  54.0 2.0 %shard_map.135 = (f32[4,64,256]{2,1,0:T(8,128)S(1)}, f32[4,64,256]{2,1,0:T(8,128)S(1)}, f32[4,64,256]{2,1,0:T(8,128)S(1)}, f32[4,64,256]{2,1,0:T(8,128)S(1)}) custom-call(s32[2]{0:T(128)S(1)} %pad_add_fusion.ids, f32[4,1]{1,0:T(4,128)S(1)} %copy-done.7, f32[64,1]{1,0:T(8,128)S(1)} %copy-done.2, f32[1,1024]{1,0:T(1,128)S(1)} %copy-done.5, ...), custom_call_target="tpu_custom_call" | custom-call | flops 26214400 | bytes 1708824 | tf_op jit(solution)/shard_map/pallas_call | solution.py:73
  56.9 1.5 %collective-permute-start.13 = (f32[16,4,256]{2,1,0:T(4,128)S(1)}, f32[16,4,256]{2,1,0:T(4,128)S(1)}, u32[]{:S(2)}, u32[]{:S(2)}) collective-permute-start(f32[16,4,256]{2,1,0:T(4,128)S(1)} %get-tuple-element.46.refs_0_), channel_id=1, source_target_pairs={{0,2},{1,3},{2,0},{3,1},{4,6},{5,7},{6,4},{7,5},{8,10},{9,11},{10,... | collective-permute-start | bytes 196616 | tf_op jit(solution)/shard_map/ppermute | solution.py:435
  58.4 2.2 %collective-permute-start.20 = (f32[4,64,256]{2,1,0:T(8,128)S(1)}, f32[4,64,256]{2,1,0:T(8,128)S(1)}, u32[]{:S(2)}, u32[]{:S(2)}) collective-permute-start(f32[4,64,256]{2,1,0:T(8,128)S(1)} %get-tuple-element.53), channel_id=1, source_target_pairs={{0,8},{4,12},{8,0},{12,4},{16,24},{20,28},{24,16},{28,20},{1,9},{5... | collective-permute-start | bytes 786440 | tf_op jit(solution)/shard_map/ppermute | solution.py:435
  61.2 2.2 %collective-permute-start.21 = (f32[4,64,256]{2,1,0:T(8,128)S(1)}, f32[4,64,256]{2,1,0:T(8,128)S(1)}, u32[]{:S(2)}, u32[]{:S(2)}) collective-permute-start(f32[4,64,256]{2,1,0:T(8,128)S(1)} %get-tuple-element.54), channel_id=1, source_target_pairs={{0,12},{4,8},{8,4},{12,0},{16,28},{20,24},{24,20},{28,16},{1,13},{... | collective-permute-start | bytes 786440 | tf_op jit(solution)/shard_map/ppermute | solution.py:435
  63.4 1.3 %collective-permute-done.12.refs_1_ = f32[16,4,256]{2,1,0:T(4,128)S(1)} collective-permute-done((f32[16,4,256]{2,1,0:T(4,128)S(1)}, f32[16,4,256]{2,1,0:T(4,128)S(1)}, u32[]{:S(2)}, u32[]{:S(2)}) %collective-permute-start.12) | collective-permute-done | bytes 65568 | tf_op jit(solution)/shard_map/ppermute | solution.py:435
  65.6 2.2 %collective-permute-start.15 = (f32[16,4,256]{2,1,0:T(4,128)S(1)}, f32[16,4,256]{2,1,0:T(4,128)S(1)}, u32[]{:S(2)}, u32[]{:S(2)}) collective-permute-start(f32[16,4,256]{2,1,0:T(4,128)S(1)} %shard_map.133.refs_5_), channel_id=1, source_target_pairs={{0,16},{4,20},{8,24},{12,28},{16,0},{20,4},{24,8},{28,12},{1,17},{... | collective-permute-start | bytes 196616 | tf_op jit(solution)/shard_map/ppermute | solution.py:435
  67.8 10.5 %collective-permute-done.15.refs_6_ = f32[16,4,256]{2,1,0:T(4,128)S(1)} collective-permute-done((f32[16,4,256]{2,1,0:T(4,128)S(1)}, f32[16,4,256]{2,1,0:T(4,128)S(1)}, u32[]{:S(2)}, u32[]{:S(2)}) %collective-permute-start.15) | collective-permute-done | bytes 65568 | tf_op jit(solution)/shard_map/ppermute | solution.py:435
  78.2 2.2 %shard_map.134 = (f32[4,64,256]{2,1,0:T(8,128)S(1)}, f32[4,64,256]{2,1,0:T(8,128)S(1)}, f32[4,64,256]{2,1,0:T(8,128)S(1)}, f32[4,64,256]{2,1,0:T(8,128)S(1)}) custom-call(s32[2]{0:T(128)S(1)} %pad_add_fusion.ids, f32[4,1]{1,0:T(4,128)S(1)} %copy-done.6, f32[64,1]{1,0:T(8,128)S(1)} %copy-done.2, f32[1,1024]{1,0:T(1,128)S(1)} %copy-done.5, ...), custom_call_target="tpu_custom_call" | custom-call | flops 26214400 | bytes 1708824 | tf_op jit(solution)/shard_map/pallas_call | solution.py:73
  81.0 3.1 %collective-permute-start.17 = (f32[4,64,256]{2,1,0:T(8,128)S(1)}, f32[4,64,256]{2,1,0:T(8,128)S(1)}, u32[]{:S(2)}, u32[]{:S(2)}) collective-permute-start(f32[4,64,256]{2,1,0:T(8,128)S(1)} %get-tuple-element.49), channel_id=1, source_target_pairs={{0,8},{4,12},{8,0},{12,4},{16,24},{20,28},{24,16},{28,20},{1,9},{5... | collective-permute-start | bytes 786440 | tf_op jit(solution)/shard_map/ppermute | solution.py:435
  84.1 5.2 %shard_map.136.refs_4_ = f32[4,64,1024]{2,1,0:T(8,128)S(1)} custom-call(s32[2]{0:T(128)S(1)} %pad_add_fusion.ids, bf16[2,2,256,256]{3,2,1,0:T(8,128)(2,1)S(1)} %copy-done, bf16[1024,1024]{1,0:T(8,128)(2,1)S(1)} %get-tuple-element.30.sxh, bf16[1024,1024]{1,0:T(8,128)(2,1)S(1)} %get-tuple-element.31.sxl, f32[4,64,256]{2,1,0:T(8,128)S(1)} %get-tuple-element.51.refs_0_, ...), custom_call_target="tpu_custom_call" | custom-call | flops 2013265920 | bytes 5767176 | tf_op jit(solution)/shard_map/pallas_call | solution.py:73
  89.3 1.8 %collective-permute-done.16.refs_1_ = f32[4,64,256]{2,1,0:T(8,128)S(1)} collective-permute-done((f32[4,64,256]{2,1,0:T(8,128)S(1)}, f32[4,64,256]{2,1,0:T(8,128)S(1)}, u32[]{:S(2)}, u32[]{:S(2)}) %collective-permute-start.16) | collective-permute-done | bytes 262176 | tf_op jit(solution)/shard_map/ppermute | solution.py:435
  91.3 3.1 %collective-permute-done.18.refs_3_ = f32[4,64,256]{2,1,0:T(8,128)S(1)} collective-permute-done((f32[4,64,256]{2,1,0:T(8,128)S(1)}, f32[4,64,256]{2,1,0:T(8,128)S(1)}, u32[]{:S(2)}, u32[]{:S(2)}) %collective-permute-start.18) | collective-permute-done | bytes 262176 | tf_op jit(solution)/shard_map/ppermute | solution.py:435
  94.4 6.1 %shard_map.137 = f32[8,64,1024]{2,1,0:T(8,128)} custom-call(s32[2]{0:T(128)S(1)} %pad_add_fusion.ids, bf16[2,2,256,256]{3,2,1,0:T(8,128)(2,1)S(1)} %copy-done, bf16[1024,1024]{1,0:T(8,128)(2,1)S(1)} %get-tuple-element.30.sxh, bf16[1024,1024]{1,0:T(8,128)(2,1)S(1)} %get-tuple-element.31.sxl, f32[4,64,256]{2,1,0:T(8,128)S(1)} %get-tuple-element.47.refs_0_, ...), custom_call_target="tpu_custom_call" | custom-call | flops 2013265920 | bytes 6815752 | tf_op jit(solution)/shard_map/pallas_call | solution.py:73
  (46 shorter events, 7.2 us)
Async XLA Ops:
  1.1 1.7 %copy-start.8 = (f32[1,8,64,1024]{3,2,1,0:T(8,128)S(1)}, f32[1,8,64,1024]{3,2,1,0:T(8,128)}, u32[]{:S(2)}) copy-start(f32[1,8,64,1024]{3,2,1,0:T(8,128)} %param.13) | copy-start | bytes 6291460
  1.1 1.7 %copy-start.9 = (bf16[2,2,256,256]{3,2,1,0:T(8,128)(2,1)S(1)}, bf16[2,2,256,256]{3,2,1,0:T(8,128)(2,1)}, u32[]{:S(2)}) copy-start(bf16[2,2,256,256]{3,2,1,0:T(8,128)(2,1)} %constant.51.both) | copy-start | bytes 1572868
  5.7 9.3 %collective-permute-start.3 = (f32[4,64,256]{2,1,0:T(8,128)S(1)}, f32[4,64,256]{2,1,0:T(8,128)S(1)}, u32[]{:S(2)}, u32[]{:S(2)}) collective-permute-start(f32[4,64,256]{2,1,0:T(8,128)S(1)} %get-tuple-element.40), channel_id=1, source_target_pairs={{0,4},{4,0},{8,12},{12,8},{16,20},{20,16},{24,28},{28,24},{1,5},{5... | collective-permute-start | bytes 786440 | tf_op jit(solution)/shard_map/ppermute | solution.py:435
  8.7 9.2 %collective-permute-start.4 = (f32[4,64,256]{2,1,0:T(8,128)S(1)}, f32[4,64,256]{2,1,0:T(8,128)S(1)}, u32[]{:S(2)}, u32[]{:S(2)}) collective-permute-start(f32[4,64,256]{2,1,0:T(8,128)S(1)} %get-tuple-element.41), channel_id=1, source_target_pairs={{0,8},{4,12},{8,0},{12,4},{16,24},{20,28},{24,16},{28,20},{1,9},{5... | collective-permute-start | bytes 786440 | tf_op jit(solution)/shard_map/ppermute | solution.py:435
  10.3 11.6 %copy-start.1 = (f32[64,2]{1,0:T(8,128)S(1)}, f32[64,2]{1,0:T(8,128)}, u32[]{:S(2)}) copy-start(f32[64,2]{1,0:T(8,128)} %constant.35.clone.edges) | copy-start | bytes 1540
  10.3 11.6 %copy-start.2 = (f32[64,1]{1,0:T(8,128)S(1)}, f32[64,1]{1,0:T(8,128)}, u32[]{:S(2)}) copy-start(f32[64,1]{1,0:T(8,128)} %constant.33.clone.smu_y) | copy-start | bytes 772
  10.3 11.6 %copy-start.5 = (f32[1,1024]{1,0:T(1,128)S(1)}, f32[1,1024]{1,0:T(1,128)}, u32[]{:S(2)}) copy-start(f32[1,1024]{1,0:T(1,128)} %constant.34.clone.smu_x) | copy-start | bytes 12292
  10.3 11.6 %copy-start.7 = (f32[4,1]{1,0:T(4,128)S(1)}, f32[4,1]{1,0:T(4,128)}, u32[]{:S(2)}) copy-start(f32[4,1]{1,0:T(4,128)} %constant.41.clone.smu_z) | copy-start | bytes 52
  10.3 29.7 %copy-start.4 = (f32[5,4,4,1024]{3,2,1,0:T(4,128)S(1)}, f32[5,4,4,1024]{3,2,1,0:T(4,128)}, u32[]{:S(2)}) copy-start(f32[5,4,4,1024]{3,2,1,0:T(4,128)} %constant.43.clone.responses) | copy-start | bytes 983044
  10.3 38.9 %copy-start.6 = (f32[4,1]{1,0:T(4,128)S(1)}, f32[4,1]{1,0:T(4,128)}, u32[]{:S(2)}) copy-start(f32[4,1]{1,0:T(4,128)} %constant.42.clone.smu_z) | copy-start | bytes 52
  10.3 11.6 %collective-permute-start.5 = (f32[4,64,256]{2,1,0:T(8,128)S(1)}, f32[4,64,256]{2,1,0:T(8,128)S(1)}, u32[]{:S(2)}, u32[]{:S(2)}) collective-permute-start(f32[4,64,256]{2,1,0:T(8,128)S(1)} %get-tuple-element.42), channel_id=1, source_target_pairs={{0,12},{4,8},{8,4},{12,0},{16,28},{20,24},{24,20},{28,16},{1,13},{... | collective-permute-start | bytes 786440 | tf_op jit(solution)/shard_map/ppermute | solution.py:435
  13.3 51.4 %copy-start.3 = (f32[5,4,4,1024]{3,2,1,0:T(4,128)S(1)}, f32[5,4,4,1024]{3,2,1,0:T(4,128)}, u32[]{:S(2)}) copy-start(f32[5,4,4,1024]{3,2,1,0:T(4,128)} %constant.44.clone.responses) | copy-start | bytes 983044
  23.9 27.9 %collective-permute-start.6 = (f32[2,4,64,256]{3,2,1,0:T(8,128)S(1)}, f32[2,4,64,256]{3,2,1,0:T(8,128)S(1)}, u32[]{:S(2)}, u32[]{:S(2)}) collective-permute-start(f32[2,4,64,256]{3,2,1,0:T(8,128)S(1)} %get-tuple-element.43), channel_id=1, source_target_pairs={{0,16},{4,20},{8,24},{12,28},{16,0},{20,4},{24,8},{28,12},{1,17},{... | collective-permute-start | bytes 1572872 | tf_op jit(solution)/shard_map/ppermute | solution.py:435
  26.7 14.4 %collective-permute-start = (f32[4,64,256]{2,1,0:T(8,128)S(1)}, f32[4,64,256]{2,1,0:T(8,128)S(1)}, u32[]{:S(2)}, u32[]{:S(2)}) collective-permute-start(f32[4,64,256]{2,1,0:T(8,128)S(1)} %get-tuple-element.35), channel_id=1, source_target_pairs={{0,4},{4,0},{8,12},{12,8},{16,20},{20,16},{24,28},{28,24},{1,5},{5... | collective-permute-start | bytes 786440 | tf_op jit(solution)/shard_map/ppermute | solution.py:435
  28.2 16.5 %collective-permute-start.1 = (f32[4,64,256]{2,1,0:T(8,128)S(1)}, f32[4,64,256]{2,1,0:T(8,128)S(1)}, u32[]{:S(2)}, u32[]{:S(2)}) collective-permute-start(f32[4,64,256]{2,1,0:T(8,128)S(1)} %get-tuple-element.36), channel_id=1, source_target_pairs={{0,8},{4,12},{8,0},{12,4},{16,24},{20,28},{24,16},{28,20},{1,9},{5... | collective-permute-start | bytes 786440 | tf_op jit(solution)/shard_map/ppermute | solution.py:435
  29.8 19.5 %collective-permute-start.2 = (f32[4,64,256]{2,1,0:T(8,128)S(1)}, f32[4,64,256]{2,1,0:T(8,128)S(1)}, u32[]{:S(2)}, u32[]{:S(2)}) collective-permute-start(f32[4,64,256]{2,1,0:T(8,128)S(1)} %get-tuple-element.37), channel_id=1, source_target_pairs={{0,12},{4,8},{8,4},{12,0},{16,28},{20,24},{24,20},{28,16},{1,13},{... | collective-permute-start | bytes 786440 | tf_op jit(solution)/shard_map/ppermute | solution.py:435
  30.1 4.3 %collective-permute-start.9 = (f32[16,4,256]{2,1,0:T(4,128)S(1)}, f32[16,4,256]{2,1,0:T(4,128)S(1)}, u32[]{:S(2)}, u32[]{:S(2)}) collective-permute-start(f32[16,4,256]{2,1,0:T(4,128)S(1)} %get-tuple-element.44.refs_0_), channel_id=1, source_target_pairs={{0,3},{1,2},{2,1},{3,0},{4,7},{5,6},{6,5},{7,4},{8,11},{9,10},{10,... | collective-permute-start | bytes 196616 | tf_op jit(solution)/shard_map/ppermute | solution.py:435
  34.5 4.3 %collective-permute-start.8 = (f32[16,4,256]{2,1,0:T(4,128)S(1)}, f32[16,4,256]{2,1,0:T(4,128)S(1)}, u32[]{:S(2)}, u32[]{:S(2)}) collective-permute-start(f32[16,4,256]{2,1,0:T(4,128)S(1)} %get-tuple-element.44.refs_0_), channel_id=1, source_target_pairs={{0,2},{1,3},{2,0},{3,1},{4,6},{5,7},{6,4},{7,5},{8,10},{9,11},{10,... | collective-permute-start | bytes 196616 | tf_op jit(solution)/shard_map/ppermute | solution.py:435
  38.8 1.3 %collective-permute-start.7 = (f32[16,4,256]{2,1,0:T(4,128)S(1)}, f32[16,4,256]{2,1,0:T(4,128)S(1)}, u32[]{:S(2)}, u32[]{:S(2)}) collective-permute-start(f32[16,4,256]{2,1,0:T(4,128)S(1)} %get-tuple-element.44.refs_0_), channel_id=1, source_target_pairs={{0,1},{1,0},{2,3},{3,2},{4,5},{5,4},{6,7},{7,6},{8,9},{9,8},{10,11... | collective-permute-start | bytes 196616 | tf_op jit(solution)/shard_map/ppermute | solution.py:435
  40.9 10.9 %collective-permute-start.10 = (f32[16,4,256]{2,1,0:T(4,128)S(1)}, f32[16,4,256]{2,1,0:T(4,128)S(1)}, u32[]{:S(2)}, u32[]{:S(2)}) collective-permute-start(f32[16,4,256]{2,1,0:T(4,128)S(1)} %shard_map.132.refs_5_), channel_id=1, source_target_pairs={{0,16},{4,20},{8,24},{12,28},{16,0},{20,4},{24,8},{28,12},{1,17},{... | collective-permute-start | bytes 196616 | tf_op jit(solution)/shard_map/ppermute | solution.py:435
  51.8 32.3 %copy-start = (bf16[2,2,256,256]{3,2,1,0:T(8,128)(2,1)S(1)}, bf16[2,2,256,256]{3,2,1,0:T(8,128)(2,1)}, u32[]{:S(2)}) copy-start(bf16[2,2,256,256]{3,2,1,0:T(8,128)(2,1)} %constant.48.both) | copy-start | bytes 1572868
  51.8 26.4 %collective-permute-start.11 = (f32[2,4,64,256]{3,2,1,0:T(8,128)S(1)}, f32[2,4,64,256]{3,2,1,0:T(8,128)S(1)}, u32[]{:S(2)}, u32[]{:S(2)}) collective-permute-start(f32[2,4,64,256]{3,2,1,0:T(8,128)S(1)} %get-tuple-element.45), channel_id=1, source_target_pairs={{0,16},{4,20},{8,24},{12,28},{16,0},{20,4},{24,8},{28,12},{1,17},{... | collective-permute-start | bytes 1572872 | tf_op jit(solution)/shard_map/ppermute | solution.py:435
  56.0 28.1 %collective-permute-start.19 = (f32[4,64,256]{2,1,0:T(8,128)S(1)}, f32[4,64,256]{2,1,0:T(8,128)S(1)}, u32[]{:S(2)}, u32[]{:S(2)}) collective-permute-start(f32[4,64,256]{2,1,0:T(8,128)S(1)} %get-tuple-element.52), channel_id=1, source_target_pairs={{0,4},{4,0},{8,12},{12,8},{16,20},{20,16},{24,28},{28,24},{1,5},{5... | collective-permute-start | bytes 786440 | tf_op jit(solution)/shard_map/ppermute | solution.py:435
  56.9 4.3 %collective-permute-start.14 = (f32[16,4,256]{2,1,0:T(4,128)S(1)}, f32[16,4,256]{2,1,0:T(4,128)S(1)}, u32[]{:S(2)}, u32[]{:S(2)}) collective-permute-start(f32[16,4,256]{2,1,0:T(4,128)S(1)} %get-tuple-element.46.refs_0_), channel_id=1, source_target_pairs={{0,3},{1,2},{2,1},{3,0},{4,7},{5,6},{6,5},{7,4},{8,11},{9,10},{10,... | collective-permute-start | bytes 196616 | tf_op jit(solution)/shard_map/ppermute | solution.py:435
  56.9 6.6 %collective-permute-start.13 = (f32[16,4,256]{2,1,0:T(4,128)S(1)}, f32[16,4,256]{2,1,0:T(4,128)S(1)}, u32[]{:S(2)}, u32[]{:S(2)}) collective-permute-start(f32[16,4,256]{2,1,0:T(4,128)S(1)} %get-tuple-element.46.refs_0_), channel_id=1, source_target_pairs={{0,2},{1,3},{2,0},{3,1},{4,6},{5,7},{6,4},{7,5},{8,10},{9,11},{10,... | collective-permute-start | bytes 196616 | tf_op jit(solution)/shard_map/ppermute | solution.py:435
  58.4 25.7 %collective-permute-start.20 = (f32[4,64,256]{2,1,0:T(8,128)S(1)}, f32[4,64,256]{2,1,0:T(8,128)S(1)}, u32[]{:S(2)}, u32[]{:S(2)}) collective-permute-start(f32[4,64,256]{2,1,0:T(8,128)S(1)} %get-tuple-element.53), channel_id=1, source_target_pairs={{0,8},{4,12},{8,0},{12,4},{16,24},{20,28},{24,16},{28,20},{1,9},{5... | collective-permute-start | bytes 786440 | tf_op jit(solution)/shard_map/ppermute | solution.py:435
  61.2 22.9 %collective-permute-start.21 = (f32[4,64,256]{2,1,0:T(8,128)S(1)}, f32[4,64,256]{2,1,0:T(8,128)S(1)}, u32[]{:S(2)}, u32[]{:S(2)}) collective-permute-start(f32[4,64,256]{2,1,0:T(8,128)S(1)} %get-tuple-element.54), channel_id=1, source_target_pairs={{0,12},{4,8},{8,4},{12,0},{16,28},{20,24},{24,20},{28,16},{1,13},{... | collective-permute-start | bytes 786440 | tf_op jit(solution)/shard_map/ppermute | solution.py:435
  63.4 1.3 %collective-permute-start.12 = (f32[16,4,256]{2,1,0:T(4,128)S(1)}, f32[16,4,256]{2,1,0:T(4,128)S(1)}, u32[]{:S(2)}, u32[]{:S(2)}) collective-permute-start(f32[16,4,256]{2,1,0:T(4,128)S(1)} %get-tuple-element.46.refs_0_), channel_id=1, source_target_pairs={{0,1},{1,0},{2,3},{3,2},{4,5},{5,4},{6,7},{7,6},{8,9},{9,8},{10,11... | collective-permute-start | bytes 196616 | tf_op jit(solution)/shard_map/ppermute | solution.py:435
  65.6 12.7 %collective-permute-start.15 = (f32[16,4,256]{2,1,0:T(4,128)S(1)}, f32[16,4,256]{2,1,0:T(4,128)S(1)}, u32[]{:S(2)}, u32[]{:S(2)}) collective-permute-start(f32[16,4,256]{2,1,0:T(4,128)S(1)} %shard_map.133.refs_5_), channel_id=1, source_target_pairs={{0,16},{4,20},{8,24},{12,28},{16,0},{20,4},{24,8},{28,12},{1,17},{... | collective-permute-start | bytes 196616 | tf_op jit(solution)/shard_map/ppermute | solution.py:435
  80.4 10.7 %collective-permute-start.16 = (f32[4,64,256]{2,1,0:T(8,128)S(1)}, f32[4,64,256]{2,1,0:T(8,128)S(1)}, u32[]{:S(2)}, u32[]{:S(2)}) collective-permute-start(f32[4,64,256]{2,1,0:T(8,128)S(1)} %get-tuple-element.48), channel_id=1, source_target_pairs={{0,4},{4,0},{8,12},{12,8},{16,20},{20,16},{24,28},{28,24},{1,5},{5... | collective-permute-start | bytes 786440 | tf_op jit(solution)/shard_map/ppermute | solution.py:435
  81.0 10.3 %collective-permute-start.17 = (f32[4,64,256]{2,1,0:T(8,128)S(1)}, f32[4,64,256]{2,1,0:T(8,128)S(1)}, u32[]{:S(2)}, u32[]{:S(2)}) collective-permute-start(f32[4,64,256]{2,1,0:T(8,128)S(1)} %get-tuple-element.49), channel_id=1, source_target_pairs={{0,8},{4,12},{8,0},{12,4},{16,24},{20,28},{24,16},{28,20},{1,9},{5... | collective-permute-start | bytes 786440 | tf_op jit(solution)/shard_map/ppermute | solution.py:435
  84.1 10.3 %collective-permute-start.18 = (f32[4,64,256]{2,1,0:T(8,128)S(1)}, f32[4,64,256]{2,1,0:T(8,128)S(1)}, u32[]{:S(2)}, u32[]{:S(2)}) collective-permute-start(f32[4,64,256]{2,1,0:T(8,128)S(1)} %get-tuple-element.50), channel_id=1, source_target_pairs={{0,12},{4,8},{8,4},{12,0},{16,28},{20,24},{24,20},{28,16},{1,13},{... | collective-permute-start | bytes 786440 | tf_op jit(solution)/shard_map/ppermute | solution.py:435
  (1 other events, 1.0 us)

commit v8 on v7

--- a/solution.py
+++ b/solution.py
@@ -173,21 +173,20 @@
     outs, (high, low) = refs[len(ready) : -2], refs[-2:]
     folds = plan.folds
     shape = folds, plan.rows, plan.block
+    total = None
     for k in range(plan.half):
-        piece = pieces[k][...].reshape(len(chunk) * plan.rows, plan.block)
-        high[k], low[k] = parts_of(piece)
+        at = plan.columns(place ^ k)
+        piece = parts_of(pieces[k][...].reshape(-1, plan.block))
+        value = dot_parts(piece, (sxh[at, :], sxl[at, :]))
+        total = value if total is None else total + value
+    high[...], low[...] = parts_of(total)
     for j in range(plan.half):
         columns = pl.ds(j * plan.block, plan.block)
-        total = None
-        for k in range(plan.half):
-            at = plan.columns(place ^ k)
-            value = dot_parts((high[k], low[k]), (sxh[at, columns], sxl[at, columns]))
-            total = value if total is None else total + value
-        total = parts_of(total)
         sums = {parity: before[parity][:, :, columns] for parity in ready}
         for parity, rows, at in by_parity(plan, chunk):
             table = both[0, parity, :, at], both[1, parity, :, at]
-            value = dot_parts(table, (total[0][rows], total[1][rows])).reshape(shape)
+            value = dot_parts(table, (high[rows, columns], low[rows, columns]))
+            value = value.reshape(shape)
             sums[parity] = sums[parity] + value if parity in sums else value
         if not last:
             for parity, out in zip(sorted(sums), outs):
@@ -310,13 +309,10 @@
 
 def join_rows(plan, ids, responses, *refs):
     groups, steps = plan.groups, plan.steps
-    views = refs[:groups]
-    out, seen, above, below = refs[groups:]
+    seen, out, above, below = refs
     place = lax.rem(ids[0], plan.half)
     me = ids[1]
     columns = plan.columns(place)
-    for k in range(groups):
-        seen[me ^ k] = views[k][...]
     radius = ALPHA_RATIO ** (1.0 / steps)
     grow = [radius**n for n in range(steps)]
     nothing = jnp.zeros(out.shape[1:], jnp.float32)
@@ -429,6 +425,11 @@
     by_place(plan, place, with_place)
 
 
+def spread(plan, pieces):
+    moved = [swap(pieces[k], "tm", plan.steps, k) for k in range(plan.half - 1, -1, -1)]
+    return moved[::-1]
+
+
 def swap(values, axis, count, distance):
     if distance == 0:
         return values
@@ -466,33 +467,37 @@
             flops,
             (ids, forth, field, *tables),
         )
-        pieces = [swap(v, "tm", steps, k) for k, v in enumerate(pieces)]
+        pieces = spread(plan, pieces)
         smu_own = jnp.asarray(smu_z[list(chunk), None], jnp.float32)
         work.append((chunk, modes, flops, (ids, smu_own, smu_y, smu_x, edges), pieces))
     first, second = work[0][-1], work[1][-1]
     first[0], second[0] = lax.optimization_barrier((first[0], second[0]))
-    sums = {}
-    far = None
+    ended = []
     for chunk, modes, flops, small, pieces in work:
         seen = f32((2 * steps, len(chunk), plan.block))
         ends, view = call(
             functools.partial(half_end, plan),
             [f32((2,) + modes.shape), seen],
-            100 * modes.size * half,
+            40000 * modes.size * half,
             (*small, *pieces),
             [pltpu.VMEM((2 * steps, len(chunk), 8, plan.block), jnp.float32)],
         )
+        ended.append([ends, seen, lax.all_gather(view, "gy")])
+    for now, later in zip(ended, ended[1:]):
+        now[2], later[0] = lax.optimization_barrier((now[2], later[0]))
+    sums = {}
+    far = None
+    for (chunk, modes, flops, small, pieces), (ends, seen, views) in zip(work, ended):
         if far is not None:
             ends, far, beside_far = lax.optimization_barrier((ends, far, beside_far))
         far = swap(ends, "tm", steps, half)
-        views = [swap(view, "gy", groups, k) for k in range(groups)]
         sides = pltpu.VMEM((groups, steps + 2) + seen.shape[1:], jnp.float32)
         beside = call(
             functools.partial(join_rows, plan),
             seen,
-            100 * seen.size,
-            (ids, jnp.asarray(responses[:, :, list(chunk)]), *views),
-            [pltpu.VMEM((groups,) + seen.shape, jnp.float32), sides, sides],
+            (100 if chunk == CHUNKS[-1] else 80000) * modes.size * half,
+            (ids, jnp.asarray(responses[:, :, list(chunk)]), views),
+            [sides, sides],
         )
         beside_far = swap(beside, "tm", steps, half)
         pieces = call(
@@ -501,9 +506,9 @@
             100 * modes.size * half,
             (*small, *pieces, far, beside, beside_far),
         )
-        pieces = [swap(v, "tm", steps, k) for k, v in enumerate(pieces)]
+        pieces = spread(plan, pieces)
         last = chunk == CHUNKS[-1]
-        part = pltpu.VMEM((half, len(chunk) * plan.rows, plan.block), jnp.bfloat16)
+        part = pltpu.VMEM((len(chunk) * plan.rows, plan.width), jnp.bfloat16)
         hold = [part, part]
         if last:
             block = field.shape[:2] + (plan.block,)

time: 101 us -> 105 us (1.040)
  blocking collectives: 0 us -> 12.7 us
  waiting for transfers between devices: 43.9 us -> 32.9 us
  starting transfers between devices: 26.9 us -> 33.4 us
  Pallas kernels: 28.3 us -> 23.8 us
    all_gather x0 -> x2, blocking collectives: none -> 12.7 us  [on_device(): ended.append([ends, seen, lax.all_gather(view, 'gy')])]
    ppermute x22 -> x16, waiting for transfers between devices: 43.9 us -> 32.9 us  [swap(): return lax.ppermute(values, axis, [(i, i ^ distance) for i in range(count)])]
    ppermute x22 -> x16, starting transfers between devices: 26.9 us -> 33.4 us  [swap(): return lax.ppermute(values, axis, [(i, i ^ distance) for i in range(count)])]
    pallas_call x11, Pallas kernels: 28.3 us -> 23.8 us  [call(): pl.pallas_call(kernel, out_shape=out_shape, in_specs=[smem] + [vmem] * (l...]
  transfers between devices with their start and end apart: 22 -> 16, of which waited for: 15 -> 8; matrix products, arithmetic and copies ran while one was open for 0% -> 0% of each run, Pallas kernels for 16% -> 15%
where the time goes in v8:
time: 105 us; the launch traced here: 104 us
  starting transfers between devices  33.4 us (32%)
  waiting for transfers between devices  32.9 us (31%)
  Pallas kernels  23.8 us (23%)
  blocking collectives  12.7 us (12%)
  local copies, waits for them, and re-layouts  1.08 us (1%)
    ppermute x16, starting transfers between devices, swap(): return lax.ppermute(values, axis, [(i, i ^ distance) for i in range(count)])  33.4 us
    ppermute x16, waiting for transfers between devices, swap(): return lax.ppermute(values, axis, [(i, i ^ distance) for i in range(count)])  32.9 us
    pallas_call x11, Pallas kernels, call(): pl.pallas_call(kernel, out_shape=out_shape, in_specs=[smem] + [vmem] * (l...  23.8 us
    all_gather x2, blocking collectives, on_device(): ended.append([ends, seen, lax.all_gather(view, 'gy')])  12.7 us
  transfers between devices with their start and end apart: 16, of which 8 were waited for; matrix products, arithmetic and copies ran while one was open for 0% of the time, Pallas kernels for 15%

profile of v8, /device:TPU:0, one launch (start us, length us, event | category | flops | bytes accessed | tf_op | source)
XLA Modules:
  0.0 104.3 jit_solution(12422385582143872017)
XLA Ops:
  0.1 1.0 copy-done.9
  1.1 1.7 %shard_map.127 = (bf16[1024,1024]{1,0:T(8,128)(2,1)S(1)}, bf16[1024,1024]{1,0:T(8,128)(2,1)S(1)}) custom-call(s32[2]{0:T(128)S(1)} %pad_add_fusion.ids, f32[128,1024]{1,0:T(8,128)S(1)} %copy-done.9), custom_call_target="tpu_custom_call" | custom-call | flops 4194304000 | bytes 524296 | tf_op jit(solution)/shard_map/pallas_call | solution.py:73
  2.9 2.8 %shard_map.128 = (f32[4,64,256]{2,1,0:T(8,128)S(1)}, f32[4,64,256]{2,1,0:T(8,128)S(1)}, f32[4,64,256]{2,1,0:T(8,128)S(1)}, f32[4,64,256]{2,1,0:T(8,128)S(1)}) custom-call(s32[2]{0:T(128)S(1)} %pad_add_fusion.ids, bf16[2,2,256,256]{3,2,1,0:T(8,128)(2,1)S(1)} %copy-done.8, f32[8,64,1024]{2,1,0:T(8,128)S(1)} %bitcast.8, ...), custom_call_target="tpu_custom_call" | custom-call | flops 2013265920 | bytes 6815752 | tf_op jit(solution)/shard_map/pallas_call | solution.py:73
  5.7 3.0 %collective-permute-start.3 = (f32[4,64,256]{2,1,0:T(8,128)S(1)}, f32[4,64,256]{2,1,0:T(8,128)S(1)}, u32[]{:S(2)}, u32[]{:S(2)}) collective-permute-start(f32[4,64,256]{2,1,0:T(8,128)S(1)} %get-tuple-element.41), channel_id=1, source_target_pairs={{0,4},{4,0},{8,12},{12,8},{16,20},{20,16},{24,28},{28,24},{1,5},{5... | collective-permute-start | bytes 786440 | tf_op jit(solution)/shard_map/ppermute | solution.py:436
  8.7 1.6 %collective-permute-start.4 = (f32[4,64,256]{2,1,0:T(8,128)S(1)}, f32[4,64,256]{2,1,0:T(8,128)S(1)}, u32[]{:S(2)}, u32[]{:S(2)}) collective-permute-start(f32[4,64,256]{2,1,0:T(8,128)S(1)} %get-tuple-element.42), channel_id=1, source_target_pairs={{0,8},{4,12},{8,0},{12,4},{16,24},{20,28},{24,16},{28,20},{1,9},{5... | collective-permute-start | bytes 786440 | tf_op jit(solution)/shard_map/ppermute | solution.py:436
  10.4 2.8 %shard_map.129 = (f32[4,64,256]{2,1,0:T(8,128)S(1)}, f32[4,64,256]{2,1,0:T(8,128)S(1)}, f32[4,64,256]{2,1,0:T(8,128)S(1)}, f32[4,64,256]{2,1,0:T(8,128)S(1)}) custom-call(s32[2]{0:T(128)S(1)} %pad_add_fusion.ids, bf16[2,2,256,256]{3,2,1,0:T(8,128)(2,1)S(1)} %copy-done.8, f32[8,64,1024]{2,1,0:T(8,128)S(1)} %bitcast.9, ...), custom_call_target="tpu_custom_call" | custom-call | flops 2013265920 | bytes 6815752 | tf_op jit(solution)/shard_map/pallas_call | solution.py:73
  13.2 2.0 %collective-permute-start = (f32[4,64,256]{2,1,0:T(8,128)S(1)}, f32[4,64,256]{2,1,0:T(8,128)S(1)}, u32[]{:S(2)}, u32[]{:S(2)}) collective-permute-start(f32[4,64,256]{2,1,0:T(8,128)S(1)} %get-tuple-element.37), channel_id=1, source_target_pairs={{0,4},{4,0},{8,12},{12,8},{16,20},{20,16},{24,28},{28,24},{1,5},{5... | collective-permute-start | bytes 786440 | tf_op jit(solution)/shard_map/ppermute | solution.py:436
  15.2 1.6 %collective-permute-start.1 = (f32[4,64,256]{2,1,0:T(8,128)S(1)}, f32[4,64,256]{2,1,0:T(8,128)S(1)}, u32[]{:S(2)}, u32[]{:S(2)}) collective-permute-start(f32[4,64,256]{2,1,0:T(8,128)S(1)} %get-tuple-element.38), channel_id=1, source_target_pairs={{0,8},{4,12},{8,0},{12,4},{16,24},{20,28},{24,16},{28,20},{1,9},{5... | collective-permute-start | bytes 786440 | tf_op jit(solution)/shard_map/ppermute | solution.py:436
  16.8 1.5 %collective-permute-start.2 = (f32[4,64,256]{2,1,0:T(8,128)S(1)}, f32[4,64,256]{2,1,0:T(8,128)S(1)}, u32[]{:S(2)}, u32[]{:S(2)}) collective-permute-start(f32[4,64,256]{2,1,0:T(8,128)S(1)} %get-tuple-element.39), channel_id=1, source_target_pairs={{0,12},{4,8},{8,4},{12,0},{16,28},{20,24},{24,20},{28,16},{1,13},{... | collective-permute-start | bytes 786440 | tf_op jit(solution)/shard_map/ppermute | solution.py:436
  18.2 4.9 %collective-permute-done.5.refs_3_ = f32[4,64,256]{2,1,0:T(8,128)S(1)} collective-permute-done((f32[4,64,256]{2,1,0:T(8,128)S(1)}, f32[4,64,256]{2,1,0:T(8,128)S(1)}, u32[]{:S(2)}, u32[]{:S(2)}) %collective-permute-start.5) | collective-permute-done | bytes 262176 | tf_op jit(solution)/shard_map/ppermute | solution.py:436
  23.1 1.9 %shard_map.130 = (f32[2,4,64,256]{3,2,1,0:T(8,128)S(1)}, f32[16,4,256]{2,1,0:T(4,128)S(1)}) custom-call(s32[2]{0:T(128)S(1)} %pad_add_fusion.ids, f32[4,1]{1,0:T(4,128)S(1)} %copy-done.6, f32[64,1]{1,0:T(8,128)S(1)} %copy-done.3, f32[1,1024]{1,0:T(1,128)S(1)} %copy-done.4, f32[64,2]{1,0:T(8,128)S(1)} %copy-done.2, ...), custom_call_target="tpu_custom_call" | custom-call | flops 10485760000 | bytes 1053464 | tf_op jit(solution)/shard_map/pallas_call | solution.py:73
  25.0 3.1 %collective-permute-start.6 = (f32[2,4,64,256]{3,2,1,0:T(8,128)S(1)}, f32[2,4,64,256]{3,2,1,0:T(8,128)S(1)}, u32[]{:S(2)}, u32[]{:S(2)}) collective-permute-start(f32[2,4,64,256]{3,2,1,0:T(8,128)S(1)} %get-tuple-element.47), channel_id=1, source_target_pairs={{0,16},{4,20},{8,24},{12,28},{16,0},{20,4},{24,8},{28,12},{1,17},{... | collective-permute-start | bytes 1572872 | tf_op jit(solution)/shard_map/ppermute | solution.py:436
  28.1 5.8 %all-gather = f32[64,4,256]{2,1,0:T(4,128)S(1)} all-gather(f32[16,4,256]{2,1,0:T(4,128)S(1)} %get-tuple-element.44), channel_id=2, replica_groups=mesh['tm'=8,'gy'=4] {'gy'}, dimensions={0}, use_global_device_ids=true | all-gather | bytes 327680 | tf_op jit(solution)/shard_map/all_gather | solution.py:485
  33.9 4.4 %collective-permute-done.1.refs_2_ = f32[4,64,256]{2,1,0:T(8,128)S(1)} collective-permute-done((f32[4,64,256]{2,1,0:T(8,128)S(1)}, f32[4,64,256]{2,1,0:T(8,128)S(1)}, u32[]{:S(2)}, u32[]{:S(2)}) %collective-permute-start.1) | collective-permute-done | bytes 262176 | tf_op jit(solution)/shard_map/ppermute | solution.py:436
  38.3 3.1 %collective-permute-done.2.refs_3_ = f32[4,64,256]{2,1,0:T(8,128)S(1)} collective-permute-done((f32[4,64,256]{2,1,0:T(8,128)S(1)}, f32[4,64,256]{2,1,0:T(8,128)S(1)}, u32[]{:S(2)}, u32[]{:S(2)}) %collective-permute-start.2) | collective-permute-done | bytes 262176 | tf_op jit(solution)/shard_map/ppermute | solution.py:436
  41.4 1.9 %shard_map.131 = (f32[2,4,64,256]{3,2,1,0:T(8,128)S(1)}, f32[16,4,256]{2,1,0:T(4,128)S(1)}) custom-call(s32[2]{0:T(128)S(1)} %pad_add_fusion.ids, f32[4,1]{1,0:T(4,128)S(1)} %copy-done.5, f32[64,1]{1,0:T(8,128)S(1)} %copy-done.3, f32[1,1024]{1,0:T(1,128)S(1)} %copy-done.4, f32[64,2]{1,0:T(8,128)S(1)} %copy-done.2, ...), custom_call_target="tpu_custom_call" | custom-call | flops 10485760000 | bytes 1053464 | tf_op jit(solution)/shard_map/pallas_call | solution.py:73
  43.3 0.8 shard_map.132.refs_5_
  44.9 6.8 %collective-permute-done.7.refs_6_ = f32[16,4,256]{2,1,0:T(4,128)S(1)} collective-permute-done((f32[16,4,256]{2,1,0:T(4,128)S(1)}, f32[16,4,256]{2,1,0:T(4,128)S(1)}, u32[]{:S(2)}, u32[]{:S(2)}) %collective-permute-start.7) | collective-permute-done | bytes 65568 | tf_op jit(solution)/shard_map/ppermute | solution.py:436
  51.7 2.0 %shard_map.135 = (f32[4,64,256]{2,1,0:T(8,128)S(1)}, f32[4,64,256]{2,1,0:T(8,128)S(1)}, f32[4,64,256]{2,1,0:T(8,128)S(1)}, f32[4,64,256]{2,1,0:T(8,128)S(1)}) custom-call(s32[2]{0:T(128)S(1)} %pad_add_fusion.ids, f32[4,1]{1,0:T(4,128)S(1)} %copy-done.6, f32[64,1]{1,0:T(8,128)S(1)} %copy-done.3, f32[1,1024]{1,0:T(1,128)S(1)} %copy-done.4, ...), custom_call_target="tpu_custom_call" | custom-call | flops 26214400 | bytes 1708824 | tf_op jit(solution)/shard_map/pallas_call | solution.py:73
  53.7 1.4 %collective-permute-start.13 = (f32[4,64,256]{2,1,0:T(8,128)S(1)}, f32[4,64,256]{2,1,0:T(8,128)S(1)}, u32[]{:S(2)}, u32[]{:S(2)}) collective-permute-start(f32[4,64,256]{2,1,0:T(8,128)S(1)} %get-tuple-element.56), channel_id=1, source_target_pairs={{0,4},{4,0},{8,12},{12,8},{16,20},{20,16},{24,28},{28,24},{1,5},{5... | collective-permute-start | bytes 786440 | tf_op jit(solution)/shard_map/ppermute | solution.py:436
  55.1 14.9 %collective-permute-start.14 = (f32[4,64,256]{2,1,0:T(8,128)S(1)}, f32[4,64,256]{2,1,0:T(8,128)S(1)}, u32[]{:S(2)}, u32[]{:S(2)}) collective-permute-start(f32[4,64,256]{2,1,0:T(8,128)S(1)} %get-tuple-element.57), channel_id=1, source_target_pairs={{0,8},{4,12},{8,0},{12,4},{16,24},{20,28},{24,16},{28,20},{1,9},{5... | collective-permute-start | bytes 786440 | tf_op jit(solution)/shard_map/ppermute | solution.py:436
  70.0 7.0 %all-gather.1 = f32[64,4,256]{2,1,0:T(4,128)S(1)} all-gather(f32[16,4,256]{2,1,0:T(4,128)S(1)} %get-tuple-element.50), channel_id=3, replica_groups=mesh['tm'=8,'gy'=4] {'gy'}, dimensions={0}, use_global_device_ids=true | all-gather | bytes 327680 | tf_op jit(solution)/shard_map/all_gather | solution.py:485
  76.9 0.8 shard_map.133.refs_5_
  77.9 5.2 %collective-permute-done.9.refs_6_ = f32[16,4,256]{2,1,0:T(4,128)S(1)} collective-permute-done((f32[16,4,256]{2,1,0:T(4,128)S(1)}, f32[16,4,256]{2,1,0:T(4,128)S(1)}, u32[]{:S(2)}, u32[]{:S(2)}) %collective-permute-start.9) | collective-permute-done | bytes 65568 | tf_op jit(solution)/shard_map/ppermute | solution.py:436
  83.1 2.2 %shard_map.134 = (f32[4,64,256]{2,1,0:T(8,128)S(1)}, f32[4,64,256]{2,1,0:T(8,128)S(1)}, f32[4,64,256]{2,1,0:T(8,128)S(1)}, f32[4,64,256]{2,1,0:T(8,128)S(1)}) custom-call(s32[2]{0:T(128)S(1)} %pad_add_fusion.ids, f32[4,1]{1,0:T(4,128)S(1)} %copy-done.5, f32[64,1]{1,0:T(8,128)S(1)} %copy-done.3, f32[1,1024]{1,0:T(1,128)S(1)} %copy-done.4, ...), custom_call_target="tpu_custom_call" | custom-call | flops 26214400 | bytes 1708824 | tf_op jit(solution)/shard_map/pallas_call | solution.py:73
  85.3 2.0 %collective-permute-start.10 = (f32[4,64,256]{2,1,0:T(8,128)S(1)}, f32[4,64,256]{2,1,0:T(8,128)S(1)}, u32[]{:S(2)}, u32[]{:S(2)}) collective-permute-start(f32[4,64,256]{2,1,0:T(8,128)S(1)} %get-tuple-element.52), channel_id=1, source_target_pairs={{0,4},{4,0},{8,12},{12,8},{16,20},{20,16},{24,28},{28,24},{1,5},{5... | collective-permute-start | bytes 786440 | tf_op jit(solution)/shard_map/ppermute | solution.py:436
  87.8 1.1 %collective-permute-start.12 = (f32[4,64,256]{2,1,0:T(8,128)S(1)}, f32[4,64,256]{2,1,0:T(8,128)S(1)}, u32[]{:S(2)}, u32[]{:S(2)}) collective-permute-start(f32[4,64,256]{2,1,0:T(8,128)S(1)} %get-tuple-element.54), channel_id=1, source_target_pairs={{0,12},{4,8},{8,4},{12,0},{16,28},{20,24},{24,20},{28,16},{1,13},{... | collective-permute-start | bytes 786440 | tf_op jit(solution)/shard_map/ppermute | solution.py:436
  88.9 2.8 %shard_map.136.refs_4_ = f32[4,64,1024]{2,1,0:T(8,128)S(1)} custom-call(s32[2]{0:T(128)S(1)} %pad_add_fusion.ids, bf16[2,2,256,256]{3,2,1,0:T(8,128)(2,1)S(1)} %copy-done, bf16[1024,1024]{1,0:T(8,128)(2,1)S(1)} %get-tuple-element.32.sxh, bf16[1024,1024]{1,0:T(8,128)(2,1)S(1)} %get-tuple-element.33.sxl, f32[4,64,256]{2,1,0:T(8,128)S(1)} %get-tuple-element.55.refs_0_, ...), custom_call_target="tpu_custom_call" | custom-call | flops 2013265920 | bytes 5767176 | tf_op jit(solution)/shard_map/pallas_call | solution.py:73
  91.7 1.4 %collective-permute-done.10.refs_1_ = f32[4,64,256]{2,1,0:T(8,128)S(1)} collective-permute-done((f32[4,64,256]{2,1,0:T(8,128)S(1)}, f32[4,64,256]{2,1,0:T(8,128)S(1)}, u32[]{:S(2)}, u32[]{:S(2)}) %collective-permute-start.10) | collective-permute-done | bytes 262176 | tf_op jit(solution)/shard_map/ppermute | solution.py:436
  93.1 3.1 %collective-permute-done.11.refs_2_ = f32[4,64,256]{2,1,0:T(8,128)S(1)} collective-permute-done((f32[4,64,256]{2,1,0:T(8,128)S(1)}, f32[4,64,256]{2,1,0:T(8,128)S(1)}, u32[]{:S(2)}, u32[]{:S(2)}) %collective-permute-start.11) | collective-permute-done | bytes 262176 | tf_op jit(solution)/shard_map/ppermute | solution.py:436
  96.3 3.9 %collective-permute-done.12.refs_3_ = f32[4,64,256]{2,1,0:T(8,128)S(1)} collective-permute-done((f32[4,64,256]{2,1,0:T(8,128)S(1)}, f32[4,64,256]{2,1,0:T(8,128)S(1)}, u32[]{:S(2)}, u32[]{:S(2)}) %collective-permute-start.12) | collective-permute-done | bytes 262176 | tf_op jit(solution)/shard_map/ppermute | solution.py:436
  100.2 4.0 %shard_map.137 = f32[8,64,1024]{2,1,0:T(8,128)} custom-call(s32[2]{0:T(128)S(1)} %pad_add_fusion.ids, bf16[2,2,256,256]{3,2,1,0:T(8,128)(2,1)S(1)} %copy-done, bf16[1024,1024]{1,0:T(8,128)(2,1)S(1)} %get-tuple-element.32.sxh, bf16[1024,1024]{1,0:T(8,128)(2,1)S(1)} %get-tuple-element.33.sxl, f32[4,64,256]{2,1,0:T(8,128)S(1)} %get-tuple-element.51.refs_0_, ...), custom_call_target="tpu_custom_call" | custom-call | flops 2013265920 | bytes 6815752 | tf_op jit(solution)/shard_map/pallas_call | solution.py:73
  (36 shorter events, 1.4 us)
Async XLA Ops:
  0.1 1.0 copy-start.9
  1.1 1.7 %copy-start.7 = (f32[1,8,64,1024]{3,2,1,0:T(8,128)S(1)}, f32[1,8,64,1024]{3,2,1,0:T(8,128)}, u32[]{:S(2)}) copy-start(f32[1,8,64,1024]{3,2,1,0:T(8,128)} %param.13) | copy-start | bytes 6291460
  1.1 1.7 %copy-start.8 = (bf16[2,2,256,256]{3,2,1,0:T(8,128)(2,1)S(1)}, bf16[2,2,256,256]{3,2,1,0:T(8,128)(2,1)}, u32[]{:S(2)}) copy-start(bf16[2,2,256,256]{3,2,1,0:T(8,128)(2,1)} %constant.51.both) | copy-start | bytes 1572868
  5.7 11.1 %collective-permute-start.3 = (f32[4,64,256]{2,1,0:T(8,128)S(1)}, f32[4,64,256]{2,1,0:T(8,128)S(1)}, u32[]{:S(2)}, u32[]{:S(2)}) collective-permute-start(f32[4,64,256]{2,1,0:T(8,128)S(1)} %get-tuple-element.41), channel_id=1, source_target_pairs={{0,4},{4,0},{8,12},{12,8},{16,20},{20,16},{24,28},{28,24},{1,5},{5... | collective-permute-start | bytes 786440 | tf_op jit(solution)/shard_map/ppermute | solution.py:436
  8.7 9.5 %collective-permute-start.4 = (f32[4,64,256]{2,1,0:T(8,128)S(1)}, f32[4,64,256]{2,1,0:T(8,128)S(1)}, u32[]{:S(2)}, u32[]{:S(2)}) collective-permute-start(f32[4,64,256]{2,1,0:T(8,128)S(1)} %get-tuple-element.42), channel_id=1, source_target_pairs={{0,8},{4,12},{8,0},{12,4},{16,24},{20,28},{24,16},{28,20},{1,9},{5... | collective-permute-start | bytes 786440 | tf_op jit(solution)/shard_map/ppermute | solution.py:436
  10.3 12.8 %copy-start.2 = (f32[64,2]{1,0:T(8,128)S(1)}, f32[64,2]{1,0:T(8,128)}, u32[]{:S(2)}) copy-start(f32[64,2]{1,0:T(8,128)} %constant.35.clone.edges) | copy-start | bytes 1540
  10.3 12.8 %copy-start.3 = (f32[64,1]{1,0:T(8,128)S(1)}, f32[64,1]{1,0:T(8,128)}, u32[]{:S(2)}) copy-start(f32[64,1]{1,0:T(8,128)} %constant.33.clone.smu_y) | copy-start | bytes 772
  10.3 12.8 %copy-start.4 = (f32[1,1024]{1,0:T(1,128)S(1)}, f32[1,1024]{1,0:T(1,128)}, u32[]{:S(2)}) copy-start(f32[1,1024]{1,0:T(1,128)} %constant.34.clone.smu_x) | copy-start | bytes 12292
  10.3 12.8 %copy-start.6 = (f32[4,1]{1,0:T(4,128)S(1)}, f32[4,1]{1,0:T(4,128)}, u32[]{:S(2)}) copy-start(f32[4,1]{1,0:T(4,128)} %constant.41.clone.smu_z) | copy-start | bytes 52
  10.3 12.8 %collective-permute-start.5 = (f32[4,64,256]{2,1,0:T(8,128)S(1)}, f32[4,64,256]{2,1,0:T(8,128)S(1)}, u32[]{:S(2)}, u32[]{:S(2)}) collective-permute-start(f32[4,64,256]{2,1,0:T(8,128)S(1)} %get-tuple-element.43), channel_id=1, source_target_pairs={{0,12},{4,8},{8,4},{12,0},{16,28},{20,24},{24,20},{28,16},{1,13},{... | collective-permute-start | bytes 786440 | tf_op jit(solution)/shard_map/ppermute | solution.py:436
  13.2 20.7 %collective-permute-start = (f32[4,64,256]{2,1,0:T(8,128)S(1)}, f32[4,64,256]{2,1,0:T(8,128)S(1)}, u32[]{:S(2)}, u32[]{:S(2)}) collective-permute-start(f32[4,64,256]{2,1,0:T(8,128)S(1)} %get-tuple-element.37), channel_id=1, source_target_pairs={{0,4},{4,0},{8,12},{12,8},{16,20},{20,16},{24,28},{28,24},{1,5},{5... | collective-permute-start | bytes 786440 | tf_op jit(solution)/shard_map/ppermute | solution.py:436
  15.2 23.1 %collective-permute-start.1 = (f32[4,64,256]{2,1,0:T(8,128)S(1)}, f32[4,64,256]{2,1,0:T(8,128)S(1)}, u32[]{:S(2)}, u32[]{:S(2)}) collective-permute-start(f32[4,64,256]{2,1,0:T(8,128)S(1)} %get-tuple-element.38), channel_id=1, source_target_pairs={{0,8},{4,12},{8,0},{12,4},{16,24},{20,28},{24,16},{28,20},{1,9},{5... | collective-permute-start | bytes 786440 | tf_op jit(solution)/shard_map/ppermute | solution.py:436
  16.7 24.7 %copy-start.5 = (f32[4,1]{1,0:T(4,128)S(1)}, f32[4,1]{1,0:T(4,128)}, u32[]{:S(2)}) copy-start(f32[4,1]{1,0:T(4,128)} %constant.42.clone.smu_z) | copy-start | bytes 52
  16.8 24.7 %collective-permute-start.2 = (f32[4,64,256]{2,1,0:T(8,128)S(1)}, f32[4,64,256]{2,1,0:T(8,128)S(1)}, u32[]{:S(2)}, u32[]{:S(2)}) collective-permute-start(f32[4,64,256]{2,1,0:T(8,128)S(1)} %get-tuple-element.39), channel_id=1, source_target_pairs={{0,12},{4,8},{8,4},{12,0},{16,28},{20,24},{24,20},{28,16},{1,13},{... | collective-permute-start | bytes 786440 | tf_op jit(solution)/shard_map/ppermute | solution.py:436
  25.0 26.7 %collective-permute-start.6 = (f32[2,4,64,256]{3,2,1,0:T(8,128)S(1)}, f32[2,4,64,256]{3,2,1,0:T(8,128)S(1)}, u32[]{:S(2)}, u32[]{:S(2)}) collective-permute-start(f32[2,4,64,256]{3,2,1,0:T(8,128)S(1)} %get-tuple-element.47), channel_id=1, source_target_pairs={{0,16},{4,20},{8,24},{12,28},{16,0},{20,4},{24,8},{28,12},{1,17},{... | collective-permute-start | bytes 1572872 | tf_op jit(solution)/shard_map/ppermute | solution.py:436
  33.9 9.4 %copy-start.10 = (f32[5,4,4,1024]{3,2,1,0:T(4,128)S(1)}, f32[5,4,4,1024]{3,2,1,0:T(4,128)}, u32[]{:S(2)}) copy-start(f32[5,4,4,1024]{3,2,1,0:T(4,128)} %constant.43.clone.responses) | copy-start | bytes 983044
  44.2 32.8 %copy-start.1 = (f32[5,4,4,1024]{3,2,1,0:T(4,128)S(1)}, f32[5,4,4,1024]{3,2,1,0:T(4,128)}, u32[]{:S(2)}) copy-start(f32[5,4,4,1024]{3,2,1,0:T(4,128)} %constant.44.clone.responses) | copy-start | bytes 983044
  44.2 44.7 %copy-start = (bf16[2,2,256,256]{3,2,1,0:T(8,128)(2,1)S(1)}, bf16[2,2,256,256]{3,2,1,0:T(8,128)(2,1)}, u32[]{:S(2)}) copy-start(bf16[2,2,256,256]{3,2,1,0:T(8,128)(2,1)} %constant.48.both) | copy-start | bytes 1572868
  44.2 7.5 %collective-permute-start.7 = (f32[16,4,256]{2,1,0:T(4,128)S(1)}, f32[16,4,256]{2,1,0:T(4,128)S(1)}, u32[]{:S(2)}, u32[]{:S(2)}) collective-permute-start(f32[16,4,256]{2,1,0:T(4,128)S(1)} %shard_map.132.refs_5_), channel_id=1, source_target_pairs={{0,16},{4,20},{8,24},{12,28},{16,0},{20,4},{24,8},{28,12},{1,17},{... | collective-permute-start | bytes 196616 | tf_op jit(solution)/shard_map/ppermute | solution.py:436
  51.7 31.4 %collective-permute-start.8 = (f32[2,4,64,256]{3,2,1,0:T(8,128)S(1)}, f32[2,4,64,256]{3,2,1,0:T(8,128)S(1)}, u32[]{:S(2)}, u32[]{:S(2)}) collective-permute-start(f32[2,4,64,256]{3,2,1,0:T(8,128)S(1)} %get-tuple-element.49), channel_id=1, source_target_pairs={{0,16},{4,20},{8,24},{12,28},{16,0},{20,4},{24,8},{28,12},{1,17},{... | collective-permute-start | bytes 1572872 | tf_op jit(solution)/shard_map/ppermute | solution.py:436
  53.7 34.0 %collective-permute-start.13 = (f32[4,64,256]{2,1,0:T(8,128)S(1)}, f32[4,64,256]{2,1,0:T(8,128)S(1)}, u32[]{:S(2)}, u32[]{:S(2)}) collective-permute-start(f32[4,64,256]{2,1,0:T(8,128)S(1)} %get-tuple-element.56), channel_id=1, source_target_pairs={{0,4},{4,0},{8,12},{12,8},{16,20},{20,16},{24,28},{28,24},{1,5},{5... | collective-permute-start | bytes 786440 | tf_op jit(solution)/shard_map/ppermute | solution.py:436
  55.1 33.7 %collective-permute-start.14 = (f32[4,64,256]{2,1,0:T(8,128)S(1)}, f32[4,64,256]{2,1,0:T(8,128)S(1)}, u32[]{:S(2)}, u32[]{:S(2)}) collective-permute-start(f32[4,64,256]{2,1,0:T(8,128)S(1)} %get-tuple-element.57), channel_id=1, source_target_pairs={{0,8},{4,12},{8,0},{12,4},{16,24},{20,28},{24,16},{28,20},{1,9},{5... | collective-permute-start | bytes 786440 | tf_op jit(solution)/shard_map/ppermute | solution.py:436
  70.0 18.9 %collective-permute-start.15 = (f32[4,64,256]{2,1,0:T(8,128)S(1)}, f32[4,64,256]{2,1,0:T(8,128)S(1)}, u32[]{:S(2)}, u32[]{:S(2)}) collective-permute-start(f32[4,64,256]{2,1,0:T(8,128)S(1)} %get-tuple-element.58), channel_id=1, source_target_pairs={{0,12},{4,8},{8,4},{12,0},{16,28},{20,24},{24,20},{28,16},{1,13},{... | collective-permute-start | bytes 786440 | tf_op jit(solution)/shard_map/ppermute | solution.py:436
  77.8 5.3 %collective-permute-start.9 = (f32[16,4,256]{2,1,0:T(4,128)S(1)}, f32[16,4,256]{2,1,0:T(4,128)S(1)}, u32[]{:S(2)}, u32[]{:S(2)}) collective-permute-start(f32[16,4,256]{2,1,0:T(4,128)S(1)} %shard_map.133.refs_5_), channel_id=1, source_target_pairs={{0,16},{4,20},{8,24},{12,28},{16,0},{20,4},{24,8},{28,12},{1,17},{... | collective-permute-start | bytes 196616 | tf_op jit(solution)/shard_map/ppermute | solution.py:436
  85.3 7.9 %collective-permute-start.10 = (f32[4,64,256]{2,1,0:T(8,128)S(1)}, f32[4,64,256]{2,1,0:T(8,128)S(1)}, u32[]{:S(2)}, u32[]{:S(2)}) collective-permute-start(f32[4,64,256]{2,1,0:T(8,128)S(1)} %get-tuple-element.52), channel_id=1, source_target_pairs={{0,4},{4,0},{8,12},{12,8},{16,20},{20,16},{24,28},{28,24},{1,5},{5... | collective-permute-start | bytes 786440 | tf_op jit(solution)/shard_map/ppermute | solution.py:436
  87.3 9.0 %collective-permute-start.11 = (f32[4,64,256]{2,1,0:T(8,128)S(1)}, f32[4,64,256]{2,1,0:T(8,128)S(1)}, u32[]{:S(2)}, u32[]{:S(2)}) collective-permute-start(f32[4,64,256]{2,1,0:T(8,128)S(1)} %get-tuple-element.53), channel_id=1, source_target_pairs={{0,8},{4,12},{8,0},{12,4},{16,24},{20,28},{24,16},{28,20},{1,9},{5... | collective-permute-start | bytes 786440 | tf_op jit(solution)/shard_map/ppermute | solution.py:436
  87.8 12.4 %collective-permute-start.12 = (f32[4,64,256]{2,1,0:T(8,128)S(1)}, f32[4,64,256]{2,1,0:T(8,128)S(1)}, u32[]{:S(2)}, u32[]{:S(2)}) collective-permute-start(f32[4,64,256]{2,1,0:T(8,128)S(1)} %get-tuple-element.54), channel_id=1, source_target_pairs={{0,12},{4,8},{8,4},{12,0},{16,28},{20,24},{24,20},{28,16},{1,13},{... | collective-permute-start | bytes 786440 | tf_op jit(solution)/shard_map/ppermute | solution.py:436

commit v9 on v8

--- a/solution.py
+++ b/solution.py
@@ -309,10 +309,13 @@
 
 def join_rows(plan, ids, responses, *refs):
     groups, steps = plan.groups, plan.steps
-    seen, out, above, below = refs
+    views = refs[:groups]
+    out, seen, above, below = refs[groups:]
     place = lax.rem(ids[0], plan.half)
     me = ids[1]
     columns = plan.columns(place)
+    for k in range(groups):
+        seen[me ^ k] = views[k][...]
     radius = ALPHA_RATIO ** (1.0 / steps)
     grow = [radius**n for n in range(steps)]
     nothing = jnp.zeros(out.shape[1:], jnp.float32)
@@ -473,31 +476,33 @@
     first, second = work[0][-1], work[1][-1]
     first[0], second[0] = lax.optimization_barrier((first[0], second[0]))
     ended = []
-    for chunk, modes, flops, small, pieces in work:
+    for at, (chunk, modes, flops, small, pieces) in enumerate(work):
         seen = f32((2 * steps, len(chunk), plan.block))
         ends, view = call(
             functools.partial(half_end, plan),
             [f32((2,) + modes.shape), seen],
-            40000 * modes.size * half,
+            (12000 if at else 40000) * modes.size * half,
             (*small, *pieces),
             [pltpu.VMEM((2 * steps, len(chunk), 8, plan.block), jnp.float32)],
         )
-        ended.append([ends, seen, lax.all_gather(view, "gy")])
-    for now, later in zip(ended, ended[1:]):
-        now[2], later[0] = lax.optimization_barrier((now[2], later[0]))
+        if at + 1 < len(work):
+            later = work[at + 1][-1]
+            view, *later[:] = lax.optimization_barrier((view, *later))
+        ended.append([ends, seen, view])
     sums = {}
     far = None
-    for (chunk, modes, flops, small, pieces), (ends, seen, views) in zip(work, ended):
+    for (chunk, modes, flops, small, pieces), (ends, seen, view) in zip(work, ended):
         if far is not None:
             ends, far, beside_far = lax.optimization_barrier((ends, far, beside_far))
         far = swap(ends, "tm", steps, half)
+        views = [swap(view, "gy", groups, k) for k in range(groups)]
         sides = pltpu.VMEM((groups, steps + 2) + seen.shape[1:], jnp.float32)
         beside = call(
             functools.partial(join_rows, plan),
             seen,
-            (100 if chunk == CHUNKS[-1] else 80000) * modes.size * half,
-            (ids, jnp.asarray(responses[:, :, list(chunk)]), views),
-            [sides, sides],
+            100 * seen.size,
+            (ids, jnp.asarray(responses[:, :, list(chunk)]), *views),
+            [pltpu.VMEM((groups,) + seen.shape, jnp.float32), sides, sides],
         )
         beside_far = swap(beside, "tm", steps, half)
         pieces = call(

time: 105 us -> 104 us (level)
  waiting for transfers between devices: 32.9 us -> 50.4 us
  blocking collectives: 12.7 us -> 0 us
  starting transfers between devices: 33.4 us -> 28 us
    ppermute x16 -> x22, waiting for transfers between devices: 32.9 us -> 50.4 us  [swap(): return lax.ppermute(values, axis, [(i, i ^ distance) for i in range(count)])]
    all_gather x2 -> x0, blocking collectives: 12.7 us -> none  [on_device(): ended.append([ends, seen, lax.all_gather(view, 'gy')])]
    ppermute x16 -> x22, starting transfers between devices: 33.4 us -> 28 us  [swap(): return lax.ppermute(values, axis, [(i, i ^ distance) for i in range(count)])]
  transfers between devices with their start and end apart: 16 -> 22, of which waited for: 8 -> 12; matrix products, arithmetic and copies ran while one was open for 0% -> 0% of each run, Pallas kernels for 15% -> 15%
where the time goes in v9:
time: 104 us
  waiting for transfers between devices  50.4 us (48%)
  starting transfers between devices  28 us (27%)
  Pallas kernels  23.9 us (23%)
  local copies, waits for them, and re-layouts  1.08 us (1%)
    ppermute x22, waiting for transfers between devices, swap(): return lax.ppermute(values, axis, [(i, i ^ distance) for i in range(count)])  50.4 us
    ppermute x22, starting transfers between devices, swap(): return lax.ppermute(values, axis, [(i, i ^ distance) for i in range(count)])  28 us
    pallas_call x11, Pallas kernels, call(): pl.pallas_call(kernel, out_shape=out_shape, in_specs=[smem] + [vmem] * (l...  23.9 us
  transfers between devices with their start and end apart: 22, of which 12 were waited for; matrix products, arithmetic and copies ran while one was open for 0% of the time, Pallas kernels for 15%

profile of v9, /device:TPU:0, one launch (start us, length us, event | category | flops | bytes accessed | tf_op | source)
XLA Modules:
  0.0 103.8 jit_solution(1084453556482508318)
XLA Ops:
  1.1 1.7 %shard_map.127 = (bf16[1024,1024]{1,0:T(8,128)(2,1)S(1)}, bf16[1024,1024]{1,0:T(8,128)(2,1)S(1)}) custom-call(s32[2]{0:T(128)S(1)} %pad_add_fusion.ids, f32[128,1024]{1,0:T(8,128)S(1)} %copy-done.10), custom_call_target="tpu_custom_call" | custom-call | flops 4194304000 | bytes 524296 | tf_op jit(solution)/shard_map/pallas_call | solution.py:73
  2.9 2.8 %shard_map.128 = (f32[4,64,256]{2,1,0:T(8,128)S(1)}, f32[4,64,256]{2,1,0:T(8,128)S(1)}, f32[4,64,256]{2,1,0:T(8,128)S(1)}, f32[4,64,256]{2,1,0:T(8,128)S(1)}) custom-call(s32[2]{0:T(128)S(1)} %pad_add_fusion.ids, bf16[2,2,256,256]{3,2,1,0:T(8,128)(2,1)S(1)} %copy-done.9, f32[8,64,1024]{2,1,0:T(8,128)S(1)} %bitcast.4, ...), custom_call_target="tpu_custom_call" | custom-call | flops 2013265920 | bytes 6815752 | tf_op jit(solution)/shard_map/pallas_call | solution.py:73
  5.7 3.0 %collective-permute-start = (f32[4,64,256]{2,1,0:T(8,128)S(1)}, f32[4,64,256]{2,1,0:T(8,128)S(1)}, u32[]{:S(2)}, u32[]{:S(2)}) collective-permute-start(f32[4,64,256]{2,1,0:T(8,128)S(1)} %get-tuple-element.40), channel_id=1, source_target_pairs={{0,4},{4,0},{8,12},{12,8},{16,20},{20,16},{24,28},{28,24},{1,5},{5... | collective-permute-start | bytes 786440 | tf_op jit(solution)/shard_map/ppermute | solution.py:439
  8.7 1.6 %collective-permute-start.1 = (f32[4,64,256]{2,1,0:T(8,128)S(1)}, f32[4,64,256]{2,1,0:T(8,128)S(1)}, u32[]{:S(2)}, u32[]{:S(2)}) collective-permute-start(f32[4,64,256]{2,1,0:T(8,128)S(1)} %get-tuple-element.41), channel_id=1, source_target_pairs={{0,8},{4,12},{8,0},{12,4},{16,24},{20,28},{24,16},{28,20},{1,9},{5... | collective-permute-start | bytes 786440 | tf_op jit(solution)/shard_map/ppermute | solution.py:439
  10.4 2.8 %shard_map.129 = (f32[4,64,256]{2,1,0:T(8,128)S(1)}, f32[4,64,256]{2,1,0:T(8,128)S(1)}, f32[4,64,256]{2,1,0:T(8,128)S(1)}, f32[4,64,256]{2,1,0:T(8,128)S(1)}) custom-call(s32[2]{0:T(128)S(1)} %pad_add_fusion.ids, bf16[2,2,256,256]{3,2,1,0:T(8,128)(2,1)S(1)} %copy-done.9, f32[8,64,1024]{2,1,0:T(8,128)S(1)} %bitcast.5, ...), custom_call_target="tpu_custom_call" | custom-call | flops 2013265920 | bytes 6815752 | tf_op jit(solution)/shard_map/pallas_call | solution.py:73
  13.2 2.0 %collective-permute-start.3 = (f32[4,64,256]{2,1,0:T(8,128)S(1)}, f32[4,64,256]{2,1,0:T(8,128)S(1)}, u32[]{:S(2)}, u32[]{:S(2)}) collective-permute-start(f32[4,64,256]{2,1,0:T(8,128)S(1)} %get-tuple-element.45), channel_id=1, source_target_pairs={{0,4},{4,0},{8,12},{12,8},{16,20},{20,16},{24,28},{28,24},{1,5},{5... | collective-permute-start | bytes 786440 | tf_op jit(solution)/shard_map/ppermute | solution.py:439
  15.2 1.6 %collective-permute-start.4 = (f32[4,64,256]{2,1,0:T(8,128)S(1)}, f32[4,64,256]{2,1,0:T(8,128)S(1)}, u32[]{:S(2)}, u32[]{:S(2)}) collective-permute-start(f32[4,64,256]{2,1,0:T(8,128)S(1)} %get-tuple-element.46), channel_id=1, source_target_pairs={{0,8},{4,12},{8,0},{12,4},{16,24},{20,28},{24,16},{28,20},{1,9},{5... | collective-permute-start | bytes 786440 | tf_op jit(solution)/shard_map/ppermute | solution.py:439
  16.8 1.4 %collective-permute-start.5 = (f32[4,64,256]{2,1,0:T(8,128)S(1)}, f32[4,64,256]{2,1,0:T(8,128)S(1)}, u32[]{:S(2)}, u32[]{:S(2)}) collective-permute-start(f32[4,64,256]{2,1,0:T(8,128)S(1)} %get-tuple-element.47), channel_id=1, source_target_pairs={{0,12},{4,8},{8,4},{12,0},{16,28},{20,24},{24,20},{28,16},{1,13},{... | collective-permute-start | bytes 786440 | tf_op jit(solution)/shard_map/ppermute | solution.py:439
  18.2 4.9 %collective-permute-done.2.refs_3_ = f32[4,64,256]{2,1,0:T(8,128)S(1)} collective-permute-done((f32[4,64,256]{2,1,0:T(8,128)S(1)}, f32[4,64,256]{2,1,0:T(8,128)S(1)}, u32[]{:S(2)}, u32[]{:S(2)}) %collective-permute-start.2) | collective-permute-done | bytes 262176 | tf_op jit(solution)/shard_map/ppermute | solution.py:439
  23.1 1.9 %shard_map.130 = (f32[2,4,64,256]{3,2,1,0:T(8,128)S(1)}, f32[16,4,256]{2,1,0:T(4,128)S(1)}) custom-call(s32[2]{0:T(128)S(1)} %pad_add_fusion.ids, f32[4,1]{1,0:T(4,128)S(1)} %copy-done.7, f32[64,1]{1,0:T(8,128)S(1)} %copy-done.4, f32[1,1024]{1,0:T(1,128)S(1)} %copy-done.5, f32[64,2]{1,0:T(8,128)S(1)} %copy-done.3, ...), custom_call_target="tpu_custom_call" | custom-call | flops 10485760000 | bytes 1053464 | tf_op jit(solution)/shard_map/pallas_call | solution.py:73
  25.0 3.1 %collective-permute-start.6 = (f32[2,4,64,256]{3,2,1,0:T(8,128)S(1)}, f32[2,4,64,256]{3,2,1,0:T(8,128)S(1)}, u32[]{:S(2)}, u32[]{:S(2)}) collective-permute-start(f32[2,4,64,256]{3,2,1,0:T(8,128)S(1)} %get-tuple-element.53), channel_id=1, source_target_pairs={{0,16},{4,20},{8,24},{12,28},{16,0},{20,4},{24,8},{28,12},{1,17},{... | collective-permute-start | bytes 1572872 | tf_op jit(solution)/shard_map/ppermute | solution.py:439
  28.2 10.2 %collective-permute-done.4.refs_2_ = f32[4,64,256]{2,1,0:T(8,128)S(1)} collective-permute-done((f32[4,64,256]{2,1,0:T(8,128)S(1)}, f32[4,64,256]{2,1,0:T(8,128)S(1)}, u32[]{:S(2)}, u32[]{:S(2)}) %collective-permute-start.4) | collective-permute-done | bytes 262176 | tf_op jit(solution)/shard_map/ppermute | solution.py:439
  38.3 3.1 %collective-permute-done.5.refs_3_ = f32[4,64,256]{2,1,0:T(8,128)S(1)} collective-permute-done((f32[4,64,256]{2,1,0:T(8,128)S(1)}, f32[4,64,256]{2,1,0:T(8,128)S(1)}, u32[]{:S(2)}, u32[]{:S(2)}) %collective-permute-start.5) | collective-permute-done | bytes 262176 | tf_op jit(solution)/shard_map/ppermute | solution.py:439
  41.4 1.7 %collective-permute-start.8 = (f32[16,4,256]{2,1,0:T(4,128)S(1)}, f32[16,4,256]{2,1,0:T(4,128)S(1)}, u32[]{:S(2)}, u32[]{:S(2)}) collective-permute-start(f32[16,4,256]{2,1,0:T(4,128)S(1)} %get-tuple-element.54.refs_0_), channel_id=1, source_target_pairs={{0,2},{1,3},{2,0},{3,1},{4,6},{5,7},{6,4},{7,5},{8,10},{9,11},{10,... | collective-permute-start | bytes 196616 | tf_op jit(solution)/shard_map/ppermute | solution.py:439
  43.3 2.3 %collective-permute-done.9.refs_3_ = f32[16,4,256]{2,1,0:T(4,128)S(1)} collective-permute-done((f32[16,4,256]{2,1,0:T(4,128)S(1)}, f32[16,4,256]{2,1,0:T(4,128)S(1)}, u32[]{:S(2)}, u32[]{:S(2)}) %collective-permute-start.9) | collective-permute-done | bytes 65568 | tf_op jit(solution)/shard_map/ppermute | solution.py:439
  45.6 1.6 %collective-permute-done.8.refs_2_ = f32[16,4,256]{2,1,0:T(4,128)S(1)} collective-permute-done((f32[16,4,256]{2,1,0:T(4,128)S(1)}, f32[16,4,256]{2,1,0:T(4,128)S(1)}, u32[]{:S(2)}, u32[]{:S(2)}) %collective-permute-start.8) | collective-permute-done | bytes 65568 | tf_op jit(solution)/shard_map/ppermute | solution.py:439
  48.8 1.9 %shard_map.131 = (f32[2,4,64,256]{3,2,1,0:T(8,128)S(1)}, f32[16,4,256]{2,1,0:T(4,128)S(1)}) custom-call(s32[2]{0:T(128)S(1)} %pad_add_fusion.ids, f32[4,1]{1,0:T(4,128)S(1)} %copy-done.6, f32[64,1]{1,0:T(8,128)S(1)} %copy-done.4, f32[1,1024]{1,0:T(1,128)S(1)} %copy-done.5, f32[64,2]{1,0:T(8,128)S(1)} %copy-done.3, ...), custom_call_target="tpu_custom_call" | custom-call | flops 3145728000 | bytes 1053464 | tf_op jit(solution)/shard_map/pallas_call | solution.py:73
  50.7 3.8 %collective-permute-done.10.refs_6_ = f32[16,4,256]{2,1,0:T(4,128)S(1)} collective-permute-done((f32[16,4,256]{2,1,0:T(4,128)S(1)}, f32[16,4,256]{2,1,0:T(4,128)S(1)}, u32[]{:S(2)}, u32[]{:S(2)}) %collective-permute-start.10) | collective-permute-done | bytes 65568 | tf_op jit(solution)/shard_map/ppermute | solution.py:439
  54.6 2.0 %shard_map.135 = (f32[4,64,256]{2,1,0:T(8,128)S(1)}, f32[4,64,256]{2,1,0:T(8,128)S(1)}, f32[4,64,256]{2,1,0:T(8,128)S(1)}, f32[4,64,256]{2,1,0:T(8,128)S(1)}) custom-call(s32[2]{0:T(128)S(1)} %pad_add_fusion.ids, f32[4,1]{1,0:T(4,128)S(1)} %copy-done.7, f32[64,1]{1,0:T(8,128)S(1)} %copy-done.4, f32[1,1024]{1,0:T(1,128)S(1)} %copy-done.5, ...), custom_call_target="tpu_custom_call" | custom-call | flops 26214400 | bytes 1708824 | tf_op jit(solution)/shard_map/pallas_call | solution.py:73
  56.6 1.6 %collective-permute-start.19 = (f32[4,64,256]{2,1,0:T(8,128)S(1)}, f32[4,64,256]{2,1,0:T(8,128)S(1)}, u32[]{:S(2)}, u32[]{:S(2)}) collective-permute-start(f32[4,64,256]{2,1,0:T(8,128)S(1)} %get-tuple-element.62), channel_id=1, source_target_pairs={{0,4},{4,0},{8,12},{12,8},{16,20},{20,16},{24,28},{28,24},{1,5},{5... | collective-permute-start | bytes 786440 | tf_op jit(solution)/shard_map/ppermute | solution.py:439
  59.2 2.9 %collective-permute-start.20 = (f32[4,64,256]{2,1,0:T(8,128)S(1)}, f32[4,64,256]{2,1,0:T(8,128)S(1)}, u32[]{:S(2)}, u32[]{:S(2)}) collective-permute-start(f32[4,64,256]{2,1,0:T(8,128)S(1)} %get-tuple-element.63), channel_id=1, source_target_pairs={{0,8},{4,12},{8,0},{12,4},{16,24},{20,28},{24,16},{28,20},{1,9},{5... | collective-permute-start | bytes 786440 | tf_op jit(solution)/shard_map/ppermute | solution.py:439
  62.4 2.4 %collective-permute-start.21 = (f32[4,64,256]{2,1,0:T(8,128)S(1)}, f32[4,64,256]{2,1,0:T(8,128)S(1)}, u32[]{:S(2)}, u32[]{:S(2)}) collective-permute-start(f32[4,64,256]{2,1,0:T(8,128)S(1)} %get-tuple-element.64), channel_id=1, source_target_pairs={{0,12},{4,8},{8,4},{12,0},{16,28},{20,24},{24,20},{28,16},{1,13},{... | collective-permute-start | bytes 786440 | tf_op jit(solution)/shard_map/ppermute | solution.py:439
  64.8 1.3 %collective-permute-done.12.refs_1_ = f32[16,4,256]{2,1,0:T(4,128)S(1)} collective-permute-done((f32[16,4,256]{2,1,0:T(4,128)S(1)}, f32[16,4,256]{2,1,0:T(4,128)S(1)}, u32[]{:S(2)}, u32[]{:S(2)}) %collective-permute-start.12) | collective-permute-done | bytes 65568 | tf_op jit(solution)/shard_map/ppermute | solution.py:439
  68.1 14.2 %collective-permute-done.15.refs_6_ = f32[16,4,256]{2,1,0:T(4,128)S(1)} collective-permute-done((f32[16,4,256]{2,1,0:T(4,128)S(1)}, f32[16,4,256]{2,1,0:T(4,128)S(1)}, u32[]{:S(2)}, u32[]{:S(2)}) %collective-permute-start.15) | collective-permute-done | bytes 65568 | tf_op jit(solution)/shard_map/ppermute | solution.py:439
  82.3 2.2 %shard_map.134 = (f32[4,64,256]{2,1,0:T(8,128)S(1)}, f32[4,64,256]{2,1,0:T(8,128)S(1)}, f32[4,64,256]{2,1,0:T(8,128)S(1)}, f32[4,64,256]{2,1,0:T(8,128)S(1)}) custom-call(s32[2]{0:T(128)S(1)} %pad_add_fusion.ids, f32[4,1]{1,0:T(4,128)S(1)} %copy-done.6, f32[64,1]{1,0:T(8,128)S(1)} %copy-done.4, f32[1,1024]{1,0:T(1,128)S(1)} %copy-done.5, ...), custom_call_target="tpu_custom_call" | custom-call | flops 26214400 | bytes 1708824 | tf_op jit(solution)/shard_map/pallas_call | solution.py:73
  84.4 2.2 %collective-permute-start.16 = (f32[4,64,256]{2,1,0:T(8,128)S(1)}, f32[4,64,256]{2,1,0:T(8,128)S(1)}, u32[]{:S(2)}, u32[]{:S(2)}) collective-permute-start(f32[4,64,256]{2,1,0:T(8,128)S(1)} %get-tuple-element.58), channel_id=1, source_target_pairs={{0,4},{4,0},{8,12},{12,8},{16,20},{20,16},{24,28},{28,24},{1,5},{5... | collective-permute-start | bytes 786440 | tf_op jit(solution)/shard_map/ppermute | solution.py:439
  86.6 1.5 %collective-permute-start.18 = (f32[4,64,256]{2,1,0:T(8,128)S(1)}, f32[4,64,256]{2,1,0:T(8,128)S(1)}, u32[]{:S(2)}, u32[]{:S(2)}) collective-permute-start(f32[4,64,256]{2,1,0:T(8,128)S(1)} %get-tuple-element.60), channel_id=1, source_target_pairs={{0,12},{4,8},{8,4},{12,0},{16,28},{20,24},{24,20},{28,16},{1,13},{... | collective-permute-start | bytes 786440 | tf_op jit(solution)/shard_map/ppermute | solution.py:439
  88.2 2.8 %shard_map.136.refs_4_ = f32[4,64,1024]{2,1,0:T(8,128)S(1)} custom-call(s32[2]{0:T(128)S(1)} %pad_add_fusion.ids, bf16[2,2,256,256]{3,2,1,0:T(8,128)(2,1)S(1)} %copy-done, bf16[1024,1024]{1,0:T(8,128)(2,1)S(1)} %get-tuple-element.35.sxh, bf16[1024,1024]{1,0:T(8,128)(2,1)S(1)} %get-tuple-element.36.sxl, f32[4,64,256]{2,1,0:T(8,128)S(1)} %get-tuple-element.61.refs_0_, ...), custom_call_target="tpu_custom_call" | custom-call | flops 2013265920 | bytes 5767176 | tf_op jit(solution)/shard_map/pallas_call | solution.py:73
  91.0 1.8 %collective-permute-done.16.refs_1_ = f32[4,64,256]{2,1,0:T(8,128)S(1)} collective-permute-done((f32[4,64,256]{2,1,0:T(8,128)S(1)}, f32[4,64,256]{2,1,0:T(8,128)S(1)}, u32[]{:S(2)}, u32[]{:S(2)}) %collective-permute-start.16) | collective-permute-done | bytes 262176 | tf_op jit(solution)/shard_map/ppermute | solution.py:439
  92.8 3.0 %collective-permute-done.17.refs_2_ = f32[4,64,256]{2,1,0:T(8,128)S(1)} collective-permute-done((f32[4,64,256]{2,1,0:T(8,128)S(1)}, f32[4,64,256]{2,1,0:T(8,128)S(1)}, u32[]{:S(2)}, u32[]{:S(2)}) %collective-permute-start.17) | collective-permute-done | bytes 262176 | tf_op jit(solution)/shard_map/ppermute | solution.py:439
  95.8 3.8 %collective-permute-done.18.refs_3_ = f32[4,64,256]{2,1,0:T(8,128)S(1)} collective-permute-done((f32[4,64,256]{2,1,0:T(8,128)S(1)}, f32[4,64,256]{2,1,0:T(8,128)S(1)}, u32[]{:S(2)}, u32[]{:S(2)}) %collective-permute-start.18) | collective-permute-done | bytes 262176 | tf_op jit(solution)/shard_map/ppermute | solution.py:439
  99.6 4.0 %shard_map.137 = f32[8,64,1024]{2,1,0:T(8,128)} custom-call(s32[2]{0:T(128)S(1)} %pad_add_fusion.ids, bf16[2,2,256,256]{3,2,1,0:T(8,128)(2,1)S(1)} %copy-done, bf16[1024,1024]{1,0:T(8,128)(2,1)S(1)} %get-tuple-element.35.sxh, bf16[1024,1024]{1,0:T(8,128)(2,1)S(1)} %get-tuple-element.36.sxl, f32[4,64,256]{2,1,0:T(8,128)S(1)} %get-tuple-element.57.refs_0_, ...), custom_call_target="tpu_custom_call" | custom-call | flops 2013265920 | bytes 6815752 | tf_op jit(solution)/shard_map/pallas_call | solution.py:73
  (46 shorter events, 6.4 us)
Async XLA Ops:
  1.1 1.7 %copy-start.8 = (f32[1,8,64,1024]{3,2,1,0:T(8,128)S(1)}, f32[1,8,64,1024]{3,2,1,0:T(8,128)}, u32[]{:S(2)}) copy-start(f32[1,8,64,1024]{3,2,1,0:T(8,128)} %param.13) | copy-start | bytes 6291460
  1.1 1.7 %copy-start.9 = (bf16[2,2,256,256]{3,2,1,0:T(8,128)(2,1)S(1)}, bf16[2,2,256,256]{3,2,1,0:T(8,128)(2,1)}, u32[]{:S(2)}) copy-start(bf16[2,2,256,256]{3,2,1,0:T(8,128)(2,1)} %constant.51.both) | copy-start | bytes 1572868
  5.7 11.1 %collective-permute-start = (f32[4,64,256]{2,1,0:T(8,128)S(1)}, f32[4,64,256]{2,1,0:T(8,128)S(1)}, u32[]{:S(2)}, u32[]{:S(2)}) collective-permute-start(f32[4,64,256]{2,1,0:T(8,128)S(1)} %get-tuple-element.40), channel_id=1, source_target_pairs={{0,4},{4,0},{8,12},{12,8},{16,20},{20,16},{24,28},{28,24},{1,5},{5... | collective-permute-start | bytes 786440 | tf_op jit(solution)/shard_map/ppermute | solution.py:439
  8.7 9.5 %collective-permute-start.1 = (f32[4,64,256]{2,1,0:T(8,128)S(1)}, f32[4,64,256]{2,1,0:T(8,128)S(1)}, u32[]{:S(2)}, u32[]{:S(2)}) collective-permute-start(f32[4,64,256]{2,1,0:T(8,128)S(1)} %get-tuple-element.41), channel_id=1, source_target_pairs={{0,8},{4,12},{8,0},{12,4},{16,24},{20,28},{24,16},{28,20},{1,9},{5... | collective-permute-start | bytes 786440 | tf_op jit(solution)/shard_map/ppermute | solution.py:439
  10.3 12.8 %copy-start.3 = (f32[64,2]{1,0:T(8,128)S(1)}, f32[64,2]{1,0:T(8,128)}, u32[]{:S(2)}) copy-start(f32[64,2]{1,0:T(8,128)} %constant.35.clone.edges) | copy-start | bytes 1540
  10.3 12.8 %copy-start.4 = (f32[64,1]{1,0:T(8,128)S(1)}, f32[64,1]{1,0:T(8,128)}, u32[]{:S(2)}) copy-start(f32[64,1]{1,0:T(8,128)} %constant.33.clone.smu_y) | copy-start | bytes 772
  10.3 12.8 %copy-start.5 = (f32[1,1024]{1,0:T(1,128)S(1)}, f32[1,1024]{1,0:T(1,128)}, u32[]{:S(2)}) copy-start(f32[1,1024]{1,0:T(1,128)} %constant.34.clone.smu_x) | copy-start | bytes 12292
  10.3 12.8 %copy-start.7 = (f32[4,1]{1,0:T(4,128)S(1)}, f32[4,1]{1,0:T(4,128)}, u32[]{:S(2)}) copy-start(f32[4,1]{1,0:T(4,128)} %constant.41.clone.smu_z) | copy-start | bytes 52
  10.3 12.8 %collective-permute-start.2 = (f32[4,64,256]{2,1,0:T(8,128)S(1)}, f32[4,64,256]{2,1,0:T(8,128)S(1)}, u32[]{:S(2)}, u32[]{:S(2)}) collective-permute-start(f32[4,64,256]{2,1,0:T(8,128)S(1)} %get-tuple-element.42), channel_id=1, source_target_pairs={{0,12},{4,8},{8,4},{12,0},{16,28},{20,24},{24,20},{28,16},{1,13},{... | collective-permute-start | bytes 786440 | tf_op jit(solution)/shard_map/ppermute | solution.py:439
  13.2 14.9 %collective-permute-start.3 = (f32[4,64,256]{2,1,0:T(8,128)S(1)}, f32[4,64,256]{2,1,0:T(8,128)S(1)}, u32[]{:S(2)}, u32[]{:S(2)}) collective-permute-start(f32[4,64,256]{2,1,0:T(8,128)S(1)} %get-tuple-element.45), channel_id=1, source_target_pairs={{0,4},{4,0},{8,12},{12,8},{16,20},{20,16},{24,28},{28,24},{1,5},{5... | collective-permute-start | bytes 786440 | tf_op jit(solution)/shard_map/ppermute | solution.py:439
  15.2 23.1 %collective-permute-start.4 = (f32[4,64,256]{2,1,0:T(8,128)S(1)}, f32[4,64,256]{2,1,0:T(8,128)S(1)}, u32[]{:S(2)}, u32[]{:S(2)}) collective-permute-start(f32[4,64,256]{2,1,0:T(8,128)S(1)} %get-tuple-element.46), channel_id=1, source_target_pairs={{0,8},{4,12},{8,0},{12,4},{16,24},{20,28},{24,16},{28,20},{1,9},{5... | collective-permute-start | bytes 786440 | tf_op jit(solution)/shard_map/ppermute | solution.py:439
  16.8 30.4 %copy-start.2 = (f32[5,4,4,1024]{3,2,1,0:T(4,128)S(1)}, f32[5,4,4,1024]{3,2,1,0:T(4,128)}, u32[]{:S(2)}) copy-start(f32[5,4,4,1024]{3,2,1,0:T(4,128)} %constant.43.clone.responses) | copy-start | bytes 983044
  16.8 32.1 %copy-start.6 = (f32[4,1]{1,0:T(4,128)S(1)}, f32[4,1]{1,0:T(4,128)}, u32[]{:S(2)}) copy-start(f32[4,1]{1,0:T(4,128)} %constant.42.clone.smu_z) | copy-start | bytes 52
  16.8 24.6 %collective-permute-start.5 = (f32[4,64,256]{2,1,0:T(8,128)S(1)}, f32[4,64,256]{2,1,0:T(8,128)S(1)}, u32[]{:S(2)}, u32[]{:S(2)}) collective-permute-start(f32[4,64,256]{2,1,0:T(8,128)S(1)} %get-tuple-element.47), channel_id=1, source_target_pairs={{0,12},{4,8},{8,4},{12,0},{16,28},{20,24},{24,20},{28,16},{1,13},{... | collective-permute-start | bytes 786440 | tf_op jit(solution)/shard_map/ppermute | solution.py:439
  25.0 29.5 %collective-permute-start.6 = (f32[2,4,64,256]{3,2,1,0:T(8,128)S(1)}, f32[2,4,64,256]{3,2,1,0:T(8,128)S(1)}, u32[]{:S(2)}, u32[]{:S(2)}) collective-permute-start(f32[2,4,64,256]{3,2,1,0:T(8,128)S(1)} %get-tuple-element.53), channel_id=1, source_target_pairs={{0,16},{4,20},{8,24},{12,28},{16,0},{20,4},{24,8},{28,12},{1,17},{... | collective-permute-start | bytes 1572872 | tf_op jit(solution)/shard_map/ppermute | solution.py:439
  41.4 4.2 %collective-permute-start.9 = (f32[16,4,256]{2,1,0:T(4,128)S(1)}, f32[16,4,256]{2,1,0:T(4,128)S(1)}, u32[]{:S(2)}, u32[]{:S(2)}) collective-permute-start(f32[16,4,256]{2,1,0:T(4,128)S(1)} %get-tuple-element.54.refs_0_), channel_id=1, source_target_pairs={{0,3},{1,2},{2,1},{3,0},{4,7},{5,6},{6,5},{7,4},{8,11},{9,10},{10,... | collective-permute-start | bytes 196616 | tf_op jit(solution)/shard_map/ppermute | solution.py:439
  41.4 5.8 %collective-permute-start.8 = (f32[16,4,256]{2,1,0:T(4,128)S(1)}, f32[16,4,256]{2,1,0:T(4,128)S(1)}, u32[]{:S(2)}, u32[]{:S(2)}) collective-permute-start(f32[16,4,256]{2,1,0:T(4,128)S(1)} %get-tuple-element.54.refs_0_), channel_id=1, source_target_pairs={{0,2},{1,3},{2,0},{3,1},{4,6},{5,7},{6,4},{7,5},{8,10},{9,11},{10,... | collective-permute-start | bytes 196616 | tf_op jit(solution)/shard_map/ppermute | solution.py:439
  43.1 4.1 %collective-permute-start.7 = (f32[16,4,256]{2,1,0:T(4,128)S(1)}, f32[16,4,256]{2,1,0:T(4,128)S(1)}, u32[]{:S(2)}, u32[]{:S(2)}) collective-permute-start(f32[16,4,256]{2,1,0:T(4,128)S(1)} %get-tuple-element.54.refs_0_), channel_id=1, source_target_pairs={{0,1},{1,0},{2,3},{3,2},{4,5},{5,4},{6,7},{7,6},{8,9},{9,8},{10,11... | collective-permute-start | bytes 196616 | tf_op jit(solution)/shard_map/ppermute | solution.py:439
  48.1 18.0 %copy-start.1 = (f32[5,4,4,1024]{3,2,1,0:T(4,128)S(1)}, f32[5,4,4,1024]{3,2,1,0:T(4,128)}, u32[]{:S(2)}) copy-start(f32[5,4,4,1024]{3,2,1,0:T(4,128)} %constant.44.clone.responses) | copy-start | bytes 983044
  48.1 6.5 %collective-permute-start.10 = (f32[16,4,256]{2,1,0:T(4,128)S(1)}, f32[16,4,256]{2,1,0:T(4,128)S(1)}, u32[]{:S(2)}, u32[]{:S(2)}) collective-permute-start(f32[16,4,256]{2,1,0:T(4,128)S(1)} %shard_map.132.refs_5_), channel_id=1, source_target_pairs={{0,16},{4,20},{8,24},{12,28},{16,0},{20,4},{24,8},{28,12},{1,17},{... | collective-permute-start | bytes 196616 | tf_op jit(solution)/shard_map/ppermute | solution.py:439
  54.6 33.6 %copy-start = (bf16[2,2,256,256]{3,2,1,0:T(8,128)(2,1)S(1)}, bf16[2,2,256,256]{3,2,1,0:T(8,128)(2,1)}, u32[]{:S(2)}) copy-start(bf16[2,2,256,256]{3,2,1,0:T(8,128)(2,1)} %constant.48.both) | copy-start | bytes 1572868
  54.6 27.7 %collective-permute-start.11 = (f32[2,4,64,256]{3,2,1,0:T(8,128)S(1)}, f32[2,4,64,256]{3,2,1,0:T(8,128)S(1)}, u32[]{:S(2)}, u32[]{:S(2)}) collective-permute-start(f32[2,4,64,256]{3,2,1,0:T(8,128)S(1)} %get-tuple-element.55), channel_id=1, source_target_pairs={{0,16},{4,20},{8,24},{12,28},{16,0},{20,4},{24,8},{28,12},{1,17},{... | collective-permute-start | bytes 1572872 | tf_op jit(solution)/shard_map/ppermute | solution.py:439
  56.6 30.0 %collective-permute-start.19 = (f32[4,64,256]{2,1,0:T(8,128)S(1)}, f32[4,64,256]{2,1,0:T(8,128)S(1)}, u32[]{:S(2)}, u32[]{:S(2)}) collective-permute-start(f32[4,64,256]{2,1,0:T(8,128)S(1)} %get-tuple-element.62), channel_id=1, source_target_pairs={{0,4},{4,0},{8,12},{12,8},{16,20},{20,16},{24,28},{28,24},{1,5},{5... | collective-permute-start | bytes 786440 | tf_op jit(solution)/shard_map/ppermute | solution.py:439
  58.2 4.3 %collective-permute-start.14 = (f32[16,4,256]{2,1,0:T(4,128)S(1)}, f32[16,4,256]{2,1,0:T(4,128)S(1)}, u32[]{:S(2)}, u32[]{:S(2)}) collective-permute-start(f32[16,4,256]{2,1,0:T(4,128)S(1)} %get-tuple-element.56.refs_0_), channel_id=1, source_target_pairs={{0,3},{1,2},{2,1},{3,0},{4,7},{5,6},{6,5},{7,4},{8,11},{9,10},{10,... | collective-permute-start | bytes 196616 | tf_op jit(solution)/shard_map/ppermute | solution.py:439
  58.2 6.7 %collective-permute-start.13 = (f32[16,4,256]{2,1,0:T(4,128)S(1)}, f32[16,4,256]{2,1,0:T(4,128)S(1)}, u32[]{:S(2)}, u32[]{:S(2)}) collective-permute-start(f32[16,4,256]{2,1,0:T(4,128)S(1)} %get-tuple-element.56.refs_0_), channel_id=1, source_target_pairs={{0,2},{1,3},{2,0},{3,1},{4,6},{5,7},{6,4},{7,5},{8,10},{9,11},{10,... | collective-permute-start | bytes 196616 | tf_op jit(solution)/shard_map/ppermute | solution.py:439
  59.2 29.0 %collective-permute-start.20 = (f32[4,64,256]{2,1,0:T(8,128)S(1)}, f32[4,64,256]{2,1,0:T(8,128)S(1)}, u32[]{:S(2)}, u32[]{:S(2)}) collective-permute-start(f32[4,64,256]{2,1,0:T(8,128)S(1)} %get-tuple-element.63), channel_id=1, source_target_pairs={{0,8},{4,12},{8,0},{12,4},{16,24},{20,28},{24,16},{28,20},{1,9},{5... | collective-permute-start | bytes 786440 | tf_op jit(solution)/shard_map/ppermute | solution.py:439
  62.4 25.7 %collective-permute-start.21 = (f32[4,64,256]{2,1,0:T(8,128)S(1)}, f32[4,64,256]{2,1,0:T(8,128)S(1)}, u32[]{:S(2)}, u32[]{:S(2)}) collective-permute-start(f32[4,64,256]{2,1,0:T(8,128)S(1)} %get-tuple-element.64), channel_id=1, source_target_pairs={{0,12},{4,8},{8,4},{12,0},{16,28},{20,24},{24,20},{28,16},{1,13},{... | collective-permute-start | bytes 786440 | tf_op jit(solution)/shard_map/ppermute | solution.py:439
  64.8 1.3 %collective-permute-start.12 = (f32[16,4,256]{2,1,0:T(4,128)S(1)}, f32[16,4,256]{2,1,0:T(4,128)S(1)}, u32[]{:S(2)}, u32[]{:S(2)}) collective-permute-start(f32[16,4,256]{2,1,0:T(4,128)S(1)} %get-tuple-element.56.refs_0_), channel_id=1, source_target_pairs={{0,1},{1,0},{2,3},{3,2},{4,5},{5,4},{6,7},{7,6},{8,9},{9,8},{10,11... | collective-permute-start | bytes 196616 | tf_op jit(solution)/shard_map/ppermute | solution.py:439
  67.0 15.3 %collective-permute-start.15 = (f32[16,4,256]{2,1,0:T(4,128)S(1)}, f32[16,4,256]{2,1,0:T(4,128)S(1)}, u32[]{:S(2)}, u32[]{:S(2)}) collective-permute-start(f32[16,4,256]{2,1,0:T(4,128)S(1)} %shard_map.133.refs_5_), channel_id=1, source_target_pairs={{0,16},{4,20},{8,24},{12,28},{16,0},{20,4},{24,8},{28,12},{1,17},{... | collective-permute-start | bytes 196616 | tf_op jit(solution)/shard_map/ppermute | solution.py:439
  84.4 8.4 %collective-permute-start.16 = (f32[4,64,256]{2,1,0:T(8,128)S(1)}, f32[4,64,256]{2,1,0:T(8,128)S(1)}, u32[]{:S(2)}, u32[]{:S(2)}) collective-permute-start(f32[4,64,256]{2,1,0:T(8,128)S(1)} %get-tuple-element.58), channel_id=1, source_target_pairs={{0,4},{4,0},{8,12},{12,8},{16,20},{20,16},{24,28},{28,24},{1,5},{5... | collective-permute-start | bytes 786440 | tf_op jit(solution)/shard_map/ppermute | solution.py:439
  86.6 9.2 %collective-permute-start.17 = (f32[4,64,256]{2,1,0:T(8,128)S(1)}, f32[4,64,256]{2,1,0:T(8,128)S(1)}, u32[]{:S(2)}, u32[]{:S(2)}) collective-permute-start(f32[4,64,256]{2,1,0:T(8,128)S(1)} %get-tuple-element.59), channel_id=1, source_target_pairs={{0,8},{4,12},{8,0},{12,4},{16,24},{20,28},{24,16},{28,20},{1,9},{5... | collective-permute-start | bytes 786440 | tf_op jit(solution)/shard_map/ppermute | solution.py:439
  86.6 13.0 %collective-permute-start.18 = (f32[4,64,256]{2,1,0:T(8,128)S(1)}, f32[4,64,256]{2,1,0:T(8,128)S(1)}, u32[]{:S(2)}, u32[]{:S(2)}) collective-permute-start(f32[4,64,256]{2,1,0:T(8,128)S(1)} %get-tuple-element.60), channel_id=1, source_target_pairs={{0,12},{4,8},{8,4},{12,0},{16,28},{20,24},{24,20},{28,16},{1,13},{... | collective-permute-start | bytes 786440 | tf_op jit(solution)/shard_map/ppermute | solution.py:439
  (1 other events, 1.0 us)

commit v10 on v9

--- a/solution.py
+++ b/solution.py
@@ -309,13 +309,12 @@
 
 def join_rows(plan, ids, responses, *refs):
     groups, steps = plan.groups, plan.steps
-    views = refs[:groups]
-    out, seen, above, below = refs[groups:]
+    views, out, seen, above, below = refs
     place = lax.rem(ids[0], plan.half)
     me = ids[1]
     columns = plan.columns(place)
     for k in range(groups):
-        seen[me ^ k] = views[k][...]
+        seen[me ^ k] = views[k]
     radius = ALPHA_RATIO ** (1.0 / steps)
     grow = [radius**n for n in range(steps)]
     nothing = jnp.zeros(out.shape[1:], jnp.float32)
@@ -481,13 +480,10 @@
         ends, view = call(
             functools.partial(half_end, plan),
             [f32((2,) + modes.shape), seen],
-            (12000 if at else 40000) * modes.size * half,
+            (3000 if at else 40000) * modes.size * half,
             (*small, *pieces),
             [pltpu.VMEM((2 * steps, len(chunk), 8, plan.block), jnp.float32)],
         )
-        if at + 1 < len(work):
-            later = work[at + 1][-1]
-            view, *later[:] = lax.optimization_barrier((view, *later))
         ended.append([ends, seen, view])
     sums = {}
     far = None
@@ -495,13 +491,16 @@
         if far is not None:
             ends, far, beside_far = lax.optimization_barrier((ends, far, beside_far))
         far = swap(ends, "tm", steps, half)
-        views = [swap(view, "gy", groups, k) for k in range(groups)]
+        views = view[None]
+        while views.shape[0] < groups:
+            beyond = swap(views, "gy", groups, views.shape[0])
+            views = jnp.concatenate([views, beyond])
         sides = pltpu.VMEM((groups, steps + 2) + seen.shape[1:], jnp.float32)
         beside = call(
             functools.partial(join_rows, plan),
             seen,
             100 * seen.size,
-            (ids, jnp.asarray(responses[:, :, list(chunk)]), *views),
+            (ids, jnp.asarray(responses[:, :, list(chunk)]), views),
             [pltpu.VMEM((groups,) + seen.shape, jnp.float32), sides, sides],
         )
         beside_far = swap(beside, "tm", steps, half)

time: 104 us -> 105 us (level)
  waiting for transfers between devices: 50.4 us -> 54.7 us
  starting transfers between devices: 28 us -> 24.6 us
    ppermute x22 -> x20, waiting for transfers between devices: 50.4 us -> 54.7 us  [swap(): return lax.ppermute(values, axis, [(i, i ^ distance) for i in range(count)])]
    ppermute x22 -> x20, starting transfers between devices: 28 us -> 24.6 us  [swap(): return lax.ppermute(values, axis, [(i, i ^ distance) for i in range(count)])]
  transfers between devices with their start and end apart: 22 -> 20, of which waited for: 12 -> 12; matrix products, arithmetic and copies ran while one was open for 0% -> 0% of each run, Pallas kernels for 15% -> 13%
where the time goes in v10:
time: 105 us
  waiting for transfers between devices  54.7 us (52%)
  starting transfers between devices  24.6 us (23%)
  Pallas kernels  23.9 us (23%)
  local copies, waits for them, and re-layouts  1.09 us (1%)
    ppermute x20, waiting for transfers between devices, swap(): return lax.ppermute(values, axis, [(i, i ^ distance) for i in range(count)])  54.7 us
    ppermute x20, starting transfers between devices, swap(): return lax.ppermute(values, axis, [(i, i ^ distance) for i in range(count)])  24.6 us
    pallas_call x11, Pallas kernels, call(): pl.pallas_call(kernel, out_shape=out_shape, in_specs=[smem] + [vmem] * (l...  23.9 us
  transfers between devices with their start and end apart: 20, of which 12 were waited for; matrix products, arithmetic and copies ran while one was open for 0% of the time, Pallas kernels for 13%

profile of v10, /device:TPU:0, one launch (start us, length us, event | category | flops | bytes accessed | tf_op | source)
XLA Modules:
  0.0 105.0 jit_solution(8944562612667144302)
XLA Ops:
  1.1 1.7 %shard_map.127 = (bf16[1024,1024]{1,0:T(8,128)(2,1)S(1)}, bf16[1024,1024]{1,0:T(8,128)(2,1)S(1)}) custom-call(s32[2]{0:T(128)S(1)} %pad_add_fusion.ids, f32[128,1024]{1,0:T(8,128)S(1)} %copy-done.10), custom_call_target="tpu_custom_call" | custom-call | flops 4194304000 | bytes 524296 | tf_op jit(solution)/shard_map/pallas_call | solution.py:73
  2.9 2.8 %shard_map.128 = (f32[4,64,256]{2,1,0:T(8,128)S(1)}, f32[4,64,256]{2,1,0:T(8,128)S(1)}, f32[4,64,256]{2,1,0:T(8,128)S(1)}, f32[4,64,256]{2,1,0:T(8,128)S(1)}) custom-call(s32[2]{0:T(128)S(1)} %pad_add_fusion.ids, bf16[2,2,256,256]{3,2,1,0:T(8,128)(2,1)S(1)} %copy-done.9, f32[8,64,1024]{2,1,0:T(8,128)S(1)} %bitcast.12, ...), custom_call_target="tpu_custom_call" | custom-call | flops 2013265920 | bytes 6815752 | tf_op jit(solution)/shard_map/pallas_call | solution.py:73
  5.7 3.0 %collective-permute-start.3 = (f32[4,64,256]{2,1,0:T(8,128)S(1)}, f32[4,64,256]{2,1,0:T(8,128)S(1)}, u32[]{:S(2)}, u32[]{:S(2)}) collective-permute-start(f32[4,64,256]{2,1,0:T(8,128)S(1)} %get-tuple-element.40), channel_id=1, source_target_pairs={{0,4},{4,0},{8,12},{12,8},{16,20},{20,16},{24,28},{28,24},{1,5},{5... | collective-permute-start | bytes 786440 | tf_op jit(solution)/shard_map/ppermute | solution.py:438
  8.7 1.6 %collective-permute-start.4 = (f32[4,64,256]{2,1,0:T(8,128)S(1)}, f32[4,64,256]{2,1,0:T(8,128)S(1)}, u32[]{:S(2)}, u32[]{:S(2)}) collective-permute-start(f32[4,64,256]{2,1,0:T(8,128)S(1)} %get-tuple-element.41), channel_id=1, source_target_pairs={{0,8},{4,12},{8,0},{12,4},{16,24},{20,28},{24,16},{28,20},{1,9},{5... | collective-permute-start | bytes 786440 | tf_op jit(solution)/shard_map/ppermute | solution.py:438
  10.4 2.8 %shard_map.129 = (f32[4,64,256]{2,1,0:T(8,128)S(1)}, f32[4,64,256]{2,1,0:T(8,128)S(1)}, f32[4,64,256]{2,1,0:T(8,128)S(1)}, f32[4,64,256]{2,1,0:T(8,128)S(1)}) custom-call(s32[2]{0:T(128)S(1)} %pad_add_fusion.ids, bf16[2,2,256,256]{3,2,1,0:T(8,128)(2,1)S(1)} %copy-done.9, f32[8,64,1024]{2,1,0:T(8,128)S(1)} %bitcast.13, ...), custom_call_target="tpu_custom_call" | custom-call | flops 2013265920 | bytes 6815752 | tf_op jit(solution)/shard_map/pallas_call | solution.py:73
  13.2 1.8 %collective-permute-done.3.refs_1_ = f32[4,64,256]{2,1,0:T(8,128)S(1)} collective-permute-done((f32[4,64,256]{2,1,0:T(8,128)S(1)}, f32[4,64,256]{2,1,0:T(8,128)S(1)}, u32[]{:S(2)}, u32[]{:S(2)}) %collective-permute-start.3) | collective-permute-done | bytes 262176 | tf_op jit(solution)/shard_map/ppermute | solution.py:438
  15.0 2.9 %collective-permute-done.4.refs_2_ = f32[4,64,256]{2,1,0:T(8,128)S(1)} collective-permute-done((f32[4,64,256]{2,1,0:T(8,128)S(1)}, f32[4,64,256]{2,1,0:T(8,128)S(1)}, u32[]{:S(2)}, u32[]{:S(2)}) %collective-permute-start.4) | collective-permute-done | bytes 262176 | tf_op jit(solution)/shard_map/ppermute | solution.py:438
  18.0 3.9 %collective-permute-done.5.refs_3_ = f32[4,64,256]{2,1,0:T(8,128)S(1)} collective-permute-done((f32[4,64,256]{2,1,0:T(8,128)S(1)}, f32[4,64,256]{2,1,0:T(8,128)S(1)}, u32[]{:S(2)}, u32[]{:S(2)}) %collective-permute-start.5) | collective-permute-done | bytes 262176 | tf_op jit(solution)/shard_map/ppermute | solution.py:438
  21.9 1.9 %shard_map.131 = (f32[2,4,64,256]{3,2,1,0:T(8,128)S(1)}, f32[16,4,256]{2,1,0:T(4,128)S(1)}) custom-call(s32[2]{0:T(128)S(1)} %pad_add_fusion.ids, f32[4,1]{1,0:T(4,128)S(1)} %copy-done.7, f32[64,1]{1,0:T(8,128)S(1)} %copy-done.4, f32[1,1024]{1,0:T(1,128)S(1)} %copy-done.5, f32[64,2]{1,0:T(8,128)S(1)} %copy-done.3, ...), custom_call_target="tpu_custom_call" | custom-call | flops 10485760000 | bytes 1053464 | tf_op jit(solution)/shard_map/pallas_call | solution.py:73
  23.8 2.8 %collective-permute-start.6 = (f32[2,4,64,256]{3,2,1,0:T(8,128)S(1)}, f32[2,4,64,256]{3,2,1,0:T(8,128)S(1)}, u32[]{:S(2)}, u32[]{:S(2)}) collective-permute-start(f32[2,4,64,256]{3,2,1,0:T(8,128)S(1)} %get-tuple-element.43), channel_id=1, source_target_pairs={{0,16},{4,20},{8,24},{12,28},{16,0},{20,4},{24,8},{28,12},{1,17},{... | collective-permute-start | bytes 1572872 | tf_op jit(solution)/shard_map/ppermute | solution.py:438
  26.6 1.5 %collective-permute-start = (f32[4,64,256]{2,1,0:T(8,128)S(1)}, f32[4,64,256]{2,1,0:T(8,128)S(1)}, u32[]{:S(2)}, u32[]{:S(2)}) collective-permute-start(f32[4,64,256]{2,1,0:T(8,128)S(1)} %get-tuple-element.35), channel_id=1, source_target_pairs={{0,4},{4,0},{8,12},{12,8},{16,20},{20,16},{24,28},{28,24},{1,5},{5... | collective-permute-start | bytes 786440 | tf_op jit(solution)/shard_map/ppermute | solution.py:438
  28.2 1.6 %collective-permute-start.1 = (f32[4,64,256]{2,1,0:T(8,128)S(1)}, f32[4,64,256]{2,1,0:T(8,128)S(1)}, u32[]{:S(2)}, u32[]{:S(2)}) collective-permute-start(f32[4,64,256]{2,1,0:T(8,128)S(1)} %get-tuple-element.36), channel_id=1, source_target_pairs={{0,8},{4,12},{8,0},{12,4},{16,24},{20,28},{24,16},{28,20},{1,9},{5... | collective-permute-start | bytes 786440 | tf_op jit(solution)/shard_map/ppermute | solution.py:438
  30.2 1.6 %collective-permute-start.8 = (f32[2,16,4,256]{3,2,1,0:T(4,128)S(1)}, f32[2,16,4,256]{3,2,1,0:T(4,128)S(1)}, u32[]{:S(2)}, u32[]{:S(2)}) collective-permute-start(f32[2,16,4,256]{3,2,1,0:T(4,128)S(1)} %pad_maximum_fusion.2), channel_id=1, source_target_pairs={{0,2},{1,3},{2,0},{3,1},{4,6},{5,7},{6,4},{7,5},{8,10},{9,11},{10,... | collective-permute-start | bytes 393224 | tf_op jit(solution)/shard_map/ppermute | solution.py:438
  31.7 3.6 %collective-permute-done.8 = f32[2,16,4,256]{3,2,1,0:T(4,128)S(1)} collective-permute-done((f32[2,16,4,256]{3,2,1,0:T(4,128)S(1)}, f32[2,16,4,256]{3,2,1,0:T(4,128)S(1)}, u32[]{:S(2)}, u32[]{:S(2)}) %collective-permute-start.8) | collective-permute-done | bytes 131104 | tf_op jit(solution)/shard_map/ppermute | solution.py:438
  36.6 8.1 %collective-permute-done.1.refs_2_ = f32[4,64,256]{2,1,0:T(8,128)S(1)} collective-permute-done((f32[4,64,256]{2,1,0:T(8,128)S(1)}, f32[4,64,256]{2,1,0:T(8,128)S(1)}, u32[]{:S(2)}, u32[]{:S(2)}) %collective-permute-start.1) | collective-permute-done | bytes 262176 | tf_op jit(solution)/shard_map/ppermute | solution.py:438
  44.6 9.1 %collective-permute-done.2.refs_3_ = f32[4,64,256]{2,1,0:T(8,128)S(1)} collective-permute-done((f32[4,64,256]{2,1,0:T(8,128)S(1)}, f32[4,64,256]{2,1,0:T(8,128)S(1)}, u32[]{:S(2)}, u32[]{:S(2)}) %collective-permute-start.2) | collective-permute-done | bytes 262176 | tf_op jit(solution)/shard_map/ppermute | solution.py:438
  53.7 1.9 %shard_map.130 = (f32[2,4,64,256]{3,2,1,0:T(8,128)S(1)}, f32[16,4,256]{2,1,0:T(4,128)S(1)}) custom-call(s32[2]{0:T(128)S(1)} %pad_add_fusion.ids, f32[4,1]{1,0:T(4,128)S(1)} %copy-done.6, f32[64,1]{1,0:T(8,128)S(1)} %copy-done.4, f32[1,1024]{1,0:T(1,128)S(1)} %copy-done.5, f32[64,2]{1,0:T(8,128)S(1)} %copy-done.3, ...), custom_call_target="tpu_custom_call" | custom-call | flops 786432000 | bytes 1053464 | tf_op jit(solution)/shard_map/pallas_call | solution.py:73
  56.2 1.3 %collective-permute-done.11 = f32[1,16,4,256]{3,2,1,0:T(4,128)S(1)} collective-permute-done((f32[1,16,4,256]{3,2,1,0:T(4,128)S(1)}, f32[1,16,4,256]{3,2,1,0:T(4,128)S(1)}, u32[]{:S(2)}, u32[]{:S(2)}) %collective-permute-start.11) | collective-permute-done | bytes 65568 | tf_op jit(solution)/shard_map/ppermute | solution.py:438
  57.5 1.6 %collective-permute-start.12 = (f32[2,16,4,256]{3,2,1,0:T(4,128)S(1)}, f32[2,16,4,256]{3,2,1,0:T(4,128)S(1)}, u32[]{:S(2)}, u32[]{:S(2)}) collective-permute-start(f32[2,16,4,256]{3,2,1,0:T(4,128)S(1)} %pad_maximum_fusion.3), channel_id=1, source_target_pairs={{0,2},{1,3},{2,0},{3,1},{4,6},{5,7},{6,4},{7,5},{8,10},{9,11},{10,... | collective-permute-start | bytes 393224 | tf_op jit(solution)/shard_map/ppermute | solution.py:438
  59.0 2.0 %shard_map.135 = (f32[4,64,256]{2,1,0:T(8,128)S(1)}, f32[4,64,256]{2,1,0:T(8,128)S(1)}, f32[4,64,256]{2,1,0:T(8,128)S(1)}, f32[4,64,256]{2,1,0:T(8,128)S(1)}) custom-call(s32[2]{0:T(128)S(1)} %pad_add_fusion.ids, f32[4,1]{1,0:T(4,128)S(1)} %copy-done.7, f32[64,1]{1,0:T(8,128)S(1)} %copy-done.4, f32[1,1024]{1,0:T(1,128)S(1)} %copy-done.5, ...), custom_call_target="tpu_custom_call" | custom-call | flops 26214400 | bytes 1708824 | tf_op jit(solution)/shard_map/pallas_call | solution.py:73
  61.0 1.1 %collective-permute-start.17 = (f32[4,64,256]{2,1,0:T(8,128)S(1)}, f32[4,64,256]{2,1,0:T(8,128)S(1)}, u32[]{:S(2)}, u32[]{:S(2)}) collective-permute-start(f32[4,64,256]{2,1,0:T(8,128)S(1)} %get-tuple-element.52), channel_id=1, source_target_pairs={{0,4},{4,0},{8,12},{12,8},{16,20},{20,16},{24,28},{28,24},{1,5},{5... | collective-permute-start | bytes 786440 | tf_op jit(solution)/shard_map/ppermute | solution.py:438
  62.2 2.9 %collective-permute-start.18 = (f32[4,64,256]{2,1,0:T(8,128)S(1)}, f32[4,64,256]{2,1,0:T(8,128)S(1)}, u32[]{:S(2)}, u32[]{:S(2)}) collective-permute-start(f32[4,64,256]{2,1,0:T(8,128)S(1)} %get-tuple-element.53), channel_id=1, source_target_pairs={{0,8},{4,12},{8,0},{12,4},{16,24},{20,28},{24,16},{28,20},{1,9},{5... | collective-permute-start | bytes 786440 | tf_op jit(solution)/shard_map/ppermute | solution.py:438
  66.0 2.0 %collective-permute-start.13 = (f32[16,4,256]{2,1,0:T(4,128)S(1)}, f32[16,4,256]{2,1,0:T(4,128)S(1)}, u32[]{:S(2)}, u32[]{:S(2)}) collective-permute-start(f32[16,4,256]{2,1,0:T(4,128)S(1)} %shard_map.133.refs_5_), channel_id=1, source_target_pairs={{0,16},{4,20},{8,24},{12,28},{16,0},{20,4},{24,8},{28,12},{1,17},{... | collective-permute-start | bytes 196616 | tf_op jit(solution)/shard_map/ppermute | solution.py:438
  68.0 15.2 %collective-permute-done.13.refs_6_ = f32[16,4,256]{2,1,0:T(4,128)S(1)} collective-permute-done((f32[16,4,256]{2,1,0:T(4,128)S(1)}, f32[16,4,256]{2,1,0:T(4,128)S(1)}, u32[]{:S(2)}, u32[]{:S(2)}) %collective-permute-start.13) | collective-permute-done | bytes 65568 | tf_op jit(solution)/shard_map/ppermute | solution.py:438
  83.2 2.2 %shard_map.134 = (f32[4,64,256]{2,1,0:T(8,128)S(1)}, f32[4,64,256]{2,1,0:T(8,128)S(1)}, f32[4,64,256]{2,1,0:T(8,128)S(1)}, f32[4,64,256]{2,1,0:T(8,128)S(1)}) custom-call(s32[2]{0:T(128)S(1)} %pad_add_fusion.ids, f32[4,1]{1,0:T(4,128)S(1)} %copy-done.6, f32[64,1]{1,0:T(8,128)S(1)} %copy-done.4, f32[1,1024]{1,0:T(1,128)S(1)} %copy-done.5, ...), custom_call_target="tpu_custom_call" | custom-call | flops 26214400 | bytes 1708824 | tf_op jit(solution)/shard_map/pallas_call | solution.py:73
  85.4 2.1 %collective-permute-start.14 = (f32[4,64,256]{2,1,0:T(8,128)S(1)}, f32[4,64,256]{2,1,0:T(8,128)S(1)}, u32[]{:S(2)}, u32[]{:S(2)}) collective-permute-start(f32[4,64,256]{2,1,0:T(8,128)S(1)} %get-tuple-element.48), channel_id=1, source_target_pairs={{0,4},{4,0},{8,12},{12,8},{16,20},{20,16},{24,28},{28,24},{1,5},{5... | collective-permute-start | bytes 786440 | tf_op jit(solution)/shard_map/ppermute | solution.py:438
  87.5 1.5 %collective-permute-start.16 = (f32[4,64,256]{2,1,0:T(8,128)S(1)}, f32[4,64,256]{2,1,0:T(8,128)S(1)}, u32[]{:S(2)}, u32[]{:S(2)}) collective-permute-start(f32[4,64,256]{2,1,0:T(8,128)S(1)} %get-tuple-element.50), channel_id=1, source_target_pairs={{0,12},{4,8},{8,4},{12,0},{16,28},{20,24},{24,20},{28,16},{1,13},{... | collective-permute-start | bytes 786440 | tf_op jit(solution)/shard_map/ppermute | solution.py:438
  89.2 2.8 %shard_map.136.refs_4_ = f32[4,64,1024]{2,1,0:T(8,128)S(1)} custom-call(s32[2]{0:T(128)S(1)} %pad_add_fusion.ids, bf16[2,2,256,256]{3,2,1,0:T(8,128)(2,1)S(1)} %copy-done, bf16[1024,1024]{1,0:T(8,128)(2,1)S(1)} %get-tuple-element.30.sxh, bf16[1024,1024]{1,0:T(8,128)(2,1)S(1)} %get-tuple-element.31.sxl, f32[4,64,256]{2,1,0:T(8,128)S(1)} %get-tuple-element.51.refs_0_, ...), custom_call_target="tpu_custom_call" | custom-call | flops 2013265920 | bytes 5767176 | tf_op jit(solution)/shard_map/pallas_call | solution.py:73
  92.0 3.2 %collective-permute-done.14.refs_1_ = f32[4,64,256]{2,1,0:T(8,128)S(1)} collective-permute-done((f32[4,64,256]{2,1,0:T(8,128)S(1)}, f32[4,64,256]{2,1,0:T(8,128)S(1)}, u32[]{:S(2)}, u32[]{:S(2)}) %collective-permute-start.14) | collective-permute-done | bytes 262176 | tf_op jit(solution)/shard_map/ppermute | solution.py:438
  95.2 1.5 %collective-permute-done.15.refs_2_ = f32[4,64,256]{2,1,0:T(8,128)S(1)} collective-permute-done((f32[4,64,256]{2,1,0:T(8,128)S(1)}, f32[4,64,256]{2,1,0:T(8,128)S(1)}, u32[]{:S(2)}, u32[]{:S(2)}) %collective-permute-start.15) | collective-permute-done | bytes 262176 | tf_op jit(solution)/shard_map/ppermute | solution.py:438
  96.7 4.1 %collective-permute-done.16.refs_3_ = f32[4,64,256]{2,1,0:T(8,128)S(1)} collective-permute-done((f32[4,64,256]{2,1,0:T(8,128)S(1)}, f32[4,64,256]{2,1,0:T(8,128)S(1)}, u32[]{:S(2)}, u32[]{:S(2)}) %collective-permute-start.16) | collective-permute-done | bytes 262176 | tf_op jit(solution)/shard_map/ppermute | solution.py:438
  100.8 4.0 %shard_map.137 = f32[8,64,1024]{2,1,0:T(8,128)} custom-call(s32[2]{0:T(128)S(1)} %pad_add_fusion.ids, bf16[2,2,256,256]{3,2,1,0:T(8,128)(2,1)S(1)} %copy-done, bf16[1024,1024]{1,0:T(8,128)(2,1)S(1)} %get-tuple-element.30.sxh, bf16[1024,1024]{1,0:T(8,128)(2,1)S(1)} %get-tuple-element.31.sxl, f32[4,64,256]{2,1,0:T(8,128)S(1)} %get-tuple-element.47.refs_0_, ...), custom_call_target="tpu_custom_call" | custom-call | flops 2013265920 | bytes 6815752 | tf_op jit(solution)/shard_map/pallas_call | solution.py:73
  (46 shorter events, 4.6 us)
Async XLA Ops:
  0.1 1.0 copy-start.10
  1.1 1.7 %copy-start.8 = (f32[1,8,64,1024]{3,2,1,0:T(8,128)S(1)}, f32[1,8,64,1024]{3,2,1,0:T(8,128)}, u32[]{:S(2)}) copy-start(f32[1,8,64,1024]{3,2,1,0:T(8,128)} %param.13) | copy-start | bytes 6291460
  1.1 1.7 %copy-start.9 = (bf16[2,2,256,256]{3,2,1,0:T(8,128)(2,1)S(1)}, bf16[2,2,256,256]{3,2,1,0:T(8,128)(2,1)}, u32[]{:S(2)}) copy-start(bf16[2,2,256,256]{3,2,1,0:T(8,128)(2,1)} %constant.51.both) | copy-start | bytes 1572868
  5.7 9.3 %collective-permute-start.3 = (f32[4,64,256]{2,1,0:T(8,128)S(1)}, f32[4,64,256]{2,1,0:T(8,128)S(1)}, u32[]{:S(2)}, u32[]{:S(2)}) collective-permute-start(f32[4,64,256]{2,1,0:T(8,128)S(1)} %get-tuple-element.40), channel_id=1, source_target_pairs={{0,4},{4,0},{8,12},{12,8},{16,20},{20,16},{24,28},{28,24},{1,5},{5... | collective-permute-start | bytes 786440 | tf_op jit(solution)/shard_map/ppermute | solution.py:438
  8.7 9.2 %collective-permute-start.4 = (f32[4,64,256]{2,1,0:T(8,128)S(1)}, f32[4,64,256]{2,1,0:T(8,128)S(1)}, u32[]{:S(2)}, u32[]{:S(2)}) collective-permute-start(f32[4,64,256]{2,1,0:T(8,128)S(1)} %get-tuple-element.41), channel_id=1, source_target_pairs={{0,8},{4,12},{8,0},{12,4},{16,24},{20,28},{24,16},{28,20},{1,9},{5... | collective-permute-start | bytes 786440 | tf_op jit(solution)/shard_map/ppermute | solution.py:438
  10.3 11.6 %copy-start.3 = (f32[64,2]{1,0:T(8,128)S(1)}, f32[64,2]{1,0:T(8,128)}, u32[]{:S(2)}) copy-start(f32[64,2]{1,0:T(8,128)} %constant.35.clone.edges) | copy-start | bytes 1540
  10.3 11.6 %copy-start.4 = (f32[64,1]{1,0:T(8,128)S(1)}, f32[64,1]{1,0:T(8,128)}, u32[]{:S(2)}) copy-start(f32[64,1]{1,0:T(8,128)} %constant.33.clone.smu_y) | copy-start | bytes 772
  10.3 11.6 %copy-start.5 = (f32[1,1024]{1,0:T(1,128)S(1)}, f32[1,1024]{1,0:T(1,128)}, u32[]{:S(2)}) copy-start(f32[1,1024]{1,0:T(1,128)} %constant.34.clone.smu_x) | copy-start | bytes 12292
  10.3 11.6 %copy-start.7 = (f32[4,1]{1,0:T(4,128)S(1)}, f32[4,1]{1,0:T(4,128)}, u32[]{:S(2)}) copy-start(f32[4,1]{1,0:T(4,128)} %constant.41.clone.smu_z) | copy-start | bytes 52
  10.3 11.6 %collective-permute-start.5 = (f32[4,64,256]{2,1,0:T(8,128)S(1)}, f32[4,64,256]{2,1,0:T(8,128)S(1)}, u32[]{:S(2)}, u32[]{:S(2)}) collective-permute-start(f32[4,64,256]{2,1,0:T(8,128)S(1)} %get-tuple-element.42), channel_id=1, source_target_pairs={{0,12},{4,8},{8,4},{12,0},{16,28},{20,24},{24,20},{28,16},{1,13},{... | collective-permute-start | bytes 786440 | tf_op jit(solution)/shard_map/ppermute | solution.py:438
  13.2 22.2 %copy-start.2 = (f32[5,4,4,1024]{3,2,1,0:T(4,128)S(1)}, f32[5,4,4,1024]{3,2,1,0:T(4,128)}, u32[]{:S(2)}) copy-start(f32[5,4,4,1024]{3,2,1,0:T(4,128)} %constant.43.clone.responses) | copy-start | bytes 983044
  13.2 40.5 %copy-start.6 = (f32[4,1]{1,0:T(4,128)S(1)}, f32[4,1]{1,0:T(4,128)}, u32[]{:S(2)}) copy-start(f32[4,1]{1,0:T(4,128)} %constant.42.clone.smu_z) | copy-start | bytes 52
  23.8 31.8 %collective-permute-start.6 = (f32[2,4,64,256]{3,2,1,0:T(8,128)S(1)}, f32[2,4,64,256]{3,2,1,0:T(8,128)S(1)}, u32[]{:S(2)}, u32[]{:S(2)}) collective-permute-start(f32[2,4,64,256]{3,2,1,0:T(8,128)S(1)} %get-tuple-element.43), channel_id=1, source_target_pairs={{0,16},{4,20},{8,24},{12,28},{16,0},{20,4},{24,8},{28,12},{1,17},{... | collective-permute-start | bytes 1572872 | tf_op jit(solution)/shard_map/ppermute | solution.py:438
  26.6 3.5 %collective-permute-start.7 = (f32[1,16,4,256]{3,2,1,0:T(4,128)S(1)}, f32[1,16,4,256]{3,2,1,0:T(4,128)S(1)}, u32[]{:S(2)}, u32[]{:S(2)}) collective-permute-start(f32[1,16,4,256]{3,2,1,0:T(4,128)S(1)} %bitcast.9), channel_id=1, source_target_pairs={{0,1},{1,0},{2,3},{3,2},{4,5},{5,4},{6,7},{7,6},{8,9},{9,8},{10,11... | collective-permute-start | bytes 196616 | tf_op jit(solution)/shard_map/ppermute | solution.py:438
  26.6 9.9 %collective-permute-start = (f32[4,64,256]{2,1,0:T(8,128)S(1)}, f32[4,64,256]{2,1,0:T(8,128)S(1)}, u32[]{:S(2)}, u32[]{:S(2)}) collective-permute-start(f32[4,64,256]{2,1,0:T(8,128)S(1)} %get-tuple-element.35), channel_id=1, source_target_pairs={{0,4},{4,0},{8,12},{12,8},{16,20},{20,16},{24,28},{28,24},{1,5},{5... | collective-permute-start | bytes 786440 | tf_op jit(solution)/shard_map/ppermute | solution.py:438
  28.2 16.5 %collective-permute-start.1 = (f32[4,64,256]{2,1,0:T(8,128)S(1)}, f32[4,64,256]{2,1,0:T(8,128)S(1)}, u32[]{:S(2)}, u32[]{:S(2)}) collective-permute-start(f32[4,64,256]{2,1,0:T(8,128)S(1)} %get-tuple-element.36), channel_id=1, source_target_pairs={{0,8},{4,12},{8,0},{12,4},{16,24},{20,28},{24,16},{28,20},{1,9},{5... | collective-permute-start | bytes 786440 | tf_op jit(solution)/shard_map/ppermute | solution.py:438
  29.7 23.9 %collective-permute-start.2 = (f32[4,64,256]{2,1,0:T(8,128)S(1)}, f32[4,64,256]{2,1,0:T(8,128)S(1)}, u32[]{:S(2)}, u32[]{:S(2)}) collective-permute-start(f32[4,64,256]{2,1,0:T(8,128)S(1)} %get-tuple-element.37), channel_id=1, source_target_pairs={{0,12},{4,8},{8,4},{12,0},{16,28},{20,24},{24,20},{28,16},{1,13},{... | collective-permute-start | bytes 786440 | tf_op jit(solution)/shard_map/ppermute | solution.py:438
  30.2 5.1 %collective-permute-start.8 = (f32[2,16,4,256]{3,2,1,0:T(4,128)S(1)}, f32[2,16,4,256]{3,2,1,0:T(4,128)S(1)}, u32[]{:S(2)}, u32[]{:S(2)}) collective-permute-start(f32[2,16,4,256]{3,2,1,0:T(4,128)S(1)} %pad_maximum_fusion.2), channel_id=1, source_target_pairs={{0,2},{1,3},{2,0},{3,1},{4,6},{5,7},{6,4},{7,5},{8,10},{9,11},{10,... | collective-permute-start | bytes 393224 | tf_op jit(solution)/shard_map/ppermute | solution.py:438
  36.2 28.9 %copy-start.1 = (f32[5,4,4,1024]{3,2,1,0:T(4,128)S(1)}, f32[5,4,4,1024]{3,2,1,0:T(4,128)}, u32[]{:S(2)}) copy-start(f32[5,4,4,1024]{3,2,1,0:T(4,128)} %constant.44.clone.responses) | copy-start | bytes 983044
  36.3 19.3 %collective-permute-start.9 = (f32[16,4,256]{2,1,0:T(4,128)S(1)}, f32[16,4,256]{2,1,0:T(4,128)S(1)}, u32[]{:S(2)}, u32[]{:S(2)}) collective-permute-start(f32[16,4,256]{2,1,0:T(4,128)S(1)} %shard_map.132.refs_5_), channel_id=1, source_target_pairs={{0,16},{4,20},{8,24},{12,28},{16,0},{20,4},{24,8},{28,12},{1,17},{... | collective-permute-start | bytes 196616 | tf_op jit(solution)/shard_map/ppermute | solution.py:438
  55.6 27.6 %collective-permute-start.10 = (f32[2,4,64,256]{3,2,1,0:T(8,128)S(1)}, f32[2,4,64,256]{3,2,1,0:T(8,128)S(1)}, u32[]{:S(2)}, u32[]{:S(2)}) collective-permute-start(f32[2,4,64,256]{3,2,1,0:T(8,128)S(1)} %get-tuple-element.45), channel_id=1, source_target_pairs={{0,16},{4,20},{8,24},{12,28},{16,0},{20,4},{24,8},{28,12},{1,17},{... | collective-permute-start | bytes 1572872 | tf_op jit(solution)/shard_map/ppermute | solution.py:438
  56.2 1.3 %collective-permute-start.11 = (f32[1,16,4,256]{3,2,1,0:T(4,128)S(1)}, f32[1,16,4,256]{3,2,1,0:T(4,128)S(1)}, u32[]{:S(2)}, u32[]{:S(2)}) collective-permute-start(f32[1,16,4,256]{3,2,1,0:T(4,128)S(1)} %bitcast.6), channel_id=1, source_target_pairs={{0,1},{1,0},{2,3},{3,2},{4,5},{5,4},{6,7},{7,6},{8,9},{9,8},{10,11... | collective-permute-start | bytes 196616 | tf_op jit(solution)/shard_map/ppermute | solution.py:438
  57.5 31.7 %copy-start = (bf16[2,2,256,256]{3,2,1,0:T(8,128)(2,1)S(1)}, bf16[2,2,256,256]{3,2,1,0:T(8,128)(2,1)}, u32[]{:S(2)}) copy-start(bf16[2,2,256,256]{3,2,1,0:T(8,128)(2,1)} %constant.48.both) | copy-start | bytes 1572868
  57.5 7.6 %collective-permute-start.12 = (f32[2,16,4,256]{3,2,1,0:T(4,128)S(1)}, f32[2,16,4,256]{3,2,1,0:T(4,128)S(1)}, u32[]{:S(2)}, u32[]{:S(2)}) collective-permute-start(f32[2,16,4,256]{3,2,1,0:T(4,128)S(1)} %pad_maximum_fusion.3), channel_id=1, source_target_pairs={{0,2},{1,3},{2,0},{3,1},{4,6},{5,7},{6,4},{7,5},{8,10},{9,11},{10,... | collective-permute-start | bytes 393224 | tf_op jit(solution)/shard_map/ppermute | solution.py:438
  61.0 26.5 %collective-permute-start.17 = (f32[4,64,256]{2,1,0:T(8,128)S(1)}, f32[4,64,256]{2,1,0:T(8,128)S(1)}, u32[]{:S(2)}, u32[]{:S(2)}) collective-permute-start(f32[4,64,256]{2,1,0:T(8,128)S(1)} %get-tuple-element.52), channel_id=1, source_target_pairs={{0,4},{4,0},{8,12},{12,8},{16,20},{20,16},{24,28},{28,24},{1,5},{5... | collective-permute-start | bytes 786440 | tf_op jit(solution)/shard_map/ppermute | solution.py:438
  62.2 26.8 %collective-permute-start.18 = (f32[4,64,256]{2,1,0:T(8,128)S(1)}, f32[4,64,256]{2,1,0:T(8,128)S(1)}, u32[]{:S(2)}, u32[]{:S(2)}) collective-permute-start(f32[4,64,256]{2,1,0:T(8,128)S(1)} %get-tuple-element.53), channel_id=1, source_target_pairs={{0,8},{4,12},{8,0},{12,4},{16,24},{20,28},{24,16},{28,20},{1,9},{5... | collective-permute-start | bytes 786440 | tf_op jit(solution)/shard_map/ppermute | solution.py:438
  65.1 24.1 %collective-permute-start.19 = (f32[4,64,256]{2,1,0:T(8,128)S(1)}, f32[4,64,256]{2,1,0:T(8,128)S(1)}, u32[]{:S(2)}, u32[]{:S(2)}) collective-permute-start(f32[4,64,256]{2,1,0:T(8,128)S(1)} %get-tuple-element.54), channel_id=1, source_target_pairs={{0,12},{4,8},{8,4},{12,0},{16,28},{20,24},{24,20},{28,16},{1,13},{... | collective-permute-start | bytes 786440 | tf_op jit(solution)/shard_map/ppermute | solution.py:438
  66.0 17.2 %collective-permute-start.13 = (f32[16,4,256]{2,1,0:T(4,128)S(1)}, f32[16,4,256]{2,1,0:T(4,128)S(1)}, u32[]{:S(2)}, u32[]{:S(2)}) collective-permute-start(f32[16,4,256]{2,1,0:T(4,128)S(1)} %shard_map.133.refs_5_), channel_id=1, source_target_pairs={{0,16},{4,20},{8,24},{12,28},{16,0},{20,4},{24,8},{28,12},{1,17},{... | collective-permute-start | bytes 196616 | tf_op jit(solution)/shard_map/ppermute | solution.py:438
  85.4 9.8 %collective-permute-start.14 = (f32[4,64,256]{2,1,0:T(8,128)S(1)}, f32[4,64,256]{2,1,0:T(8,128)S(1)}, u32[]{:S(2)}, u32[]{:S(2)}) collective-permute-start(f32[4,64,256]{2,1,0:T(8,128)S(1)} %get-tuple-element.48), channel_id=1, source_target_pairs={{0,4},{4,0},{8,12},{12,8},{16,20},{20,16},{24,28},{28,24},{1,5},{5... | collective-permute-start | bytes 786440 | tf_op jit(solution)/shard_map/ppermute | solution.py:438
  87.5 9.2 %collective-permute-start.15 = (f32[4,64,256]{2,1,0:T(8,128)S(1)}, f32[4,64,256]{2,1,0:T(8,128)S(1)}, u32[]{:S(2)}, u32[]{:S(2)}) collective-permute-start(f32[4,64,256]{2,1,0:T(8,128)S(1)} %get-tuple-element.49), channel_id=1, source_target_pairs={{0,8},{4,12},{8,0},{12,4},{16,24},{20,28},{24,16},{28,20},{1,9},{5... | collective-permute-start | bytes 786440 | tf_op jit(solution)/shard_map/ppermute | solution.py:438
  87.5 13.3 %collective-permute-start.16 = (f32[4,64,256]{2,1,0:T(8,128)S(1)}, f32[4,64,256]{2,1,0:T(8,128)S(1)}, u32[]{:S(2)}, u32[]{:S(2)}) collective-permute-start(f32[4,64,256]{2,1,0:T(8,128)S(1)} %get-tuple-element.50), channel_id=1, source_target_pairs={{0,12},{4,8},{8,4},{12,0},{16,28},{20,24},{24,20},{28,16},{1,13},{... | collective-permute-start | bytes 786440 | tf_op jit(solution)/shard_map/ppermute | solution.py:438

commit v11 on v10

--- a/solution.py
+++ b/solution.py
@@ -484,6 +484,9 @@
             (*small, *pieces),
             [pltpu.VMEM((2 * steps, len(chunk), 8, plan.block), jnp.float32)],
         )
+        if at + 1 < len(work):
+            later = work[at + 1][-1]
+            view, *later[1:-1] = lax.optimization_barrier((view, *later[1:-1]))
         ended.append([ends, seen, view])
     sums = {}
     far = None

time: 105 us -> 110 us (1.048)
  starting transfers between devices: 24.6 us -> 39.6 us
  waiting for transfers between devices: 54.7 us -> 44.3 us
    ppermute x20, starting transfers between devices: 24.6 us -> 39.6 us  [swap(): return lax.ppermute(values, axis, [(i, i ^ distance) for i in range(count)])]
    ppermute x20, waiting for transfers between devices: 54.7 us -> 44.3 us  [swap(): return lax.ppermute(values, axis, [(i, i ^ distance) for i in range(count)])]
  transfers between devices with their start and end apart: 20 -> 20, of which waited for: 12 -> 11; matrix products, arithmetic and copies ran while one was open for 0% -> 0% of each run, Pallas kernels for 13% -> 14%
where the time goes in v11:
time: 110 us
  waiting for transfers between devices  44.3 us (40%)
  starting transfers between devices  39.6 us (36%)
  Pallas kernels  23.9 us (22%)
    ppermute x20, waiting for transfers between devices, swap(): return lax.ppermute(values, axis, [(i, i ^ distance) for i in range(count)])  44.3 us
    ppermute x20, starting transfers between devices, swap(): return lax.ppermute(values, axis, [(i, i ^ distance) for i in range(count)])  39.6 us
    pallas_call x11, Pallas kernels, call(): pl.pallas_call(kernel, out_shape=out_shape, in_specs=[smem] + [vmem] * (l...  23.9 us
  transfers between devices with their start and end apart: 20, of which 11 were waited for; matrix products, arithmetic and copies ran while one was open for 0% of the time, Pallas kernels for 14%

profile of v11, /device:TPU:0, one launch (start us, length us, event | category | flops | bytes accessed | tf_op | source)
XLA Modules:
  0.0 109.5 jit_solution(14723743988148793958)
XLA Ops:
  0.1 1.0 copy-done.10
  1.1 1.7 %shard_map.127 = (bf16[1024,1024]{1,0:T(8,128)(2,1)S(1)}, bf16[1024,1024]{1,0:T(8,128)(2,1)S(1)}) custom-call(s32[2]{0:T(128)S(1)} %pad_add_fusion.ids, f32[128,1024]{1,0:T(8,128)S(1)} %copy-done.10), custom_call_target="tpu_custom_call" | custom-call | flops 4194304000 | bytes 524296 | tf_op jit(solution)/shard_map/pallas_call | solution.py:73
  2.9 2.8 %shard_map.128 = (f32[4,64,256]{2,1,0:T(8,128)S(1)}, f32[4,64,256]{2,1,0:T(8,128)S(1)}, f32[4,64,256]{2,1,0:T(8,128)S(1)}, f32[4,64,256]{2,1,0:T(8,128)S(1)}) custom-call(s32[2]{0:T(128)S(1)} %pad_add_fusion.ids, bf16[2,2,256,256]{3,2,1,0:T(8,128)(2,1)S(1)} %copy-done.9, f32[8,64,1024]{2,1,0:T(8,128)S(1)} %bitcast.12, ...), custom_call_target="tpu_custom_call" | custom-call | flops 2013265920 | bytes 6815752 | tf_op jit(solution)/shard_map/pallas_call | solution.py:73
  5.7 3.0 %collective-permute-start = (f32[4,64,256]{2,1,0:T(8,128)S(1)}, f32[4,64,256]{2,1,0:T(8,128)S(1)}, u32[]{:S(2)}, u32[]{:S(2)}) collective-permute-start(f32[4,64,256]{2,1,0:T(8,128)S(1)} %get-tuple-element.39), channel_id=1, source_target_pairs={{0,4},{4,0},{8,12},{12,8},{16,20},{20,16},{24,28},{28,24},{1,5},{5... | collective-permute-start | bytes 786440 | tf_op jit(solution)/shard_map/ppermute | solution.py:438
  8.7 1.6 %collective-permute-start.1 = (f32[4,64,256]{2,1,0:T(8,128)S(1)}, f32[4,64,256]{2,1,0:T(8,128)S(1)}, u32[]{:S(2)}, u32[]{:S(2)}) collective-permute-start(f32[4,64,256]{2,1,0:T(8,128)S(1)} %get-tuple-element.40), channel_id=1, source_target_pairs={{0,8},{4,12},{8,0},{12,4},{16,24},{20,28},{24,16},{28,20},{1,9},{5... | collective-permute-start | bytes 786440 | tf_op jit(solution)/shard_map/ppermute | solution.py:438
  10.4 2.8 %shard_map.129 = (f32[4,64,256]{2,1,0:T(8,128)S(1)}, f32[4,64,256]{2,1,0:T(8,128)S(1)}, f32[4,64,256]{2,1,0:T(8,128)S(1)}, f32[4,64,256]{2,1,0:T(8,128)S(1)}) custom-call(s32[2]{0:T(128)S(1)} %pad_add_fusion.ids, bf16[2,2,256,256]{3,2,1,0:T(8,128)(2,1)S(1)} %copy-done.9, f32[8,64,1024]{2,1,0:T(8,128)S(1)} %bitcast.13, ...), custom_call_target="tpu_custom_call" | custom-call | flops 2013265920 | bytes 6815752 | tf_op jit(solution)/shard_map/pallas_call | solution.py:73
  13.2 2.0 %collective-permute-start.3 = (f32[4,64,256]{2,1,0:T(8,128)S(1)}, f32[4,64,256]{2,1,0:T(8,128)S(1)}, u32[]{:S(2)}, u32[]{:S(2)}) collective-permute-start(f32[4,64,256]{2,1,0:T(8,128)S(1)} %get-tuple-element.43), channel_id=1, source_target_pairs={{0,4},{4,0},{8,12},{12,8},{16,20},{20,16},{24,28},{28,24},{1,5},{5... | collective-permute-start | bytes 786440 | tf_op jit(solution)/shard_map/ppermute | solution.py:438
  15.2 1.6 %collective-permute-start.4 = (f32[4,64,256]{2,1,0:T(8,128)S(1)}, f32[4,64,256]{2,1,0:T(8,128)S(1)}, u32[]{:S(2)}, u32[]{:S(2)}) collective-permute-start(f32[4,64,256]{2,1,0:T(8,128)S(1)} %get-tuple-element.44), channel_id=1, source_target_pairs={{0,8},{4,12},{8,0},{12,4},{16,24},{20,28},{24,16},{28,20},{1,9},{5... | collective-permute-start | bytes 786440 | tf_op jit(solution)/shard_map/ppermute | solution.py:438
  16.8 1.2 %collective-permute-done.1.refs_2_ = f32[4,64,256]{2,1,0:T(8,128)S(1)} collective-permute-done((f32[4,64,256]{2,1,0:T(8,128)S(1)}, f32[4,64,256]{2,1,0:T(8,128)S(1)}, u32[]{:S(2)}, u32[]{:S(2)}) %collective-permute-start.1) | collective-permute-done | bytes 262176 | tf_op jit(solution)/shard_map/ppermute | solution.py:438
  18.0 5.1 %collective-permute-done.2.refs_3_ = f32[4,64,256]{2,1,0:T(8,128)S(1)} collective-permute-done((f32[4,64,256]{2,1,0:T(8,128)S(1)}, f32[4,64,256]{2,1,0:T(8,128)S(1)}, u32[]{:S(2)}, u32[]{:S(2)}) %collective-permute-start.2) | collective-permute-done | bytes 262176 | tf_op jit(solution)/shard_map/ppermute | solution.py:438
  23.1 1.9 %shard_map.130 = (f32[2,4,64,256]{3,2,1,0:T(8,128)S(1)}, f32[16,4,256]{2,1,0:T(4,128)S(1)}) custom-call(s32[2]{0:T(128)S(1)} %pad_add_fusion.ids, f32[4,1]{1,0:T(4,128)S(1)} %copy-done.7, f32[64,1]{1,0:T(8,128)S(1)} %copy-done.4, f32[1,1024]{1,0:T(1,128)S(1)} %copy-done.5, f32[64,2]{1,0:T(8,128)S(1)} %copy-done.3, ...), custom_call_target="tpu_custom_call" | custom-call | flops 10485760000 | bytes 1053464 | tf_op jit(solution)/shard_map/pallas_call | solution.py:73
  25.0 3.1 %collective-permute-start.6 = (f32[2,4,64,256]{3,2,1,0:T(8,128)S(1)}, f32[2,4,64,256]{3,2,1,0:T(8,128)S(1)}, u32[]{:S(2)}, u32[]{:S(2)}) collective-permute-start(f32[2,4,64,256]{3,2,1,0:T(8,128)S(1)} %get-tuple-element.49), channel_id=1, source_target_pairs={{0,16},{4,20},{8,24},{12,28},{16,0},{20,4},{24,8},{28,12},{1,17},{... | collective-permute-start | bytes 1572872 | tf_op jit(solution)/shard_map/ppermute | solution.py:438
  28.2 2.8 %collective-permute-done.4.refs_2_ = f32[4,64,256]{2,1,0:T(8,128)S(1)} collective-permute-done((f32[4,64,256]{2,1,0:T(8,128)S(1)}, f32[4,64,256]{2,1,0:T(8,128)S(1)}, u32[]{:S(2)}, u32[]{:S(2)}) %collective-permute-start.4) | collective-permute-done | bytes 262176 | tf_op jit(solution)/shard_map/ppermute | solution.py:438
  31.0 1.2 %collective-permute-done.7 = f32[1,16,4,256]{3,2,1,0:T(4,128)S(1)} collective-permute-done((f32[1,16,4,256]{3,2,1,0:T(4,128)S(1)}, f32[1,16,4,256]{3,2,1,0:T(4,128)S(1)}, u32[]{:S(2)}, u32[]{:S(2)}) %collective-permute-start.7) | collective-permute-done | bytes 65568 | tf_op jit(solution)/shard_map/ppermute | solution.py:438
  32.3 2.0 %collective-permute-start.8 = (f32[2,16,4,256]{3,2,1,0:T(4,128)S(1)}, f32[2,16,4,256]{3,2,1,0:T(4,128)S(1)}, u32[]{:S(2)}, u32[]{:S(2)}) collective-permute-start(f32[2,16,4,256]{3,2,1,0:T(4,128)S(1)} %pad_maximum_fusion.2), channel_id=1, source_target_pairs={{0,2},{1,3},{2,0},{3,1},{4,6},{5,7},{6,4},{7,5},{8,10},{9,11},{10,... | collective-permute-start | bytes 393224 | tf_op jit(solution)/shard_map/ppermute | solution.py:438
  34.2 3.8 %collective-permute-done.8 = f32[2,16,4,256]{3,2,1,0:T(4,128)S(1)} collective-permute-done((f32[2,16,4,256]{3,2,1,0:T(4,128)S(1)}, f32[2,16,4,256]{3,2,1,0:T(4,128)S(1)}, u32[]{:S(2)}, u32[]{:S(2)}) %collective-permute-start.8) | collective-permute-done | bytes 131104 | tf_op jit(solution)/shard_map/ppermute | solution.py:438
  38.1 0.9 shard_map.132.refs_5_
  39.8 4.7 %collective-permute-done.5.refs_3_ = f32[4,64,256]{2,1,0:T(8,128)S(1)} collective-permute-done((f32[4,64,256]{2,1,0:T(8,128)S(1)}, f32[4,64,256]{2,1,0:T(8,128)S(1)}, u32[]{:S(2)}, u32[]{:S(2)}) %collective-permute-start.5) | collective-permute-done | bytes 262176 | tf_op jit(solution)/shard_map/ppermute | solution.py:438
  44.5 1.9 %shard_map.131 = (f32[2,4,64,256]{3,2,1,0:T(8,128)S(1)}, f32[16,4,256]{2,1,0:T(4,128)S(1)}) custom-call(s32[2]{0:T(128)S(1)} %pad_add_fusion.ids, f32[4,1]{1,0:T(4,128)S(1)} %copy-done.6, f32[64,1]{1,0:T(8,128)S(1)} %copy-done.4, f32[1,1024]{1,0:T(1,128)S(1)} %copy-done.5, f32[64,2]{1,0:T(8,128)S(1)} %copy-done.3, ...), custom_call_target="tpu_custom_call" | custom-call | flops 786432000 | bytes 1053464 | tf_op jit(solution)/shard_map/pallas_call | solution.py:73
  46.4 5.3 %collective-permute-done.9.refs_6_ = f32[16,4,256]{2,1,0:T(4,128)S(1)} collective-permute-done((f32[16,4,256]{2,1,0:T(4,128)S(1)}, f32[16,4,256]{2,1,0:T(4,128)S(1)}, u32[]{:S(2)}, u32[]{:S(2)}) %collective-permute-start.9) | collective-permute-done | bytes 65568 | tf_op jit(solution)/shard_map/ppermute | solution.py:438
  51.7 1.2 %collective-permute-done.11 = f32[1,16,4,256]{3,2,1,0:T(4,128)S(1)} collective-permute-done((f32[1,16,4,256]{3,2,1,0:T(4,128)S(1)}, f32[1,16,4,256]{3,2,1,0:T(4,128)S(1)}, u32[]{:S(2)}, u32[]{:S(2)}) %collective-permute-start.11) | collective-permute-done | bytes 65568 | tf_op jit(solution)/shard_map/ppermute | solution.py:438
  53.0 1.4 %collective-permute-start.12 = (f32[2,16,4,256]{3,2,1,0:T(4,128)S(1)}, f32[2,16,4,256]{3,2,1,0:T(4,128)S(1)}, u32[]{:S(2)}, u32[]{:S(2)}) collective-permute-start(f32[2,16,4,256]{3,2,1,0:T(4,128)S(1)} %pad_maximum_fusion.3), channel_id=1, source_target_pairs={{0,2},{1,3},{2,0},{3,1},{4,6},{5,7},{6,4},{7,5},{8,10},{9,11},{10,... | collective-permute-start | bytes 393224 | tf_op jit(solution)/shard_map/ppermute | solution.py:438
  54.4 2.0 %shard_map.135 = (f32[4,64,256]{2,1,0:T(8,128)S(1)}, f32[4,64,256]{2,1,0:T(8,128)S(1)}, f32[4,64,256]{2,1,0:T(8,128)S(1)}, f32[4,64,256]{2,1,0:T(8,128)S(1)}) custom-call(s32[2]{0:T(128)S(1)} %pad_add_fusion.ids, f32[4,1]{1,0:T(4,128)S(1)} %copy-done.7, f32[64,1]{1,0:T(8,128)S(1)} %copy-done.4, f32[1,1024]{1,0:T(1,128)S(1)} %copy-done.5, ...), custom_call_target="tpu_custom_call" | custom-call | flops 26214400 | bytes 1708824 | tf_op jit(solution)/shard_map/pallas_call | solution.py:73
  56.4 1.6 %collective-permute-start.17 = (f32[4,64,256]{2,1,0:T(8,128)S(1)}, f32[4,64,256]{2,1,0:T(8,128)S(1)}, u32[]{:S(2)}, u32[]{:S(2)}) collective-permute-start(f32[4,64,256]{2,1,0:T(8,128)S(1)} %get-tuple-element.58), channel_id=1, source_target_pairs={{0,4},{4,0},{8,12},{12,8},{16,20},{20,16},{24,28},{28,24},{1,5},{5... | collective-permute-start | bytes 786440 | tf_op jit(solution)/shard_map/ppermute | solution.py:438
  58.0 15.3 %collective-permute-start.18 = (f32[4,64,256]{2,1,0:T(8,128)S(1)}, f32[4,64,256]{2,1,0:T(8,128)S(1)}, u32[]{:S(2)}, u32[]{:S(2)}) collective-permute-start(f32[4,64,256]{2,1,0:T(8,128)S(1)} %get-tuple-element.59), channel_id=1, source_target_pairs={{0,8},{4,12},{8,0},{12,4},{16,24},{20,28},{24,16},{28,20},{1,9},{5... | collective-permute-start | bytes 786440 | tf_op jit(solution)/shard_map/ppermute | solution.py:438
  74.4 11.3 %collective-permute-done.13.refs_6_ = f32[16,4,256]{2,1,0:T(4,128)S(1)} collective-permute-done((f32[16,4,256]{2,1,0:T(4,128)S(1)}, f32[16,4,256]{2,1,0:T(4,128)S(1)}, u32[]{:S(2)}, u32[]{:S(2)}) %collective-permute-start.13) | collective-permute-done | bytes 65568 | tf_op jit(solution)/shard_map/ppermute | solution.py:438
  85.7 2.2 %shard_map.134 = (f32[4,64,256]{2,1,0:T(8,128)S(1)}, f32[4,64,256]{2,1,0:T(8,128)S(1)}, f32[4,64,256]{2,1,0:T(8,128)S(1)}, f32[4,64,256]{2,1,0:T(8,128)S(1)}) custom-call(s32[2]{0:T(128)S(1)} %pad_add_fusion.ids, f32[4,1]{1,0:T(4,128)S(1)} %copy-done.6, f32[64,1]{1,0:T(8,128)S(1)} %copy-done.4, f32[1,1024]{1,0:T(1,128)S(1)} %copy-done.5, ...), custom_call_target="tpu_custom_call" | custom-call | flops 26214400 | bytes 1708824 | tf_op jit(solution)/shard_map/pallas_call | solution.py:73
  88.4 6.6 %collective-permute-start.15 = (f32[4,64,256]{2,1,0:T(8,128)S(1)}, f32[4,64,256]{2,1,0:T(8,128)S(1)}, u32[]{:S(2)}, u32[]{:S(2)}) collective-permute-start(f32[4,64,256]{2,1,0:T(8,128)S(1)} %get-tuple-element.55), channel_id=1, source_target_pairs={{0,8},{4,12},{8,0},{12,4},{16,24},{20,28},{24,16},{28,20},{1,9},{5... | collective-permute-start | bytes 786440 | tf_op jit(solution)/shard_map/ppermute | solution.py:438
  95.0 2.8 %shard_map.136.refs_4_ = f32[4,64,1024]{2,1,0:T(8,128)S(1)} custom-call(s32[2]{0:T(128)S(1)} %pad_add_fusion.ids, bf16[2,2,256,256]{3,2,1,0:T(8,128)(2,1)S(1)} %copy-done, bf16[1024,1024]{1,0:T(8,128)(2,1)S(1)} %get-tuple-element.33.sxh, bf16[1024,1024]{1,0:T(8,128)(2,1)S(1)} %get-tuple-element.34.sxl, f32[4,64,256]{2,1,0:T(8,128)S(1)} %get-tuple-element.57.refs_0_, ...), custom_call_target="tpu_custom_call" | custom-call | flops 2013265920 | bytes 5767176 | tf_op jit(solution)/shard_map/pallas_call | solution.py:73
  97.9 4.3 %collective-permute-done.15.refs_2_ = f32[4,64,256]{2,1,0:T(8,128)S(1)} collective-permute-done((f32[4,64,256]{2,1,0:T(8,128)S(1)}, f32[4,64,256]{2,1,0:T(8,128)S(1)}, u32[]{:S(2)}, u32[]{:S(2)}) %collective-permute-start.15) | collective-permute-done | bytes 262176 | tf_op jit(solution)/shard_map/ppermute | solution.py:438
  102.2 3.1 %collective-permute-done.16.refs_3_ = f32[4,64,256]{2,1,0:T(8,128)S(1)} collective-permute-done((f32[4,64,256]{2,1,0:T(8,128)S(1)}, f32[4,64,256]{2,1,0:T(8,128)S(1)}, u32[]{:S(2)}, u32[]{:S(2)}) %collective-permute-start.16) | collective-permute-done | bytes 262176 | tf_op jit(solution)/shard_map/ppermute | solution.py:438
  105.3 4.0 %shard_map.137 = f32[8,64,1024]{2,1,0:T(8,128)} custom-call(s32[2]{0:T(128)S(1)} %pad_add_fusion.ids, bf16[2,2,256,256]{3,2,1,0:T(8,128)(2,1)S(1)} %copy-done, bf16[1024,1024]{1,0:T(8,128)(2,1)S(1)} %get-tuple-element.33.sxh, bf16[1024,1024]{1,0:T(8,128)(2,1)S(1)} %get-tuple-element.34.sxl, f32[4,64,256]{2,1,0:T(8,128)S(1)} %get-tuple-element.53.refs_0_, ...), custom_call_target="tpu_custom_call" | custom-call | flops 2013265920 | bytes 6815752 | tf_op jit(solution)/shard_map/pallas_call | solution.py:73
  (46 shorter events, 2.7 us)
Async XLA Ops:
  0.1 1.0 copy-start.10
  1.1 1.7 %copy-start.8 = (f32[1,8,64,1024]{3,2,1,0:T(8,128)S(1)}, f32[1,8,64,1024]{3,2,1,0:T(8,128)}, u32[]{:S(2)}) copy-start(f32[1,8,64,1024]{3,2,1,0:T(8,128)} %param.13) | copy-start | bytes 6291460
  1.1 1.7 %copy-start.9 = (bf16[2,2,256,256]{3,2,1,0:T(8,128)(2,1)S(1)}, bf16[2,2,256,256]{3,2,1,0:T(8,128)(2,1)}, u32[]{:S(2)}) copy-start(bf16[2,2,256,256]{3,2,1,0:T(8,128)(2,1)} %constant.51.both) | copy-start | bytes 1572868
  5.7 11.1 %collective-permute-start = (f32[4,64,256]{2,1,0:T(8,128)S(1)}, f32[4,64,256]{2,1,0:T(8,128)S(1)}, u32[]{:S(2)}, u32[]{:S(2)}) collective-permute-start(f32[4,64,256]{2,1,0:T(8,128)S(1)} %get-tuple-element.39), channel_id=1, source_target_pairs={{0,4},{4,0},{8,12},{12,8},{16,20},{20,16},{24,28},{28,24},{1,5},{5... | collective-permute-start | bytes 786440 | tf_op jit(solution)/shard_map/ppermute | solution.py:438
  8.7 9.2 %collective-permute-start.1 = (f32[4,64,256]{2,1,0:T(8,128)S(1)}, f32[4,64,256]{2,1,0:T(8,128)S(1)}, u32[]{:S(2)}, u32[]{:S(2)}) collective-permute-start(f32[4,64,256]{2,1,0:T(8,128)S(1)} %get-tuple-element.40), channel_id=1, source_target_pairs={{0,8},{4,12},{8,0},{12,4},{16,24},{20,28},{24,16},{28,20},{1,9},{5... | collective-permute-start | bytes 786440 | tf_op jit(solution)/shard_map/ppermute | solution.py:438
  10.3 12.8 %copy-start.3 = (f32[64,2]{1,0:T(8,128)S(1)}, f32[64,2]{1,0:T(8,128)}, u32[]{:S(2)}) copy-start(f32[64,2]{1,0:T(8,128)} %constant.35.clone.edges) | copy-start | bytes 1540
  10.3 12.8 %copy-start.4 = (f32[64,1]{1,0:T(8,128)S(1)}, f32[64,1]{1,0:T(8,128)}, u32[]{:S(2)}) copy-start(f32[64,1]{1,0:T(8,128)} %constant.33.clone.smu_y) | copy-start | bytes 772
  10.3 12.8 %copy-start.5 = (f32[1,1024]{1,0:T(1,128)S(1)}, f32[1,1024]{1,0:T(1,128)}, u32[]{:S(2)}) copy-start(f32[1,1024]{1,0:T(1,128)} %constant.34.clone.smu_x) | copy-start | bytes 12292
  10.3 12.8 %copy-start.7 = (f32[4,1]{1,0:T(4,128)S(1)}, f32[4,1]{1,0:T(4,128)}, u32[]{:S(2)}) copy-start(f32[4,1]{1,0:T(4,128)} %constant.41.clone.smu_z) | copy-start | bytes 52
  10.3 12.8 %collective-permute-start.2 = (f32[4,64,256]{2,1,0:T(8,128)S(1)}, f32[4,64,256]{2,1,0:T(8,128)S(1)}, u32[]{:S(2)}, u32[]{:S(2)}) collective-permute-start(f32[4,64,256]{2,1,0:T(8,128)S(1)} %get-tuple-element.41), channel_id=1, source_target_pairs={{0,12},{4,8},{8,4},{12,0},{16,28},{20,24},{24,20},{28,16},{1,13},{... | collective-permute-start | bytes 786440 | tf_op jit(solution)/shard_map/ppermute | solution.py:438
  13.2 14.9 %collective-permute-start.3 = (f32[4,64,256]{2,1,0:T(8,128)S(1)}, f32[4,64,256]{2,1,0:T(8,128)S(1)}, u32[]{:S(2)}, u32[]{:S(2)}) collective-permute-start(f32[4,64,256]{2,1,0:T(8,128)S(1)} %get-tuple-element.43), channel_id=1, source_target_pairs={{0,4},{4,0},{8,12},{12,8},{16,20},{20,16},{24,28},{28,24},{1,5},{5... | collective-permute-start | bytes 786440 | tf_op jit(solution)/shard_map/ppermute | solution.py:438
  15.2 15.8 %collective-permute-start.4 = (f32[4,64,256]{2,1,0:T(8,128)S(1)}, f32[4,64,256]{2,1,0:T(8,128)S(1)}, u32[]{:S(2)}, u32[]{:S(2)}) collective-permute-start(f32[4,64,256]{2,1,0:T(8,128)S(1)} %get-tuple-element.44), channel_id=1, source_target_pairs={{0,8},{4,12},{8,0},{12,4},{16,24},{20,28},{24,16},{28,20},{1,9},{5... | collective-permute-start | bytes 786440 | tf_op jit(solution)/shard_map/ppermute | solution.py:438
  16.8 21.4 %copy-start.2 = (f32[5,4,4,1024]{3,2,1,0:T(4,128)S(1)}, f32[5,4,4,1024]{3,2,1,0:T(4,128)}, u32[]{:S(2)}) copy-start(f32[5,4,4,1024]{3,2,1,0:T(4,128)} %constant.43.clone.responses) | copy-start | bytes 983044
  16.8 27.7 %copy-start.6 = (f32[4,1]{1,0:T(4,128)S(1)}, f32[4,1]{1,0:T(4,128)}, u32[]{:S(2)}) copy-start(f32[4,1]{1,0:T(4,128)} %constant.42.clone.smu_z) | copy-start | bytes 52
  25.0 26.7 %collective-permute-start.6 = (f32[2,4,64,256]{3,2,1,0:T(8,128)S(1)}, f32[2,4,64,256]{3,2,1,0:T(8,128)S(1)}, u32[]{:S(2)}, u32[]{:S(2)}) collective-permute-start(f32[2,4,64,256]{3,2,1,0:T(8,128)S(1)} %get-tuple-element.49), channel_id=1, source_target_pairs={{0,16},{4,20},{8,24},{12,28},{16,0},{20,4},{24,8},{28,12},{1,17},{... | collective-permute-start | bytes 1572872 | tf_op jit(solution)/shard_map/ppermute | solution.py:438
  31.0 1.3 %collective-permute-start.7 = (f32[1,16,4,256]{3,2,1,0:T(4,128)S(1)}, f32[1,16,4,256]{3,2,1,0:T(4,128)S(1)}, u32[]{:S(2)}, u32[]{:S(2)}) collective-permute-start(f32[1,16,4,256]{3,2,1,0:T(4,128)S(1)} %bitcast.9), channel_id=1, source_target_pairs={{0,1},{1,0},{2,3},{3,2},{4,5},{5,4},{6,7},{7,6},{8,9},{9,8},{10,11... | collective-permute-start | bytes 196616 | tf_op jit(solution)/shard_map/ppermute | solution.py:438
  31.0 13.5 %collective-permute-start.5 = (f32[4,64,256]{2,1,0:T(8,128)S(1)}, f32[4,64,256]{2,1,0:T(8,128)S(1)}, u32[]{:S(2)}, u32[]{:S(2)}) collective-permute-start(f32[4,64,256]{2,1,0:T(8,128)S(1)} %get-tuple-element.47), channel_id=1, source_target_pairs={{0,12},{4,8},{8,4},{12,0},{16,28},{20,24},{24,20},{28,16},{1,13},{... | collective-permute-start | bytes 786440 | tf_op jit(solution)/shard_map/ppermute | solution.py:438
  32.3 5.8 %collective-permute-start.8 = (f32[2,16,4,256]{3,2,1,0:T(4,128)S(1)}, f32[2,16,4,256]{3,2,1,0:T(4,128)S(1)}, u32[]{:S(2)}, u32[]{:S(2)}) collective-permute-start(f32[2,16,4,256]{3,2,1,0:T(4,128)S(1)} %pad_maximum_fusion.2), channel_id=1, source_target_pairs={{0,2},{1,3},{2,0},{3,1},{4,6},{5,7},{6,4},{7,5},{8,10},{9,11},{10,... | collective-permute-start | bytes 393224 | tf_op jit(solution)/shard_map/ppermute | solution.py:438
  39.0 34.4 %copy-start.1 = (f32[5,4,4,1024]{3,2,1,0:T(4,128)S(1)}, f32[5,4,4,1024]{3,2,1,0:T(4,128)}, u32[]{:S(2)}) copy-start(f32[5,4,4,1024]{3,2,1,0:T(4,128)} %constant.44.clone.responses) | copy-start | bytes 983044
  39.0 12.7 %collective-permute-start.9 = (f32[16,4,256]{2,1,0:T(4,128)S(1)}, f32[16,4,256]{2,1,0:T(4,128)S(1)}, u32[]{:S(2)}, u32[]{:S(2)}) collective-permute-start(f32[16,4,256]{2,1,0:T(4,128)S(1)} %shard_map.132.refs_5_), channel_id=1, source_target_pairs={{0,16},{4,20},{8,24},{12,28},{16,0},{20,4},{24,8},{28,12},{1,17},{... | collective-permute-start | bytes 196616 | tf_op jit(solution)/shard_map/ppermute | solution.py:438
  51.7 34.0 %collective-permute-start.10 = (f32[2,4,64,256]{3,2,1,0:T(8,128)S(1)}, f32[2,4,64,256]{3,2,1,0:T(8,128)S(1)}, u32[]{:S(2)}, u32[]{:S(2)}) collective-permute-start(f32[2,4,64,256]{3,2,1,0:T(8,128)S(1)} %get-tuple-element.51), channel_id=1, source_target_pairs={{0,16},{4,20},{8,24},{12,28},{16,0},{20,4},{24,8},{28,12},{1,17},{... | collective-permute-start | bytes 1572872 | tf_op jit(solution)/shard_map/ppermute | solution.py:438
  51.7 1.3 %collective-permute-start.11 = (f32[1,16,4,256]{3,2,1,0:T(4,128)S(1)}, f32[1,16,4,256]{3,2,1,0:T(4,128)S(1)}, u32[]{:S(2)}, u32[]{:S(2)}) collective-permute-start(f32[1,16,4,256]{3,2,1,0:T(4,128)S(1)} %bitcast.6), channel_id=1, source_target_pairs={{0,1},{1,0},{2,3},{3,2},{4,5},{5,4},{6,7},{7,6},{8,9},{9,8},{10,11... | collective-permute-start | bytes 196616 | tf_op jit(solution)/shard_map/ppermute | solution.py:438
  53.0 42.0 %copy-start = (bf16[2,2,256,256]{3,2,1,0:T(8,128)(2,1)S(1)}, bf16[2,2,256,256]{3,2,1,0:T(8,128)(2,1)}, u32[]{:S(2)}) copy-start(bf16[2,2,256,256]{3,2,1,0:T(8,128)(2,1)} %constant.48.both) | copy-start | bytes 1572868
  53.0 20.3 %collective-permute-start.12 = (f32[2,16,4,256]{3,2,1,0:T(4,128)S(1)}, f32[2,16,4,256]{3,2,1,0:T(4,128)S(1)}, u32[]{:S(2)}, u32[]{:S(2)}) collective-permute-start(f32[2,16,4,256]{3,2,1,0:T(4,128)S(1)} %pad_maximum_fusion.3), channel_id=1, source_target_pairs={{0,2},{1,3},{2,0},{3,1},{4,6},{5,7},{6,4},{7,5},{8,10},{9,11},{10,... | collective-permute-start | bytes 393224 | tf_op jit(solution)/shard_map/ppermute | solution.py:438
  56.4 38.6 %collective-permute-start.17 = (f32[4,64,256]{2,1,0:T(8,128)S(1)}, f32[4,64,256]{2,1,0:T(8,128)S(1)}, u32[]{:S(2)}, u32[]{:S(2)}) collective-permute-start(f32[4,64,256]{2,1,0:T(8,128)S(1)} %get-tuple-element.58), channel_id=1, source_target_pairs={{0,4},{4,0},{8,12},{12,8},{16,20},{20,16},{24,28},{28,24},{1,5},{5... | collective-permute-start | bytes 786440 | tf_op jit(solution)/shard_map/ppermute | solution.py:438
  58.0 37.0 %collective-permute-start.18 = (f32[4,64,256]{2,1,0:T(8,128)S(1)}, f32[4,64,256]{2,1,0:T(8,128)S(1)}, u32[]{:S(2)}, u32[]{:S(2)}) collective-permute-start(f32[4,64,256]{2,1,0:T(8,128)S(1)} %get-tuple-element.59), channel_id=1, source_target_pairs={{0,8},{4,12},{8,0},{12,4},{16,24},{20,28},{24,16},{28,20},{1,9},{5... | collective-permute-start | bytes 786440 | tf_op jit(solution)/shard_map/ppermute | solution.py:438
  73.3 21.7 %collective-permute-start.19 = (f32[4,64,256]{2,1,0:T(8,128)S(1)}, f32[4,64,256]{2,1,0:T(8,128)S(1)}, u32[]{:S(2)}, u32[]{:S(2)}) collective-permute-start(f32[4,64,256]{2,1,0:T(8,128)S(1)} %get-tuple-element.60), channel_id=1, source_target_pairs={{0,12},{4,8},{8,4},{12,0},{16,28},{20,24},{24,20},{28,16},{1,13},{... | collective-permute-start | bytes 786440 | tf_op jit(solution)/shard_map/ppermute | solution.py:438
  74.3 11.4 %collective-permute-start.13 = (f32[16,4,256]{2,1,0:T(4,128)S(1)}, f32[16,4,256]{2,1,0:T(4,128)S(1)}, u32[]{:S(2)}, u32[]{:S(2)}) collective-permute-start(f32[16,4,256]{2,1,0:T(4,128)S(1)} %shard_map.133.refs_5_), channel_id=1, source_target_pairs={{0,16},{4,20},{8,24},{12,28},{16,0},{20,4},{24,8},{28,12},{1,17},{... | collective-permute-start | bytes 196616 | tf_op jit(solution)/shard_map/ppermute | solution.py:438
  87.9 10.0 %collective-permute-start.14 = (f32[4,64,256]{2,1,0:T(8,128)S(1)}, f32[4,64,256]{2,1,0:T(8,128)S(1)}, u32[]{:S(2)}, u32[]{:S(2)}) collective-permute-start(f32[4,64,256]{2,1,0:T(8,128)S(1)} %get-tuple-element.54), channel_id=1, source_target_pairs={{0,4},{4,0},{8,12},{12,8},{16,20},{20,16},{24,28},{28,24},{1,5},{5... | collective-permute-start | bytes 786440 | tf_op jit(solution)/shard_map/ppermute | solution.py:438
  88.4 13.8 %collective-permute-start.15 = (f32[4,64,256]{2,1,0:T(8,128)S(1)}, f32[4,64,256]{2,1,0:T(8,128)S(1)}, u32[]{:S(2)}, u32[]{:S(2)}) collective-permute-start(f32[4,64,256]{2,1,0:T(8,128)S(1)} %get-tuple-element.55), channel_id=1, source_target_pairs={{0,8},{4,12},{8,0},{12,4},{16,24},{20,28},{24,16},{28,20},{1,9},{5... | collective-permute-start | bytes 786440 | tf_op jit(solution)/shard_map/ppermute | solution.py:438
  95.0 10.3 %collective-permute-start.16 = (f32[4,64,256]{2,1,0:T(8,128)S(1)}, f32[4,64,256]{2,1,0:T(8,128)S(1)}, u32[]{:S(2)}, u32[]{:S(2)}) collective-permute-start(f32[4,64,256]{2,1,0:T(8,128)S(1)} %get-tuple-element.56), channel_id=1, source_target_pairs={{0,12},{4,8},{8,4},{12,0},{16,28},{20,24},{24,20},{28,16},{1,13},{... | collective-permute-start | bytes 786440 | tf_op jit(solution)/shard_map/ppermute | solution.py:438

commit v12 on v7

--- a/solution.py
+++ b/solution.py
@@ -173,21 +173,20 @@
     outs, (high, low) = refs[len(ready) : -2], refs[-2:]
     folds = plan.folds
     shape = folds, plan.rows, plan.block
+    total = None
     for k in range(plan.half):
-        piece = pieces[k][...].reshape(len(chunk) * plan.rows, plan.block)
-        high[k], low[k] = parts_of(piece)
+        at = plan.columns(place ^ k)
+        piece = parts_of(pieces[k][...].reshape(-1, plan.block))
+        value = dot_parts(piece, (sxh[at, :], sxl[at, :]))
+        total = value if total is None else total + value
+    high[...], low[...] = parts_of(total)
     for j in range(plan.half):
         columns = pl.ds(j * plan.block, plan.block)
-        total = None
-        for k in range(plan.half):
-            at = plan.columns(place ^ k)
-            value = dot_parts((high[k], low[k]), (sxh[at, columns], sxl[at, columns]))
-            total = value if total is None else total + value
-        total = parts_of(total)
         sums = {parity: before[parity][:, :, columns] for parity in ready}
         for parity, rows, at in by_parity(plan, chunk):
             table = both[0, parity, :, at], both[1, parity, :, at]
-            value = dot_parts(table, (total[0][rows], total[1][rows])).reshape(shape)
+            value = dot_parts(table, (high[rows, columns], low[rows, columns]))
+            value = value.reshape(shape)
             sums[parity] = sums[parity] + value if parity in sums else value
         if not last:
             for parity, out in zip(sorted(sums), outs):
@@ -503,7 +502,7 @@
         )
         pieces = [swap(v, "tm", steps, k) for k, v in enumerate(pieces)]
         last = chunk == CHUNKS[-1]
-        part = pltpu.VMEM((half, len(chunk) * plan.rows, plan.block), jnp.bfloat16)
+        part = pltpu.VMEM((len(chunk) * plan.rows, plan.width), jnp.bfloat16)
         hold = [part, part]
         if last:
             block = field.shape[:2] + (plan.block,)

time: 101 us -> 98.8 us (0.978)
  Pallas kernels: 28.3 us -> 23.9 us
  waiting for transfers between devices: 43.9 us -> 46.3 us
    pallas_call x11, Pallas kernels: 28.3 us -> 23.9 us  [call(): pl.pallas_call(kernel, out_shape=out_shape, in_specs=[smem] + [vmem] * (l...]
    ppermute x22, waiting for transfers between devices: 43.9 us -> 46.3 us  [swap(): return lax.ppermute(values, axis, [(i, i ^ distance) for i in range(count)])]
  transfers between devices with their start and end apart: 22 -> 22, of which waited for: 15 -> 15; matrix products, arithmetic and copies ran while one was open for 0% -> 0% of each run, Pallas kernels for 16% -> 14%
where the time goes in v12:
time: 98.8 us; the launch traced here: 98.6 us
  waiting for transfers between devices  46.3 us (47%)
  starting transfers between devices  26.9 us (27%)
  Pallas kernels  23.9 us (24%)
  local copies, waits for them, and re-layouts  1.09 us (1%)
    ppermute x22, waiting for transfers between devices, swap(): return lax.ppermute(values, axis, [(i, i ^ distance) for i in range(count)])  46.3 us
    ppermute x22, starting transfers between devices, swap(): return lax.ppermute(values, axis, [(i, i ^ distance) for i in range(count)])  26.9 us
    pallas_call x11, Pallas kernels, call(): pl.pallas_call(kernel, out_shape=out_shape, in_specs=[smem] + [vmem] * (l...  23.9 us
  transfers between devices with their start and end apart: 22, of which 15 were waited for; matrix products, arithmetic and copies ran while one was open for 0% of the time, Pallas kernels for 14%

profile of v12, /device:TPU:0, one launch (start us, length us, event | category | flops | bytes accessed | tf_op | source)
XLA Modules:
  0.0 98.6 jit_solution(11235492476981011145)
XLA Ops:
  1.1 1.7 %shard_map.127 = (bf16[1024,1024]{1,0:T(8,128)(2,1)S(1)}, bf16[1024,1024]{1,0:T(8,128)(2,1)S(1)}) custom-call(s32[2]{0:T(128)S(1)} %pad_add_fusion.ids, f32[128,1024]{1,0:T(8,128)S(1)} %copy-done.10), custom_call_target="tpu_custom_call" | custom-call | flops 4194304000 | bytes 524296 | tf_op jit(solution)/shard_map/pallas_call | solution.py:73
  2.9 2.8 %shard_map.128 = (f32[4,64,256]{2,1,0:T(8,128)S(1)}, f32[4,64,256]{2,1,0:T(8,128)S(1)}, f32[4,64,256]{2,1,0:T(8,128)S(1)}, f32[4,64,256]{2,1,0:T(8,128)S(1)}) custom-call(s32[2]{0:T(128)S(1)} %pad_add_fusion.ids, bf16[2,2,256,256]{3,2,1,0:T(8,128)(2,1)S(1)} %copy-done.9, f32[8,64,1024]{2,1,0:T(8,128)S(1)} %bitcast.4, ...), custom_call_target="tpu_custom_call" | custom-call | flops 2013265920 | bytes 6815752 | tf_op jit(solution)/shard_map/pallas_call | solution.py:73
  5.7 3.0 %collective-permute-start.3 = (f32[4,64,256]{2,1,0:T(8,128)S(1)}, f32[4,64,256]{2,1,0:T(8,128)S(1)}, u32[]{:S(2)}, u32[]{:S(2)}) collective-permute-start(f32[4,64,256]{2,1,0:T(8,128)S(1)} %get-tuple-element.40), channel_id=1, source_target_pairs={{0,4},{4,0},{8,12},{12,8},{16,20},{20,16},{24,28},{28,24},{1,5},{5... | collective-permute-start | bytes 786440 | tf_op jit(solution)/shard_map/ppermute | solution.py:434
  8.7 1.6 %collective-permute-start.4 = (f32[4,64,256]{2,1,0:T(8,128)S(1)}, f32[4,64,256]{2,1,0:T(8,128)S(1)}, u32[]{:S(2)}, u32[]{:S(2)}) collective-permute-start(f32[4,64,256]{2,1,0:T(8,128)S(1)} %get-tuple-element.41), channel_id=1, source_target_pairs={{0,8},{4,12},{8,0},{12,4},{16,24},{20,28},{24,16},{28,20},{1,9},{5... | collective-permute-start | bytes 786440 | tf_op jit(solution)/shard_map/ppermute | solution.py:434
  10.4 2.8 %shard_map.129 = (f32[4,64,256]{2,1,0:T(8,128)S(1)}, f32[4,64,256]{2,1,0:T(8,128)S(1)}, f32[4,64,256]{2,1,0:T(8,128)S(1)}, f32[4,64,256]{2,1,0:T(8,128)S(1)}) custom-call(s32[2]{0:T(128)S(1)} %pad_add_fusion.ids, bf16[2,2,256,256]{3,2,1,0:T(8,128)(2,1)S(1)} %copy-done.9, f32[8,64,1024]{2,1,0:T(8,128)S(1)} %bitcast.5, ...), custom_call_target="tpu_custom_call" | custom-call | flops 2013265920 | bytes 6815752 | tf_op jit(solution)/shard_map/pallas_call | solution.py:73
  13.3 1.8 %collective-permute-done.3.refs_1_ = f32[4,64,256]{2,1,0:T(8,128)S(1)} collective-permute-done((f32[4,64,256]{2,1,0:T(8,128)S(1)}, f32[4,64,256]{2,1,0:T(8,128)S(1)}, u32[]{:S(2)}, u32[]{:S(2)}) %collective-permute-start.3) | collective-permute-done | bytes 262176 | tf_op jit(solution)/shard_map/ppermute | solution.py:434
  15.0 2.9 %collective-permute-done.4.refs_2_ = f32[4,64,256]{2,1,0:T(8,128)S(1)} collective-permute-done((f32[4,64,256]{2,1,0:T(8,128)S(1)}, f32[4,64,256]{2,1,0:T(8,128)S(1)}, u32[]{:S(2)}, u32[]{:S(2)}) %collective-permute-start.4) | collective-permute-done | bytes 262176 | tf_op jit(solution)/shard_map/ppermute | solution.py:434
  18.0 3.9 %collective-permute-done.5.refs_3_ = f32[4,64,256]{2,1,0:T(8,128)S(1)} collective-permute-done((f32[4,64,256]{2,1,0:T(8,128)S(1)}, f32[4,64,256]{2,1,0:T(8,128)S(1)}, u32[]{:S(2)}, u32[]{:S(2)}) %collective-permute-start.5) | collective-permute-done | bytes 262176 | tf_op jit(solution)/shard_map/ppermute | solution.py:434
  21.9 1.9 %shard_map.131 = (f32[2,4,64,256]{3,2,1,0:T(8,128)S(1)}, f32[16,4,256]{2,1,0:T(4,128)S(1)}) custom-call(s32[2]{0:T(128)S(1)} %pad_add_fusion.ids, f32[4,1]{1,0:T(4,128)S(1)} %copy-done.7, f32[64,1]{1,0:T(8,128)S(1)} %copy-done.2, f32[1,1024]{1,0:T(1,128)S(1)} %copy-done.5, f32[64,2]{1,0:T(8,128)S(1)} %copy-done.1, ...), custom_call_target="tpu_custom_call" | custom-call | flops 26214400 | bytes 1053464 | tf_op jit(solution)/shard_map/pallas_call | solution.py:73
  23.9 2.8 %collective-permute-start.6 = (f32[2,4,64,256]{3,2,1,0:T(8,128)S(1)}, f32[2,4,64,256]{3,2,1,0:T(8,128)S(1)}, u32[]{:S(2)}, u32[]{:S(2)}) collective-permute-start(f32[2,4,64,256]{3,2,1,0:T(8,128)S(1)} %get-tuple-element.43), channel_id=1, source_target_pairs={{0,16},{4,20},{8,24},{12,28},{16,0},{20,4},{24,8},{28,12},{1,17},{... | collective-permute-start | bytes 1572872 | tf_op jit(solution)/shard_map/ppermute | solution.py:434
  26.7 1.5 %collective-permute-start = (f32[4,64,256]{2,1,0:T(8,128)S(1)}, f32[4,64,256]{2,1,0:T(8,128)S(1)}, u32[]{:S(2)}, u32[]{:S(2)}) collective-permute-start(f32[4,64,256]{2,1,0:T(8,128)S(1)} %get-tuple-element.35), channel_id=1, source_target_pairs={{0,4},{4,0},{8,12},{12,8},{16,20},{20,16},{24,28},{28,24},{1,5},{5... | collective-permute-start | bytes 786440 | tf_op jit(solution)/shard_map/ppermute | solution.py:434
  28.2 1.6 %collective-permute-start.1 = (f32[4,64,256]{2,1,0:T(8,128)S(1)}, f32[4,64,256]{2,1,0:T(8,128)S(1)}, u32[]{:S(2)}, u32[]{:S(2)}) collective-permute-start(f32[4,64,256]{2,1,0:T(8,128)S(1)} %get-tuple-element.36), channel_id=1, source_target_pairs={{0,8},{4,12},{8,0},{12,4},{16,24},{20,28},{24,16},{28,20},{1,9},{5... | collective-permute-start | bytes 786440 | tf_op jit(solution)/shard_map/ppermute | solution.py:434
  30.1 4.3 %collective-permute-done.9.refs_3_ = f32[16,4,256]{2,1,0:T(4,128)S(1)} collective-permute-done((f32[16,4,256]{2,1,0:T(4,128)S(1)}, f32[16,4,256]{2,1,0:T(4,128)S(1)}, u32[]{:S(2)}, u32[]{:S(2)}) %collective-permute-start.9) | collective-permute-done | bytes 65568 | tf_op jit(solution)/shard_map/ppermute | solution.py:434
  35.3 3.4 %collective-permute-done.8.refs_2_ = f32[16,4,256]{2,1,0:T(4,128)S(1)} collective-permute-done((f32[16,4,256]{2,1,0:T(4,128)S(1)}, f32[16,4,256]{2,1,0:T(4,128)S(1)}, u32[]{:S(2)}, u32[]{:S(2)}) %collective-permute-start.8) | collective-permute-done | bytes 65568 | tf_op jit(solution)/shard_map/ppermute | solution.py:434
  38.8 1.3 %collective-permute-done.7.refs_1_ = f32[16,4,256]{2,1,0:T(4,128)S(1)} collective-permute-done((f32[16,4,256]{2,1,0:T(4,128)S(1)}, f32[16,4,256]{2,1,0:T(4,128)S(1)}, u32[]{:S(2)}, u32[]{:S(2)}) %collective-permute-start.7) | collective-permute-done | bytes 65568 | tf_op jit(solution)/shard_map/ppermute | solution.py:434
  41.0 3.6 %collective-permute-done.1.refs_2_ = f32[4,64,256]{2,1,0:T(8,128)S(1)} collective-permute-done((f32[4,64,256]{2,1,0:T(8,128)S(1)}, f32[4,64,256]{2,1,0:T(8,128)S(1)}, u32[]{:S(2)}, u32[]{:S(2)}) %collective-permute-start.1) | collective-permute-done | bytes 262176 | tf_op jit(solution)/shard_map/ppermute | solution.py:434
  44.6 4.6 %collective-permute-done.2.refs_3_ = f32[4,64,256]{2,1,0:T(8,128)S(1)} collective-permute-done((f32[4,64,256]{2,1,0:T(8,128)S(1)}, f32[4,64,256]{2,1,0:T(8,128)S(1)}, u32[]{:S(2)}, u32[]{:S(2)}) %collective-permute-start.2) | collective-permute-done | bytes 262176 | tf_op jit(solution)/shard_map/ppermute | solution.py:434
  49.3 1.9 %shard_map.130 = (f32[2,4,64,256]{3,2,1,0:T(8,128)S(1)}, f32[16,4,256]{2,1,0:T(4,128)S(1)}) custom-call(s32[2]{0:T(128)S(1)} %pad_add_fusion.ids, f32[4,1]{1,0:T(4,128)S(1)} %copy-done.6, f32[64,1]{1,0:T(8,128)S(1)} %copy-done.2, f32[1,1024]{1,0:T(1,128)S(1)} %copy-done.5, f32[64,2]{1,0:T(8,128)S(1)} %copy-done.1, ...), custom_call_target="tpu_custom_call" | custom-call | flops 26214400 | bytes 1053464 | tf_op jit(solution)/shard_map/pallas_call | solution.py:73
  51.8 2.2 %collective-permute-start.11 = (f32[2,4,64,256]{3,2,1,0:T(8,128)S(1)}, f32[2,4,64,256]{3,2,1,0:T(8,128)S(1)}, u32[]{:S(2)}, u32[]{:S(2)}) collective-permute-start(f32[2,4,64,256]{3,2,1,0:T(8,128)S(1)} %get-tuple-element.45), channel_id=1, source_target_pairs={{0,16},{4,20},{8,24},{12,28},{16,0},{20,4},{24,8},{28,12},{1,17},{... | collective-permute-start | bytes 1572872 | tf_op jit(solution)/shard_map/ppermute | solution.py:434
  54.0 2.0 %shard_map.135 = (f32[4,64,256]{2,1,0:T(8,128)S(1)}, f32[4,64,256]{2,1,0:T(8,128)S(1)}, f32[4,64,256]{2,1,0:T(8,128)S(1)}, f32[4,64,256]{2,1,0:T(8,128)S(1)}) custom-call(s32[2]{0:T(128)S(1)} %pad_add_fusion.ids, f32[4,1]{1,0:T(4,128)S(1)} %copy-done.7, f32[64,1]{1,0:T(8,128)S(1)} %copy-done.2, f32[1,1024]{1,0:T(1,128)S(1)} %copy-done.5, ...), custom_call_target="tpu_custom_call" | custom-call | flops 26214400 | bytes 1708824 | tf_op jit(solution)/shard_map/pallas_call | solution.py:73
  56.9 1.5 %collective-permute-start.13 = (f32[16,4,256]{2,1,0:T(4,128)S(1)}, f32[16,4,256]{2,1,0:T(4,128)S(1)}, u32[]{:S(2)}, u32[]{:S(2)}) collective-permute-start(f32[16,4,256]{2,1,0:T(4,128)S(1)} %get-tuple-element.46.refs_0_), channel_id=1, source_target_pairs={{0,2},{1,3},{2,0},{3,1},{4,6},{5,7},{6,4},{7,5},{8,10},{9,11},{10,... | collective-permute-start | bytes 196616 | tf_op jit(solution)/shard_map/ppermute | solution.py:434
  58.4 2.2 %collective-permute-start.20 = (f32[4,64,256]{2,1,0:T(8,128)S(1)}, f32[4,64,256]{2,1,0:T(8,128)S(1)}, u32[]{:S(2)}, u32[]{:S(2)}) collective-permute-start(f32[4,64,256]{2,1,0:T(8,128)S(1)} %get-tuple-element.53), channel_id=1, source_target_pairs={{0,8},{4,12},{8,0},{12,4},{16,24},{20,28},{24,16},{28,20},{1,9},{5... | collective-permute-start | bytes 786440 | tf_op jit(solution)/shard_map/ppermute | solution.py:434
  61.2 2.2 %collective-permute-start.21 = (f32[4,64,256]{2,1,0:T(8,128)S(1)}, f32[4,64,256]{2,1,0:T(8,128)S(1)}, u32[]{:S(2)}, u32[]{:S(2)}) collective-permute-start(f32[4,64,256]{2,1,0:T(8,128)S(1)} %get-tuple-element.54), channel_id=1, source_target_pairs={{0,12},{4,8},{8,4},{12,0},{16,28},{20,24},{24,20},{28,16},{1,13},{... | collective-permute-start | bytes 786440 | tf_op jit(solution)/shard_map/ppermute | solution.py:434
  63.4 1.3 %collective-permute-done.12.refs_1_ = f32[16,4,256]{2,1,0:T(4,128)S(1)} collective-permute-done((f32[16,4,256]{2,1,0:T(4,128)S(1)}, f32[16,4,256]{2,1,0:T(4,128)S(1)}, u32[]{:S(2)}, u32[]{:S(2)}) %collective-permute-start.12) | collective-permute-done | bytes 65568 | tf_op jit(solution)/shard_map/ppermute | solution.py:434
  65.6 2.2 %collective-permute-start.15 = (f32[16,4,256]{2,1,0:T(4,128)S(1)}, f32[16,4,256]{2,1,0:T(4,128)S(1)}, u32[]{:S(2)}, u32[]{:S(2)}) collective-permute-start(f32[16,4,256]{2,1,0:T(4,128)S(1)} %shard_map.133.refs_5_), channel_id=1, source_target_pairs={{0,16},{4,20},{8,24},{12,28},{16,0},{20,4},{24,8},{28,12},{1,17},{... | collective-permute-start | bytes 196616 | tf_op jit(solution)/shard_map/ppermute | solution.py:434
  67.8 10.5 %collective-permute-done.15.refs_6_ = f32[16,4,256]{2,1,0:T(4,128)S(1)} collective-permute-done((f32[16,4,256]{2,1,0:T(4,128)S(1)}, f32[16,4,256]{2,1,0:T(4,128)S(1)}, u32[]{:S(2)}, u32[]{:S(2)}) %collective-permute-start.15) | collective-permute-done | bytes 65568 | tf_op jit(solution)/shard_map/ppermute | solution.py:434
  78.2 2.2 %shard_map.134 = (f32[4,64,256]{2,1,0:T(8,128)S(1)}, f32[4,64,256]{2,1,0:T(8,128)S(1)}, f32[4,64,256]{2,1,0:T(8,128)S(1)}, f32[4,64,256]{2,1,0:T(8,128)S(1)}) custom-call(s32[2]{0:T(128)S(1)} %pad_add_fusion.ids, f32[4,1]{1,0:T(4,128)S(1)} %copy-done.6, f32[64,1]{1,0:T(8,128)S(1)} %copy-done.2, f32[1,1024]{1,0:T(1,128)S(1)} %copy-done.5, ...), custom_call_target="tpu_custom_call" | custom-call | flops 26214400 | bytes 1708824 | tf_op jit(solution)/shard_map/pallas_call | solution.py:73
  81.0 3.1 %collective-permute-start.17 = (f32[4,64,256]{2,1,0:T(8,128)S(1)}, f32[4,64,256]{2,1,0:T(8,128)S(1)}, u32[]{:S(2)}, u32[]{:S(2)}) collective-permute-start(f32[4,64,256]{2,1,0:T(8,128)S(1)} %get-tuple-element.49), channel_id=1, source_target_pairs={{0,8},{4,12},{8,0},{12,4},{16,24},{20,28},{24,16},{28,20},{1,9},{5... | collective-permute-start | bytes 786440 | tf_op jit(solution)/shard_map/ppermute | solution.py:434
  84.1 2.8 %shard_map.136.refs_4_ = f32[4,64,1024]{2,1,0:T(8,128)S(1)} custom-call(s32[2]{0:T(128)S(1)} %pad_add_fusion.ids, bf16[2,2,256,256]{3,2,1,0:T(8,128)(2,1)S(1)} %copy-done, bf16[1024,1024]{1,0:T(8,128)(2,1)S(1)} %get-tuple-element.30.sxh, bf16[1024,1024]{1,0:T(8,128)(2,1)S(1)} %get-tuple-element.31.sxl, f32[4,64,256]{2,1,0:T(8,128)S(1)} %get-tuple-element.51.refs_0_, ...), custom_call_target="tpu_custom_call" | custom-call | flops 2013265920 | bytes 5767176 | tf_op jit(solution)/shard_map/pallas_call | solution.py:73
  87.0 4.2 %collective-permute-done.16.refs_1_ = f32[4,64,256]{2,1,0:T(8,128)S(1)} collective-permute-done((f32[4,64,256]{2,1,0:T(8,128)S(1)}, f32[4,64,256]{2,1,0:T(8,128)S(1)}, u32[]{:S(2)}, u32[]{:S(2)}) %collective-permute-start.16) | collective-permute-done | bytes 262176 | tf_op jit(solution)/shard_map/ppermute | solution.py:434
  91.3 3.1 %collective-permute-done.18.refs_3_ = f32[4,64,256]{2,1,0:T(8,128)S(1)} collective-permute-done((f32[4,64,256]{2,1,0:T(8,128)S(1)}, f32[4,64,256]{2,1,0:T(8,128)S(1)}, u32[]{:S(2)}, u32[]{:S(2)}) %collective-permute-start.18) | collective-permute-done | bytes 262176 | tf_op jit(solution)/shard_map/ppermute | solution.py:434
  94.4 4.0 %shard_map.137 = f32[8,64,1024]{2,1,0:T(8,128)} custom-call(s32[2]{0:T(128)S(1)} %pad_add_fusion.ids, bf16[2,2,256,256]{3,2,1,0:T(8,128)(2,1)S(1)} %copy-done, bf16[1024,1024]{1,0:T(8,128)(2,1)S(1)} %get-tuple-element.30.sxh, bf16[1024,1024]{1,0:T(8,128)(2,1)S(1)} %get-tuple-element.31.sxl, f32[4,64,256]{2,1,0:T(8,128)S(1)} %get-tuple-element.47.refs_0_, ...), custom_call_target="tpu_custom_call" | custom-call | flops 2013265920 | bytes 6815752 | tf_op jit(solution)/shard_map/pallas_call | solution.py:73
  (46 shorter events, 7.2 us)
Async XLA Ops:
  1.1 1.7 %copy-start.8 = (f32[1,8,64,1024]{3,2,1,0:T(8,128)S(1)}, f32[1,8,64,1024]{3,2,1,0:T(8,128)}, u32[]{:S(2)}) copy-start(f32[1,8,64,1024]{3,2,1,0:T(8,128)} %param.13) | copy-start | bytes 6291460
  1.1 1.7 %copy-start.9 = (bf16[2,2,256,256]{3,2,1,0:T(8,128)(2,1)S(1)}, bf16[2,2,256,256]{3,2,1,0:T(8,128)(2,1)}, u32[]{:S(2)}) copy-start(bf16[2,2,256,256]{3,2,1,0:T(8,128)(2,1)} %constant.51.both) | copy-start | bytes 1572868
  5.7 9.3 %collective-permute-start.3 = (f32[4,64,256]{2,1,0:T(8,128)S(1)}, f32[4,64,256]{2,1,0:T(8,128)S(1)}, u32[]{:S(2)}, u32[]{:S(2)}) collective-permute-start(f32[4,64,256]{2,1,0:T(8,128)S(1)} %get-tuple-element.40), channel_id=1, source_target_pairs={{0,4},{4,0},{8,12},{12,8},{16,20},{20,16},{24,28},{28,24},{1,5},{5... | collective-permute-start | bytes 786440 | tf_op jit(solution)/shard_map/ppermute | solution.py:434
  8.7 9.2 %collective-permute-start.4 = (f32[4,64,256]{2,1,0:T(8,128)S(1)}, f32[4,64,256]{2,1,0:T(8,128)S(1)}, u32[]{:S(2)}, u32[]{:S(2)}) collective-permute-start(f32[4,64,256]{2,1,0:T(8,128)S(1)} %get-tuple-element.41), channel_id=1, source_target_pairs={{0,8},{4,12},{8,0},{12,4},{16,24},{20,28},{24,16},{28,20},{1,9},{5... | collective-permute-start | bytes 786440 | tf_op jit(solution)/shard_map/ppermute | solution.py:434
  10.3 11.6 %copy-start.1 = (f32[64,2]{1,0:T(8,128)S(1)}, f32[64,2]{1,0:T(8,128)}, u32[]{:S(2)}) copy-start(f32[64,2]{1,0:T(8,128)} %constant.35.clone.edges) | copy-start | bytes 1540
  10.3 11.6 %copy-start.2 = (f32[64,1]{1,0:T(8,128)S(1)}, f32[64,1]{1,0:T(8,128)}, u32[]{:S(2)}) copy-start(f32[64,1]{1,0:T(8,128)} %constant.33.clone.smu_y) | copy-start | bytes 772
  10.3 11.6 %copy-start.5 = (f32[1,1024]{1,0:T(1,128)S(1)}, f32[1,1024]{1,0:T(1,128)}, u32[]{:S(2)}) copy-start(f32[1,1024]{1,0:T(1,128)} %constant.34.clone.smu_x) | copy-start | bytes 12292
  10.3 11.6 %copy-start.7 = (f32[4,1]{1,0:T(4,128)S(1)}, f32[4,1]{1,0:T(4,128)}, u32[]{:S(2)}) copy-start(f32[4,1]{1,0:T(4,128)} %constant.41.clone.smu_z) | copy-start | bytes 52
  10.3 29.7 %copy-start.4 = (f32[5,4,4,1024]{3,2,1,0:T(4,128)S(1)}, f32[5,4,4,1024]{3,2,1,0:T(4,128)}, u32[]{:S(2)}) copy-start(f32[5,4,4,1024]{3,2,1,0:T(4,128)} %constant.43.clone.responses) | copy-start | bytes 983044
  10.3 38.9 %copy-start.6 = (f32[4,1]{1,0:T(4,128)S(1)}, f32[4,1]{1,0:T(4,128)}, u32[]{:S(2)}) copy-start(f32[4,1]{1,0:T(4,128)} %constant.42.clone.smu_z) | copy-start | bytes 52
  10.3 11.6 %collective-permute-start.5 = (f32[4,64,256]{2,1,0:T(8,128)S(1)}, f32[4,64,256]{2,1,0:T(8,128)S(1)}, u32[]{:S(2)}, u32[]{:S(2)}) collective-permute-start(f32[4,64,256]{2,1,0:T(8,128)S(1)} %get-tuple-element.42), channel_id=1, source_target_pairs={{0,12},{4,8},{8,4},{12,0},{16,28},{20,24},{24,20},{28,16},{1,13},{... | collective-permute-start | bytes 786440 | tf_op jit(solution)/shard_map/ppermute | solution.py:434
  13.3 51.4 %copy-start.3 = (f32[5,4,4,1024]{3,2,1,0:T(4,128)S(1)}, f32[5,4,4,1024]{3,2,1,0:T(4,128)}, u32[]{:S(2)}) copy-start(f32[5,4,4,1024]{3,2,1,0:T(4,128)} %constant.44.clone.responses) | copy-start | bytes 983044
  23.9 27.9 %collective-permute-start.6 = (f32[2,4,64,256]{3,2,1,0:T(8,128)S(1)}, f32[2,4,64,256]{3,2,1,0:T(8,128)S(1)}, u32[]{:S(2)}, u32[]{:S(2)}) collective-permute-start(f32[2,4,64,256]{3,2,1,0:T(8,128)S(1)} %get-tuple-element.43), channel_id=1, source_target_pairs={{0,16},{4,20},{8,24},{12,28},{16,0},{20,4},{24,8},{28,12},{1,17},{... | collective-permute-start | bytes 1572872 | tf_op jit(solution)/shard_map/ppermute | solution.py:434
  26.7 14.4 %collective-permute-start = (f32[4,64,256]{2,1,0:T(8,128)S(1)}, f32[4,64,256]{2,1,0:T(8,128)S(1)}, u32[]{:S(2)}, u32[]{:S(2)}) collective-permute-start(f32[4,64,256]{2,1,0:T(8,128)S(1)} %get-tuple-element.35), channel_id=1, source_target_pairs={{0,4},{4,0},{8,12},{12,8},{16,20},{20,16},{24,28},{28,24},{1,5},{5... | collective-permute-start | bytes 786440 | tf_op jit(solution)/shard_map/ppermute | solution.py:434
  28.2 16.5 %collective-permute-start.1 = (f32[4,64,256]{2,1,0:T(8,128)S(1)}, f32[4,64,256]{2,1,0:T(8,128)S(1)}, u32[]{:S(2)}, u32[]{:S(2)}) collective-permute-start(f32[4,64,256]{2,1,0:T(8,128)S(1)} %get-tuple-element.36), channel_id=1, source_target_pairs={{0,8},{4,12},{8,0},{12,4},{16,24},{20,28},{24,16},{28,20},{1,9},{5... | collective-permute-start | bytes 786440 | tf_op jit(solution)/shard_map/ppermute | solution.py:434
  29.8 19.5 %collective-permute-start.2 = (f32[4,64,256]{2,1,0:T(8,128)S(1)}, f32[4,64,256]{2,1,0:T(8,128)S(1)}, u32[]{:S(2)}, u32[]{:S(2)}) collective-permute-start(f32[4,64,256]{2,1,0:T(8,128)S(1)} %get-tuple-element.37), channel_id=1, source_target_pairs={{0,12},{4,8},{8,4},{12,0},{16,28},{20,24},{24,20},{28,16},{1,13},{... | collective-permute-start | bytes 786440 | tf_op jit(solution)/shard_map/ppermute | solution.py:434
  30.1 4.3 %collective-permute-start.9 = (f32[16,4,256]{2,1,0:T(4,128)S(1)}, f32[16,4,256]{2,1,0:T(4,128)S(1)}, u32[]{:S(2)}, u32[]{:S(2)}) collective-permute-start(f32[16,4,256]{2,1,0:T(4,128)S(1)} %get-tuple-element.44.refs_0_), channel_id=1, source_target_pairs={{0,3},{1,2},{2,1},{3,0},{4,7},{5,6},{6,5},{7,4},{8,11},{9,10},{10,... | collective-permute-start | bytes 196616 | tf_op jit(solution)/shard_map/ppermute | solution.py:434
  34.5 4.3 %collective-permute-start.8 = (f32[16,4,256]{2,1,0:T(4,128)S(1)}, f32[16,4,256]{2,1,0:T(4,128)S(1)}, u32[]{:S(2)}, u32[]{:S(2)}) collective-permute-start(f32[16,4,256]{2,1,0:T(4,128)S(1)} %get-tuple-element.44.refs_0_), channel_id=1, source_target_pairs={{0,2},{1,3},{2,0},{3,1},{4,6},{5,7},{6,4},{7,5},{8,10},{9,11},{10,... | collective-permute-start | bytes 196616 | tf_op jit(solution)/shard_map/ppermute | solution.py:434
  38.8 1.3 %collective-permute-start.7 = (f32[16,4,256]{2,1,0:T(4,128)S(1)}, f32[16,4,256]{2,1,0:T(4,128)S(1)}, u32[]{:S(2)}, u32[]{:S(2)}) collective-permute-start(f32[16,4,256]{2,1,0:T(4,128)S(1)} %get-tuple-element.44.refs_0_), channel_id=1, source_target_pairs={{0,1},{1,0},{2,3},{3,2},{4,5},{5,4},{6,7},{7,6},{8,9},{9,8},{10,11... | collective-permute-start | bytes 196616 | tf_op jit(solution)/shard_map/ppermute | solution.py:434
  40.9 10.9 %collective-permute-start.10 = (f32[16,4,256]{2,1,0:T(4,128)S(1)}, f32[16,4,256]{2,1,0:T(4,128)S(1)}, u32[]{:S(2)}, u32[]{:S(2)}) collective-permute-start(f32[16,4,256]{2,1,0:T(4,128)S(1)} %shard_map.132.refs_5_), channel_id=1, source_target_pairs={{0,16},{4,20},{8,24},{12,28},{16,0},{20,4},{24,8},{28,12},{1,17},{... | collective-permute-start | bytes 196616 | tf_op jit(solution)/shard_map/ppermute | solution.py:434
  51.8 32.3 %copy-start = (bf16[2,2,256,256]{3,2,1,0:T(8,128)(2,1)S(1)}, bf16[2,2,256,256]{3,2,1,0:T(8,128)(2,1)}, u32[]{:S(2)}) copy-start(bf16[2,2,256,256]{3,2,1,0:T(8,128)(2,1)} %constant.48.both) | copy-start | bytes 1572868
  51.8 26.4 %collective-permute-start.11 = (f32[2,4,64,256]{3,2,1,0:T(8,128)S(1)}, f32[2,4,64,256]{3,2,1,0:T(8,128)S(1)}, u32[]{:S(2)}, u32[]{:S(2)}) collective-permute-start(f32[2,4,64,256]{3,2,1,0:T(8,128)S(1)} %get-tuple-element.45), channel_id=1, source_target_pairs={{0,16},{4,20},{8,24},{12,28},{16,0},{20,4},{24,8},{28,12},{1,17},{... | collective-permute-start | bytes 1572872 | tf_op jit(solution)/shard_map/ppermute | solution.py:434
  56.0 28.1 %collective-permute-start.19 = (f32[4,64,256]{2,1,0:T(8,128)S(1)}, f32[4,64,256]{2,1,0:T(8,128)S(1)}, u32[]{:S(2)}, u32[]{:S(2)}) collective-permute-start(f32[4,64,256]{2,1,0:T(8,128)S(1)} %get-tuple-element.52), channel_id=1, source_target_pairs={{0,4},{4,0},{8,12},{12,8},{16,20},{20,16},{24,28},{28,24},{1,5},{5... | collective-permute-start | bytes 786440 | tf_op jit(solution)/shard_map/ppermute | solution.py:434
  56.9 4.3 %collective-permute-start.14 = (f32[16,4,256]{2,1,0:T(4,128)S(1)}, f32[16,4,256]{2,1,0:T(4,128)S(1)}, u32[]{:S(2)}, u32[]{:S(2)}) collective-permute-start(f32[16,4,256]{2,1,0:T(4,128)S(1)} %get-tuple-element.46.refs_0_), channel_id=1, source_target_pairs={{0,3},{1,2},{2,1},{3,0},{4,7},{5,6},{6,5},{7,4},{8,11},{9,10},{10,... | collective-permute-start | bytes 196616 | tf_op jit(solution)/shard_map/ppermute | solution.py:434
  56.9 6.6 %collective-permute-start.13 = (f32[16,4,256]{2,1,0:T(4,128)S(1)}, f32[16,4,256]{2,1,0:T(4,128)S(1)}, u32[]{:S(2)}, u32[]{:S(2)}) collective-permute-start(f32[16,4,256]{2,1,0:T(4,128)S(1)} %get-tuple-element.46.refs_0_), channel_id=1, source_target_pairs={{0,2},{1,3},{2,0},{3,1},{4,6},{5,7},{6,4},{7,5},{8,10},{9,11},{10,... | collective-permute-start | bytes 196616 | tf_op jit(solution)/shard_map/ppermute | solution.py:434
  58.4 25.7 %collective-permute-start.20 = (f32[4,64,256]{2,1,0:T(8,128)S(1)}, f32[4,64,256]{2,1,0:T(8,128)S(1)}, u32[]{:S(2)}, u32[]{:S(2)}) collective-permute-start(f32[4,64,256]{2,1,0:T(8,128)S(1)} %get-tuple-element.53), channel_id=1, source_target_pairs={{0,8},{4,12},{8,0},{12,4},{16,24},{20,28},{24,16},{28,20},{1,9},{5... | collective-permute-start | bytes 786440 | tf_op jit(solution)/shard_map/ppermute | solution.py:434
  61.2 22.9 %collective-permute-start.21 = (f32[4,64,256]{2,1,0:T(8,128)S(1)}, f32[4,64,256]{2,1,0:T(8,128)S(1)}, u32[]{:S(2)}, u32[]{:S(2)}) collective-permute-start(f32[4,64,256]{2,1,0:T(8,128)S(1)} %get-tuple-element.54), channel_id=1, source_target_pairs={{0,12},{4,8},{8,4},{12,0},{16,28},{20,24},{24,20},{28,16},{1,13},{... | collective-permute-start | bytes 786440 | tf_op jit(solution)/shard_map/ppermute | solution.py:434
  63.4 1.3 %collective-permute-start.12 = (f32[16,4,256]{2,1,0:T(4,128)S(1)}, f32[16,4,256]{2,1,0:T(4,128)S(1)}, u32[]{:S(2)}, u32[]{:S(2)}) collective-permute-start(f32[16,4,256]{2,1,0:T(4,128)S(1)} %get-tuple-element.46.refs_0_), channel_id=1, source_target_pairs={{0,1},{1,0},{2,3},{3,2},{4,5},{5,4},{6,7},{7,6},{8,9},{9,8},{10,11... | collective-permute-start | bytes 196616 | tf_op jit(solution)/shard_map/ppermute | solution.py:434
  65.6 12.7 %collective-permute-start.15 = (f32[16,4,256]{2,1,0:T(4,128)S(1)}, f32[16,4,256]{2,1,0:T(4,128)S(1)}, u32[]{:S(2)}, u32[]{:S(2)}) collective-permute-start(f32[16,4,256]{2,1,0:T(4,128)S(1)} %shard_map.133.refs_5_), channel_id=1, source_target_pairs={{0,16},{4,20},{8,24},{12,28},{16,0},{20,4},{24,8},{28,12},{1,17},{... | collective-permute-start | bytes 196616 | tf_op jit(solution)/shard_map/ppermute | solution.py:434
  80.4 10.7 %collective-permute-start.16 = (f32[4,64,256]{2,1,0:T(8,128)S(1)}, f32[4,64,256]{2,1,0:T(8,128)S(1)}, u32[]{:S(2)}, u32[]{:S(2)}) collective-permute-start(f32[4,64,256]{2,1,0:T(8,128)S(1)} %get-tuple-element.48), channel_id=1, source_target_pairs={{0,4},{4,0},{8,12},{12,8},{16,20},{20,16},{24,28},{28,24},{1,5},{5... | collective-permute-start | bytes 786440 | tf_op jit(solution)/shard_map/ppermute | solution.py:434
  81.0 10.3 %collective-permute-start.17 = (f32[4,64,256]{2,1,0:T(8,128)S(1)}, f32[4,64,256]{2,1,0:T(8,128)S(1)}, u32[]{:S(2)}, u32[]{:S(2)}) collective-permute-start(f32[4,64,256]{2,1,0:T(8,128)S(1)} %get-tuple-element.49), channel_id=1, source_target_pairs={{0,8},{4,12},{8,0},{12,4},{16,24},{20,28},{24,16},{28,20},{1,9},{5... | collective-permute-start | bytes 786440 | tf_op jit(solution)/shard_map/ppermute | solution.py:434
  84.1 10.3 %collective-permute-start.18 = (f32[4,64,256]{2,1,0:T(8,128)S(1)}, f32[4,64,256]{2,1,0:T(8,128)S(1)}, u32[]{:S(2)}, u32[]{:S(2)}) collective-permute-start(f32[4,64,256]{2,1,0:T(8,128)S(1)} %get-tuple-element.50), channel_id=1, source_target_pairs={{0,12},{4,8},{8,4},{12,0},{16,28},{20,24},{24,20},{28,16},{1,13},{... | collective-permute-start | bytes 786440 | tf_op jit(solution)/shard_map/ppermute | solution.py:434
  (1 other events, 1.0 us)

commit v13 on v12

--- a/solution.py
+++ b/solution.py
@@ -149,8 +149,9 @@
             start += count
 
 
-def forward(plan, chunk, ids, both, x, sxh, sxl, *outs):
+def forward(plan, chunk, ids, both, x, sxh, sxl, *refs):
     place = lax.rem(ids[0], plan.half)
+    outs, (high, low) = refs[:-2], refs[-2:]
     folds = plan.folds
     mirror = jnp.stack([x[plan.depth - 1 - z] for z in range(folds)])
     left = []
@@ -158,27 +159,47 @@
         folded = x[:folds] - mirror if parity else x[:folds] + mirror
         folded = parts_of(folded.reshape(folds * plan.rows, plan.width))
         table = both[0, parity, at], both[1, parity, at]
-        left.append(parts_of(dot_parts(table, folded)))
-    for k in range(plan.half):
+        left.append(dot_parts(table, folded))
+    high[...], low[...] = parts_of(jnp.concatenate(left))
+    for k in range(1, plan.half):
         columns = plan.columns(place ^ k)
-        right = sxh[:, columns], sxl[:, columns]
-        value = jnp.concatenate([dot_parts(part, right) for part in left])
-        outs[k][...] = value.reshape(len(chunk), plan.rows, plan.block)
+        value = dot_parts((high[...], low[...]), (sxh[:, columns], sxl[:, columns]))
+        outs[k - 1][...] = value.reshape(len(chunk), plan.rows, plan.block)
+
+
+def forward_own(plan, chunk, ids, high, low, sxh, sxl, out):
+    columns = plan.columns(lax.rem(ids[0], plan.half))
+    value = dot_parts((high[...], low[...]), (sxh[:, columns], sxl[:, columns]))
+    out[...] = value.reshape(len(chunk), plan.rows, plan.block)
+
+
+def x_rows(plan, place, pieces, start, sxh, sxl):
+    total = None
+    for k, piece in enumerate(pieces, start):
+        at = plan.columns(place ^ k)
+        piece = parts_of(piece[...].reshape(-1, plan.block))
+        value = dot_parts(piece, (sxh[at, :], sxl[at, :]))
+        total = value if total is None else total + value
+    return total
+
+
+def first_rows(plan, ids, sxh, sxl, *refs):
+    place = lax.rem(ids[0], plan.half)
+    refs[-1][...] = x_rows(plan, place, refs[:-1], 0, sxh, sxl)
 
 
 def backward(plan, chunk, ready, last, ids, both, sxh, sxl, *refs):
     place = lax.rem(ids[0], plan.half)
-    pieces, refs = refs[: plan.half], refs[plan.half :]
+    count = 2 if last else plan.half
+    pieces, refs = refs[:count], refs[count:]
     before = dict(zip(ready, refs))
     outs, (high, low) = refs[len(ready) : -2], refs[-2:]
     folds = plan.folds
     shape = folds, plan.rows, plan.block
-    total = None
-    for k in range(plan.half):
-        at = plan.columns(place ^ k)
-        piece = parts_of(pieces[k][...].reshape(-1, plan.block))
-        value = dot_parts(piece, (sxh[at, :], sxl[at, :]))
-        total = value if total is None else total + value
+    if last:
+        total = pieces[0][...] + x_rows(plan, place, pieces[1:], plan.half - 1, sxh, sxl)
+    else:
+        total = x_rows(plan, place, pieces, 0, sxh, sxl)
     high[...], low[...] = parts_of(total)
     for j in range(plan.half):
         columns = pl.ds(j * plan.block, plan.block)
@@ -261,9 +282,29 @@
 
 
 def half_end(plan, ids, smu_z, smu_y, smu_x, edges, *refs):
+    pieces, ends = refs[: plan.half], refs[plan.half]
+    place = lax.rem(ids[0], plan.half)
+
+    def with_place(case):
+        def body(u, rows, smu, weights):
+            kappa = 2.0 - smu
+            before = pieces[case][u, rows, :]
+            last = kappa * before + pieces[case ^ 1][u, rows, :]
+            for j in range(2, plan.half):
+                value = pieces[case ^ j][u, rows, :]
+                before, last = last, kappa * last - before + value
+            ends[0, u, rows, :] = before
+            ends[1, u, rows, :] = last
+
+        per_strip(plan, place, smu_z, smu_y, smu_x, edges, body)
+
+    by_place(plan, place, with_place)
+
+
+def edge_rows(plan, ids, smu_z, smu_y, smu_x, edges, *refs):
     pieces = refs[: plan.half]
     ends, seen, sums = refs[plan.half :]
-    steps, half = plan.steps, plan.half
+    half = plan.half
     place = lax.rem(ids[0], half)
     mine = ids[0] // half
     leaving = jnp.where(mine == 0, 1.0, ALPHA_RATIO).astype(jnp.float32)
@@ -273,9 +314,7 @@
         def body(u, rows, smu, weights):
             cyclic = Cyclic(smu, half)
             sources = [pieces[case ^ j][u, rows, :] for j in range(half)]
-            before, last = cyclic.start(sources)
-            ends[0, u, rows, :] = before
-            ends[1, u, rows, :] = last
+            before, last = ends[0, u, rows, :], ends[1, u, rows, :]
             entry = cyclic.entry(ALPHA_RATIO * before, ALPHA_RATIO * last)
             before, last, own = cyclic.run(*entry, sources)
             _, _, other = cyclic.run(leaving * before, leaving * last, [None] * half)
@@ -459,12 +498,20 @@
         modes = f32((len(chunk), plan.rows, plan.block))
         count = len(chunk) * plan.rows * plan.width
         flops = 6 * count * (plan.width + plan.folds * plan.rows)
-        pieces = call(
+        part = jax.ShapeDtypeStruct((len(chunk) * plan.rows, plan.width), jnp.bfloat16)
+        *pieces, high, low = call(
             functools.partial(forward, plan, chunk),
-            [modes] * half,
+            [modes] * (half - 1) + [part, part],
             flops,
             (ids, forth, field, *tables),
         )
+        own = call(
+            functools.partial(forward_own, plan, chunk),
+            modes,
+            flops // plan.half,
+            (ids, high, low, *tables),
+        )
+        pieces = [own, *pieces]
         pieces = [swap(v, "tm", steps, k) for k, v in enumerate(pieces)]
         smu_own = jnp.asarray(smu_z[list(chunk), None], jnp.float32)
         work.append((chunk, modes, flops, (ids, smu_own, smu_y, smu_x, edges), pieces))
@@ -474,11 +521,17 @@
     far = None
     for chunk, modes, flops, small, pieces in work:
         seen = f32((2 * steps, len(chunk), plan.block))
-        ends, view = call(
+        ends = call(
             functools.partial(half_end, plan),
-            [f32((2,) + modes.shape), seen],
+            f32((2,) + modes.shape),
+            10 * modes.size * half,
+            (*small, *pieces),
+        )
+        view = call(
+            functools.partial(edge_rows, plan),
+            seen,
             100 * modes.size * half,
-            (*small, *pieces),
+            (*small, *pieces, ends),
             [pltpu.VMEM((2 * steps, len(chunk), 8, plan.block), jnp.float32)],
         )
         if far is not None:
@@ -510,6 +563,13 @@
                 pltpu.VMEM((half,) + block, jnp.float32),
                 pltpu.SemaphoreType.DMA((half,)),
             ] + hold
+            early = call(
+                functools.partial(first_rows, plan),
+                f32((len(chunk) * plan.rows, plan.width)),
+                flops // 2,
+                (ids, *tables, *pieces[:-1]),
+            )
+            pieces = [early, pieces[-1]]
         ready = tuple(sorted(sums))
         parities = sorted(set(ready) | {c % 2 for c in chunk})
         result = call(

time: 98.8 us -> 104 us (1.053)
  starting transfers between devices: 26.9 us -> 34.8 us
  waiting for transfers between devices: 46.3 us -> 38.7 us
  Pallas kernels: 23.9 us -> 29 us
    ppermute x22, starting transfers between devices: 26.9 us -> 34.8 us  [swap(): return lax.ppermute(values, axis, [(i, i ^ distance) for i in range(count)])]
    ppermute x22, waiting for transfers between devices: 46.3 us -> 38.7 us  [swap(): return lax.ppermute(values, axis, [(i, i ^ distance) for i in range(count)])]
    pallas_call x11 -> x16, Pallas kernels: 23.9 us -> 29 us  [call(): pl.pallas_call(kernel, out_shape=out_shape, in_specs=[smem] + [vmem] * (l...]
  transfers between devices with their start and end apart: 22 -> 22, of which waited for: 15 -> 13; matrix products, arithmetic and copies ran while one was open for 0% -> 0% of each run, Pallas kernels for 14% -> 20%
where the time goes in v13:
time: 104 us
  waiting for transfers between devices  38.7 us (37%)
  starting transfers between devices  34.8 us (33%)
  Pallas kernels  29 us (28%)
  local copies, waits for them, and re-layouts  1.1 us (1%)
    ppermute x22, waiting for transfers between devices, swap(): return lax.ppermute(values, axis, [(i, i ^ distance) for i in range(count)])  38.7 us
    ppermute x22, starting transfers between devices, swap(): return lax.ppermute(values, axis, [(i, i ^ distance) for i in range(count)])  34.8 us
    pallas_call x16, Pallas kernels, call(): pl.pallas_call(kernel, out_shape=out_shape, in_specs=[smem] + [vmem] * (l...  29 us
  transfers between devices with their start and end apart: 22, of which 13 were waited for; matrix products, arithmetic and copies ran while one was open for 0% of the time, Pallas kernels for 20%

profile of v13, /device:TPU:0, one launch (start us, length us, event | category | flops | bytes accessed | tf_op | source)
XLA Modules:
  0.0 104.1 jit_solution(4850879996788640723)
XLA Ops:
  1.1 1.7 %shard_map.127 = (bf16[1024,1024]{1,0:T(8,128)(2,1)S(1)}, bf16[1024,1024]{1,0:T(8,128)(2,1)S(1)}) custom-call(s32[2]{0:T(128)S(1)} %pad_add_fusion.ids, f32[128,1024]{1,0:T(8,128)S(1)} %copy-done.10), custom_call_target="tpu_custom_call" | custom-call | flops 4194304000 | bytes 524296 | tf_op jit(solution)/shard_map/pallas_call | solution.py:73
  2.9 3.0 %shard_map.128 = (f32[4,64,256]{2,1,0:T(8,128)S(1)}, f32[4,64,256]{2,1,0:T(8,128)S(1)}, f32[4,64,256]{2,1,0:T(8,128)S(1)}, bf16[256,1024]{1,0:T(8,128)(2,1)S(1)}, bf16[256,1024]{1,0:T(8,128)(2,1)S(1)}) custom-call(s32[2]{0:T(128)S(1)} %pad_add_fusion.ids, bf16[2,2,256,256]{3,2,1,0:T(8,128)(2,1)S(1)} %copy-done.9, f32[8,64,1024]{2,1,0:T(8,128)S(1)} %bitcast.4, ...), custom_call_target="tpu_custom_call" | custom-call | flops 2013265920 | bytes 6815752 | tf_op jit(solution)/shard_map/pallas_call | solution.py:73
  5.9 3.0 %collective-permute-start.3 = (f32[4,64,256]{2,1,0:T(8,128)S(1)}, f32[4,64,256]{2,1,0:T(8,128)S(1)}, u32[]{:S(2)}, u32[]{:S(2)}) collective-permute-start(f32[4,64,256]{2,1,0:T(8,128)S(1)} %get-tuple-element.39), channel_id=1, source_target_pairs={{0,4},{4,0},{8,12},{12,8},{16,20},{20,16},{24,28},{28,24},{1,5},{5... | collective-permute-start | bytes 786440 | tf_op jit(solution)/shard_map/ppermute | solution.py:473
  8.9 1.6 %collective-permute-start.4 = (f32[4,64,256]{2,1,0:T(8,128)S(1)}, f32[4,64,256]{2,1,0:T(8,128)S(1)}, u32[]{:S(2)}, u32[]{:S(2)}) collective-permute-start(f32[4,64,256]{2,1,0:T(8,128)S(1)} %get-tuple-element.40), channel_id=1, source_target_pairs={{0,8},{4,12},{8,0},{12,4},{16,24},{20,28},{24,16},{28,20},{1,9},{5... | collective-permute-start | bytes 786440 | tf_op jit(solution)/shard_map/ppermute | solution.py:473
  10.5 3.0 %shard_map.130 = (f32[4,64,256]{2,1,0:T(8,128)S(1)}, f32[4,64,256]{2,1,0:T(8,128)S(1)}, f32[4,64,256]{2,1,0:T(8,128)S(1)}, bf16[256,1024]{1,0:T(8,128)(2,1)S(1)}, bf16[256,1024]{1,0:T(8,128)(2,1)S(1)}) custom-call(s32[2]{0:T(128)S(1)} %pad_add_fusion.ids, bf16[2,2,256,256]{3,2,1,0:T(8,128)(2,1)S(1)} %copy-done.9, f32[8,64,1024]{2,1,0:T(8,128)S(1)} %bitcast.5, ...), custom_call_target="tpu_custom_call" | custom-call | flops 2013265920 | bytes 6815752 | tf_op jit(solution)/shard_map/pallas_call | solution.py:73
  15.9 2.2 %collective-permute-done.4.refs_2_ = f32[4,64,256]{2,1,0:T(8,128)S(1)} collective-permute-done((f32[4,64,256]{2,1,0:T(8,128)S(1)}, f32[4,64,256]{2,1,0:T(8,128)S(1)}, u32[]{:S(2)}, u32[]{:S(2)}) %collective-permute-start.4) | collective-permute-done | bytes 262176 | tf_op jit(solution)/shard_map/ppermute | solution.py:473
  18.2 3.9 %collective-permute-done.5.refs_3_ = f32[4,64,256]{2,1,0:T(8,128)S(1)} collective-permute-done((f32[4,64,256]{2,1,0:T(8,128)S(1)}, f32[4,64,256]{2,1,0:T(8,128)S(1)}, u32[]{:S(2)}, u32[]{:S(2)}) %collective-permute-start.5) | collective-permute-done | bytes 262176 | tf_op jit(solution)/shard_map/ppermute | solution.py:473
  23.1 2.8 %collective-permute-start.6 = (f32[2,4,64,256]{3,2,1,0:T(8,128)S(1)}, f32[2,4,64,256]{3,2,1,0:T(8,128)S(1)}, u32[]{:S(2)}, u32[]{:S(2)}) collective-permute-start(f32[2,4,64,256]{3,2,1,0:T(8,128)S(1)} %shard_map.133.refs_4_), channel_id=1, source_target_pairs={{0,16},{4,20},{8,24},{12,28},{16,0},{20,4},{24,8},{28,12},{1,17},{... | collective-permute-start | bytes 1572872 | tf_op jit(solution)/shard_map/ppermute | solution.py:473
  25.9 1.5 %collective-permute-start = (f32[4,64,256]{2,1,0:T(8,128)S(1)}, f32[4,64,256]{2,1,0:T(8,128)S(1)}, u32[]{:S(2)}, u32[]{:S(2)}) collective-permute-start(f32[4,64,256]{2,1,0:T(8,128)S(1)} %get-tuple-element.35), channel_id=1, source_target_pairs={{0,4},{4,0},{8,12},{12,8},{16,20},{20,16},{24,28},{28,24},{1,5},{5... | collective-permute-start | bytes 786440 | tf_op jit(solution)/shard_map/ppermute | solution.py:473
  27.4 1.6 %collective-permute-start.1 = (f32[4,64,256]{2,1,0:T(8,128)S(1)}, f32[4,64,256]{2,1,0:T(8,128)S(1)}, u32[]{:S(2)}, u32[]{:S(2)}) collective-permute-start(f32[4,64,256]{2,1,0:T(8,128)S(1)} %get-tuple-element.36), channel_id=1, source_target_pairs={{0,8},{4,12},{8,0},{12,4},{16,24},{20,28},{24,16},{28,20},{1,9},{5... | collective-permute-start | bytes 786440 | tf_op jit(solution)/shard_map/ppermute | solution.py:473
  29.4 1.8 %shard_map.134.refs_0_ = f32[16,4,256]{2,1,0:T(4,128)S(1)} custom-call(s32[2]{0:T(128)S(1)} %pad_add_fusion.ids, f32[4,1]{1,0:T(4,128)S(1)} %copy-done.7, f32[64,1]{1,0:T(8,128)S(1)} %copy-done, f32[1,1024]{1,0:T(1,128)S(1)} %copy-done.5, f32[64,2]{1,0:T(8,128)S(1)} %copy-done.1, f32[4,64,256]{2,1,0:T(8,128)S(1)} %shard_map.129.refs_0_, ...), custom_call_target="tpu_custom_call" | custom-call | flops 26214400 | bytes 1577752 | tf_op jit(solution)/shard_map/pallas_call | solution.py:73
  32.5 1.5 %collective-permute-start.8 = (f32[16,4,256]{2,1,0:T(4,128)S(1)}, f32[16,4,256]{2,1,0:T(4,128)S(1)}, u32[]{:S(2)}, u32[]{:S(2)}) collective-permute-start(f32[16,4,256]{2,1,0:T(4,128)S(1)} %shard_map.134.refs_0_), channel_id=1, source_target_pairs={{0,2},{1,3},{2,0},{3,1},{4,6},{5,7},{6,4},{7,5},{8,10},{9,11},{10,... | collective-permute-start | bytes 196616 | tf_op jit(solution)/shard_map/ppermute | solution.py:473
  34.0 2.8 %collective-permute-done.8.refs_2_ = f32[16,4,256]{2,1,0:T(4,128)S(1)} collective-permute-done((f32[16,4,256]{2,1,0:T(4,128)S(1)}, f32[16,4,256]{2,1,0:T(4,128)S(1)}, u32[]{:S(2)}, u32[]{:S(2)}) %collective-permute-start.8) | collective-permute-done | bytes 65568 | tf_op jit(solution)/shard_map/ppermute | solution.py:473
  37.2 4.0 %collective-permute-done.9.refs_3_ = f32[16,4,256]{2,1,0:T(4,128)S(1)} collective-permute-done((f32[16,4,256]{2,1,0:T(4,128)S(1)}, f32[16,4,256]{2,1,0:T(4,128)S(1)}, u32[]{:S(2)}, u32[]{:S(2)}) %collective-permute-start.9) | collective-permute-done | bytes 65568 | tf_op jit(solution)/shard_map/ppermute | solution.py:473
  42.1 1.8 %collective-permute-done.1.refs_2_ = f32[4,64,256]{2,1,0:T(8,128)S(1)} collective-permute-done((f32[4,64,256]{2,1,0:T(8,128)S(1)}, f32[4,64,256]{2,1,0:T(8,128)S(1)}, u32[]{:S(2)}, u32[]{:S(2)}) %collective-permute-start.1) | collective-permute-done | bytes 262176 | tf_op jit(solution)/shard_map/ppermute | solution.py:473
  43.9 4.8 %collective-permute-done.2.refs_3_ = f32[4,64,256]{2,1,0:T(8,128)S(1)} collective-permute-done((f32[4,64,256]{2,1,0:T(8,128)S(1)}, f32[4,64,256]{2,1,0:T(8,128)S(1)}, u32[]{:S(2)}, u32[]{:S(2)}) %collective-permute-start.2) | collective-permute-done | bytes 262176 | tf_op jit(solution)/shard_map/ppermute | solution.py:473
  52.2 1.8 %shard_map.136.refs_0_ = f32[16,4,256]{2,1,0:T(4,128)S(1)} custom-call(s32[2]{0:T(128)S(1)} %pad_add_fusion.ids, f32[4,1]{1,0:T(4,128)S(1)} %copy-done.6, f32[64,1]{1,0:T(8,128)S(1)} %copy-done, f32[1,1024]{1,0:T(1,128)S(1)} %copy-done.5, f32[64,2]{1,0:T(8,128)S(1)} %copy-done.1, f32[4,64,256]{2,1,0:T(8,128)S(1)} %shard_map.131.refs_0_, ...), custom_call_target="tpu_custom_call" | custom-call | flops 26214400 | bytes 1577752 | tf_op jit(solution)/shard_map/pallas_call | solution.py:73
  54.2 1.6 %collective-permute-start.13 = (f32[16,4,256]{2,1,0:T(4,128)S(1)}, f32[16,4,256]{2,1,0:T(4,128)S(1)}, u32[]{:S(2)}, u32[]{:S(2)}) collective-permute-start(f32[16,4,256]{2,1,0:T(4,128)S(1)} %shard_map.136.refs_0_), channel_id=1, source_target_pairs={{0,2},{1,3},{2,0},{3,1},{4,6},{5,7},{6,4},{7,5},{8,10},{9,11},{10,... | collective-permute-start | bytes 196616 | tf_op jit(solution)/shard_map/ppermute | solution.py:473
  55.7 2.0 %shard_map.140 = (f32[4,64,256]{2,1,0:T(8,128)S(1)}, f32[4,64,256]{2,1,0:T(8,128)S(1)}, f32[4,64,256]{2,1,0:T(8,128)S(1)}, f32[4,64,256]{2,1,0:T(8,128)S(1)}) custom-call(s32[2]{0:T(128)S(1)} %pad_add_fusion.ids, f32[4,1]{1,0:T(4,128)S(1)} %copy-done.7, f32[64,1]{1,0:T(8,128)S(1)} %copy-done, f32[1,1024]{1,0:T(1,128)S(1)} %copy-done.5, ...), custom_call_target="tpu_custom_call" | custom-call | flops 26214400 | bytes 1708824 | tf_op jit(solution)/shard_map/pallas_call | solution.py:73
  57.7 1.4 %collective-permute-start.19 = (f32[4,64,256]{2,1,0:T(8,128)S(1)}, f32[4,64,256]{2,1,0:T(8,128)S(1)}, u32[]{:S(2)}, u32[]{:S(2)}) collective-permute-start(f32[4,64,256]{2,1,0:T(8,128)S(1)} %get-tuple-element.48), channel_id=1, source_target_pairs={{0,4},{4,0},{8,12},{12,8},{16,20},{20,16},{24,28},{28,24},{1,5},{5... | collective-permute-start | bytes 786440 | tf_op jit(solution)/shard_map/ppermute | solution.py:473
  59.1 12.6 %collective-permute-start.20 = (f32[4,64,256]{2,1,0:T(8,128)S(1)}, f32[4,64,256]{2,1,0:T(8,128)S(1)}, u32[]{:S(2)}, u32[]{:S(2)}) collective-permute-start(f32[4,64,256]{2,1,0:T(8,128)S(1)} %get-tuple-element.49), channel_id=1, source_target_pairs={{0,8},{4,12},{8,0},{12,4},{16,24},{20,28},{24,16},{28,20},{1,9},{5... | collective-permute-start | bytes 786440 | tf_op jit(solution)/shard_map/ppermute | solution.py:473
  71.7 1.4 %collective-permute-start.21 = (f32[4,64,256]{2,1,0:T(8,128)S(1)}, f32[4,64,256]{2,1,0:T(8,128)S(1)}, u32[]{:S(2)}, u32[]{:S(2)}) collective-permute-start(f32[4,64,256]{2,1,0:T(8,128)S(1)} %get-tuple-element.50), channel_id=1, source_target_pairs={{0,12},{4,8},{8,4},{12,0},{16,28},{20,24},{24,20},{28,16},{1,13},{... | collective-permute-start | bytes 786440 | tf_op jit(solution)/shard_map/ppermute | solution.py:473
  73.1 4.2 %collective-permute-done.14.refs_3_ = f32[16,4,256]{2,1,0:T(4,128)S(1)} collective-permute-done((f32[16,4,256]{2,1,0:T(4,128)S(1)}, f32[16,4,256]{2,1,0:T(4,128)S(1)}, u32[]{:S(2)}, u32[]{:S(2)}) %collective-permute-start.14) | collective-permute-done | bytes 65568 | tf_op jit(solution)/shard_map/ppermute | solution.py:473
  78.2 6.4 %collective-permute-done.15.refs_6_ = f32[16,4,256]{2,1,0:T(4,128)S(1)} collective-permute-done((f32[16,4,256]{2,1,0:T(4,128)S(1)}, f32[16,4,256]{2,1,0:T(4,128)S(1)}, u32[]{:S(2)}, u32[]{:S(2)}) %collective-permute-start.15) | collective-permute-done | bytes 65568 | tf_op jit(solution)/shard_map/ppermute | solution.py:473
  84.6 2.2 %shard_map.138 = (f32[4,64,256]{2,1,0:T(8,128)S(1)}, f32[4,64,256]{2,1,0:T(8,128)S(1)}, f32[4,64,256]{2,1,0:T(8,128)S(1)}, f32[4,64,256]{2,1,0:T(8,128)S(1)}) custom-call(s32[2]{0:T(128)S(1)} %pad_add_fusion.ids, f32[4,1]{1,0:T(4,128)S(1)} %copy-done.6, f32[64,1]{1,0:T(8,128)S(1)} %copy-done, f32[1,1024]{1,0:T(1,128)S(1)} %copy-done.5, ...), custom_call_target="tpu_custom_call" | custom-call | flops 26214400 | bytes 1708824 | tf_op jit(solution)/shard_map/pallas_call | solution.py:73
  86.8 1.7 %collective-permute-start.16 = (f32[4,64,256]{2,1,0:T(8,128)S(1)}, f32[4,64,256]{2,1,0:T(8,128)S(1)}, u32[]{:S(2)}, u32[]{:S(2)}) collective-permute-start(f32[4,64,256]{2,1,0:T(8,128)S(1)} %get-tuple-element.44), channel_id=1, source_target_pairs={{0,4},{4,0},{8,12},{12,8},{16,20},{20,16},{24,28},{28,24},{1,5},{5... | collective-permute-start | bytes 786440 | tf_op jit(solution)/shard_map/ppermute | solution.py:473
  90.3 2.8 %shard_map.141.refs_2_ = f32[4,64,1024]{2,1,0:T(8,128)S(1)} custom-call(s32[2]{0:T(128)S(1)} %pad_add_fusion.ids, bf16[2,2,256,256]{3,2,1,0:T(8,128)(2,1)S(1)} %copy-done.2, bf16[1024,1024]{1,0:T(8,128)(2,1)S(1)} %get-tuple-element.28.sxh, bf16[1024,1024]{1,0:T(8,128)(2,1)S(1)} %get-tuple-element.29.sxl, f32[4,64,256]{2,1,0:T(8,128)S(1)} %get-tuple-element.47.refs_0_, ...), custom_call_target="tpu_custom_call" | custom-call | flops 2013265920 | bytes 5767176 | tf_op jit(solution)/shard_map/pallas_call | solution.py:73
  93.2 2.0 %collective-permute-done.16.refs_1_ = f32[4,64,256]{2,1,0:T(8,128)S(1)} collective-permute-done((f32[4,64,256]{2,1,0:T(8,128)S(1)}, f32[4,64,256]{2,1,0:T(8,128)S(1)}, u32[]{:S(2)}, u32[]{:S(2)}) %collective-permute-start.16) | collective-permute-done | bytes 262176 | tf_op jit(solution)/shard_map/ppermute | solution.py:473
  95.2 2.6 %collective-permute-done.17.refs_2_ = f32[4,64,256]{2,1,0:T(8,128)S(1)} collective-permute-done((f32[4,64,256]{2,1,0:T(8,128)S(1)}, f32[4,64,256]{2,1,0:T(8,128)S(1)}, u32[]{:S(2)}, u32[]{:S(2)}) %collective-permute-start.17) | collective-permute-done | bytes 262176 | tf_op jit(solution)/shard_map/ppermute | solution.py:473
  97.7 1.9 %shard_map.139.refs_0_ = f32[256,1024]{1,0:T(8,128)S(1)} custom-call(s32[2]{0:T(128)S(1)} %pad_add_fusion.ids, bf16[1024,1024]{1,0:T(8,128)(2,1)S(1)} %get-tuple-element.28.sxh, bf16[1024,1024]{1,0:T(8,128)(2,1)S(1)} %get-tuple-element.29.sxl, f32[4,64,256]{2,1,0:T(8,128)S(1)} %get-tuple-element.43.refs_0_, ...), custom_call_target="tpu_custom_call" | custom-call | flops 1006632960 | bytes 4980744 | tf_op jit(solution)/shard_map/pallas_call | solution.py:73
  99.7 1.5 %collective-permute-done.18.refs_1_ = f32[4,64,256]{2,1,0:T(8,128)S(1)} collective-permute-done((f32[4,64,256]{2,1,0:T(8,128)S(1)}, f32[4,64,256]{2,1,0:T(8,128)S(1)}, u32[]{:S(2)}, u32[]{:S(2)}) %collective-permute-start.18) | collective-permute-done | bytes 262176 | tf_op jit(solution)/shard_map/ppermute | solution.py:473
  101.2 2.8 %shard_map.142 = f32[8,64,1024]{2,1,0:T(8,128)} custom-call(s32[2]{0:T(128)S(1)} %pad_add_fusion.ids, bf16[2,2,256,256]{3,2,1,0:T(8,128)(2,1)S(1)} %copy-done.2, bf16[1024,1024]{1,0:T(8,128)(2,1)S(1)} %get-tuple-element.28.sxh, bf16[1024,1024]{1,0:T(8,128)(2,1)S(1)} %get-tuple-element.29.sxl, f32[256,1024]{1,0:T(8,128)S(1)} %shard_map.139.refs_0_, ...), custom_call_target="tpu_custom_call" | custom-call | flops 2013265920 | bytes 7077896 | tf_op jit(solution)/shard_map/pallas_call | solution.py:73
  (51 shorter events, 13.8 us)
Async XLA Ops:
  1.1 1.7 %copy-start.8 = (f32[1,8,64,1024]{3,2,1,0:T(8,128)S(1)}, f32[1,8,64,1024]{3,2,1,0:T(8,128)}, u32[]{:S(2)}) copy-start(f32[1,8,64,1024]{3,2,1,0:T(8,128)} %param.13) | copy-start | bytes 6291460
  1.1 1.7 %copy-start.9 = (bf16[2,2,256,256]{3,2,1,0:T(8,128)(2,1)S(1)}, bf16[2,2,256,256]{3,2,1,0:T(8,128)(2,1)}, u32[]{:S(2)}) copy-start(bf16[2,2,256,256]{3,2,1,0:T(8,128)(2,1)} %constant.51.both) | copy-start | bytes 1572868
  5.9 10.0 %collective-permute-start.3 = (f32[4,64,256]{2,1,0:T(8,128)S(1)}, f32[4,64,256]{2,1,0:T(8,128)S(1)}, u32[]{:S(2)}, u32[]{:S(2)}) collective-permute-start(f32[4,64,256]{2,1,0:T(8,128)S(1)} %get-tuple-element.39), channel_id=1, source_target_pairs={{0,4},{4,0},{8,12},{12,8},{16,20},{20,16},{24,28},{28,24},{1,5},{5... | collective-permute-start | bytes 786440 | tf_op jit(solution)/shard_map/ppermute | solution.py:473
  8.9 9.2 %collective-permute-start.4 = (f32[4,64,256]{2,1,0:T(8,128)S(1)}, f32[4,64,256]{2,1,0:T(8,128)S(1)}, u32[]{:S(2)}, u32[]{:S(2)}) collective-permute-start(f32[4,64,256]{2,1,0:T(8,128)S(1)} %get-tuple-element.40), channel_id=1, source_target_pairs={{0,8},{4,12},{8,0},{12,4},{16,24},{20,28},{24,16},{28,20},{1,9},{5... | collective-permute-start | bytes 786440 | tf_op jit(solution)/shard_map/ppermute | solution.py:473
  10.5 11.6 %collective-permute-start.5 = (f32[4,64,256]{2,1,0:T(8,128)S(1)}, f32[4,64,256]{2,1,0:T(8,128)S(1)}, u32[]{:S(2)}, u32[]{:S(2)}) collective-permute-start(f32[4,64,256]{2,1,0:T(8,128)S(1)} %get-tuple-element.41), channel_id=1, source_target_pairs={{0,12},{4,8},{8,4},{12,0},{16,28},{20,24},{24,20},{28,16},{1,13},{... | collective-permute-start | bytes 786440 | tf_op jit(solution)/shard_map/ppermute | solution.py:473
  14.7 7.4 %copy-start = (f32[64,1]{1,0:T(8,128)S(1)}, f32[64,1]{1,0:T(8,128)}, u32[]{:S(2)}) copy-start(f32[64,1]{1,0:T(8,128)} %constant.33.clone.smu_y) | copy-start | bytes 772
  14.7 7.4 %copy-start.1 = (f32[64,2]{1,0:T(8,128)S(1)}, f32[64,2]{1,0:T(8,128)}, u32[]{:S(2)}) copy-start(f32[64,2]{1,0:T(8,128)} %constant.35.clone.edges) | copy-start | bytes 1540
  14.7 7.4 %copy-start.5 = (f32[1,1024]{1,0:T(1,128)S(1)}, f32[1,1024]{1,0:T(1,128)}, u32[]{:S(2)}) copy-start(f32[1,1024]{1,0:T(1,128)} %constant.34.clone.smu_x) | copy-start | bytes 12292
  14.7 7.4 %copy-start.7 = (f32[4,1]{1,0:T(4,128)S(1)}, f32[4,1]{1,0:T(4,128)}, u32[]{:S(2)}) copy-start(f32[4,1]{1,0:T(4,128)} %constant.41.clone.smu_z) | copy-start | bytes 52
  15.9 25.2 %copy-start.4 = (f32[5,4,4,1024]{3,2,1,0:T(4,128)S(1)}, f32[5,4,4,1024]{3,2,1,0:T(4,128)}, u32[]{:S(2)}) copy-start(f32[5,4,4,1024]{3,2,1,0:T(4,128)} %constant.43.clone.responses) | copy-start | bytes 983044
  15.9 32.8 %copy-start.6 = (f32[4,1]{1,0:T(4,128)S(1)}, f32[4,1]{1,0:T(4,128)}, u32[]{:S(2)}) copy-start(f32[4,1]{1,0:T(4,128)} %constant.42.clone.smu_z) | copy-start | bytes 52
  23.1 27.9 %collective-permute-start.6 = (f32[2,4,64,256]{3,2,1,0:T(8,128)S(1)}, f32[2,4,64,256]{3,2,1,0:T(8,128)S(1)}, u32[]{:S(2)}, u32[]{:S(2)}) collective-permute-start(f32[2,4,64,256]{3,2,1,0:T(8,128)S(1)} %shard_map.133.refs_4_), channel_id=1, source_target_pairs={{0,16},{4,20},{8,24},{12,28},{16,0},{20,4},{24,8},{28,12},{1,17},{... | collective-permute-start | bytes 1572872 | tf_op jit(solution)/shard_map/ppermute | solution.py:473
  25.9 16.2 %collective-permute-start = (f32[4,64,256]{2,1,0:T(8,128)S(1)}, f32[4,64,256]{2,1,0:T(8,128)S(1)}, u32[]{:S(2)}, u32[]{:S(2)}) collective-permute-start(f32[4,64,256]{2,1,0:T(8,128)S(1)} %get-tuple-element.35), channel_id=1, source_target_pairs={{0,4},{4,0},{8,12},{12,8},{16,20},{20,16},{24,28},{28,24},{1,5},{5... | collective-permute-start | bytes 786440 | tf_op jit(solution)/shard_map/ppermute | solution.py:473
  27.4 16.5 %collective-permute-start.1 = (f32[4,64,256]{2,1,0:T(8,128)S(1)}, f32[4,64,256]{2,1,0:T(8,128)S(1)}, u32[]{:S(2)}, u32[]{:S(2)}) collective-permute-start(f32[4,64,256]{2,1,0:T(8,128)S(1)} %get-tuple-element.36), channel_id=1, source_target_pairs={{0,8},{4,12},{8,0},{12,4},{16,24},{20,28},{24,16},{28,20},{1,9},{5... | collective-permute-start | bytes 786440 | tf_op jit(solution)/shard_map/ppermute | solution.py:473
  29.0 19.7 %collective-permute-start.2 = (f32[4,64,256]{2,1,0:T(8,128)S(1)}, f32[4,64,256]{2,1,0:T(8,128)S(1)}, u32[]{:S(2)}, u32[]{:S(2)}) collective-permute-start(f32[4,64,256]{2,1,0:T(8,128)S(1)} %get-tuple-element.37), channel_id=1, source_target_pairs={{0,12},{4,8},{8,4},{12,0},{16,28},{20,24},{24,20},{28,16},{1,13},{... | collective-permute-start | bytes 786440 | tf_op jit(solution)/shard_map/ppermute | solution.py:473
  31.2 1.3 %collective-permute-start.7 = (f32[16,4,256]{2,1,0:T(4,128)S(1)}, f32[16,4,256]{2,1,0:T(4,128)S(1)}, u32[]{:S(2)}, u32[]{:S(2)}) collective-permute-start(f32[16,4,256]{2,1,0:T(4,128)S(1)} %shard_map.134.refs_0_), channel_id=1, source_target_pairs={{0,1},{1,0},{2,3},{3,2},{4,5},{5,4},{6,7},{7,6},{8,9},{9,8},{10,11... | collective-permute-start | bytes 196616 | tf_op jit(solution)/shard_map/ppermute | solution.py:473
  32.5 4.3 %collective-permute-start.8 = (f32[16,4,256]{2,1,0:T(4,128)S(1)}, f32[16,4,256]{2,1,0:T(4,128)S(1)}, u32[]{:S(2)}, u32[]{:S(2)}) collective-permute-start(f32[16,4,256]{2,1,0:T(4,128)S(1)} %shard_map.134.refs_0_), channel_id=1, source_target_pairs={{0,2},{1,3},{2,0},{3,1},{4,6},{5,7},{6,4},{7,5},{8,10},{9,11},{10,... | collective-permute-start | bytes 196616 | tf_op jit(solution)/shard_map/ppermute | solution.py:473
  36.8 4.3 %collective-permute-start.9 = (f32[16,4,256]{2,1,0:T(4,128)S(1)}, f32[16,4,256]{2,1,0:T(4,128)S(1)}, u32[]{:S(2)}, u32[]{:S(2)}) collective-permute-start(f32[16,4,256]{2,1,0:T(4,128)S(1)} %shard_map.134.refs_0_), channel_id=1, source_target_pairs={{0,3},{1,2},{2,1},{3,0},{4,7},{5,6},{6,5},{7,4},{8,11},{9,10},{10,... | collective-permute-start | bytes 196616 | tf_op jit(solution)/shard_map/ppermute | solution.py:473
  42.0 9.0 %collective-permute-start.10 = (f32[16,4,256]{2,1,0:T(4,128)S(1)}, f32[16,4,256]{2,1,0:T(4,128)S(1)}, u32[]{:S(2)}, u32[]{:S(2)}) collective-permute-start(f32[16,4,256]{2,1,0:T(4,128)S(1)} %shard_map.135.refs_5_), channel_id=1, source_target_pairs={{0,16},{4,20},{8,24},{12,28},{16,0},{20,4},{24,8},{28,12},{1,17},{... | collective-permute-start | bytes 196616 | tf_op jit(solution)/shard_map/ppermute | solution.py:473
  49.7 27.6 %copy-start.3 = (f32[5,4,4,1024]{3,2,1,0:T(4,128)S(1)}, f32[5,4,4,1024]{3,2,1,0:T(4,128)}, u32[]{:S(2)}) copy-start(f32[5,4,4,1024]{3,2,1,0:T(4,128)} %constant.44.clone.responses) | copy-start | bytes 983044
  51.0 33.6 %collective-permute-start.11 = (f32[2,4,64,256]{3,2,1,0:T(8,128)S(1)}, f32[2,4,64,256]{3,2,1,0:T(8,128)S(1)}, u32[]{:S(2)}, u32[]{:S(2)}) collective-permute-start(f32[2,4,64,256]{3,2,1,0:T(8,128)S(1)} %shard_map.132.refs_4_), channel_id=1, source_target_pairs={{0,16},{4,20},{8,24},{12,28},{16,0},{20,4},{24,8},{28,12},{1,17},{... | collective-permute-start | bytes 1572872 | tf_op jit(solution)/shard_map/ppermute | solution.py:473
  54.1 36.3 %copy-start.2 = (bf16[2,2,256,256]{3,2,1,0:T(8,128)(2,1)S(1)}, bf16[2,2,256,256]{3,2,1,0:T(8,128)(2,1)}, u32[]{:S(2)}) copy-start(bf16[2,2,256,256]{3,2,1,0:T(8,128)(2,1)} %constant.48.both) | copy-start | bytes 1572868
  54.1 17.6 %collective-permute-start.12 = (f32[16,4,256]{2,1,0:T(4,128)S(1)}, f32[16,4,256]{2,1,0:T(4,128)S(1)}, u32[]{:S(2)}, u32[]{:S(2)}) collective-permute-start(f32[16,4,256]{2,1,0:T(4,128)S(1)} %shard_map.136.refs_0_), channel_id=1, source_target_pairs={{0,1},{1,0},{2,3},{3,2},{4,5},{5,4},{6,7},{7,6},{8,9},{9,8},{10,11... | collective-permute-start | bytes 196616 | tf_op jit(solution)/shard_map/ppermute | solution.py:473
  54.2 18.9 %collective-permute-start.13 = (f32[16,4,256]{2,1,0:T(4,128)S(1)}, f32[16,4,256]{2,1,0:T(4,128)S(1)}, u32[]{:S(2)}, u32[]{:S(2)}) collective-permute-start(f32[16,4,256]{2,1,0:T(4,128)S(1)} %shard_map.136.refs_0_), channel_id=1, source_target_pairs={{0,2},{1,3},{2,0},{3,1},{4,6},{5,7},{6,4},{7,5},{8,10},{9,11},{10,... | collective-permute-start | bytes 196616 | tf_op jit(solution)/shard_map/ppermute | solution.py:473
  57.7 31.5 %collective-permute-start.19 = (f32[4,64,256]{2,1,0:T(8,128)S(1)}, f32[4,64,256]{2,1,0:T(8,128)S(1)}, u32[]{:S(2)}, u32[]{:S(2)}) collective-permute-start(f32[4,64,256]{2,1,0:T(8,128)S(1)} %get-tuple-element.48), channel_id=1, source_target_pairs={{0,4},{4,0},{8,12},{12,8},{16,20},{20,16},{24,28},{28,24},{1,5},{5... | collective-permute-start | bytes 786440 | tf_op jit(solution)/shard_map/ppermute | solution.py:473
  59.1 31.2 %collective-permute-start.20 = (f32[4,64,256]{2,1,0:T(8,128)S(1)}, f32[4,64,256]{2,1,0:T(8,128)S(1)}, u32[]{:S(2)}, u32[]{:S(2)}) collective-permute-start(f32[4,64,256]{2,1,0:T(8,128)S(1)} %get-tuple-element.49), channel_id=1, source_target_pairs={{0,8},{4,12},{8,0},{12,4},{16,24},{20,28},{24,16},{28,20},{1,9},{5... | collective-permute-start | bytes 786440 | tf_op jit(solution)/shard_map/ppermute | solution.py:473
  71.7 18.7 %collective-permute-start.21 = (f32[4,64,256]{2,1,0:T(8,128)S(1)}, f32[4,64,256]{2,1,0:T(8,128)S(1)}, u32[]{:S(2)}, u32[]{:S(2)}) collective-permute-start(f32[4,64,256]{2,1,0:T(8,128)S(1)} %get-tuple-element.50), channel_id=1, source_target_pairs={{0,12},{4,8},{8,4},{12,0},{16,28},{20,24},{24,20},{28,16},{1,13},{... | collective-permute-start | bytes 786440 | tf_op jit(solution)/shard_map/ppermute | solution.py:473
  73.1 4.2 %collective-permute-start.14 = (f32[16,4,256]{2,1,0:T(4,128)S(1)}, f32[16,4,256]{2,1,0:T(4,128)S(1)}, u32[]{:S(2)}, u32[]{:S(2)}) collective-permute-start(f32[16,4,256]{2,1,0:T(4,128)S(1)} %shard_map.136.refs_0_), channel_id=1, source_target_pairs={{0,3},{1,2},{2,1},{3,0},{4,7},{5,6},{6,5},{7,4},{8,11},{9,10},{10,... | collective-permute-start | bytes 196616 | tf_op jit(solution)/shard_map/ppermute | solution.py:473
  78.1 6.5 %collective-permute-start.15 = (f32[16,4,256]{2,1,0:T(4,128)S(1)}, f32[16,4,256]{2,1,0:T(4,128)S(1)}, u32[]{:S(2)}, u32[]{:S(2)}) collective-permute-start(f32[16,4,256]{2,1,0:T(4,128)S(1)} %shard_map.137.refs_5_), channel_id=1, source_target_pairs={{0,16},{4,20},{8,24},{12,28},{16,0},{20,4},{24,8},{28,12},{1,17},{... | collective-permute-start | bytes 196616 | tf_op jit(solution)/shard_map/ppermute | solution.py:473
  86.8 8.4 %collective-permute-start.16 = (f32[4,64,256]{2,1,0:T(8,128)S(1)}, f32[4,64,256]{2,1,0:T(8,128)S(1)}, u32[]{:S(2)}, u32[]{:S(2)}) collective-permute-start(f32[4,64,256]{2,1,0:T(8,128)S(1)} %get-tuple-element.44), channel_id=1, source_target_pairs={{0,4},{4,0},{8,12},{12,8},{16,20},{20,16},{24,28},{28,24},{1,5},{5... | collective-permute-start | bytes 786440 | tf_op jit(solution)/shard_map/ppermute | solution.py:473
  88.5 9.2 %collective-permute-start.17 = (f32[4,64,256]{2,1,0:T(8,128)S(1)}, f32[4,64,256]{2,1,0:T(8,128)S(1)}, u32[]{:S(2)}, u32[]{:S(2)}) collective-permute-start(f32[4,64,256]{2,1,0:T(8,128)S(1)} %get-tuple-element.45), channel_id=1, source_target_pairs={{0,8},{4,12},{8,0},{12,4},{16,24},{20,28},{24,16},{28,20},{1,9},{5... | collective-permute-start | bytes 786440 | tf_op jit(solution)/shard_map/ppermute | solution.py:473
  89.2 11.9 %collective-permute-start.18 = (f32[4,64,256]{2,1,0:T(8,128)S(1)}, f32[4,64,256]{2,1,0:T(8,128)S(1)}, u32[]{:S(2)}, u32[]{:S(2)}) collective-permute-start(f32[4,64,256]{2,1,0:T(8,128)S(1)} %get-tuple-element.46), channel_id=1, source_target_pairs={{0,12},{4,8},{8,4},{12,0},{16,28},{20,24},{24,20},{28,16},{1,13},{... | collective-permute-start | bytes 786440 | tf_op jit(solution)/shard_map/ppermute | solution.py:473
  (1 other events, 1.0 us)

commit v14 on v12

--- a/solution.py
+++ b/solution.py
@@ -166,19 +166,33 @@
         outs[k][...] = value.reshape(len(chunk), plan.rows, plan.block)
 
 
+def x_rows(plan, place, pieces, start, sxh, sxl):
+    total = None
+    for k, piece in enumerate(pieces, start):
+        at = plan.columns(place ^ k)
+        piece = parts_of(piece[...].reshape(-1, plan.block))
+        value = dot_parts(piece, (sxh[at, :], sxl[at, :]))
+        total = value if total is None else total + value
+    return total
+
+
+def first_rows(plan, ids, sxh, sxl, *refs):
+    place = lax.rem(ids[0], plan.half)
+    refs[-1][...] = x_rows(plan, place, refs[:-1], 0, sxh, sxl)
+
+
 def backward(plan, chunk, ready, last, ids, both, sxh, sxl, *refs):
     place = lax.rem(ids[0], plan.half)
-    pieces, refs = refs[: plan.half], refs[plan.half :]
+    count = 2 if last else plan.half
+    pieces, refs = refs[:count], refs[count:]
     before = dict(zip(ready, refs))
     outs, (high, low) = refs[len(ready) : -2], refs[-2:]
     folds = plan.folds
     shape = folds, plan.rows, plan.block
-    total = None
-    for k in range(plan.half):
-        at = plan.columns(place ^ k)
-        piece = parts_of(pieces[k][...].reshape(-1, plan.block))
-        value = dot_parts(piece, (sxh[at, :], sxl[at, :]))
-        total = value if total is None else total + value
+    if last:
+        total = pieces[0][...] + x_rows(plan, place, pieces[1:], plan.half - 1, sxh, sxl)
+    else:
+        total = x_rows(plan, place, pieces, 0, sxh, sxl)
     high[...], low[...] = parts_of(total)
     for j in range(plan.half):
         columns = pl.ds(j * plan.block, plan.block)
@@ -204,18 +218,18 @@
             pltpu.make_async_copy(held.at[j], out.at[:, :, columns], sent.at[j]).wait()
 
 
-def per_strip(plan, place, smu_z, smu_y, smu_x, edges, body):
+def per_strip(plan, place, smu_z, smu_y, smu_x, edges, body, strip=STRIP):
     across = smu_x[:, plan.columns(place)]
 
     def step(index, carry):
-        rows = pl.ds(pl.multiple_of(index * STRIP, STRIP), STRIP)
+        rows = pl.ds(pl.multiple_of(index * strip, strip), strip)
         plane = across + smu_y[rows, :]
         weights = edges[rows, 0:1], edges[rows, 1:2]
         for u in range(smu_z.shape[0]):
             body(u, rows, plane + smu_z[u : u + 1, :], weights)
         return carry
 
-    lax.fori_loop(0, plan.rows // STRIP, step, 0)
+    lax.fori_loop(0, plan.rows // strip, step, 0)
 
 
 class Cyclic:
@@ -423,7 +437,7 @@
             for j, value in enumerate(values):
                 outs[case ^ j][u, rows, :] = value
 
-        per_strip(plan, place, smu_z, smu_y, smu_x, edges, body)
+        per_strip(plan, place, smu_z, smu_y, smu_x, edges, body, 2 * STRIP)
 
     by_place(plan, place, with_place)
 
@@ -510,6 +524,13 @@
                 pltpu.VMEM((half,) + block, jnp.float32),
                 pltpu.SemaphoreType.DMA((half,)),
             ] + hold
+            early = call(
+                functools.partial(first_rows, plan),
+                f32((len(chunk) * plan.rows, plan.width)),
+                flops // 2,
+                (ids, *tables, *pieces[:-1]),
+            )
+            pieces = [early, pieces[-1]]
         ready = tuple(sorted(sums))
         parities = sorted(set(ready) | {c % 2 for c in chunk})
         result = call(

time: 98.8 us -> 97.4 us (0.986)
  starting transfers between devices: 26.9 us -> 24.8 us
    ppermute x22, starting transfers between devices: 26.9 us -> 24.8 us  [swap(): return lax.ppermute(values, axis, [(i, i ^ distance) for i in range(count)])]
    pallas_call x11 -> x12, Pallas kernels: 23.9 us -> 24.4 us  [call(): pl.pallas_call(kernel, out_shape=out_shape, in_specs=[smem] + [vmem] * (l...]
  transfers between devices with their start and end apart: 22 -> 22, of which waited for: 15 -> 14; matrix products, arithmetic and copies ran while one was open for 0% -> 0% of each run, Pallas kernels for 14% -> 16%
where the time goes in v14:
time: 97.4 us; the launch traced here: 97.3 us
  waiting for transfers between devices  46.6 us (48%)
  starting transfers between devices  24.8 us (25%)
  Pallas kernels  24.4 us (25%)
  local copies, waits for them, and re-layouts  1.09 us (1%)
    ppermute x22, waiting for transfers between devices, swap(): return lax.ppermute(values, axis, [(i, i ^ distance) for i in range(count)])  46.6 us
    ppermute x22, starting transfers between devices, swap(): return lax.ppermute(values, axis, [(i, i ^ distance) for i in range(count)])  24.8 us
    pallas_call x12, Pallas kernels, call(): pl.pallas_call(kernel, out_shape=out_shape, in_specs=[smem] + [vmem] * (l...  24.4 us
  transfers between devices with their start and end apart: 22, of which 14 were waited for; matrix products, arithmetic and copies ran while one was open for 0% of the time, Pallas kernels for 16%

profile of v14, /device:TPU:0, one launch (start us, length us, event | category | flops | bytes accessed | tf_op | source)
XLA Modules:
  0.0 97.3 jit_solution(13720176946230666894)
XLA Ops:
  1.1 1.7 %shard_map.127 = (bf16[1024,1024]{1,0:T(8,128)(2,1)S(1)}, bf16[1024,1024]{1,0:T(8,128)(2,1)S(1)}) custom-call(s32[2]{0:T(128)S(1)} %pad_add_fusion.ids, f32[128,1024]{1,0:T(8,128)S(1)} %copy-done.10), custom_call_target="tpu_custom_call" | custom-call | flops 4194304000 | bytes 524296 | tf_op jit(solution)/shard_map/pallas_call | solution.py:73
  2.9 2.8 %shard_map.128 = (f32[4,64,256]{2,1,0:T(8,128)S(1)}, f32[4,64,256]{2,1,0:T(8,128)S(1)}, f32[4,64,256]{2,1,0:T(8,128)S(1)}, f32[4,64,256]{2,1,0:T(8,128)S(1)}) custom-call(s32[2]{0:T(128)S(1)} %pad_add_fusion.ids, bf16[2,2,256,256]{3,2,1,0:T(8,128)(2,1)S(1)} %copy-done.9, f32[8,64,1024]{2,1,0:T(8,128)S(1)} %bitcast.4, ...), custom_call_target="tpu_custom_call" | custom-call | flops 2013265920 | bytes 6815752 | tf_op jit(solution)/shard_map/pallas_call | solution.py:73
  5.7 3.0 %collective-permute-start.3 = (f32[4,64,256]{2,1,0:T(8,128)S(1)}, f32[4,64,256]{2,1,0:T(8,128)S(1)}, u32[]{:S(2)}, u32[]{:S(2)}) collective-permute-start(f32[4,64,256]{2,1,0:T(8,128)S(1)} %get-tuple-element.40), channel_id=1, source_target_pairs={{0,4},{4,0},{8,12},{12,8},{16,20},{20,16},{24,28},{28,24},{1,5},{5... | collective-permute-start | bytes 786440 | tf_op jit(solution)/shard_map/ppermute | solution.py:448
  8.7 1.6 %collective-permute-start.4 = (f32[4,64,256]{2,1,0:T(8,128)S(1)}, f32[4,64,256]{2,1,0:T(8,128)S(1)}, u32[]{:S(2)}, u32[]{:S(2)}) collective-permute-start(f32[4,64,256]{2,1,0:T(8,128)S(1)} %get-tuple-element.41), channel_id=1, source_target_pairs={{0,8},{4,12},{8,0},{12,4},{16,24},{20,28},{24,16},{28,20},{1,9},{5... | collective-permute-start | bytes 786440 | tf_op jit(solution)/shard_map/ppermute | solution.py:448
  10.4 2.8 %shard_map.129 = (f32[4,64,256]{2,1,0:T(8,128)S(1)}, f32[4,64,256]{2,1,0:T(8,128)S(1)}, f32[4,64,256]{2,1,0:T(8,128)S(1)}, f32[4,64,256]{2,1,0:T(8,128)S(1)}) custom-call(s32[2]{0:T(128)S(1)} %pad_add_fusion.ids, bf16[2,2,256,256]{3,2,1,0:T(8,128)(2,1)S(1)} %copy-done.9, f32[8,64,1024]{2,1,0:T(8,128)S(1)} %bitcast.5, ...), custom_call_target="tpu_custom_call" | custom-call | flops 2013265920 | bytes 6815752 | tf_op jit(solution)/shard_map/pallas_call | solution.py:73
  13.3 1.8 %collective-permute-done.3.refs_1_ = f32[4,64,256]{2,1,0:T(8,128)S(1)} collective-permute-done((f32[4,64,256]{2,1,0:T(8,128)S(1)}, f32[4,64,256]{2,1,0:T(8,128)S(1)}, u32[]{:S(2)}, u32[]{:S(2)}) %collective-permute-start.3) | collective-permute-done | bytes 262176 | tf_op jit(solution)/shard_map/ppermute | solution.py:448
  15.0 2.9 %collective-permute-done.4.refs_2_ = f32[4,64,256]{2,1,0:T(8,128)S(1)} collective-permute-done((f32[4,64,256]{2,1,0:T(8,128)S(1)}, f32[4,64,256]{2,1,0:T(8,128)S(1)}, u32[]{:S(2)}, u32[]{:S(2)}) %collective-permute-start.4) | collective-permute-done | bytes 262176 | tf_op jit(solution)/shard_map/ppermute | solution.py:448
  18.0 3.9 %collective-permute-done.5.refs_3_ = f32[4,64,256]{2,1,0:T(8,128)S(1)} collective-permute-done((f32[4,64,256]{2,1,0:T(8,128)S(1)}, f32[4,64,256]{2,1,0:T(8,128)S(1)}, u32[]{:S(2)}, u32[]{:S(2)}) %collective-permute-start.5) | collective-permute-done | bytes 262176 | tf_op jit(solution)/shard_map/ppermute | solution.py:448
  21.9 1.9 %shard_map.131 = (f32[2,4,64,256]{3,2,1,0:T(8,128)S(1)}, f32[16,4,256]{2,1,0:T(4,128)S(1)}) custom-call(s32[2]{0:T(128)S(1)} %pad_add_fusion.ids, f32[4,1]{1,0:T(4,128)S(1)} %copy-done.7, f32[64,1]{1,0:T(8,128)S(1)} %copy-done.2, f32[1,1024]{1,0:T(1,128)S(1)} %copy-done.5, f32[64,2]{1,0:T(8,128)S(1)} %copy-done.1, ...), custom_call_target="tpu_custom_call" | custom-call | flops 26214400 | bytes 1053464 | tf_op jit(solution)/shard_map/pallas_call | solution.py:73
  23.8 2.8 %collective-permute-start.6 = (f32[2,4,64,256]{3,2,1,0:T(8,128)S(1)}, f32[2,4,64,256]{3,2,1,0:T(8,128)S(1)}, u32[]{:S(2)}, u32[]{:S(2)}) collective-permute-start(f32[2,4,64,256]{3,2,1,0:T(8,128)S(1)} %get-tuple-element.43), channel_id=1, source_target_pairs={{0,16},{4,20},{8,24},{12,28},{16,0},{20,4},{24,8},{28,12},{1,17},{... | collective-permute-start | bytes 1572872 | tf_op jit(solution)/shard_map/ppermute | solution.py:448
  26.6 1.5 %collective-permute-start = (f32[4,64,256]{2,1,0:T(8,128)S(1)}, f32[4,64,256]{2,1,0:T(8,128)S(1)}, u32[]{:S(2)}, u32[]{:S(2)}) collective-permute-start(f32[4,64,256]{2,1,0:T(8,128)S(1)} %get-tuple-element.35), channel_id=1, source_target_pairs={{0,4},{4,0},{8,12},{12,8},{16,20},{20,16},{24,28},{28,24},{1,5},{5... | collective-permute-start | bytes 786440 | tf_op jit(solution)/shard_map/ppermute | solution.py:448
  28.2 1.6 %collective-permute-start.1 = (f32[4,64,256]{2,1,0:T(8,128)S(1)}, f32[4,64,256]{2,1,0:T(8,128)S(1)}, u32[]{:S(2)}, u32[]{:S(2)}) collective-permute-start(f32[4,64,256]{2,1,0:T(8,128)S(1)} %get-tuple-element.36), channel_id=1, source_target_pairs={{0,8},{4,12},{8,0},{12,4},{16,24},{20,28},{24,16},{28,20},{1,9},{5... | collective-permute-start | bytes 786440 | tf_op jit(solution)/shard_map/ppermute | solution.py:448
  30.1 4.3 %collective-permute-done.9.refs_3_ = f32[16,4,256]{2,1,0:T(4,128)S(1)} collective-permute-done((f32[16,4,256]{2,1,0:T(4,128)S(1)}, f32[16,4,256]{2,1,0:T(4,128)S(1)}, u32[]{:S(2)}, u32[]{:S(2)}) %collective-permute-start.9) | collective-permute-done | bytes 65568 | tf_op jit(solution)/shard_map/ppermute | solution.py:448
  35.3 3.4 %collective-permute-done.8.refs_2_ = f32[16,4,256]{2,1,0:T(4,128)S(1)} collective-permute-done((f32[16,4,256]{2,1,0:T(4,128)S(1)}, f32[16,4,256]{2,1,0:T(4,128)S(1)}, u32[]{:S(2)}, u32[]{:S(2)}) %collective-permute-start.8) | collective-permute-done | bytes 65568 | tf_op jit(solution)/shard_map/ppermute | solution.py:448
  38.8 1.3 %collective-permute-done.7.refs_1_ = f32[16,4,256]{2,1,0:T(4,128)S(1)} collective-permute-done((f32[16,4,256]{2,1,0:T(4,128)S(1)}, f32[16,4,256]{2,1,0:T(4,128)S(1)}, u32[]{:S(2)}, u32[]{:S(2)}) %collective-permute-start.7) | collective-permute-done | bytes 65568 | tf_op jit(solution)/shard_map/ppermute | solution.py:448
  41.0 3.6 %collective-permute-done.1.refs_2_ = f32[4,64,256]{2,1,0:T(8,128)S(1)} collective-permute-done((f32[4,64,256]{2,1,0:T(8,128)S(1)}, f32[4,64,256]{2,1,0:T(8,128)S(1)}, u32[]{:S(2)}, u32[]{:S(2)}) %collective-permute-start.1) | collective-permute-done | bytes 262176 | tf_op jit(solution)/shard_map/ppermute | solution.py:448
  44.6 4.6 %collective-permute-done.2.refs_3_ = f32[4,64,256]{2,1,0:T(8,128)S(1)} collective-permute-done((f32[4,64,256]{2,1,0:T(8,128)S(1)}, f32[4,64,256]{2,1,0:T(8,128)S(1)}, u32[]{:S(2)}, u32[]{:S(2)}) %collective-permute-start.2) | collective-permute-done | bytes 262176 | tf_op jit(solution)/shard_map/ppermute | solution.py:448
  49.3 1.9 %shard_map.130 = (f32[2,4,64,256]{3,2,1,0:T(8,128)S(1)}, f32[16,4,256]{2,1,0:T(4,128)S(1)}) custom-call(s32[2]{0:T(128)S(1)} %pad_add_fusion.ids, f32[4,1]{1,0:T(4,128)S(1)} %copy-done.6, f32[64,1]{1,0:T(8,128)S(1)} %copy-done.2, f32[1,1024]{1,0:T(1,128)S(1)} %copy-done.5, f32[64,2]{1,0:T(8,128)S(1)} %copy-done.1, ...), custom_call_target="tpu_custom_call" | custom-call | flops 26214400 | bytes 1053464 | tf_op jit(solution)/shard_map/pallas_call | solution.py:73
  51.8 2.2 %collective-permute-start.11 = (f32[2,4,64,256]{3,2,1,0:T(8,128)S(1)}, f32[2,4,64,256]{3,2,1,0:T(8,128)S(1)}, u32[]{:S(2)}, u32[]{:S(2)}) collective-permute-start(f32[2,4,64,256]{3,2,1,0:T(8,128)S(1)} %get-tuple-element.45), channel_id=1, source_target_pairs={{0,16},{4,20},{8,24},{12,28},{16,0},{20,4},{24,8},{28,12},{1,17},{... | collective-permute-start | bytes 1572872 | tf_op jit(solution)/shard_map/ppermute | solution.py:448
  54.0 1.5 %collective-permute-start.13 = (f32[16,4,256]{2,1,0:T(4,128)S(1)}, f32[16,4,256]{2,1,0:T(4,128)S(1)}, u32[]{:S(2)}, u32[]{:S(2)}) collective-permute-start(f32[16,4,256]{2,1,0:T(4,128)S(1)} %get-tuple-element.46.refs_0_), channel_id=1, source_target_pairs={{0,2},{1,3},{2,0},{3,1},{4,6},{5,7},{6,4},{7,5},{8,10},{9,11},{10,... | collective-permute-start | bytes 196616 | tf_op jit(solution)/shard_map/ppermute | solution.py:448
  55.5 1.9 %shard_map.136 = (f32[4,64,256]{2,1,0:T(8,128)S(1)}, f32[4,64,256]{2,1,0:T(8,128)S(1)}, f32[4,64,256]{2,1,0:T(8,128)S(1)}, f32[4,64,256]{2,1,0:T(8,128)S(1)}) custom-call(s32[2]{0:T(128)S(1)} %pad_add_fusion.ids, f32[4,1]{1,0:T(4,128)S(1)} %copy-done.7, f32[64,1]{1,0:T(8,128)S(1)} %copy-done.2, f32[1,1024]{1,0:T(1,128)S(1)} %copy-done.5, ...), custom_call_target="tpu_custom_call" | custom-call | flops 26214400 | bytes 1708824 | tf_op jit(solution)/shard_map/pallas_call | solution.py:73
  58.4 2.1 %collective-permute-start.20 = (f32[4,64,256]{2,1,0:T(8,128)S(1)}, f32[4,64,256]{2,1,0:T(8,128)S(1)}, u32[]{:S(2)}, u32[]{:S(2)}) collective-permute-start(f32[4,64,256]{2,1,0:T(8,128)S(1)} %get-tuple-element.53), channel_id=1, source_target_pairs={{0,8},{4,12},{8,0},{12,4},{16,24},{20,28},{24,16},{28,20},{1,9},{5... | collective-permute-start | bytes 786440 | tf_op jit(solution)/shard_map/ppermute | solution.py:448
  60.9 1.3 %collective-permute-done.12.refs_1_ = f32[16,4,256]{2,1,0:T(4,128)S(1)} collective-permute-done((f32[16,4,256]{2,1,0:T(4,128)S(1)}, f32[16,4,256]{2,1,0:T(4,128)S(1)}, u32[]{:S(2)}, u32[]{:S(2)}) %collective-permute-start.12) | collective-permute-done | bytes 65568 | tf_op jit(solution)/shard_map/ppermute | solution.py:448
  63.0 1.9 %collective-permute-start.15 = (f32[16,4,256]{2,1,0:T(4,128)S(1)}, f32[16,4,256]{2,1,0:T(4,128)S(1)}, u32[]{:S(2)}, u32[]{:S(2)}) collective-permute-start(f32[16,4,256]{2,1,0:T(4,128)S(1)} %shard_map.133.refs_5_), channel_id=1, source_target_pairs={{0,16},{4,20},{8,24},{12,28},{16,0},{20,4},{24,8},{28,12},{1,17},{... | collective-permute-start | bytes 196616 | tf_op jit(solution)/shard_map/ppermute | solution.py:448
  64.9 13.3 %collective-permute-done.15.refs_6_ = f32[16,4,256]{2,1,0:T(4,128)S(1)} collective-permute-done((f32[16,4,256]{2,1,0:T(4,128)S(1)}, f32[16,4,256]{2,1,0:T(4,128)S(1)}, u32[]{:S(2)}, u32[]{:S(2)}) %collective-permute-start.15) | collective-permute-done | bytes 65568 | tf_op jit(solution)/shard_map/ppermute | solution.py:448
  78.2 2.0 %shard_map.134 = (f32[4,64,256]{2,1,0:T(8,128)S(1)}, f32[4,64,256]{2,1,0:T(8,128)S(1)}, f32[4,64,256]{2,1,0:T(8,128)S(1)}, f32[4,64,256]{2,1,0:T(8,128)S(1)}) custom-call(s32[2]{0:T(128)S(1)} %pad_add_fusion.ids, f32[4,1]{1,0:T(4,128)S(1)} %copy-done.6, f32[64,1]{1,0:T(8,128)S(1)} %copy-done.2, f32[1,1024]{1,0:T(1,128)S(1)} %copy-done.5, ...), custom_call_target="tpu_custom_call" | custom-call | flops 26214400 | bytes 1708824 | tf_op jit(solution)/shard_map/pallas_call | solution.py:73
  80.9 3.1 %collective-permute-start.17 = (f32[4,64,256]{2,1,0:T(8,128)S(1)}, f32[4,64,256]{2,1,0:T(8,128)S(1)}, u32[]{:S(2)}, u32[]{:S(2)}) collective-permute-start(f32[4,64,256]{2,1,0:T(8,128)S(1)} %get-tuple-element.49), channel_id=1, source_target_pairs={{0,8},{4,12},{8,0},{12,4},{16,24},{20,28},{24,16},{28,20},{1,9},{5... | collective-permute-start | bytes 786440 | tf_op jit(solution)/shard_map/ppermute | solution.py:448
  84.0 2.8 %shard_map.137.refs_2_ = f32[4,64,1024]{2,1,0:T(8,128)S(1)} custom-call(s32[2]{0:T(128)S(1)} %pad_add_fusion.ids, bf16[2,2,256,256]{3,2,1,0:T(8,128)(2,1)S(1)} %copy-done, bf16[1024,1024]{1,0:T(8,128)(2,1)S(1)} %get-tuple-element.30.sxh, bf16[1024,1024]{1,0:T(8,128)(2,1)S(1)} %get-tuple-element.31.sxl, f32[4,64,256]{2,1,0:T(8,128)S(1)} %get-tuple-element.51.refs_0_, ...), custom_call_target="tpu_custom_call" | custom-call | flops 2013265920 | bytes 5767176 | tf_op jit(solution)/shard_map/pallas_call | solution.py:73
  86.8 3.6 %collective-permute-done.16.refs_1_ = f32[4,64,256]{2,1,0:T(8,128)S(1)} collective-permute-done((f32[4,64,256]{2,1,0:T(8,128)S(1)}, f32[4,64,256]{2,1,0:T(8,128)S(1)}, u32[]{:S(2)}, u32[]{:S(2)}) %collective-permute-start.16) | collective-permute-done | bytes 262176 | tf_op jit(solution)/shard_map/ppermute | solution.py:448
  91.2 1.9 %shard_map.135.refs_0_ = f32[256,1024]{1,0:T(8,128)S(1)} custom-call(s32[2]{0:T(128)S(1)} %pad_add_fusion.ids, bf16[1024,1024]{1,0:T(8,128)(2,1)S(1)} %get-tuple-element.30.sxh, bf16[1024,1024]{1,0:T(8,128)(2,1)S(1)} %get-tuple-element.31.sxl, f32[4,64,256]{2,1,0:T(8,128)S(1)} %get-tuple-element.47.refs_0_, ...), custom_call_target="tpu_custom_call" | custom-call | flops 1006632960 | bytes 4980744 | tf_op jit(solution)/shard_map/pallas_call | solution.py:73
  93.1 1.2 %collective-permute-done.18.refs_1_ = f32[4,64,256]{2,1,0:T(8,128)S(1)} collective-permute-done((f32[4,64,256]{2,1,0:T(8,128)S(1)}, f32[4,64,256]{2,1,0:T(8,128)S(1)}, u32[]{:S(2)}, u32[]{:S(2)}) %collective-permute-start.18) | collective-permute-done | bytes 262176 | tf_op jit(solution)/shard_map/ppermute | solution.py:448
  94.3 2.8 %shard_map.138 = f32[8,64,1024]{2,1,0:T(8,128)} custom-call(s32[2]{0:T(128)S(1)} %pad_add_fusion.ids, bf16[2,2,256,256]{3,2,1,0:T(8,128)(2,1)S(1)} %copy-done, bf16[1024,1024]{1,0:T(8,128)(2,1)S(1)} %get-tuple-element.30.sxh, bf16[1024,1024]{1,0:T(8,128)(2,1)S(1)} %get-tuple-element.31.sxl, f32[256,1024]{1,0:T(8,128)S(1)} %shard_map.135.refs_0_, ...), custom_call_target="tpu_custom_call" | custom-call | flops 2013265920 | bytes 7077896 | tf_op jit(solution)/shard_map/pallas_call | solution.py:73
  (47 shorter events, 7.7 us)
Async XLA Ops:
  1.1 1.7 %copy-start.8 = (f32[1,8,64,1024]{3,2,1,0:T(8,128)S(1)}, f32[1,8,64,1024]{3,2,1,0:T(8,128)}, u32[]{:S(2)}) copy-start(f32[1,8,64,1024]{3,2,1,0:T(8,128)} %param.13) | copy-start | bytes 6291460
  1.1 1.7 %copy-start.9 = (bf16[2,2,256,256]{3,2,1,0:T(8,128)(2,1)S(1)}, bf16[2,2,256,256]{3,2,1,0:T(8,128)(2,1)}, u32[]{:S(2)}) copy-start(bf16[2,2,256,256]{3,2,1,0:T(8,128)(2,1)} %constant.51.both) | copy-start | bytes 1572868
  5.7 9.3 %collective-permute-start.3 = (f32[4,64,256]{2,1,0:T(8,128)S(1)}, f32[4,64,256]{2,1,0:T(8,128)S(1)}, u32[]{:S(2)}, u32[]{:S(2)}) collective-permute-start(f32[4,64,256]{2,1,0:T(8,128)S(1)} %get-tuple-element.40), channel_id=1, source_target_pairs={{0,4},{4,0},{8,12},{12,8},{16,20},{20,16},{24,28},{28,24},{1,5},{5... | collective-permute-start | bytes 786440 | tf_op jit(solution)/shard_map/ppermute | solution.py:448
  8.7 9.2 %collective-permute-start.4 = (f32[4,64,256]{2,1,0:T(8,128)S(1)}, f32[4,64,256]{2,1,0:T(8,128)S(1)}, u32[]{:S(2)}, u32[]{:S(2)}) collective-permute-start(f32[4,64,256]{2,1,0:T(8,128)S(1)} %get-tuple-element.41), channel_id=1, source_target_pairs={{0,8},{4,12},{8,0},{12,4},{16,24},{20,28},{24,16},{28,20},{1,9},{5... | collective-permute-start | bytes 786440 | tf_op jit(solution)/shard_map/ppermute | solution.py:448
  10.3 11.6 %copy-start.1 = (f32[64,2]{1,0:T(8,128)S(1)}, f32[64,2]{1,0:T(8,128)}, u32[]{:S(2)}) copy-start(f32[64,2]{1,0:T(8,128)} %constant.35.clone.edges) | copy-start | bytes 1540
  10.3 11.6 %copy-start.2 = (f32[64,1]{1,0:T(8,128)S(1)}, f32[64,1]{1,0:T(8,128)}, u32[]{:S(2)}) copy-start(f32[64,1]{1,0:T(8,128)} %constant.33.clone.smu_y) | copy-start | bytes 772
  10.3 11.6 %copy-start.5 = (f32[1,1024]{1,0:T(1,128)S(1)}, f32[1,1024]{1,0:T(1,128)}, u32[]{:S(2)}) copy-start(f32[1,1024]{1,0:T(1,128)} %constant.34.clone.smu_x) | copy-start | bytes 12292
  10.3 11.6 %copy-start.7 = (f32[4,1]{1,0:T(4,128)S(1)}, f32[4,1]{1,0:T(4,128)}, u32[]{:S(2)}) copy-start(f32[4,1]{1,0:T(4,128)} %constant.41.clone.smu_z) | copy-start | bytes 52
  10.3 29.7 %copy-start.4 = (f32[5,4,4,1024]{3,2,1,0:T(4,128)S(1)}, f32[5,4,4,1024]{3,2,1,0:T(4,128)}, u32[]{:S(2)}) copy-start(f32[5,4,4,1024]{3,2,1,0:T(4,128)} %constant.43.clone.responses) | copy-start | bytes 983044
  10.3 38.9 %copy-start.6 = (f32[4,1]{1,0:T(4,128)S(1)}, f32[4,1]{1,0:T(4,128)}, u32[]{:S(2)}) copy-start(f32[4,1]{1,0:T(4,128)} %constant.42.clone.smu_z) | copy-start | bytes 52
  10.3 11.6 %collective-permute-start.5 = (f32[4,64,256]{2,1,0:T(8,128)S(1)}, f32[4,64,256]{2,1,0:T(8,128)S(1)}, u32[]{:S(2)}, u32[]{:S(2)}) collective-permute-start(f32[4,64,256]{2,1,0:T(8,128)S(1)} %get-tuple-element.42), channel_id=1, source_target_pairs={{0,12},{4,8},{8,4},{12,0},{16,28},{20,24},{24,20},{28,16},{1,13},{... | collective-permute-start | bytes 786440 | tf_op jit(solution)/shard_map/ppermute | solution.py:448
  13.3 48.9 %copy-start.3 = (f32[5,4,4,1024]{3,2,1,0:T(4,128)S(1)}, f32[5,4,4,1024]{3,2,1,0:T(4,128)}, u32[]{:S(2)}) copy-start(f32[5,4,4,1024]{3,2,1,0:T(4,128)} %constant.44.clone.responses) | copy-start | bytes 983044
  23.8 27.9 %collective-permute-start.6 = (f32[2,4,64,256]{3,2,1,0:T(8,128)S(1)}, f32[2,4,64,256]{3,2,1,0:T(8,128)S(1)}, u32[]{:S(2)}, u32[]{:S(2)}) collective-permute-start(f32[2,4,64,256]{3,2,1,0:T(8,128)S(1)} %get-tuple-element.43), channel_id=1, source_target_pairs={{0,16},{4,20},{8,24},{12,28},{16,0},{20,4},{24,8},{28,12},{1,17},{... | collective-permute-start | bytes 1572872 | tf_op jit(solution)/shard_map/ppermute | solution.py:448
  26.6 14.4 %collective-permute-start = (f32[4,64,256]{2,1,0:T(8,128)S(1)}, f32[4,64,256]{2,1,0:T(8,128)S(1)}, u32[]{:S(2)}, u32[]{:S(2)}) collective-permute-start(f32[4,64,256]{2,1,0:T(8,128)S(1)} %get-tuple-element.35), channel_id=1, source_target_pairs={{0,4},{4,0},{8,12},{12,8},{16,20},{20,16},{24,28},{28,24},{1,5},{5... | collective-permute-start | bytes 786440 | tf_op jit(solution)/shard_map/ppermute | solution.py:448
  28.2 16.5 %collective-permute-start.1 = (f32[4,64,256]{2,1,0:T(8,128)S(1)}, f32[4,64,256]{2,1,0:T(8,128)S(1)}, u32[]{:S(2)}, u32[]{:S(2)}) collective-permute-start(f32[4,64,256]{2,1,0:T(8,128)S(1)} %get-tuple-element.36), channel_id=1, source_target_pairs={{0,8},{4,12},{8,0},{12,4},{16,24},{20,28},{24,16},{28,20},{1,9},{5... | collective-permute-start | bytes 786440 | tf_op jit(solution)/shard_map/ppermute | solution.py:448
  29.8 19.5 %collective-permute-start.2 = (f32[4,64,256]{2,1,0:T(8,128)S(1)}, f32[4,64,256]{2,1,0:T(8,128)S(1)}, u32[]{:S(2)}, u32[]{:S(2)}) collective-permute-start(f32[4,64,256]{2,1,0:T(8,128)S(1)} %get-tuple-element.37), channel_id=1, source_target_pairs={{0,12},{4,8},{8,4},{12,0},{16,28},{20,24},{24,20},{28,16},{1,13},{... | collective-permute-start | bytes 786440 | tf_op jit(solution)/shard_map/ppermute | solution.py:448
  30.1 4.3 %collective-permute-start.9 = (f32[16,4,256]{2,1,0:T(4,128)S(1)}, f32[16,4,256]{2,1,0:T(4,128)S(1)}, u32[]{:S(2)}, u32[]{:S(2)}) collective-permute-start(f32[16,4,256]{2,1,0:T(4,128)S(1)} %get-tuple-element.44.refs_0_), channel_id=1, source_target_pairs={{0,3},{1,2},{2,1},{3,0},{4,7},{5,6},{6,5},{7,4},{8,11},{9,10},{10,... | collective-permute-start | bytes 196616 | tf_op jit(solution)/shard_map/ppermute | solution.py:448
  34.5 4.3 %collective-permute-start.8 = (f32[16,4,256]{2,1,0:T(4,128)S(1)}, f32[16,4,256]{2,1,0:T(4,128)S(1)}, u32[]{:S(2)}, u32[]{:S(2)}) collective-permute-start(f32[16,4,256]{2,1,0:T(4,128)S(1)} %get-tuple-element.44.refs_0_), channel_id=1, source_target_pairs={{0,2},{1,3},{2,0},{3,1},{4,6},{5,7},{6,4},{7,5},{8,10},{9,11},{10,... | collective-permute-start | bytes 196616 | tf_op jit(solution)/shard_map/ppermute | solution.py:448
  38.7 1.3 %collective-permute-start.7 = (f32[16,4,256]{2,1,0:T(4,128)S(1)}, f32[16,4,256]{2,1,0:T(4,128)S(1)}, u32[]{:S(2)}, u32[]{:S(2)}) collective-permute-start(f32[16,4,256]{2,1,0:T(4,128)S(1)} %get-tuple-element.44.refs_0_), channel_id=1, source_target_pairs={{0,1},{1,0},{2,3},{3,2},{4,5},{5,4},{6,7},{7,6},{8,9},{9,8},{10,11... | collective-permute-start | bytes 196616 | tf_op jit(solution)/shard_map/ppermute | solution.py:448
  40.9 10.9 %collective-permute-start.10 = (f32[16,4,256]{2,1,0:T(4,128)S(1)}, f32[16,4,256]{2,1,0:T(4,128)S(1)}, u32[]{:S(2)}, u32[]{:S(2)}) collective-permute-start(f32[16,4,256]{2,1,0:T(4,128)S(1)} %shard_map.132.refs_5_), channel_id=1, source_target_pairs={{0,16},{4,20},{8,24},{12,28},{16,0},{20,4},{24,8},{28,12},{1,17},{... | collective-permute-start | bytes 196616 | tf_op jit(solution)/shard_map/ppermute | solution.py:448
  51.8 26.4 %collective-permute-start.11 = (f32[2,4,64,256]{3,2,1,0:T(8,128)S(1)}, f32[2,4,64,256]{3,2,1,0:T(8,128)S(1)}, u32[]{:S(2)}, u32[]{:S(2)}) collective-permute-start(f32[2,4,64,256]{3,2,1,0:T(8,128)S(1)} %get-tuple-element.45), channel_id=1, source_target_pairs={{0,16},{4,20},{8,24},{12,28},{16,0},{20,4},{24,8},{28,12},{1,17},{... | collective-permute-start | bytes 1572872 | tf_op jit(solution)/shard_map/ppermute | solution.py:448
  53.9 30.0 %copy-start = (bf16[2,2,256,256]{3,2,1,0:T(8,128)(2,1)S(1)}, bf16[2,2,256,256]{3,2,1,0:T(8,128)(2,1)}, u32[]{:S(2)}) copy-start(bf16[2,2,256,256]{3,2,1,0:T(8,128)(2,1)} %constant.48.both) | copy-start | bytes 1572868
  54.0 6.6 %collective-permute-start.14 = (f32[16,4,256]{2,1,0:T(4,128)S(1)}, f32[16,4,256]{2,1,0:T(4,128)S(1)}, u32[]{:S(2)}, u32[]{:S(2)}) collective-permute-start(f32[16,4,256]{2,1,0:T(4,128)S(1)} %get-tuple-element.46.refs_0_), channel_id=1, source_target_pairs={{0,3},{1,2},{2,1},{3,0},{4,7},{5,6},{6,5},{7,4},{8,11},{9,10},{10,... | collective-permute-start | bytes 196616 | tf_op jit(solution)/shard_map/ppermute | solution.py:448
  54.0 7.0 %collective-permute-start.13 = (f32[16,4,256]{2,1,0:T(4,128)S(1)}, f32[16,4,256]{2,1,0:T(4,128)S(1)}, u32[]{:S(2)}, u32[]{:S(2)}) collective-permute-start(f32[16,4,256]{2,1,0:T(4,128)S(1)} %get-tuple-element.46.refs_0_), channel_id=1, source_target_pairs={{0,2},{1,3},{2,0},{3,1},{4,6},{5,7},{6,4},{7,5},{8,10},{9,11},{10,... | collective-permute-start | bytes 196616 | tf_op jit(solution)/shard_map/ppermute | solution.py:448
  57.3 26.6 %collective-permute-start.19 = (f32[4,64,256]{2,1,0:T(8,128)S(1)}, f32[4,64,256]{2,1,0:T(8,128)S(1)}, u32[]{:S(2)}, u32[]{:S(2)}) collective-permute-start(f32[4,64,256]{2,1,0:T(8,128)S(1)} %get-tuple-element.52), channel_id=1, source_target_pairs={{0,4},{4,0},{8,12},{12,8},{16,20},{20,16},{24,28},{28,24},{1,5},{5... | collective-permute-start | bytes 786440 | tf_op jit(solution)/shard_map/ppermute | solution.py:448
  58.4 25.6 %collective-permute-start.20 = (f32[4,64,256]{2,1,0:T(8,128)S(1)}, f32[4,64,256]{2,1,0:T(8,128)S(1)}, u32[]{:S(2)}, u32[]{:S(2)}) collective-permute-start(f32[4,64,256]{2,1,0:T(8,128)S(1)} %get-tuple-element.53), channel_id=1, source_target_pairs={{0,8},{4,12},{8,0},{12,4},{16,24},{20,28},{24,16},{28,20},{1,9},{5... | collective-permute-start | bytes 786440 | tf_op jit(solution)/shard_map/ppermute | solution.py:448
  60.5 23.4 %collective-permute-start.21 = (f32[4,64,256]{2,1,0:T(8,128)S(1)}, f32[4,64,256]{2,1,0:T(8,128)S(1)}, u32[]{:S(2)}, u32[]{:S(2)}) collective-permute-start(f32[4,64,256]{2,1,0:T(8,128)S(1)} %get-tuple-element.54), channel_id=1, source_target_pairs={{0,12},{4,8},{8,4},{12,0},{16,28},{20,24},{24,20},{28,16},{1,13},{... | collective-permute-start | bytes 786440 | tf_op jit(solution)/shard_map/ppermute | solution.py:448
  60.9 1.3 %collective-permute-start.12 = (f32[16,4,256]{2,1,0:T(4,128)S(1)}, f32[16,4,256]{2,1,0:T(4,128)S(1)}, u32[]{:S(2)}, u32[]{:S(2)}) collective-permute-start(f32[16,4,256]{2,1,0:T(4,128)S(1)} %get-tuple-element.46.refs_0_), channel_id=1, source_target_pairs={{0,1},{1,0},{2,3},{3,2},{4,5},{5,4},{6,7},{7,6},{8,9},{9,8},{10,11... | collective-permute-start | bytes 196616 | tf_op jit(solution)/shard_map/ppermute | solution.py:448
  63.0 15.2 %collective-permute-start.15 = (f32[16,4,256]{2,1,0:T(4,128)S(1)}, f32[16,4,256]{2,1,0:T(4,128)S(1)}, u32[]{:S(2)}, u32[]{:S(2)}) collective-permute-start(f32[16,4,256]{2,1,0:T(4,128)S(1)} %shard_map.133.refs_5_), channel_id=1, source_target_pairs={{0,16},{4,20},{8,24},{12,28},{16,0},{20,4},{24,8},{28,12},{1,17},{... | collective-permute-start | bytes 196616 | tf_op jit(solution)/shard_map/ppermute | solution.py:448
  80.3 10.2 %collective-permute-start.16 = (f32[4,64,256]{2,1,0:T(8,128)S(1)}, f32[4,64,256]{2,1,0:T(8,128)S(1)}, u32[]{:S(2)}, u32[]{:S(2)}) collective-permute-start(f32[4,64,256]{2,1,0:T(8,128)S(1)} %get-tuple-element.48), channel_id=1, source_target_pairs={{0,4},{4,0},{8,12},{12,8},{16,20},{20,16},{24,28},{28,24},{1,5},{5... | collective-permute-start | bytes 786440 | tf_op jit(solution)/shard_map/ppermute | solution.py:448
  80.9 10.3 %collective-permute-start.17 = (f32[4,64,256]{2,1,0:T(8,128)S(1)}, f32[4,64,256]{2,1,0:T(8,128)S(1)}, u32[]{:S(2)}, u32[]{:S(2)}) collective-permute-start(f32[4,64,256]{2,1,0:T(8,128)S(1)} %get-tuple-element.49), channel_id=1, source_target_pairs={{0,8},{4,12},{8,0},{12,4},{16,24},{20,28},{24,16},{28,20},{1,9},{5... | collective-permute-start | bytes 786440 | tf_op jit(solution)/shard_map/ppermute | solution.py:448
  83.9 10.4 %collective-permute-start.18 = (f32[4,64,256]{2,1,0:T(8,128)S(1)}, f32[4,64,256]{2,1,0:T(8,128)S(1)}, u32[]{:S(2)}, u32[]{:S(2)}) collective-permute-start(f32[4,64,256]{2,1,0:T(8,128)S(1)} %get-tuple-element.50), channel_id=1, source_target_pairs={{0,12},{4,8},{8,4},{12,0},{16,28},{20,24},{24,20},{28,16},{1,13},{... | collective-permute-start | bytes 786440 | tf_op jit(solution)/shard_map/ppermute | solution.py:448
  (1 other events, 1.0 us)

commit v15 on v14

--- a/solution.py
+++ b/solution.py
@@ -93,6 +93,13 @@
         self.block = self.width // self.half
         self.folds = self.depth // 2
 
+    @property
+    def order(self):
+        return [0] + list(range(self.half - 1, 0, -1))
+
+    def by_distance(self, refs):
+        return [ref for _, ref in sorted(zip(self.order, refs), key=lambda x: x[0])]
+
     def columns(self, owner):
         return pl.ds(pl.multiple_of(owner * self.block, LANES), self.block)
 
@@ -168,7 +175,7 @@
 
 def x_rows(plan, place, pieces, start, sxh, sxl):
     total = None
-    for k, piece in enumerate(pieces, start):
+    for k, piece in zip(plan.order[start:], pieces):
         at = plan.columns(place ^ k)
         piece = parts_of(piece[...].reshape(-1, plan.block))
         value = dot_parts(piece, (sxh[at, :], sxl[at, :]))
@@ -275,7 +282,7 @@
 
 
 def half_end(plan, ids, smu_z, smu_y, smu_x, edges, *refs):
-    pieces = refs[: plan.half]
+    pieces = plan.by_distance(refs[: plan.half])
     ends, seen, sums = refs[plan.half :]
     steps, half = plan.steps, plan.half
     place = lax.rem(ids[0], half)
@@ -402,7 +409,7 @@
 
 
 def half_solve(plan, ids, smu_z, smu_y, smu_x, edges, *refs):
-    pieces = refs[: plan.half]
+    pieces = plan.by_distance(refs[: plan.half])
     far, beside, beside_far = refs[plan.half : plan.half + 3]
     outs = refs[plan.half + 3 :]
     half = plan.half
@@ -479,7 +486,7 @@
             flops,
             (ids, forth, field, *tables),
         )
-        pieces = [swap(v, "tm", steps, k) for k, v in enumerate(pieces)]
+        pieces = [swap(pieces[k], "tm", steps, k) for k in plan.order]
         smu_own = jnp.asarray(smu_z[list(chunk), None], jnp.float32)
         work.append((chunk, modes, flops, (ids, smu_own, smu_y, smu_x, edges), pieces))
     first, second = work[0][-1], work[1][-1]
@@ -514,7 +521,7 @@
             100 * modes.size * half,
             (*small, *pieces, far, beside, beside_far),
         )
-        pieces = [swap(v, "tm", steps, k) for k, v in enumerate(pieces)]
+        pieces = [swap(pieces[k], "tm", steps, k) for k in plan.order]
         last = chunk == CHUNKS[-1]
         part = pltpu.VMEM((len(chunk) * plan.rows, plan.width), jnp.bfloat16)
         hold = [part, part]

time: 97.4 us -> 99.7 us (1.024)
  waiting for transfers between devices: 46.6 us -> 48.1 us
    ppermute x22, waiting for transfers between devices: 46.6 us -> 48.1 us  [swap(): return lax.ppermute(values, axis, [(i, i ^ distance) for i in range(count)])]
  transfers between devices with their start and end apart: 22 -> 22, of which waited for: 14 -> 11; matrix products, arithmetic and copies ran while one was open for 0% -> 0% of each run, Pallas kernels for 16% -> 15%
where the time goes in v15:
time: 99.7 us; the launch traced here: 99.5 us
  waiting for transfers between devices  48.1 us (48%)
  starting transfers between devices  25.5 us (26%)
  Pallas kernels  24.4 us (24%)
  local copies, waits for them, and re-layouts  1.09 us (1%)
    ppermute x22, waiting for transfers between devices, swap(): return lax.ppermute(values, axis, [(i, i ^ distance) for i in range(count)])  48.1 us
    ppermute x22, starting transfers between devices, swap(): return lax.ppermute(values, axis, [(i, i ^ distance) for i in range(count)])  25.5 us
    pallas_call x12, Pallas kernels, call(): pl.pallas_call(kernel, out_shape=out_shape, in_specs=[smem] + [vmem] * (l...  24.4 us
  transfers between devices with their start and end apart: 22, of which 11 were waited for; matrix products, arithmetic and copies ran while one was open for 0% of the time, Pallas kernels for 15%

profile of v15, /device:TPU:0, one launch (start us, length us, event | category | flops | bytes accessed | tf_op | source)
XLA Modules:
  0.0 99.5 jit_solution(2264758973949459964)
XLA Ops:
  0.1 1.0 %copy-done.10 = f32[128,1024]{1,0:T(8,128)S(1)} copy-done((f32[128,1024]{1,0:T(8,128)S(1)}, f32[128,1024]{1,0:T(8,128)}, u32[]{:S(2)}) %copy-start.10) | copy-done | bytes 524312
  1.1 1.7 %shard_map.127 = (bf16[1024,1024]{1,0:T(8,128)(2,1)S(1)}, bf16[1024,1024]{1,0:T(8,128)(2,1)S(1)}) custom-call(s32[2]{0:T(128)S(1)} %pad_add_fusion.ids, f32[128,1024]{1,0:T(8,128)S(1)} %copy-done.10), custom_call_target="tpu_custom_call" | custom-call | flops 4194304000 | bytes 524296 | tf_op jit(solution)/shard_map/pallas_call | solution.py:73
  2.9 2.8 %shard_map.128 = (f32[4,64,256]{2,1,0:T(8,128)S(1)}, f32[4,64,256]{2,1,0:T(8,128)S(1)}, f32[4,64,256]{2,1,0:T(8,128)S(1)}, f32[4,64,256]{2,1,0:T(8,128)S(1)}) custom-call(s32[2]{0:T(128)S(1)} %pad_add_fusion.ids, bf16[2,2,256,256]{3,2,1,0:T(8,128)(2,1)S(1)} %copy-done.9, f32[8,64,1024]{2,1,0:T(8,128)S(1)} %bitcast.4, ...), custom_call_target="tpu_custom_call" | custom-call | flops 2013265920 | bytes 6815752 | tf_op jit(solution)/shard_map/pallas_call | solution.py:73
  5.7 4.1 %collective-permute-start.3 = (f32[4,64,256]{2,1,0:T(8,128)S(1)}, f32[4,64,256]{2,1,0:T(8,128)S(1)}, u32[]{:S(2)}, u32[]{:S(2)}) collective-permute-start(f32[4,64,256]{2,1,0:T(8,128)S(1)} %get-tuple-element.40), channel_id=1, source_target_pairs={{0,12},{4,8},{8,4},{12,0},{16,28},{20,24},{24,20},{28,16},{1,13},{... | collective-permute-start | bytes 786440 | tf_op jit(solution)/shard_map/ppermute | solution.py:455
  10.5 2.8 %shard_map.129 = (f32[4,64,256]{2,1,0:T(8,128)S(1)}, f32[4,64,256]{2,1,0:T(8,128)S(1)}, f32[4,64,256]{2,1,0:T(8,128)S(1)}, f32[4,64,256]{2,1,0:T(8,128)S(1)}) custom-call(s32[2]{0:T(128)S(1)} %pad_add_fusion.ids, bf16[2,2,256,256]{3,2,1,0:T(8,128)(2,1)S(1)} %copy-done.9, f32[8,64,1024]{2,1,0:T(8,128)S(1)} %bitcast.5, ...), custom_call_target="tpu_custom_call" | custom-call | flops 2013265920 | bytes 6815752 | tf_op jit(solution)/shard_map/pallas_call | solution.py:73
  13.3 3.6 %collective-permute-done.3.refs_1_ = f32[4,64,256]{2,1,0:T(8,128)S(1)} collective-permute-done((f32[4,64,256]{2,1,0:T(8,128)S(1)}, f32[4,64,256]{2,1,0:T(8,128)S(1)}, u32[]{:S(2)}, u32[]{:S(2)}) %collective-permute-start.3) | collective-permute-done | bytes 262176 | tf_op jit(solution)/shard_map/ppermute | solution.py:455
  16.9 4.9 %collective-permute-done.4.refs_2_ = f32[4,64,256]{2,1,0:T(8,128)S(1)} collective-permute-done((f32[4,64,256]{2,1,0:T(8,128)S(1)}, f32[4,64,256]{2,1,0:T(8,128)S(1)}, u32[]{:S(2)}, u32[]{:S(2)}) %collective-permute-start.4) | collective-permute-done | bytes 262176 | tf_op jit(solution)/shard_map/ppermute | solution.py:455
  21.9 1.9 %shard_map.131 = (f32[2,4,64,256]{3,2,1,0:T(8,128)S(1)}, f32[16,4,256]{2,1,0:T(4,128)S(1)}) custom-call(s32[2]{0:T(128)S(1)} %pad_add_fusion.ids, f32[4,1]{1,0:T(4,128)S(1)} %copy-done.7, f32[64,1]{1,0:T(8,128)S(1)} %copy-done.2, f32[1,1024]{1,0:T(1,128)S(1)} %copy-done.5, f32[64,2]{1,0:T(8,128)S(1)} %copy-done.1, ...), custom_call_target="tpu_custom_call" | custom-call | flops 26214400 | bytes 1053464 | tf_op jit(solution)/shard_map/pallas_call | solution.py:73
  23.8 2.7 %collective-permute-start.6 = (f32[2,4,64,256]{3,2,1,0:T(8,128)S(1)}, f32[2,4,64,256]{3,2,1,0:T(8,128)S(1)}, u32[]{:S(2)}, u32[]{:S(2)}) collective-permute-start(f32[2,4,64,256]{3,2,1,0:T(8,128)S(1)} %get-tuple-element.43), channel_id=1, source_target_pairs={{0,16},{4,20},{8,24},{12,28},{16,0},{20,4},{24,8},{28,12},{1,17},{... | collective-permute-start | bytes 1572872 | tf_op jit(solution)/shard_map/ppermute | solution.py:455
  26.5 2.4 %collective-permute-start = (f32[4,64,256]{2,1,0:T(8,128)S(1)}, f32[4,64,256]{2,1,0:T(8,128)S(1)}, u32[]{:S(2)}, u32[]{:S(2)}) collective-permute-start(f32[4,64,256]{2,1,0:T(8,128)S(1)} %get-tuple-element.35), channel_id=1, source_target_pairs={{0,12},{4,8},{8,4},{12,0},{16,28},{20,24},{24,20},{28,16},{1,13},{... | collective-permute-start | bytes 786440 | tf_op jit(solution)/shard_map/ppermute | solution.py:455
  30.0 4.3 %collective-permute-done.9.refs_3_ = f32[16,4,256]{2,1,0:T(4,128)S(1)} collective-permute-done((f32[16,4,256]{2,1,0:T(4,128)S(1)}, f32[16,4,256]{2,1,0:T(4,128)S(1)}, u32[]{:S(2)}, u32[]{:S(2)}) %collective-permute-start.9) | collective-permute-done | bytes 65568 | tf_op jit(solution)/shard_map/ppermute | solution.py:455
  34.3 0.8 collective-permute-start.8
  35.1 3.4 %collective-permute-done.8.refs_2_ = f32[16,4,256]{2,1,0:T(4,128)S(1)} collective-permute-done((f32[16,4,256]{2,1,0:T(4,128)S(1)}, f32[16,4,256]{2,1,0:T(4,128)S(1)}, u32[]{:S(2)}, u32[]{:S(2)}) %collective-permute-start.8) | collective-permute-done | bytes 65568 | tf_op jit(solution)/shard_map/ppermute | solution.py:455
  38.6 1.3 %collective-permute-done.7.refs_1_ = f32[16,4,256]{2,1,0:T(4,128)S(1)} collective-permute-done((f32[16,4,256]{2,1,0:T(4,128)S(1)}, f32[16,4,256]{2,1,0:T(4,128)S(1)}, u32[]{:S(2)}, u32[]{:S(2)}) %collective-permute-start.7) | collective-permute-done | bytes 65568 | tf_op jit(solution)/shard_map/ppermute | solution.py:455
  39.8 0.9 shard_map.132.refs_5_
  41.1 3.3 %collective-permute-done.refs_1_ = f32[4,64,256]{2,1,0:T(8,128)S(1)} collective-permute-done((f32[4,64,256]{2,1,0:T(8,128)S(1)}, f32[4,64,256]{2,1,0:T(8,128)S(1)}, u32[]{:S(2)}, u32[]{:S(2)}) %collective-permute-start) | collective-permute-done | bytes 262176 | tf_op jit(solution)/shard_map/ppermute | solution.py:455
  44.5 7.7 %collective-permute-done.1.refs_2_ = f32[4,64,256]{2,1,0:T(8,128)S(1)} collective-permute-done((f32[4,64,256]{2,1,0:T(8,128)S(1)}, f32[4,64,256]{2,1,0:T(8,128)S(1)}, u32[]{:S(2)}, u32[]{:S(2)}) %collective-permute-start.1) | collective-permute-done | bytes 262176 | tf_op jit(solution)/shard_map/ppermute | solution.py:455
  52.2 1.9 %shard_map.130 = (f32[2,4,64,256]{3,2,1,0:T(8,128)S(1)}, f32[16,4,256]{2,1,0:T(4,128)S(1)}) custom-call(s32[2]{0:T(128)S(1)} %pad_add_fusion.ids, f32[4,1]{1,0:T(4,128)S(1)} %copy-done.6, f32[64,1]{1,0:T(8,128)S(1)} %copy-done.2, f32[1,1024]{1,0:T(1,128)S(1)} %copy-done.5, f32[64,2]{1,0:T(8,128)S(1)} %copy-done.1, ...), custom_call_target="tpu_custom_call" | custom-call | flops 26214400 | bytes 1053464 | tf_op jit(solution)/shard_map/pallas_call | solution.py:73
  54.3 1.6 %collective-permute-start.13 = (f32[16,4,256]{2,1,0:T(4,128)S(1)}, f32[16,4,256]{2,1,0:T(4,128)S(1)}, u32[]{:S(2)}, u32[]{:S(2)}) collective-permute-start(f32[16,4,256]{2,1,0:T(4,128)S(1)} %get-tuple-element.46.refs_0_), channel_id=1, source_target_pairs={{0,2},{1,3},{2,0},{3,1},{4,6},{5,7},{6,4},{7,5},{8,10},{9,11},{10,... | collective-permute-start | bytes 196616 | tf_op jit(solution)/shard_map/ppermute | solution.py:455
  55.8 1.9 %shard_map.136 = (f32[4,64,256]{2,1,0:T(8,128)S(1)}, f32[4,64,256]{2,1,0:T(8,128)S(1)}, f32[4,64,256]{2,1,0:T(8,128)S(1)}, f32[4,64,256]{2,1,0:T(8,128)S(1)}) custom-call(s32[2]{0:T(128)S(1)} %pad_add_fusion.ids, f32[4,1]{1,0:T(4,128)S(1)} %copy-done.7, f32[64,1]{1,0:T(8,128)S(1)} %copy-done.2, f32[1,1024]{1,0:T(1,128)S(1)} %copy-done.5, ...), custom_call_target="tpu_custom_call" | custom-call | flops 26214400 | bytes 1708824 | tf_op jit(solution)/shard_map/pallas_call | solution.py:73
  57.7 3.3 %collective-permute-start.19 = (f32[4,64,256]{2,1,0:T(8,128)S(1)}, f32[4,64,256]{2,1,0:T(8,128)S(1)}, u32[]{:S(2)}, u32[]{:S(2)}) collective-permute-start(f32[4,64,256]{2,1,0:T(8,128)S(1)} %get-tuple-element.52), channel_id=1, source_target_pairs={{0,12},{4,8},{8,4},{12,0},{16,28},{20,24},{24,20},{28,16},{1,13},{... | collective-permute-start | bytes 786440 | tf_op jit(solution)/shard_map/ppermute | solution.py:455
  61.7 1.3 %collective-permute-done.12.refs_1_ = f32[16,4,256]{2,1,0:T(4,128)S(1)} collective-permute-done((f32[16,4,256]{2,1,0:T(4,128)S(1)}, f32[16,4,256]{2,1,0:T(4,128)S(1)}, u32[]{:S(2)}, u32[]{:S(2)}) %collective-permute-start.12) | collective-permute-done | bytes 65568 | tf_op jit(solution)/shard_map/ppermute | solution.py:455
  62.9 0.9 shard_map.133.refs_5_
  63.8 2.4 %collective-permute-start.15 = (f32[16,4,256]{2,1,0:T(4,128)S(1)}, f32[16,4,256]{2,1,0:T(4,128)S(1)}, u32[]{:S(2)}, u32[]{:S(2)}) collective-permute-start(f32[16,4,256]{2,1,0:T(4,128)S(1)} %shard_map.133.refs_5_), channel_id=1, source_target_pairs={{0,16},{4,20},{8,24},{12,28},{16,0},{20,4},{24,8},{28,12},{1,17},{... | collective-permute-start | bytes 196616 | tf_op jit(solution)/shard_map/ppermute | solution.py:455
  66.2 11.6 %collective-permute-done.15.refs_6_ = f32[16,4,256]{2,1,0:T(4,128)S(1)} collective-permute-done((f32[16,4,256]{2,1,0:T(4,128)S(1)}, f32[16,4,256]{2,1,0:T(4,128)S(1)}, u32[]{:S(2)}, u32[]{:S(2)}) %collective-permute-start.15) | collective-permute-done | bytes 65568 | tf_op jit(solution)/shard_map/ppermute | solution.py:455
  77.9 2.0 %shard_map.134 = (f32[4,64,256]{2,1,0:T(8,128)S(1)}, f32[4,64,256]{2,1,0:T(8,128)S(1)}, f32[4,64,256]{2,1,0:T(8,128)S(1)}, f32[4,64,256]{2,1,0:T(8,128)S(1)}) custom-call(s32[2]{0:T(128)S(1)} %pad_add_fusion.ids, f32[4,1]{1,0:T(4,128)S(1)} %copy-done.6, f32[64,1]{1,0:T(8,128)S(1)} %copy-done.2, f32[1,1024]{1,0:T(1,128)S(1)} %copy-done.5, ...), custom_call_target="tpu_custom_call" | custom-call | flops 26214400 | bytes 1708824 | tf_op jit(solution)/shard_map/pallas_call | solution.py:73
  79.9 4.6 %collective-permute-start.16 = (f32[4,64,256]{2,1,0:T(8,128)S(1)}, f32[4,64,256]{2,1,0:T(8,128)S(1)}, u32[]{:S(2)}, u32[]{:S(2)}) collective-permute-start(f32[4,64,256]{2,1,0:T(8,128)S(1)} %get-tuple-element.48), channel_id=1, source_target_pairs={{0,12},{4,8},{8,4},{12,0},{16,28},{20,24},{24,20},{28,16},{1,13},{... | collective-permute-start | bytes 786440 | tf_op jit(solution)/shard_map/ppermute | solution.py:455
  85.2 2.8 %shard_map.137.refs_2_ = f32[4,64,1024]{2,1,0:T(8,128)S(1)} custom-call(s32[2]{0:T(128)S(1)} %pad_add_fusion.ids, bf16[2,2,256,256]{3,2,1,0:T(8,128)(2,1)S(1)} %copy-done, bf16[1024,1024]{1,0:T(8,128)(2,1)S(1)} %get-tuple-element.30.sxh, bf16[1024,1024]{1,0:T(8,128)(2,1)S(1)} %get-tuple-element.31.sxl, f32[4,64,256]{2,1,0:T(8,128)S(1)} %get-tuple-element.51.refs_0_, ...), custom_call_target="tpu_custom_call" | custom-call | flops 2013265920 | bytes 5767176 | tf_op jit(solution)/shard_map/pallas_call | solution.py:73
  88.0 3.8 %collective-permute-done.16.refs_1_ = f32[4,64,256]{2,1,0:T(8,128)S(1)} collective-permute-done((f32[4,64,256]{2,1,0:T(8,128)S(1)}, f32[4,64,256]{2,1,0:T(8,128)S(1)}, u32[]{:S(2)}, u32[]{:S(2)}) %collective-permute-start.16) | collective-permute-done | bytes 262176 | tf_op jit(solution)/shard_map/ppermute | solution.py:455
  91.8 2.8 %collective-permute-done.17.refs_2_ = f32[4,64,256]{2,1,0:T(8,128)S(1)} collective-permute-done((f32[4,64,256]{2,1,0:T(8,128)S(1)}, f32[4,64,256]{2,1,0:T(8,128)S(1)}, u32[]{:S(2)}, u32[]{:S(2)}) %collective-permute-start.17) | collective-permute-done | bytes 262176 | tf_op jit(solution)/shard_map/ppermute | solution.py:455
  94.6 1.9 %shard_map.135.refs_0_ = f32[256,1024]{1,0:T(8,128)S(1)} custom-call(s32[2]{0:T(128)S(1)} %pad_add_fusion.ids, bf16[1024,1024]{1,0:T(8,128)(2,1)S(1)} %get-tuple-element.30.sxh, bf16[1024,1024]{1,0:T(8,128)(2,1)S(1)} %get-tuple-element.31.sxl, f32[4,64,256]{2,1,0:T(8,128)S(1)} %get-tuple-element.47.refs_0_, ...), custom_call_target="tpu_custom_call" | custom-call | flops 1006632960 | bytes 4980744 | tf_op jit(solution)/shard_map/pallas_call | solution.py:73
  96.5 2.8 %shard_map.138 = f32[8,64,1024]{2,1,0:T(8,128)} custom-call(s32[2]{0:T(128)S(1)} %pad_add_fusion.ids, bf16[2,2,256,256]{3,2,1,0:T(8,128)(2,1)S(1)} %copy-done, bf16[1024,1024]{1,0:T(8,128)(2,1)S(1)} %get-tuple-element.30.sxh, bf16[1024,1024]{1,0:T(8,128)(2,1)S(1)} %get-tuple-element.31.sxl, f32[256,1024]{1,0:T(8,128)S(1)} %shard_map.135.refs_0_, ...), custom_call_target="tpu_custom_call" | custom-call | flops 2013265920 | bytes 7077896 | tf_op jit(solution)/shard_map/pallas_call | solution.py:73
  (47 shorter events, 3.8 us)
Async XLA Ops:
  1.1 1.7 %copy-start.8 = (f32[1,8,64,1024]{3,2,1,0:T(8,128)S(1)}, f32[1,8,64,1024]{3,2,1,0:T(8,128)}, u32[]{:S(2)}) copy-start(f32[1,8,64,1024]{3,2,1,0:T(8,128)} %param.13) | copy-start | bytes 6291460
  1.1 1.7 %copy-start.9 = (bf16[2,2,256,256]{3,2,1,0:T(8,128)(2,1)S(1)}, bf16[2,2,256,256]{3,2,1,0:T(8,128)(2,1)}, u32[]{:S(2)}) copy-start(bf16[2,2,256,256]{3,2,1,0:T(8,128)(2,1)} %constant.51.both) | copy-start | bytes 1572868
  5.7 11.2 %collective-permute-start.3 = (f32[4,64,256]{2,1,0:T(8,128)S(1)}, f32[4,64,256]{2,1,0:T(8,128)S(1)}, u32[]{:S(2)}, u32[]{:S(2)}) collective-permute-start(f32[4,64,256]{2,1,0:T(8,128)S(1)} %get-tuple-element.40), channel_id=1, source_target_pairs={{0,12},{4,8},{8,4},{12,0},{16,28},{20,24},{24,20},{28,16},{1,13},{... | collective-permute-start | bytes 786440 | tf_op jit(solution)/shard_map/ppermute | solution.py:455
  9.7 12.1 %collective-permute-start.4 = (f32[4,64,256]{2,1,0:T(8,128)S(1)}, f32[4,64,256]{2,1,0:T(8,128)S(1)}, u32[]{:S(2)}, u32[]{:S(2)}) collective-permute-start(f32[4,64,256]{2,1,0:T(8,128)S(1)} %get-tuple-element.41), channel_id=1, source_target_pairs={{0,8},{4,12},{8,0},{12,4},{16,24},{20,28},{24,16},{28,20},{1,9},{5... | collective-permute-start | bytes 786440 | tf_op jit(solution)/shard_map/ppermute | solution.py:455
  10.2 11.7 %copy-start.1 = (f32[64,2]{1,0:T(8,128)S(1)}, f32[64,2]{1,0:T(8,128)}, u32[]{:S(2)}) copy-start(f32[64,2]{1,0:T(8,128)} %constant.35.clone.edges) | copy-start | bytes 1540
  10.2 11.7 %copy-start.2 = (f32[64,1]{1,0:T(8,128)S(1)}, f32[64,1]{1,0:T(8,128)}, u32[]{:S(2)}) copy-start(f32[64,1]{1,0:T(8,128)} %constant.33.clone.smu_y) | copy-start | bytes 772
  10.2 11.7 %copy-start.5 = (f32[1,1024]{1,0:T(1,128)S(1)}, f32[1,1024]{1,0:T(1,128)}, u32[]{:S(2)}) copy-start(f32[1,1024]{1,0:T(1,128)} %constant.34.clone.smu_x) | copy-start | bytes 12292
  10.2 11.7 %copy-start.7 = (f32[4,1]{1,0:T(4,128)S(1)}, f32[4,1]{1,0:T(4,128)}, u32[]{:S(2)}) copy-start(f32[4,1]{1,0:T(4,128)} %constant.41.clone.smu_z) | copy-start | bytes 52
  10.2 29.6 %copy-start.4 = (f32[5,4,4,1024]{3,2,1,0:T(4,128)S(1)}, f32[5,4,4,1024]{3,2,1,0:T(4,128)}, u32[]{:S(2)}) copy-start(f32[5,4,4,1024]{3,2,1,0:T(4,128)} %constant.43.clone.responses) | copy-start | bytes 983044
  10.2 42.0 %copy-start.6 = (f32[4,1]{1,0:T(4,128)S(1)}, f32[4,1]{1,0:T(4,128)}, u32[]{:S(2)}) copy-start(f32[4,1]{1,0:T(4,128)} %constant.42.clone.smu_z) | copy-start | bytes 52
  10.2 11.6 %collective-permute-start.5 = (f32[4,64,256]{2,1,0:T(8,128)S(1)}, f32[4,64,256]{2,1,0:T(8,128)S(1)}, u32[]{:S(2)}, u32[]{:S(2)}) collective-permute-start(f32[4,64,256]{2,1,0:T(8,128)S(1)} %get-tuple-element.42), channel_id=1, source_target_pairs={{0,4},{4,0},{8,12},{12,8},{16,20},{20,16},{24,28},{28,24},{1,5},{5... | collective-permute-start | bytes 786440 | tf_op jit(solution)/shard_map/ppermute | solution.py:455
  13.3 49.6 %copy-start.3 = (f32[5,4,4,1024]{3,2,1,0:T(4,128)S(1)}, f32[5,4,4,1024]{3,2,1,0:T(4,128)}, u32[]{:S(2)}) copy-start(f32[5,4,4,1024]{3,2,1,0:T(4,128)} %constant.44.clone.responses) | copy-start | bytes 983044
  23.8 30.3 %collective-permute-start.6 = (f32[2,4,64,256]{3,2,1,0:T(8,128)S(1)}, f32[2,4,64,256]{3,2,1,0:T(8,128)S(1)}, u32[]{:S(2)}, u32[]{:S(2)}) collective-permute-start(f32[2,4,64,256]{3,2,1,0:T(8,128)S(1)} %get-tuple-element.43), channel_id=1, source_target_pairs={{0,16},{4,20},{8,24},{12,28},{16,0},{20,4},{24,8},{28,12},{1,17},{... | collective-permute-start | bytes 1572872 | tf_op jit(solution)/shard_map/ppermute | solution.py:455
  26.5 18.0 %collective-permute-start = (f32[4,64,256]{2,1,0:T(8,128)S(1)}, f32[4,64,256]{2,1,0:T(8,128)S(1)}, u32[]{:S(2)}, u32[]{:S(2)}) collective-permute-start(f32[4,64,256]{2,1,0:T(8,128)S(1)} %get-tuple-element.35), channel_id=1, source_target_pairs={{0,12},{4,8},{8,4},{12,0},{16,28},{20,24},{24,20},{28,16},{1,13},{... | collective-permute-start | bytes 786440 | tf_op jit(solution)/shard_map/ppermute | solution.py:455
  28.9 23.3 %collective-permute-start.1 = (f32[4,64,256]{2,1,0:T(8,128)S(1)}, f32[4,64,256]{2,1,0:T(8,128)S(1)}, u32[]{:S(2)}, u32[]{:S(2)}) collective-permute-start(f32[4,64,256]{2,1,0:T(8,128)S(1)} %get-tuple-element.36), channel_id=1, source_target_pairs={{0,8},{4,12},{8,0},{12,4},{16,24},{20,28},{24,16},{28,20},{1,9},{5... | collective-permute-start | bytes 786440 | tf_op jit(solution)/shard_map/ppermute | solution.py:455
  29.3 22.8 %collective-permute-start.2 = (f32[4,64,256]{2,1,0:T(8,128)S(1)}, f32[4,64,256]{2,1,0:T(8,128)S(1)}, u32[]{:S(2)}, u32[]{:S(2)}) collective-permute-start(f32[4,64,256]{2,1,0:T(8,128)S(1)} %get-tuple-element.37), channel_id=1, source_target_pairs={{0,4},{4,0},{8,12},{12,8},{16,20},{20,16},{24,28},{28,24},{1,5},{5... | collective-permute-start | bytes 786440 | tf_op jit(solution)/shard_map/ppermute | solution.py:455
  30.0 4.3 %collective-permute-start.9 = (f32[16,4,256]{2,1,0:T(4,128)S(1)}, f32[16,4,256]{2,1,0:T(4,128)S(1)}, u32[]{:S(2)}, u32[]{:S(2)}) collective-permute-start(f32[16,4,256]{2,1,0:T(4,128)S(1)} %get-tuple-element.44.refs_0_), channel_id=1, source_target_pairs={{0,3},{1,2},{2,1},{3,0},{4,7},{5,6},{6,5},{7,4},{8,11},{9,10},{10,... | collective-permute-start | bytes 196616 | tf_op jit(solution)/shard_map/ppermute | solution.py:455
  34.3 4.3 %collective-permute-start.8 = (f32[16,4,256]{2,1,0:T(4,128)S(1)}, f32[16,4,256]{2,1,0:T(4,128)S(1)}, u32[]{:S(2)}, u32[]{:S(2)}) collective-permute-start(f32[16,4,256]{2,1,0:T(4,128)S(1)} %get-tuple-element.44.refs_0_), channel_id=1, source_target_pairs={{0,2},{1,3},{2,0},{3,1},{4,6},{5,7},{6,4},{7,5},{8,10},{9,11},{10,... | collective-permute-start | bytes 196616 | tf_op jit(solution)/shard_map/ppermute | solution.py:455
  38.6 1.3 %collective-permute-start.7 = (f32[16,4,256]{2,1,0:T(4,128)S(1)}, f32[16,4,256]{2,1,0:T(4,128)S(1)}, u32[]{:S(2)}, u32[]{:S(2)}) collective-permute-start(f32[16,4,256]{2,1,0:T(4,128)S(1)} %get-tuple-element.44.refs_0_), channel_id=1, source_target_pairs={{0,1},{1,0},{2,3},{3,2},{4,5},{5,4},{6,7},{7,6},{8,9},{9,8},{10,11... | collective-permute-start | bytes 196616 | tf_op jit(solution)/shard_map/ppermute | solution.py:455
  40.7 13.4 %collective-permute-start.10 = (f32[16,4,256]{2,1,0:T(4,128)S(1)}, f32[16,4,256]{2,1,0:T(4,128)S(1)}, u32[]{:S(2)}, u32[]{:S(2)}) collective-permute-start(f32[16,4,256]{2,1,0:T(4,128)S(1)} %shard_map.132.refs_5_), channel_id=1, source_target_pairs={{0,16},{4,20},{8,24},{12,28},{16,0},{20,4},{24,8},{28,12},{1,17},{... | collective-permute-start | bytes 196616 | tf_op jit(solution)/shard_map/ppermute | solution.py:455
  54.1 23.8 %collective-permute-start.11 = (f32[2,4,64,256]{3,2,1,0:T(8,128)S(1)}, f32[2,4,64,256]{3,2,1,0:T(8,128)S(1)}, u32[]{:S(2)}, u32[]{:S(2)}) collective-permute-start(f32[2,4,64,256]{3,2,1,0:T(8,128)S(1)} %get-tuple-element.45), channel_id=1, source_target_pairs={{0,16},{4,20},{8,24},{12,28},{16,0},{20,4},{24,8},{28,12},{1,17},{... | collective-permute-start | bytes 1572872 | tf_op jit(solution)/shard_map/ppermute | solution.py:455
  54.2 31.0 %copy-start = (bf16[2,2,256,256]{3,2,1,0:T(8,128)(2,1)S(1)}, bf16[2,2,256,256]{3,2,1,0:T(8,128)(2,1)}, u32[]{:S(2)}) copy-start(bf16[2,2,256,256]{3,2,1,0:T(8,128)(2,1)} %constant.48.both) | copy-start | bytes 1572868
  54.2 6.9 %collective-permute-start.14 = (f32[16,4,256]{2,1,0:T(4,128)S(1)}, f32[16,4,256]{2,1,0:T(4,128)S(1)}, u32[]{:S(2)}, u32[]{:S(2)}) collective-permute-start(f32[16,4,256]{2,1,0:T(4,128)S(1)} %get-tuple-element.46.refs_0_), channel_id=1, source_target_pairs={{0,3},{1,2},{2,1},{3,0},{4,7},{5,6},{6,5},{7,4},{8,11},{9,10},{10,... | collective-permute-start | bytes 196616 | tf_op jit(solution)/shard_map/ppermute | solution.py:455
  54.3 7.4 %collective-permute-start.13 = (f32[16,4,256]{2,1,0:T(4,128)S(1)}, f32[16,4,256]{2,1,0:T(4,128)S(1)}, u32[]{:S(2)}, u32[]{:S(2)}) collective-permute-start(f32[16,4,256]{2,1,0:T(4,128)S(1)} %get-tuple-element.46.refs_0_), channel_id=1, source_target_pairs={{0,2},{1,3},{2,0},{3,1},{4,6},{5,7},{6,4},{7,5},{8,10},{9,11},{10,... | collective-permute-start | bytes 196616 | tf_op jit(solution)/shard_map/ppermute | solution.py:455
  57.7 26.8 %collective-permute-start.19 = (f32[4,64,256]{2,1,0:T(8,128)S(1)}, f32[4,64,256]{2,1,0:T(8,128)S(1)}, u32[]{:S(2)}, u32[]{:S(2)}) collective-permute-start(f32[4,64,256]{2,1,0:T(8,128)S(1)} %get-tuple-element.52), channel_id=1, source_target_pairs={{0,12},{4,8},{8,4},{12,0},{16,28},{20,24},{24,20},{28,16},{1,13},{... | collective-permute-start | bytes 786440 | tf_op jit(solution)/shard_map/ppermute | solution.py:455
  61.0 24.1 %collective-permute-start.20 = (f32[4,64,256]{2,1,0:T(8,128)S(1)}, f32[4,64,256]{2,1,0:T(8,128)S(1)}, u32[]{:S(2)}, u32[]{:S(2)}) collective-permute-start(f32[4,64,256]{2,1,0:T(8,128)S(1)} %get-tuple-element.53), channel_id=1, source_target_pairs={{0,8},{4,12},{8,0},{12,4},{16,24},{20,28},{24,16},{28,20},{1,9},{5... | collective-permute-start | bytes 786440 | tf_op jit(solution)/shard_map/ppermute | solution.py:455
  61.0 24.1 %collective-permute-start.21 = (f32[4,64,256]{2,1,0:T(8,128)S(1)}, f32[4,64,256]{2,1,0:T(8,128)S(1)}, u32[]{:S(2)}, u32[]{:S(2)}) collective-permute-start(f32[4,64,256]{2,1,0:T(8,128)S(1)} %get-tuple-element.54), channel_id=1, source_target_pairs={{0,4},{4,0},{8,12},{12,8},{16,20},{20,16},{24,28},{28,24},{1,5},{5... | collective-permute-start | bytes 786440 | tf_op jit(solution)/shard_map/ppermute | solution.py:455
  61.7 1.3 %collective-permute-start.12 = (f32[16,4,256]{2,1,0:T(4,128)S(1)}, f32[16,4,256]{2,1,0:T(4,128)S(1)}, u32[]{:S(2)}, u32[]{:S(2)}) collective-permute-start(f32[16,4,256]{2,1,0:T(4,128)S(1)} %get-tuple-element.46.refs_0_), channel_id=1, source_target_pairs={{0,1},{1,0},{2,3},{3,2},{4,5},{5,4},{6,7},{7,6},{8,9},{9,8},{10,11... | collective-permute-start | bytes 196616 | tf_op jit(solution)/shard_map/ppermute | solution.py:455
  63.8 14.0 %collective-permute-start.15 = (f32[16,4,256]{2,1,0:T(4,128)S(1)}, f32[16,4,256]{2,1,0:T(4,128)S(1)}, u32[]{:S(2)}, u32[]{:S(2)}) collective-permute-start(f32[16,4,256]{2,1,0:T(4,128)S(1)} %shard_map.133.refs_5_), channel_id=1, source_target_pairs={{0,16},{4,20},{8,24},{12,28},{16,0},{20,4},{24,8},{28,12},{1,17},{... | collective-permute-start | bytes 196616 | tf_op jit(solution)/shard_map/ppermute | solution.py:455
  79.9 11.9 %collective-permute-start.16 = (f32[4,64,256]{2,1,0:T(8,128)S(1)}, f32[4,64,256]{2,1,0:T(8,128)S(1)}, u32[]{:S(2)}, u32[]{:S(2)}) collective-permute-start(f32[4,64,256]{2,1,0:T(8,128)S(1)} %get-tuple-element.48), channel_id=1, source_target_pairs={{0,12},{4,8},{8,4},{12,0},{16,28},{20,24},{24,20},{28,16},{1,13},{... | collective-permute-start | bytes 786440 | tf_op jit(solution)/shard_map/ppermute | solution.py:455
  84.5 10.1 %collective-permute-start.17 = (f32[4,64,256]{2,1,0:T(8,128)S(1)}, f32[4,64,256]{2,1,0:T(8,128)S(1)}, u32[]{:S(2)}, u32[]{:S(2)}) collective-permute-start(f32[4,64,256]{2,1,0:T(8,128)S(1)} %get-tuple-element.49), channel_id=1, source_target_pairs={{0,8},{4,12},{8,0},{12,4},{16,24},{20,28},{24,16},{28,20},{1,9},{5... | collective-permute-start | bytes 786440 | tf_op jit(solution)/shard_map/ppermute | solution.py:455
  84.5 12.0 %collective-permute-start.18 = (f32[4,64,256]{2,1,0:T(8,128)S(1)}, f32[4,64,256]{2,1,0:T(8,128)S(1)}, u32[]{:S(2)}, u32[]{:S(2)}) collective-permute-start(f32[4,64,256]{2,1,0:T(8,128)S(1)} %get-tuple-element.50), channel_id=1, source_target_pairs={{0,4},{4,0},{8,12},{12,8},{16,20},{20,16},{24,28},{28,24},{1,5},{5... | collective-permute-start | bytes 786440 | tf_op jit(solution)/shard_map/ppermute | solution.py:455
  (1 other events, 1.0 us)

commit v16 on v14

--- a/solution.py
+++ b/solution.py
@@ -224,7 +224,7 @@
     def step(index, carry):
         rows = pl.ds(pl.multiple_of(index * strip, strip), strip)
         plane = across + smu_y[rows, :]
-        weights = edges[rows, 0:1], edges[rows, 1:2]
+        weights = edges[rows, :]
         for u in range(smu_z.shape[0]):
             body(u, rows, plane + smu_z[u : u + 1, :], weights)
         return carry
@@ -272,6 +272,11 @@
 def by_place(plan, place, body):
     for case in range(plan.half):
         pl.when(place == case)(functools.partial(body, case))
+
+
+def row_sign():
+    index = lax.broadcasted_iota(jnp.int32, (8, 1), 0)
+    return (1 - 2 * (index % 2)).astype(jnp.float32)
 
 
 def half_end(plan, ids, smu_z, smu_y, smu_x, edges, *refs):
@@ -295,15 +300,18 @@
             _, _, other = cyclic.run(leaving * before, leaving * last, [None] * half)
             for values, window in ((own, mine), (other, 1 - mine)):
                 for j, value in enumerate(values):
-                    for edge in range(2):
-                        term = weights[edge] * value
-                        term = sum(term[i : i + 8] for i in range(0, STRIP, 8))
-                        sums[2 * (window * half + j) + edge, u] += term
-
-        per_strip(plan, place, smu_z, smu_y, smu_x, edges, body)
+                    term = weights * value
+                    term = sum(term[i : i + 8] for i in range(0, term.shape[0], 8))
+                    sums[window * half + j, u] += term
+
+        per_strip(plan, place, smu_z, smu_y, smu_x, edges, body, 2 * STRIP)
 
     by_place(plan, place, with_place)
-    seen[...] = jnp.sum(sums[...], axis=2)
+    sign = row_sign()
+    for n in range(steps):
+        total = sums[n]
+        seen[2 * n] = jnp.sum(total, axis=1)
+        seen[2 * n + 1] = jnp.sum(total * sign, axis=1)
 
 
 def c_mul(a, b):
@@ -404,8 +412,16 @@
 def half_solve(plan, ids, smu_z, smu_y, smu_x, edges, *refs):
     pieces = refs[: plan.half]
     far, beside, beside_far = refs[plan.half : plan.half + 3]
-    outs = refs[plan.half + 3 :]
+    outs, around = refs[plan.half + 3 : -1], refs[-1]
     half = plan.half
+    sign = row_sign()
+    for n in range(plan.steps):
+        for u in range(around.shape[1]):
+            above, below = (
+                beside[2 * n + edge, u : u + 1, :] + beside_far[2 * n + edge, u : u + 1, :]
+                for edge in range(2)
+            )
+            around[n, u] = above + sign * below
     place = lax.rem(ids[0], half)
     mine = ids[0] // half
     entering = jnp.where(mine == 0, ALPHA_RATIO, 1.0).astype(jnp.float32)
@@ -415,13 +431,8 @@
             cyclic = Cyclic(smu, half)
 
             def source(window, j):
-                total = None
-                for edge in range(2):
-                    at = 2 * (window * half + j) + edge
-                    row = beside[at, u : u + 1, :] + beside_far[at, u : u + 1, :]
-                    term = weights[edge] * row
-                    total = term if total is None else total + term
-                return total
+                rows = around[window * half + j, u]
+                return weights * jnp.concatenate([rows] * (weights.shape[0] // 8))
 
             own = [pieces[case ^ j][u, rows, :] + source(mine, j) for j in range(half)]
             other = [source(1 - mine, j) for j in range(half)]
@@ -457,7 +468,7 @@
     )
     smu_y = jnp.asarray(smu_y[:, None], jnp.float32)
     smu_x = jnp.asarray(smu_x[None, :], jnp.float32)
-    edges = jnp.asarray(sine_rows[:, [0, plan.rows - 1]], jnp.float32)
+    edges = jnp.asarray(sine_rows[:, :1], jnp.float32)
     responses = edge_responses(steps, plan.depth, plan.rows, plan.width)
     field = residual[0]
     f32 = functools.partial(jax.ShapeDtypeStruct, dtype=jnp.float32)
@@ -493,7 +504,7 @@
             [f32((2,) + modes.shape), seen],
             100 * modes.size * half,
             (*small, *pieces),
-            [pltpu.VMEM((2 * steps, len(chunk), 8, plan.block), jnp.float32)],
+            [pltpu.VMEM((steps, len(chunk), 8, plan.block), jnp.float32)],
         )
         if far is not None:
             ends, far, beside_far = lax.optimization_barrier((ends, far, beside_far))
@@ -513,6 +524,7 @@
             [modes] * half,
             100 * modes.size * half,
             (*small, *pieces, far, beside, beside_far),
+            [pltpu.VMEM((steps, len(chunk), 8, plan.block), jnp.float32)],
         )
         pieces = [swap(v, "tm", steps, k) for k, v in enumerate(pieces)]
         last = chunk == CHUNKS[-1]

time: 97.4 us -> 97.2 us (level)
  waiting for transfers between devices: 46.6 us -> 47.8 us
  Pallas kernels: 24.4 us -> 23.3 us
    ppermute x22, waiting for transfers between devices: 46.6 us -> 47.8 us  [swap(): return lax.ppermute(values, axis, [(i, i ^ distance) for i in range(count)])]
    pallas_call x12, Pallas kernels: 24.4 us -> 23.3 us  [call(): pl.pallas_call(kernel, out_shape=out_shape, in_specs=[smem] + [vmem] * (l...]
  transfers between devices with their start and end apart: 22 -> 22, of which waited for: 14 -> 14; matrix products, arithmetic and copies ran while one was open for 0% -> 0% of each run, Pallas kernels for 16% -> 15%
where the time goes in v16:
time: 97.2 us; the launch traced here: 97 us
  waiting for transfers between devices  47.8 us (49%)
  starting transfers between devices  24.5 us (25%)
  Pallas kernels  23.3 us (24%)
  local copies, waits for them, and re-layouts  1.09 us (1%)
    ppermute x22, waiting for transfers between devices, swap(): return lax.ppermute(values, axis, [(i, i ^ distance) for i in range(count)])  47.8 us
    ppermute x22, starting transfers between devices, swap(): return lax.ppermute(values, axis, [(i, i ^ distance) for i in range(count)])  24.5 us
    pallas_call x12, Pallas kernels, call(): pl.pallas_call(kernel, out_shape=out_shape, in_specs=[smem] + [vmem] * (l...  23.3 us
  transfers between devices with their start and end apart: 22, of which 14 were waited for; matrix products, arithmetic and copies ran while one was open for 0% of the time, Pallas kernels for 15%

profile of v16, /device:TPU:0, one launch (start us, length us, event | category | flops | bytes accessed | tf_op | source)
XLA Modules:
  0.0 97.0 jit_solution(9749775869062718114)
XLA Ops:
  1.1 1.7 %shard_map.127 = (bf16[1024,1024]{1,0:T(8,128)(2,1)S(1)}, bf16[1024,1024]{1,0:T(8,128)(2,1)S(1)}) custom-call(s32[2]{0:T(128)S(1)} %pad_add_fusion.ids, f32[128,1024]{1,0:T(8,128)S(1)} %copy-done.10), custom_call_target="tpu_custom_call" | custom-call | flops 4194304000 | bytes 524296 | tf_op jit(solution)/shard_map/pallas_call | solution.py:73
  2.9 2.8 %shard_map.128 = (f32[4,64,256]{2,1,0:T(8,128)S(1)}, f32[4,64,256]{2,1,0:T(8,128)S(1)}, f32[4,64,256]{2,1,0:T(8,128)S(1)}, f32[4,64,256]{2,1,0:T(8,128)S(1)}) custom-call(s32[2]{0:T(128)S(1)} %pad_add_fusion.ids, bf16[2,2,256,256]{3,2,1,0:T(8,128)(2,1)S(1)} %copy-done.9, f32[8,64,1024]{2,1,0:T(8,128)S(1)} %bitcast.4, ...), custom_call_target="tpu_custom_call" | custom-call | flops 2013265920 | bytes 6815752 | tf_op jit(solution)/shard_map/pallas_call | solution.py:73
  5.7 3.0 %collective-permute-start.3 = (f32[4,64,256]{2,1,0:T(8,128)S(1)}, f32[4,64,256]{2,1,0:T(8,128)S(1)}, u32[]{:S(2)}, u32[]{:S(2)}) collective-permute-start(f32[4,64,256]{2,1,0:T(8,128)S(1)} %get-tuple-element.40), channel_id=1, source_target_pairs={{0,4},{4,0},{8,12},{12,8},{16,20},{20,16},{24,28},{28,24},{1,5},{5... | collective-permute-start | bytes 786440 | tf_op jit(solution)/shard_map/ppermute | solution.py:459
  8.7 1.6 %collective-permute-start.4 = (f32[4,64,256]{2,1,0:T(8,128)S(1)}, f32[4,64,256]{2,1,0:T(8,128)S(1)}, u32[]{:S(2)}, u32[]{:S(2)}) collective-permute-start(f32[4,64,256]{2,1,0:T(8,128)S(1)} %get-tuple-element.41), channel_id=1, source_target_pairs={{0,8},{4,12},{8,0},{12,4},{16,24},{20,28},{24,16},{28,20},{1,9},{5... | collective-permute-start | bytes 786440 | tf_op jit(solution)/shard_map/ppermute | solution.py:459
  10.4 2.8 %shard_map.129 = (f32[4,64,256]{2,1,0:T(8,128)S(1)}, f32[4,64,256]{2,1,0:T(8,128)S(1)}, f32[4,64,256]{2,1,0:T(8,128)S(1)}, f32[4,64,256]{2,1,0:T(8,128)S(1)}) custom-call(s32[2]{0:T(128)S(1)} %pad_add_fusion.ids, bf16[2,2,256,256]{3,2,1,0:T(8,128)(2,1)S(1)} %copy-done.9, f32[8,64,1024]{2,1,0:T(8,128)S(1)} %bitcast.5, ...), custom_call_target="tpu_custom_call" | custom-call | flops 2013265920 | bytes 6815752 | tf_op jit(solution)/shard_map/pallas_call | solution.py:73
  13.3 1.8 %collective-permute-done.3.refs_1_ = f32[4,64,256]{2,1,0:T(8,128)S(1)} collective-permute-done((f32[4,64,256]{2,1,0:T(8,128)S(1)}, f32[4,64,256]{2,1,0:T(8,128)S(1)}, u32[]{:S(2)}, u32[]{:S(2)}) %collective-permute-start.3) | collective-permute-done | bytes 262176 | tf_op jit(solution)/shard_map/ppermute | solution.py:459
  15.0 2.9 %collective-permute-done.4.refs_2_ = f32[4,64,256]{2,1,0:T(8,128)S(1)} collective-permute-done((f32[4,64,256]{2,1,0:T(8,128)S(1)}, f32[4,64,256]{2,1,0:T(8,128)S(1)}, u32[]{:S(2)}, u32[]{:S(2)}) %collective-permute-start.4) | collective-permute-done | bytes 262176 | tf_op jit(solution)/shard_map/ppermute | solution.py:459
  18.0 3.9 %collective-permute-done.5.refs_3_ = f32[4,64,256]{2,1,0:T(8,128)S(1)} collective-permute-done((f32[4,64,256]{2,1,0:T(8,128)S(1)}, f32[4,64,256]{2,1,0:T(8,128)S(1)}, u32[]{:S(2)}, u32[]{:S(2)}) %collective-permute-start.5) | collective-permute-done | bytes 262176 | tf_op jit(solution)/shard_map/ppermute | solution.py:459
  21.9 1.6 %shard_map.131 = (f32[2,4,64,256]{3,2,1,0:T(8,128)S(1)}, f32[16,4,256]{2,1,0:T(4,128)S(1)}) custom-call(s32[2]{0:T(128)S(1)} %pad_add_fusion.ids, f32[4,1]{1,0:T(4,128)S(1)} %copy-done.7, f32[64,1]{1,0:T(8,128)S(1)} %copy-done.2, f32[1,1024]{1,0:T(1,128)S(1)} %copy-done.5, f32[64,1]{1,0:T(8,128)S(1)} %copy-done.1, ...), custom_call_target="tpu_custom_call" | custom-call | flops 26214400 | bytes 1053208 | tf_op jit(solution)/shard_map/pallas_call | solution.py:73
  23.5 2.8 %collective-permute-start.6 = (f32[2,4,64,256]{3,2,1,0:T(8,128)S(1)}, f32[2,4,64,256]{3,2,1,0:T(8,128)S(1)}, u32[]{:S(2)}, u32[]{:S(2)}) collective-permute-start(f32[2,4,64,256]{3,2,1,0:T(8,128)S(1)} %get-tuple-element.43), channel_id=1, source_target_pairs={{0,16},{4,20},{8,24},{12,28},{16,0},{20,4},{24,8},{28,12},{1,17},{... | collective-permute-start | bytes 1572872 | tf_op jit(solution)/shard_map/ppermute | solution.py:459
  26.3 1.5 %collective-permute-start = (f32[4,64,256]{2,1,0:T(8,128)S(1)}, f32[4,64,256]{2,1,0:T(8,128)S(1)}, u32[]{:S(2)}, u32[]{:S(2)}) collective-permute-start(f32[4,64,256]{2,1,0:T(8,128)S(1)} %get-tuple-element.35), channel_id=1, source_target_pairs={{0,4},{4,0},{8,12},{12,8},{16,20},{20,16},{24,28},{28,24},{1,5},{5... | collective-permute-start | bytes 786440 | tf_op jit(solution)/shard_map/ppermute | solution.py:459
  27.8 1.6 %collective-permute-start.1 = (f32[4,64,256]{2,1,0:T(8,128)S(1)}, f32[4,64,256]{2,1,0:T(8,128)S(1)}, u32[]{:S(2)}, u32[]{:S(2)}) collective-permute-start(f32[4,64,256]{2,1,0:T(8,128)S(1)} %get-tuple-element.36), channel_id=1, source_target_pairs={{0,8},{4,12},{8,0},{12,4},{16,24},{20,28},{24,16},{28,20},{1,9},{5... | collective-permute-start | bytes 786440 | tf_op jit(solution)/shard_map/ppermute | solution.py:459
  29.8 4.3 %collective-permute-done.9.refs_3_ = f32[16,4,256]{2,1,0:T(4,128)S(1)} collective-permute-done((f32[16,4,256]{2,1,0:T(4,128)S(1)}, f32[16,4,256]{2,1,0:T(4,128)S(1)}, u32[]{:S(2)}, u32[]{:S(2)}) %collective-permute-start.9) | collective-permute-done | bytes 65568 | tf_op jit(solution)/shard_map/ppermute | solution.py:459
  35.0 3.4 %collective-permute-done.8.refs_2_ = f32[16,4,256]{2,1,0:T(4,128)S(1)} collective-permute-done((f32[16,4,256]{2,1,0:T(4,128)S(1)}, f32[16,4,256]{2,1,0:T(4,128)S(1)}, u32[]{:S(2)}, u32[]{:S(2)}) %collective-permute-start.8) | collective-permute-done | bytes 65568 | tf_op jit(solution)/shard_map/ppermute | solution.py:459
  40.7 3.6 %collective-permute-done.1.refs_2_ = f32[4,64,256]{2,1,0:T(8,128)S(1)} collective-permute-done((f32[4,64,256]{2,1,0:T(8,128)S(1)}, f32[4,64,256]{2,1,0:T(8,128)S(1)}, u32[]{:S(2)}, u32[]{:S(2)}) %collective-permute-start.1) | collective-permute-done | bytes 262176 | tf_op jit(solution)/shard_map/ppermute | solution.py:459
  44.3 4.6 %collective-permute-done.2.refs_3_ = f32[4,64,256]{2,1,0:T(8,128)S(1)} collective-permute-done((f32[4,64,256]{2,1,0:T(8,128)S(1)}, f32[4,64,256]{2,1,0:T(8,128)S(1)}, u32[]{:S(2)}, u32[]{:S(2)}) %collective-permute-start.2) | collective-permute-done | bytes 262176 | tf_op jit(solution)/shard_map/ppermute | solution.py:459
  48.9 1.6 %shard_map.130 = (f32[2,4,64,256]{3,2,1,0:T(8,128)S(1)}, f32[16,4,256]{2,1,0:T(4,128)S(1)}) custom-call(s32[2]{0:T(128)S(1)} %pad_add_fusion.ids, f32[4,1]{1,0:T(4,128)S(1)} %copy-done.6, f32[64,1]{1,0:T(8,128)S(1)} %copy-done.2, f32[1,1024]{1,0:T(1,128)S(1)} %copy-done.5, f32[64,1]{1,0:T(8,128)S(1)} %copy-done.1, ...), custom_call_target="tpu_custom_call" | custom-call | flops 26214400 | bytes 1053208 | tf_op jit(solution)/shard_map/pallas_call | solution.py:73
  51.5 1.9 %collective-permute-start.11 = (f32[2,4,64,256]{3,2,1,0:T(8,128)S(1)}, f32[2,4,64,256]{3,2,1,0:T(8,128)S(1)}, u32[]{:S(2)}, u32[]{:S(2)}) collective-permute-start(f32[2,4,64,256]{3,2,1,0:T(8,128)S(1)} %get-tuple-element.45), channel_id=1, source_target_pairs={{0,16},{4,20},{8,24},{12,28},{16,0},{20,4},{24,8},{28,12},{1,17},{... | collective-permute-start | bytes 1572872 | tf_op jit(solution)/shard_map/ppermute | solution.py:459
  53.3 1.5 %collective-permute-start.13 = (f32[16,4,256]{2,1,0:T(4,128)S(1)}, f32[16,4,256]{2,1,0:T(4,128)S(1)}, u32[]{:S(2)}, u32[]{:S(2)}) collective-permute-start(f32[16,4,256]{2,1,0:T(4,128)S(1)} %get-tuple-element.46.refs_0_), channel_id=1, source_target_pairs={{0,2},{1,3},{2,0},{3,1},{4,6},{5,7},{6,4},{7,5},{8,10},{9,11},{10,... | collective-permute-start | bytes 196616 | tf_op jit(solution)/shard_map/ppermute | solution.py:459
  54.8 1.6 %shard_map.136 = (f32[4,64,256]{2,1,0:T(8,128)S(1)}, f32[4,64,256]{2,1,0:T(8,128)S(1)}, f32[4,64,256]{2,1,0:T(8,128)S(1)}, f32[4,64,256]{2,1,0:T(8,128)S(1)}) custom-call(s32[2]{0:T(128)S(1)} %pad_add_fusion.ids, f32[4,1]{1,0:T(4,128)S(1)} %copy-done.7, f32[64,1]{1,0:T(8,128)S(1)} %copy-done.2, f32[1,1024]{1,0:T(1,128)S(1)} %copy-done.5, ...), custom_call_target="tpu_custom_call" | custom-call | flops 26214400 | bytes 1708568 | tf_op jit(solution)/shard_map/pallas_call | solution.py:73
  57.5 2.5 %collective-permute-start.20 = (f32[4,64,256]{2,1,0:T(8,128)S(1)}, f32[4,64,256]{2,1,0:T(8,128)S(1)}, u32[]{:S(2)}, u32[]{:S(2)}) collective-permute-start(f32[4,64,256]{2,1,0:T(8,128)S(1)} %get-tuple-element.53), channel_id=1, source_target_pairs={{0,8},{4,12},{8,0},{12,4},{16,24},{20,28},{24,16},{28,20},{1,9},{5... | collective-permute-start | bytes 786440 | tf_op jit(solution)/shard_map/ppermute | solution.py:459
  60.5 1.3 %collective-permute-done.12.refs_1_ = f32[16,4,256]{2,1,0:T(4,128)S(1)} collective-permute-done((f32[16,4,256]{2,1,0:T(4,128)S(1)}, f32[16,4,256]{2,1,0:T(4,128)S(1)}, u32[]{:S(2)}, u32[]{:S(2)}) %collective-permute-start.12) | collective-permute-done | bytes 65568 | tf_op jit(solution)/shard_map/ppermute | solution.py:459
  62.6 1.4 %collective-permute-start.15 = (f32[16,4,256]{2,1,0:T(4,128)S(1)}, f32[16,4,256]{2,1,0:T(4,128)S(1)}, u32[]{:S(2)}, u32[]{:S(2)}) collective-permute-start(f32[16,4,256]{2,1,0:T(4,128)S(1)} %shard_map.133.refs_5_), channel_id=1, source_target_pairs={{0,16},{4,20},{8,24},{12,28},{16,0},{20,4},{24,8},{28,12},{1,17},{... | collective-permute-start | bytes 196616 | tf_op jit(solution)/shard_map/ppermute | solution.py:459
  64.1 13.8 %collective-permute-done.15.refs_6_ = f32[16,4,256]{2,1,0:T(4,128)S(1)} collective-permute-done((f32[16,4,256]{2,1,0:T(4,128)S(1)}, f32[16,4,256]{2,1,0:T(4,128)S(1)}, u32[]{:S(2)}, u32[]{:S(2)}) %collective-permute-start.15) | collective-permute-done | bytes 65568 | tf_op jit(solution)/shard_map/ppermute | solution.py:459
  77.9 1.8 %shard_map.134 = (f32[4,64,256]{2,1,0:T(8,128)S(1)}, f32[4,64,256]{2,1,0:T(8,128)S(1)}, f32[4,64,256]{2,1,0:T(8,128)S(1)}, f32[4,64,256]{2,1,0:T(8,128)S(1)}) custom-call(s32[2]{0:T(128)S(1)} %pad_add_fusion.ids, f32[4,1]{1,0:T(4,128)S(1)} %copy-done.6, f32[64,1]{1,0:T(8,128)S(1)} %copy-done.2, f32[1,1024]{1,0:T(1,128)S(1)} %copy-done.5, ...), custom_call_target="tpu_custom_call" | custom-call | flops 26214400 | bytes 1708568 | tf_op jit(solution)/shard_map/pallas_call | solution.py:73
  80.3 3.1 %collective-permute-start.17 = (f32[4,64,256]{2,1,0:T(8,128)S(1)}, f32[4,64,256]{2,1,0:T(8,128)S(1)}, u32[]{:S(2)}, u32[]{:S(2)}) collective-permute-start(f32[4,64,256]{2,1,0:T(8,128)S(1)} %get-tuple-element.49), channel_id=1, source_target_pairs={{0,8},{4,12},{8,0},{12,4},{16,24},{20,28},{24,16},{28,20},{1,9},{5... | collective-permute-start | bytes 786440 | tf_op jit(solution)/shard_map/ppermute | solution.py:459
  83.4 2.8 %shard_map.137.refs_2_ = f32[4,64,1024]{2,1,0:T(8,128)S(1)} custom-call(s32[2]{0:T(128)S(1)} %pad_add_fusion.ids, bf16[2,2,256,256]{3,2,1,0:T(8,128)(2,1)S(1)} %copy-done, bf16[1024,1024]{1,0:T(8,128)(2,1)S(1)} %get-tuple-element.30.sxh, bf16[1024,1024]{1,0:T(8,128)(2,1)S(1)} %get-tuple-element.31.sxl, f32[4,64,256]{2,1,0:T(8,128)S(1)} %get-tuple-element.51.refs_0_, ...), custom_call_target="tpu_custom_call" | custom-call | flops 2013265920 | bytes 5767176 | tf_op jit(solution)/shard_map/pallas_call | solution.py:73
  86.3 2.7 %collective-permute-done.16.refs_1_ = f32[4,64,256]{2,1,0:T(8,128)S(1)} collective-permute-done((f32[4,64,256]{2,1,0:T(8,128)S(1)}, f32[4,64,256]{2,1,0:T(8,128)S(1)}, u32[]{:S(2)}, u32[]{:S(2)}) %collective-permute-start.16) | collective-permute-done | bytes 262176 | tf_op jit(solution)/shard_map/ppermute | solution.py:459
  89.0 1.6 %collective-permute-done.17.refs_2_ = f32[4,64,256]{2,1,0:T(8,128)S(1)} collective-permute-done((f32[4,64,256]{2,1,0:T(8,128)S(1)}, f32[4,64,256]{2,1,0:T(8,128)S(1)}, u32[]{:S(2)}, u32[]{:S(2)}) %collective-permute-start.17) | collective-permute-done | bytes 262176 | tf_op jit(solution)/shard_map/ppermute | solution.py:459
  90.6 1.9 %shard_map.135.refs_0_ = f32[256,1024]{1,0:T(8,128)S(1)} custom-call(s32[2]{0:T(128)S(1)} %pad_add_fusion.ids, bf16[1024,1024]{1,0:T(8,128)(2,1)S(1)} %get-tuple-element.30.sxh, bf16[1024,1024]{1,0:T(8,128)(2,1)S(1)} %get-tuple-element.31.sxl, f32[4,64,256]{2,1,0:T(8,128)S(1)} %get-tuple-element.47.refs_0_, ...), custom_call_target="tpu_custom_call" | custom-call | flops 1006632960 | bytes 4980744 | tf_op jit(solution)/shard_map/pallas_call | solution.py:73
  92.6 1.5 %collective-permute-done.18.refs_1_ = f32[4,64,256]{2,1,0:T(8,128)S(1)} collective-permute-done((f32[4,64,256]{2,1,0:T(8,128)S(1)}, f32[4,64,256]{2,1,0:T(8,128)S(1)}, u32[]{:S(2)}, u32[]{:S(2)}) %collective-permute-start.18) | collective-permute-done | bytes 262176 | tf_op jit(solution)/shard_map/ppermute | solution.py:459
  94.1 2.8 %shard_map.138 = f32[8,64,1024]{2,1,0:T(8,128)} custom-call(s32[2]{0:T(128)S(1)} %pad_add_fusion.ids, bf16[2,2,256,256]{3,2,1,0:T(8,128)(2,1)S(1)} %copy-done, bf16[1024,1024]{1,0:T(8,128)(2,1)S(1)} %get-tuple-element.30.sxh, bf16[1024,1024]{1,0:T(8,128)(2,1)S(1)} %get-tuple-element.31.sxl, f32[256,1024]{1,0:T(8,128)S(1)} %shard_map.135.refs_0_, ...), custom_call_target="tpu_custom_call" | custom-call | flops 2013265920 | bytes 7077896 | tf_op jit(solution)/shard_map/pallas_call | solution.py:73
  (47 shorter events, 8.7 us)
Async XLA Ops:
  1.1 1.7 %copy-start.8 = (f32[1,8,64,1024]{3,2,1,0:T(8,128)S(1)}, f32[1,8,64,1024]{3,2,1,0:T(8,128)}, u32[]{:S(2)}) copy-start(f32[1,8,64,1024]{3,2,1,0:T(8,128)} %param.13) | copy-start | bytes 6291460
  1.1 1.7 %copy-start.9 = (bf16[2,2,256,256]{3,2,1,0:T(8,128)(2,1)S(1)}, bf16[2,2,256,256]{3,2,1,0:T(8,128)(2,1)}, u32[]{:S(2)}) copy-start(bf16[2,2,256,256]{3,2,1,0:T(8,128)(2,1)} %constant.51.both) | copy-start | bytes 1572868
  5.7 9.3 %collective-permute-start.3 = (f32[4,64,256]{2,1,0:T(8,128)S(1)}, f32[4,64,256]{2,1,0:T(8,128)S(1)}, u32[]{:S(2)}, u32[]{:S(2)}) collective-permute-start(f32[4,64,256]{2,1,0:T(8,128)S(1)} %get-tuple-element.40), channel_id=1, source_target_pairs={{0,4},{4,0},{8,12},{12,8},{16,20},{20,16},{24,28},{28,24},{1,5},{5... | collective-permute-start | bytes 786440 | tf_op jit(solution)/shard_map/ppermute | solution.py:459
  8.7 9.2 %collective-permute-start.4 = (f32[4,64,256]{2,1,0:T(8,128)S(1)}, f32[4,64,256]{2,1,0:T(8,128)S(1)}, u32[]{:S(2)}, u32[]{:S(2)}) collective-permute-start(f32[4,64,256]{2,1,0:T(8,128)S(1)} %get-tuple-element.41), channel_id=1, source_target_pairs={{0,8},{4,12},{8,0},{12,4},{16,24},{20,28},{24,16},{28,20},{1,9},{5... | collective-permute-start | bytes 786440 | tf_op jit(solution)/shard_map/ppermute | solution.py:459
  10.3 11.6 %copy-start.1 = (f32[64,1]{1,0:T(8,128)S(1)}, f32[64,1]{1,0:T(8,128)}, u32[]{:S(2)}) copy-start(f32[64,1]{1,0:T(8,128)} %constant.35.clone.edges) | copy-start | bytes 772
  10.3 11.6 %copy-start.2 = (f32[64,1]{1,0:T(8,128)S(1)}, f32[64,1]{1,0:T(8,128)}, u32[]{:S(2)}) copy-start(f32[64,1]{1,0:T(8,128)} %constant.33.clone.smu_y) | copy-start | bytes 772
  10.3 11.6 %copy-start.5 = (f32[1,1024]{1,0:T(1,128)S(1)}, f32[1,1024]{1,0:T(1,128)}, u32[]{:S(2)}) copy-start(f32[1,1024]{1,0:T(1,128)} %constant.34.clone.smu_x) | copy-start | bytes 12292
  10.3 11.6 %copy-start.7 = (f32[4,1]{1,0:T(4,128)S(1)}, f32[4,1]{1,0:T(4,128)}, u32[]{:S(2)}) copy-start(f32[4,1]{1,0:T(4,128)} %constant.41.clone.smu_z) | copy-start | bytes 52
  10.3 29.4 %copy-start.4 = (f32[5,4,4,1024]{3,2,1,0:T(4,128)S(1)}, f32[5,4,4,1024]{3,2,1,0:T(4,128)}, u32[]{:S(2)}) copy-start(f32[5,4,4,1024]{3,2,1,0:T(4,128)} %constant.43.clone.responses) | copy-start | bytes 983044
  10.3 38.6 %copy-start.6 = (f32[4,1]{1,0:T(4,128)S(1)}, f32[4,1]{1,0:T(4,128)}, u32[]{:S(2)}) copy-start(f32[4,1]{1,0:T(4,128)} %constant.42.clone.smu_z) | copy-start | bytes 52
  10.3 11.6 %collective-permute-start.5 = (f32[4,64,256]{2,1,0:T(8,128)S(1)}, f32[4,64,256]{2,1,0:T(8,128)S(1)}, u32[]{:S(2)}, u32[]{:S(2)}) collective-permute-start(f32[4,64,256]{2,1,0:T(8,128)S(1)} %get-tuple-element.42), channel_id=1, source_target_pairs={{0,12},{4,8},{8,4},{12,0},{16,28},{20,24},{24,20},{28,16},{1,13},{... | collective-permute-start | bytes 786440 | tf_op jit(solution)/shard_map/ppermute | solution.py:459
  13.3 48.5 %copy-start.3 = (f32[5,4,4,1024]{3,2,1,0:T(4,128)S(1)}, f32[5,4,4,1024]{3,2,1,0:T(4,128)}, u32[]{:S(2)}) copy-start(f32[5,4,4,1024]{3,2,1,0:T(4,128)} %constant.44.clone.responses) | copy-start | bytes 983044
  23.5 27.9 %collective-permute-start.6 = (f32[2,4,64,256]{3,2,1,0:T(8,128)S(1)}, f32[2,4,64,256]{3,2,1,0:T(8,128)S(1)}, u32[]{:S(2)}, u32[]{:S(2)}) collective-permute-start(f32[2,4,64,256]{3,2,1,0:T(8,128)S(1)} %get-tuple-element.43), channel_id=1, source_target_pairs={{0,16},{4,20},{8,24},{12,28},{16,0},{20,4},{24,8},{28,12},{1,17},{... | collective-permute-start | bytes 1572872 | tf_op jit(solution)/shard_map/ppermute | solution.py:459
  26.3 14.4 %collective-permute-start = (f32[4,64,256]{2,1,0:T(8,128)S(1)}, f32[4,64,256]{2,1,0:T(8,128)S(1)}, u32[]{:S(2)}, u32[]{:S(2)}) collective-permute-start(f32[4,64,256]{2,1,0:T(8,128)S(1)} %get-tuple-element.35), channel_id=1, source_target_pairs={{0,4},{4,0},{8,12},{12,8},{16,20},{20,16},{24,28},{28,24},{1,5},{5... | collective-permute-start | bytes 786440 | tf_op jit(solution)/shard_map/ppermute | solution.py:459
  27.8 16.5 %collective-permute-start.1 = (f32[4,64,256]{2,1,0:T(8,128)S(1)}, f32[4,64,256]{2,1,0:T(8,128)S(1)}, u32[]{:S(2)}, u32[]{:S(2)}) collective-permute-start(f32[4,64,256]{2,1,0:T(8,128)S(1)} %get-tuple-element.36), channel_id=1, source_target_pairs={{0,8},{4,12},{8,0},{12,4},{16,24},{20,28},{24,16},{28,20},{1,9},{5... | collective-permute-start | bytes 786440 | tf_op jit(solution)/shard_map/ppermute | solution.py:459
  29.4 19.5 %collective-permute-start.2 = (f32[4,64,256]{2,1,0:T(8,128)S(1)}, f32[4,64,256]{2,1,0:T(8,128)S(1)}, u32[]{:S(2)}, u32[]{:S(2)}) collective-permute-start(f32[4,64,256]{2,1,0:T(8,128)S(1)} %get-tuple-element.37), channel_id=1, source_target_pairs={{0,12},{4,8},{8,4},{12,0},{16,28},{20,24},{24,20},{28,16},{1,13},{... | collective-permute-start | bytes 786440 | tf_op jit(solution)/shard_map/ppermute | solution.py:459
  29.8 4.3 %collective-permute-start.9 = (f32[16,4,256]{2,1,0:T(4,128)S(1)}, f32[16,4,256]{2,1,0:T(4,128)S(1)}, u32[]{:S(2)}, u32[]{:S(2)}) collective-permute-start(f32[16,4,256]{2,1,0:T(4,128)S(1)} %get-tuple-element.44.refs_0_), channel_id=1, source_target_pairs={{0,3},{1,2},{2,1},{3,0},{4,7},{5,6},{6,5},{7,4},{8,11},{9,10},{10,... | collective-permute-start | bytes 196616 | tf_op jit(solution)/shard_map/ppermute | solution.py:459
  34.2 4.3 %collective-permute-start.8 = (f32[16,4,256]{2,1,0:T(4,128)S(1)}, f32[16,4,256]{2,1,0:T(4,128)S(1)}, u32[]{:S(2)}, u32[]{:S(2)}) collective-permute-start(f32[16,4,256]{2,1,0:T(4,128)S(1)} %get-tuple-element.44.refs_0_), channel_id=1, source_target_pairs={{0,2},{1,3},{2,0},{3,1},{4,6},{5,7},{6,4},{7,5},{8,10},{9,11},{10,... | collective-permute-start | bytes 196616 | tf_op jit(solution)/shard_map/ppermute | solution.py:459
  38.4 1.3 %collective-permute-start.7 = (f32[16,4,256]{2,1,0:T(4,128)S(1)}, f32[16,4,256]{2,1,0:T(4,128)S(1)}, u32[]{:S(2)}, u32[]{:S(2)}) collective-permute-start(f32[16,4,256]{2,1,0:T(4,128)S(1)} %get-tuple-element.44.refs_0_), channel_id=1, source_target_pairs={{0,1},{1,0},{2,3},{3,2},{4,5},{5,4},{6,7},{7,6},{8,9},{9,8},{10,11... | collective-permute-start | bytes 196616 | tf_op jit(solution)/shard_map/ppermute | solution.py:459
  40.6 10.9 %collective-permute-start.10 = (f32[16,4,256]{2,1,0:T(4,128)S(1)}, f32[16,4,256]{2,1,0:T(4,128)S(1)}, u32[]{:S(2)}, u32[]{:S(2)}) collective-permute-start(f32[16,4,256]{2,1,0:T(4,128)S(1)} %shard_map.132.refs_5_), channel_id=1, source_target_pairs={{0,16},{4,20},{8,24},{12,28},{16,0},{20,4},{24,8},{28,12},{1,17},{... | collective-permute-start | bytes 196616 | tf_op jit(solution)/shard_map/ppermute | solution.py:459
  51.5 26.4 %collective-permute-start.11 = (f32[2,4,64,256]{3,2,1,0:T(8,128)S(1)}, f32[2,4,64,256]{3,2,1,0:T(8,128)S(1)}, u32[]{:S(2)}, u32[]{:S(2)}) collective-permute-start(f32[2,4,64,256]{3,2,1,0:T(8,128)S(1)} %get-tuple-element.45), channel_id=1, source_target_pairs={{0,16},{4,20},{8,24},{12,28},{16,0},{20,4},{24,8},{28,12},{1,17},{... | collective-permute-start | bytes 1572872 | tf_op jit(solution)/shard_map/ppermute | solution.py:459
  53.3 30.1 %copy-start = (bf16[2,2,256,256]{3,2,1,0:T(8,128)(2,1)S(1)}, bf16[2,2,256,256]{3,2,1,0:T(8,128)(2,1)}, u32[]{:S(2)}) copy-start(bf16[2,2,256,256]{3,2,1,0:T(8,128)(2,1)} %constant.48.both) | copy-start | bytes 1572868
  53.3 6.7 %collective-permute-start.14 = (f32[16,4,256]{2,1,0:T(4,128)S(1)}, f32[16,4,256]{2,1,0:T(4,128)S(1)}, u32[]{:S(2)}, u32[]{:S(2)}) collective-permute-start(f32[16,4,256]{2,1,0:T(4,128)S(1)} %get-tuple-element.46.refs_0_), channel_id=1, source_target_pairs={{0,3},{1,2},{2,1},{3,0},{4,7},{5,6},{6,5},{7,4},{8,11},{9,10},{10,... | collective-permute-start | bytes 196616 | tf_op jit(solution)/shard_map/ppermute | solution.py:459
  53.3 7.2 %collective-permute-start.13 = (f32[16,4,256]{2,1,0:T(4,128)S(1)}, f32[16,4,256]{2,1,0:T(4,128)S(1)}, u32[]{:S(2)}, u32[]{:S(2)}) collective-permute-start(f32[16,4,256]{2,1,0:T(4,128)S(1)} %get-tuple-element.46.refs_0_), channel_id=1, source_target_pairs={{0,2},{1,3},{2,0},{3,1},{4,6},{5,7},{6,4},{7,5},{8,10},{9,11},{10,... | collective-permute-start | bytes 196616 | tf_op jit(solution)/shard_map/ppermute | solution.py:459
  56.5 26.9 %collective-permute-start.19 = (f32[4,64,256]{2,1,0:T(8,128)S(1)}, f32[4,64,256]{2,1,0:T(8,128)S(1)}, u32[]{:S(2)}, u32[]{:S(2)}) collective-permute-start(f32[4,64,256]{2,1,0:T(8,128)S(1)} %get-tuple-element.52), channel_id=1, source_target_pairs={{0,4},{4,0},{8,12},{12,8},{16,20},{20,16},{24,28},{28,24},{1,5},{5... | collective-permute-start | bytes 786440 | tf_op jit(solution)/shard_map/ppermute | solution.py:459
  57.5 25.9 %collective-permute-start.20 = (f32[4,64,256]{2,1,0:T(8,128)S(1)}, f32[4,64,256]{2,1,0:T(8,128)S(1)}, u32[]{:S(2)}, u32[]{:S(2)}) collective-permute-start(f32[4,64,256]{2,1,0:T(8,128)S(1)} %get-tuple-element.53), channel_id=1, source_target_pairs={{0,8},{4,12},{8,0},{12,4},{16,24},{20,28},{24,16},{28,20},{1,9},{5... | collective-permute-start | bytes 786440 | tf_op jit(solution)/shard_map/ppermute | solution.py:459
  60.0 23.4 %collective-permute-start.21 = (f32[4,64,256]{2,1,0:T(8,128)S(1)}, f32[4,64,256]{2,1,0:T(8,128)S(1)}, u32[]{:S(2)}, u32[]{:S(2)}) collective-permute-start(f32[4,64,256]{2,1,0:T(8,128)S(1)} %get-tuple-element.54), channel_id=1, source_target_pairs={{0,12},{4,8},{8,4},{12,0},{16,28},{20,24},{24,20},{28,16},{1,13},{... | collective-permute-start | bytes 786440 | tf_op jit(solution)/shard_map/ppermute | solution.py:459
  60.5 1.3 %collective-permute-start.12 = (f32[16,4,256]{2,1,0:T(4,128)S(1)}, f32[16,4,256]{2,1,0:T(4,128)S(1)}, u32[]{:S(2)}, u32[]{:S(2)}) collective-permute-start(f32[16,4,256]{2,1,0:T(4,128)S(1)} %get-tuple-element.46.refs_0_), channel_id=1, source_target_pairs={{0,1},{1,0},{2,3},{3,2},{4,5},{5,4},{6,7},{7,6},{8,9},{9,8},{10,11... | collective-permute-start | bytes 196616 | tf_op jit(solution)/shard_map/ppermute | solution.py:459
  62.6 15.2 %collective-permute-start.15 = (f32[16,4,256]{2,1,0:T(4,128)S(1)}, f32[16,4,256]{2,1,0:T(4,128)S(1)}, u32[]{:S(2)}, u32[]{:S(2)}) collective-permute-start(f32[16,4,256]{2,1,0:T(4,128)S(1)} %shard_map.133.refs_5_), channel_id=1, source_target_pairs={{0,16},{4,20},{8,24},{12,28},{16,0},{20,4},{24,8},{28,12},{1,17},{... | collective-permute-start | bytes 196616 | tf_op jit(solution)/shard_map/ppermute | solution.py:459
  79.7 9.3 %collective-permute-start.16 = (f32[4,64,256]{2,1,0:T(8,128)S(1)}, f32[4,64,256]{2,1,0:T(8,128)S(1)}, u32[]{:S(2)}, u32[]{:S(2)}) collective-permute-start(f32[4,64,256]{2,1,0:T(8,128)S(1)} %get-tuple-element.48), channel_id=1, source_target_pairs={{0,4},{4,0},{8,12},{12,8},{16,20},{20,16},{24,28},{28,24},{1,5},{5... | collective-permute-start | bytes 786440 | tf_op jit(solution)/shard_map/ppermute | solution.py:459
  80.3 10.3 %collective-permute-start.17 = (f32[4,64,256]{2,1,0:T(8,128)S(1)}, f32[4,64,256]{2,1,0:T(8,128)S(1)}, u32[]{:S(2)}, u32[]{:S(2)}) collective-permute-start(f32[4,64,256]{2,1,0:T(8,128)S(1)} %get-tuple-element.49), channel_id=1, source_target_pairs={{0,8},{4,12},{8,0},{12,4},{16,24},{20,28},{24,16},{28,20},{1,9},{5... | collective-permute-start | bytes 786440 | tf_op jit(solution)/shard_map/ppermute | solution.py:459
  83.4 10.7 %collective-permute-start.18 = (f32[4,64,256]{2,1,0:T(8,128)S(1)}, f32[4,64,256]{2,1,0:T(8,128)S(1)}, u32[]{:S(2)}, u32[]{:S(2)}) collective-permute-start(f32[4,64,256]{2,1,0:T(8,128)S(1)} %get-tuple-element.50), channel_id=1, source_target_pairs={{0,12},{4,8},{8,4},{12,0},{16,28},{20,24},{24,20},{28,16},{1,13},{... | collective-permute-start | bytes 786440 | tf_op jit(solution)/shard_map/ppermute | solution.py:459
  (1 other events, 1.0 us)

commit v17 on v16

--- a/solution.py
+++ b/solution.py
@@ -176,9 +176,33 @@
     return total
 
 
-def first_rows(plan, ids, sxh, sxl, *refs):
+def first_rows(plan, ids, both, sxh, sxl, *refs):
     place = lax.rem(ids[0], plan.half)
-    refs[-1][...] = x_rows(plan, place, refs[:-1], 0, sxh, sxl)
+    total = parts_of(x_rows(plan, place, refs[:-1], 0, sxh, sxl))
+    value = dot_parts((both[0, 1], both[1, 1]), total)
+    refs[-1][...] = value.reshape(refs[-1].shape)
+
+
+def finish(plan, ids, both, sxh, sxl, early, piece, even, out, held, sent):
+    folds = plan.folds
+    at = plan.columns(lax.rem(ids[0], plan.half) ^ (plan.half - 1))
+    modes = parts_of(piece[...].reshape(-1, plan.block))
+    left = parts_of(dot_parts((both[0, 1], both[1, 1]), modes))
+    copies = []
+    for j in range(plan.half):
+        columns = pl.ds(j * plan.block, plan.block)
+        value = dot_parts(left, (sxh[at, columns], sxl[at, columns]))
+        value = value.reshape(folds, plan.rows, plan.block) + early[:, :, columns]
+        other = even[:, :, columns]
+        held[j, :folds] = other + value
+        for z in range(folds):
+            held[j, plan.depth - 1 - z] = other[z] - value[z]
+        copies.append(
+            pltpu.make_async_copy(held.at[j], out.at[:, :, columns], sent.at[j])
+        )
+        copies[-1].start()
+    for copy in copies:
+        copy.wait()
 
 
 def backward(plan, chunk, ready, last, ids, both, sxh, sxl, *refs):
@@ -538,11 +562,19 @@
             ] + hold
             early = call(
                 functools.partial(first_rows, plan),
-                f32((len(chunk) * plan.rows, plan.width)),
+                f32((plan.folds,) + field.shape[1:]),
                 flops // 2,
-                (ids, *tables, *pieces[:-1]),
+                (ids, back, *tables, *pieces[:-1]),
             )
-            pieces = [early, pieces[-1]]
+            result = call(
+                functools.partial(finish, plan),
+                f32(field.shape),
+                flops // 2,
+                (ids, back, *tables, early, pieces[-1], sums[0]),
+                hold[:2],
+                pl.BlockSpec(memory_space=pltpu.HBM),
+            )
+            break
         ready = tuple(sorted(sums))
         parities = sorted(set(ready) | {c % 2 for c in chunk})
         result = call(

time: 97.2 us -> 96.9 us (level)
  no operation moved by 1% of the time
where the time goes in v17:
time: 96.9 us; the launch traced here: 96.7 us
  waiting for transfers between devices  47.3 us (49%)
  starting transfers between devices  24.5 us (25%)
  Pallas kernels  23.4 us (24%)
  local copies, waits for them, and re-layouts  1.09 us (1%)
    ppermute x22, waiting for transfers between devices, swap(): return lax.ppermute(values, axis, [(i, i ^ distance) for i in range(count)])  47.3 us
    ppermute x22, starting transfers between devices, swap(): return lax.ppermute(values, axis, [(i, i ^ distance) for i in range(count)])  24.5 us
    pallas_call x12, Pallas kernels, call(): pl.pallas_call(kernel, out_shape=out_shape, in_specs=[smem] + [vmem] * (l...  23.4 us
  transfers between devices with their start and end apart: 22, of which 14 were waited for; matrix products, arithmetic and copies ran while one was open for 0% of the time, Pallas kernels for 15%

profile of v17, /device:TPU:0, one launch (start us, length us, event | category | flops | bytes accessed | tf_op | source)
XLA Modules:
  0.0 96.7 jit_solution(4134823121899849738)
XLA Ops:
  1.1 1.7 %shard_map.127 = (bf16[1024,1024]{1,0:T(8,128)(2,1)S(1)}, bf16[1024,1024]{1,0:T(8,128)(2,1)S(1)}) custom-call(s32[2]{0:T(128)S(1)} %pad_add_fusion.ids, f32[128,1024]{1,0:T(8,128)S(1)} %copy-done.10), custom_call_target="tpu_custom_call" | custom-call | flops 4194304000 | bytes 524296 | tf_op jit(solution)/shard_map/pallas_call | solution.py:73
  2.9 2.8 %shard_map.128 = (f32[4,64,256]{2,1,0:T(8,128)S(1)}, f32[4,64,256]{2,1,0:T(8,128)S(1)}, f32[4,64,256]{2,1,0:T(8,128)S(1)}, f32[4,64,256]{2,1,0:T(8,128)S(1)}) custom-call(s32[2]{0:T(128)S(1)} %pad_add_fusion.ids, bf16[2,2,256,256]{3,2,1,0:T(8,128)(2,1)S(1)} %copy-done.9, f32[8,64,1024]{2,1,0:T(8,128)S(1)} %bitcast.4, ...), custom_call_target="tpu_custom_call" | custom-call | flops 2013265920 | bytes 6815752 | tf_op jit(solution)/shard_map/pallas_call | solution.py:73
  5.7 3.0 %collective-permute-start.3 = (f32[4,64,256]{2,1,0:T(8,128)S(1)}, f32[4,64,256]{2,1,0:T(8,128)S(1)}, u32[]{:S(2)}, u32[]{:S(2)}) collective-permute-start(f32[4,64,256]{2,1,0:T(8,128)S(1)} %get-tuple-element.40), channel_id=1, source_target_pairs={{0,4},{4,0},{8,12},{12,8},{16,20},{20,16},{24,28},{28,24},{1,5},{5... | collective-permute-start | bytes 786440 | tf_op jit(solution)/shard_map/ppermute | solution.py:483
  8.7 1.6 %collective-permute-start.4 = (f32[4,64,256]{2,1,0:T(8,128)S(1)}, f32[4,64,256]{2,1,0:T(8,128)S(1)}, u32[]{:S(2)}, u32[]{:S(2)}) collective-permute-start(f32[4,64,256]{2,1,0:T(8,128)S(1)} %get-tuple-element.41), channel_id=1, source_target_pairs={{0,8},{4,12},{8,0},{12,4},{16,24},{20,28},{24,16},{28,20},{1,9},{5... | collective-permute-start | bytes 786440 | tf_op jit(solution)/shard_map/ppermute | solution.py:483
  10.4 2.8 %shard_map.129 = (f32[4,64,256]{2,1,0:T(8,128)S(1)}, f32[4,64,256]{2,1,0:T(8,128)S(1)}, f32[4,64,256]{2,1,0:T(8,128)S(1)}, f32[4,64,256]{2,1,0:T(8,128)S(1)}) custom-call(s32[2]{0:T(128)S(1)} %pad_add_fusion.ids, bf16[2,2,256,256]{3,2,1,0:T(8,128)(2,1)S(1)} %copy-done.9, f32[8,64,1024]{2,1,0:T(8,128)S(1)} %bitcast.5, ...), custom_call_target="tpu_custom_call" | custom-call | flops 2013265920 | bytes 6815752 | tf_op jit(solution)/shard_map/pallas_call | solution.py:73
  13.3 1.8 %collective-permute-done.3.refs_1_ = f32[4,64,256]{2,1,0:T(8,128)S(1)} collective-permute-done((f32[4,64,256]{2,1,0:T(8,128)S(1)}, f32[4,64,256]{2,1,0:T(8,128)S(1)}, u32[]{:S(2)}, u32[]{:S(2)}) %collective-permute-start.3) | collective-permute-done | bytes 262176 | tf_op jit(solution)/shard_map/ppermute | solution.py:483
  15.0 2.9 %collective-permute-done.4.refs_2_ = f32[4,64,256]{2,1,0:T(8,128)S(1)} collective-permute-done((f32[4,64,256]{2,1,0:T(8,128)S(1)}, f32[4,64,256]{2,1,0:T(8,128)S(1)}, u32[]{:S(2)}, u32[]{:S(2)}) %collective-permute-start.4) | collective-permute-done | bytes 262176 | tf_op jit(solution)/shard_map/ppermute | solution.py:483
  18.0 3.9 %collective-permute-done.5.refs_3_ = f32[4,64,256]{2,1,0:T(8,128)S(1)} collective-permute-done((f32[4,64,256]{2,1,0:T(8,128)S(1)}, f32[4,64,256]{2,1,0:T(8,128)S(1)}, u32[]{:S(2)}, u32[]{:S(2)}) %collective-permute-start.5) | collective-permute-done | bytes 262176 | tf_op jit(solution)/shard_map/ppermute | solution.py:483
  21.9 1.6 %shard_map.131 = (f32[2,4,64,256]{3,2,1,0:T(8,128)S(1)}, f32[16,4,256]{2,1,0:T(4,128)S(1)}) custom-call(s32[2]{0:T(128)S(1)} %pad_add_fusion.ids, f32[4,1]{1,0:T(4,128)S(1)} %copy-done.7, f32[64,1]{1,0:T(8,128)S(1)} %copy-done.2, f32[1,1024]{1,0:T(1,128)S(1)} %copy-done.5, f32[64,1]{1,0:T(8,128)S(1)} %copy-done.1, ...), custom_call_target="tpu_custom_call" | custom-call | flops 26214400 | bytes 1053208 | tf_op jit(solution)/shard_map/pallas_call | solution.py:73
  23.5 2.8 %collective-permute-start.6 = (f32[2,4,64,256]{3,2,1,0:T(8,128)S(1)}, f32[2,4,64,256]{3,2,1,0:T(8,128)S(1)}, u32[]{:S(2)}, u32[]{:S(2)}) collective-permute-start(f32[2,4,64,256]{3,2,1,0:T(8,128)S(1)} %get-tuple-element.43), channel_id=1, source_target_pairs={{0,16},{4,20},{8,24},{12,28},{16,0},{20,4},{24,8},{28,12},{1,17},{... | collective-permute-start | bytes 1572872 | tf_op jit(solution)/shard_map/ppermute | solution.py:483
  26.3 1.5 %collective-permute-start = (f32[4,64,256]{2,1,0:T(8,128)S(1)}, f32[4,64,256]{2,1,0:T(8,128)S(1)}, u32[]{:S(2)}, u32[]{:S(2)}) collective-permute-start(f32[4,64,256]{2,1,0:T(8,128)S(1)} %get-tuple-element.35), channel_id=1, source_target_pairs={{0,4},{4,0},{8,12},{12,8},{16,20},{20,16},{24,28},{28,24},{1,5},{5... | collective-permute-start | bytes 786440 | tf_op jit(solution)/shard_map/ppermute | solution.py:483
  27.8 1.6 %collective-permute-start.1 = (f32[4,64,256]{2,1,0:T(8,128)S(1)}, f32[4,64,256]{2,1,0:T(8,128)S(1)}, u32[]{:S(2)}, u32[]{:S(2)}) collective-permute-start(f32[4,64,256]{2,1,0:T(8,128)S(1)} %get-tuple-element.36), channel_id=1, source_target_pairs={{0,8},{4,12},{8,0},{12,4},{16,24},{20,28},{24,16},{28,20},{1,9},{5... | collective-permute-start | bytes 786440 | tf_op jit(solution)/shard_map/ppermute | solution.py:483
  29.8 4.3 %collective-permute-done.9.refs_3_ = f32[16,4,256]{2,1,0:T(4,128)S(1)} collective-permute-done((f32[16,4,256]{2,1,0:T(4,128)S(1)}, f32[16,4,256]{2,1,0:T(4,128)S(1)}, u32[]{:S(2)}, u32[]{:S(2)}) %collective-permute-start.9) | collective-permute-done | bytes 65568 | tf_op jit(solution)/shard_map/ppermute | solution.py:483
  35.0 3.4 %collective-permute-done.8.refs_2_ = f32[16,4,256]{2,1,0:T(4,128)S(1)} collective-permute-done((f32[16,4,256]{2,1,0:T(4,128)S(1)}, f32[16,4,256]{2,1,0:T(4,128)S(1)}, u32[]{:S(2)}, u32[]{:S(2)}) %collective-permute-start.8) | collective-permute-done | bytes 65568 | tf_op jit(solution)/shard_map/ppermute | solution.py:483
  38.4 1.3 %collective-permute-done.7.refs_1_ = f32[16,4,256]{2,1,0:T(4,128)S(1)} collective-permute-done((f32[16,4,256]{2,1,0:T(4,128)S(1)}, f32[16,4,256]{2,1,0:T(4,128)S(1)}, u32[]{:S(2)}, u32[]{:S(2)}) %collective-permute-start.7) | collective-permute-done | bytes 65568 | tf_op jit(solution)/shard_map/ppermute | solution.py:483
  40.7 3.6 %collective-permute-done.1.refs_2_ = f32[4,64,256]{2,1,0:T(8,128)S(1)} collective-permute-done((f32[4,64,256]{2,1,0:T(8,128)S(1)}, f32[4,64,256]{2,1,0:T(8,128)S(1)}, u32[]{:S(2)}, u32[]{:S(2)}) %collective-permute-start.1) | collective-permute-done | bytes 262176 | tf_op jit(solution)/shard_map/ppermute | solution.py:483
  44.3 4.6 %collective-permute-done.2.refs_3_ = f32[4,64,256]{2,1,0:T(8,128)S(1)} collective-permute-done((f32[4,64,256]{2,1,0:T(8,128)S(1)}, f32[4,64,256]{2,1,0:T(8,128)S(1)}, u32[]{:S(2)}, u32[]{:S(2)}) %collective-permute-start.2) | collective-permute-done | bytes 262176 | tf_op jit(solution)/shard_map/ppermute | solution.py:483
  48.9 1.6 %shard_map.130 = (f32[2,4,64,256]{3,2,1,0:T(8,128)S(1)}, f32[16,4,256]{2,1,0:T(4,128)S(1)}) custom-call(s32[2]{0:T(128)S(1)} %pad_add_fusion.ids, f32[4,1]{1,0:T(4,128)S(1)} %copy-done.6, f32[64,1]{1,0:T(8,128)S(1)} %copy-done.2, f32[1,1024]{1,0:T(1,128)S(1)} %copy-done.5, f32[64,1]{1,0:T(8,128)S(1)} %copy-done.1, ...), custom_call_target="tpu_custom_call" | custom-call | flops 26214400 | bytes 1053208 | tf_op jit(solution)/shard_map/pallas_call | solution.py:73
  51.5 1.9 %collective-permute-start.11 = (f32[2,4,64,256]{3,2,1,0:T(8,128)S(1)}, f32[2,4,64,256]{3,2,1,0:T(8,128)S(1)}, u32[]{:S(2)}, u32[]{:S(2)}) collective-permute-start(f32[2,4,64,256]{3,2,1,0:T(8,128)S(1)} %get-tuple-element.45), channel_id=1, source_target_pairs={{0,16},{4,20},{8,24},{12,28},{16,0},{20,4},{24,8},{28,12},{1,17},{... | collective-permute-start | bytes 1572872 | tf_op jit(solution)/shard_map/ppermute | solution.py:483
  53.3 1.5 %collective-permute-start.13 = (f32[16,4,256]{2,1,0:T(4,128)S(1)}, f32[16,4,256]{2,1,0:T(4,128)S(1)}, u32[]{:S(2)}, u32[]{:S(2)}) collective-permute-start(f32[16,4,256]{2,1,0:T(4,128)S(1)} %get-tuple-element.46.refs_0_), channel_id=1, source_target_pairs={{0,2},{1,3},{2,0},{3,1},{4,6},{5,7},{6,4},{7,5},{8,10},{9,11},{10,... | collective-permute-start | bytes 196616 | tf_op jit(solution)/shard_map/ppermute | solution.py:483
  54.8 1.6 %shard_map.136 = (f32[4,64,256]{2,1,0:T(8,128)S(1)}, f32[4,64,256]{2,1,0:T(8,128)S(1)}, f32[4,64,256]{2,1,0:T(8,128)S(1)}, f32[4,64,256]{2,1,0:T(8,128)S(1)}) custom-call(s32[2]{0:T(128)S(1)} %pad_add_fusion.ids, f32[4,1]{1,0:T(4,128)S(1)} %copy-done.7, f32[64,1]{1,0:T(8,128)S(1)} %copy-done.2, f32[1,1024]{1,0:T(1,128)S(1)} %copy-done.5, ...), custom_call_target="tpu_custom_call" | custom-call | flops 26214400 | bytes 1708568 | tf_op jit(solution)/shard_map/pallas_call | solution.py:73
  57.5 2.4 %collective-permute-start.20 = (f32[4,64,256]{2,1,0:T(8,128)S(1)}, f32[4,64,256]{2,1,0:T(8,128)S(1)}, u32[]{:S(2)}, u32[]{:S(2)}) collective-permute-start(f32[4,64,256]{2,1,0:T(8,128)S(1)} %get-tuple-element.53), channel_id=1, source_target_pairs={{0,8},{4,12},{8,0},{12,4},{16,24},{20,28},{24,16},{28,20},{1,9},{5... | collective-permute-start | bytes 786440 | tf_op jit(solution)/shard_map/ppermute | solution.py:483
  60.5 1.3 %collective-permute-done.12.refs_1_ = f32[16,4,256]{2,1,0:T(4,128)S(1)} collective-permute-done((f32[16,4,256]{2,1,0:T(4,128)S(1)}, f32[16,4,256]{2,1,0:T(4,128)S(1)}, u32[]{:S(2)}, u32[]{:S(2)}) %collective-permute-start.12) | collective-permute-done | bytes 65568 | tf_op jit(solution)/shard_map/ppermute | solution.py:483
  62.7 1.4 %collective-permute-start.15 = (f32[16,4,256]{2,1,0:T(4,128)S(1)}, f32[16,4,256]{2,1,0:T(4,128)S(1)}, u32[]{:S(2)}, u32[]{:S(2)}) collective-permute-start(f32[16,4,256]{2,1,0:T(4,128)S(1)} %shard_map.133.refs_5_), channel_id=1, source_target_pairs={{0,16},{4,20},{8,24},{12,28},{16,0},{20,4},{24,8},{28,12},{1,17},{... | collective-permute-start | bytes 196616 | tf_op jit(solution)/shard_map/ppermute | solution.py:483
  64.1 13.8 %collective-permute-done.15.refs_6_ = f32[16,4,256]{2,1,0:T(4,128)S(1)} collective-permute-done((f32[16,4,256]{2,1,0:T(4,128)S(1)}, f32[16,4,256]{2,1,0:T(4,128)S(1)}, u32[]{:S(2)}, u32[]{:S(2)}) %collective-permute-start.15) | collective-permute-done | bytes 65568 | tf_op jit(solution)/shard_map/ppermute | solution.py:483
  77.9 1.8 %shard_map.134 = (f32[4,64,256]{2,1,0:T(8,128)S(1)}, f32[4,64,256]{2,1,0:T(8,128)S(1)}, f32[4,64,256]{2,1,0:T(8,128)S(1)}, f32[4,64,256]{2,1,0:T(8,128)S(1)}) custom-call(s32[2]{0:T(128)S(1)} %pad_add_fusion.ids, f32[4,1]{1,0:T(4,128)S(1)} %copy-done.6, f32[64,1]{1,0:T(8,128)S(1)} %copy-done.2, f32[1,1024]{1,0:T(1,128)S(1)} %copy-done.5, ...), custom_call_target="tpu_custom_call" | custom-call | flops 26214400 | bytes 1708568 | tf_op jit(solution)/shard_map/pallas_call | solution.py:73
  80.3 3.1 %collective-permute-start.17 = (f32[4,64,256]{2,1,0:T(8,128)S(1)}, f32[4,64,256]{2,1,0:T(8,128)S(1)}, u32[]{:S(2)}, u32[]{:S(2)}) collective-permute-start(f32[4,64,256]{2,1,0:T(8,128)S(1)} %get-tuple-element.49), channel_id=1, source_target_pairs={{0,8},{4,12},{8,0},{12,4},{16,24},{20,28},{24,16},{28,20},{1,9},{5... | collective-permute-start | bytes 786440 | tf_op jit(solution)/shard_map/ppermute | solution.py:483
  83.4 2.8 %shard_map.137.even = f32[4,64,1024]{2,1,0:T(8,128)S(1)} custom-call(s32[2]{0:T(128)S(1)} %pad_add_fusion.ids, bf16[2,2,256,256]{3,2,1,0:T(8,128)(2,1)S(1)} %copy-done, bf16[1024,1024]{1,0:T(8,128)(2,1)S(1)} %get-tuple-element.30.sxh, bf16[1024,1024]{1,0:T(8,128)(2,1)S(1)} %get-tuple-element.31.sxl, f32[4,64,256]{2,1,0:T(8,128)S(1)} %get-tuple-element.51.refs_0_, ...), custom_call_target="tpu_custom_call" | custom-call | flops 2013265920 | bytes 5767176 | tf_op jit(solution)/shard_map/pallas_call | solution.py:73
  86.3 2.7 %collective-permute-done.16.refs_1_ = f32[4,64,256]{2,1,0:T(8,128)S(1)} collective-permute-done((f32[4,64,256]{2,1,0:T(8,128)S(1)}, f32[4,64,256]{2,1,0:T(8,128)S(1)}, u32[]{:S(2)}, u32[]{:S(2)}) %collective-permute-start.16) | collective-permute-done | bytes 262176 | tf_op jit(solution)/shard_map/ppermute | solution.py:483
  89.0 1.6 %collective-permute-done.17.refs_2_ = f32[4,64,256]{2,1,0:T(8,128)S(1)} collective-permute-done((f32[4,64,256]{2,1,0:T(8,128)S(1)}, f32[4,64,256]{2,1,0:T(8,128)S(1)}, u32[]{:S(2)}, u32[]{:S(2)}) %collective-permute-start.17) | collective-permute-done | bytes 262176 | tf_op jit(solution)/shard_map/ppermute | solution.py:483
  90.6 2.4 %shard_map.135.early = f32[4,64,1024]{2,1,0:T(8,128)S(1)} custom-call(s32[2]{0:T(128)S(1)} %pad_add_fusion.ids, bf16[2,2,256,256]{3,2,1,0:T(8,128)(2,1)S(1)} %copy-done, bf16[1024,1024]{1,0:T(8,128)(2,1)S(1)} %get-tuple-element.30.sxh, bf16[1024,1024]{1,0:T(8,128)(2,1)S(1)} %get-tuple-element.31.sxl, f32[4,64,256]{2,1,0:T(8,128)S(1)} %get-tuple-element.47.refs_0_, ...), custom_call_target="tpu_custom_call" | custom-call | flops 1006632960 | bytes 5505032 | tf_op jit(solution)/shard_map/pallas_call | solution.py:73
  94.1 2.5 %shard_map.138 = f32[8,64,1024]{2,1,0:T(8,128)} custom-call(s32[2]{0:T(128)S(1)} %pad_add_fusion.ids, bf16[2,2,256,256]{3,2,1,0:T(8,128)(2,1)S(1)} %copy-done, bf16[1024,1024]{1,0:T(8,128)(2,1)S(1)} %get-tuple-element.30.sxh, bf16[1024,1024]{1,0:T(8,128)(2,1)S(1)} %get-tuple-element.31.sxl, f32[4,64,1024]{2,1,0:T(8,128)S(1)} %shard_map.135.early, ...), custom_call_target="tpu_custom_call" | custom-call | flops 1006632960 | bytes 7077896 | tf_op jit(solution)/shard_map/pallas_call | solution.py:73
  (47 shorter events, 8.5 us)
Async XLA Ops:
  1.1 1.7 %copy-start.8 = (f32[1,8,64,1024]{3,2,1,0:T(8,128)S(1)}, f32[1,8,64,1024]{3,2,1,0:T(8,128)}, u32[]{:S(2)}) copy-start(f32[1,8,64,1024]{3,2,1,0:T(8,128)} %param.13) | copy-start | bytes 6291460
  1.1 1.7 %copy-start.9 = (bf16[2,2,256,256]{3,2,1,0:T(8,128)(2,1)S(1)}, bf16[2,2,256,256]{3,2,1,0:T(8,128)(2,1)}, u32[]{:S(2)}) copy-start(bf16[2,2,256,256]{3,2,1,0:T(8,128)(2,1)} %constant.51.both) | copy-start | bytes 1572868
  5.7 9.3 %collective-permute-start.3 = (f32[4,64,256]{2,1,0:T(8,128)S(1)}, f32[4,64,256]{2,1,0:T(8,128)S(1)}, u32[]{:S(2)}, u32[]{:S(2)}) collective-permute-start(f32[4,64,256]{2,1,0:T(8,128)S(1)} %get-tuple-element.40), channel_id=1, source_target_pairs={{0,4},{4,0},{8,12},{12,8},{16,20},{20,16},{24,28},{28,24},{1,5},{5... | collective-permute-start | bytes 786440 | tf_op jit(solution)/shard_map/ppermute | solution.py:483
  8.7 9.2 %collective-permute-start.4 = (f32[4,64,256]{2,1,0:T(8,128)S(1)}, f32[4,64,256]{2,1,0:T(8,128)S(1)}, u32[]{:S(2)}, u32[]{:S(2)}) collective-permute-start(f32[4,64,256]{2,1,0:T(8,128)S(1)} %get-tuple-element.41), channel_id=1, source_target_pairs={{0,8},{4,12},{8,0},{12,4},{16,24},{20,28},{24,16},{28,20},{1,9},{5... | collective-permute-start | bytes 786440 | tf_op jit(solution)/shard_map/ppermute | solution.py:483
  10.3 11.6 %copy-start.1 = (f32[64,1]{1,0:T(8,128)S(1)}, f32[64,1]{1,0:T(8,128)}, u32[]{:S(2)}) copy-start(f32[64,1]{1,0:T(8,128)} %constant.35.clone.edges) | copy-start | bytes 772
  10.3 11.6 %copy-start.2 = (f32[64,1]{1,0:T(8,128)S(1)}, f32[64,1]{1,0:T(8,128)}, u32[]{:S(2)}) copy-start(f32[64,1]{1,0:T(8,128)} %constant.33.clone.smu_y) | copy-start | bytes 772
  10.3 11.6 %copy-start.5 = (f32[1,1024]{1,0:T(1,128)S(1)}, f32[1,1024]{1,0:T(1,128)}, u32[]{:S(2)}) copy-start(f32[1,1024]{1,0:T(1,128)} %constant.34.clone.smu_x) | copy-start | bytes 12292
  10.3 11.6 %copy-start.7 = (f32[4,1]{1,0:T(4,128)S(1)}, f32[4,1]{1,0:T(4,128)}, u32[]{:S(2)}) copy-start(f32[4,1]{1,0:T(4,128)} %constant.41.clone.smu_z) | copy-start | bytes 52
  10.3 29.4 %copy-start.4 = (f32[5,4,4,1024]{3,2,1,0:T(4,128)S(1)}, f32[5,4,4,1024]{3,2,1,0:T(4,128)}, u32[]{:S(2)}) copy-start(f32[5,4,4,1024]{3,2,1,0:T(4,128)} %constant.43.clone.responses) | copy-start | bytes 983044
  10.3 38.6 %copy-start.6 = (f32[4,1]{1,0:T(4,128)S(1)}, f32[4,1]{1,0:T(4,128)}, u32[]{:S(2)}) copy-start(f32[4,1]{1,0:T(4,128)} %constant.42.clone.smu_z) | copy-start | bytes 52
  10.3 11.6 %collective-permute-start.5 = (f32[4,64,256]{2,1,0:T(8,128)S(1)}, f32[4,64,256]{2,1,0:T(8,128)S(1)}, u32[]{:S(2)}, u32[]{:S(2)}) collective-permute-start(f32[4,64,256]{2,1,0:T(8,128)S(1)} %get-tuple-element.42), channel_id=1, source_target_pairs={{0,12},{4,8},{8,4},{12,0},{16,28},{20,24},{24,20},{28,16},{1,13},{... | collective-permute-start | bytes 786440 | tf_op jit(solution)/shard_map/ppermute | solution.py:483
  13.3 48.5 %copy-start.3 = (f32[5,4,4,1024]{3,2,1,0:T(4,128)S(1)}, f32[5,4,4,1024]{3,2,1,0:T(4,128)}, u32[]{:S(2)}) copy-start(f32[5,4,4,1024]{3,2,1,0:T(4,128)} %constant.44.clone.responses) | copy-start | bytes 983044
  23.5 27.9 %collective-permute-start.6 = (f32[2,4,64,256]{3,2,1,0:T(8,128)S(1)}, f32[2,4,64,256]{3,2,1,0:T(8,128)S(1)}, u32[]{:S(2)}, u32[]{:S(2)}) collective-permute-start(f32[2,4,64,256]{3,2,1,0:T(8,128)S(1)} %get-tuple-element.43), channel_id=1, source_target_pairs={{0,16},{4,20},{8,24},{12,28},{16,0},{20,4},{24,8},{28,12},{1,17},{... | collective-permute-start | bytes 1572872 | tf_op jit(solution)/shard_map/ppermute | solution.py:483
  26.3 14.4 %collective-permute-start = (f32[4,64,256]{2,1,0:T(8,128)S(1)}, f32[4,64,256]{2,1,0:T(8,128)S(1)}, u32[]{:S(2)}, u32[]{:S(2)}) collective-permute-start(f32[4,64,256]{2,1,0:T(8,128)S(1)} %get-tuple-element.35), channel_id=1, source_target_pairs={{0,4},{4,0},{8,12},{12,8},{16,20},{20,16},{24,28},{28,24},{1,5},{5... | collective-permute-start | bytes 786440 | tf_op jit(solution)/shard_map/ppermute | solution.py:483
  27.8 16.5 %collective-permute-start.1 = (f32[4,64,256]{2,1,0:T(8,128)S(1)}, f32[4,64,256]{2,1,0:T(8,128)S(1)}, u32[]{:S(2)}, u32[]{:S(2)}) collective-permute-start(f32[4,64,256]{2,1,0:T(8,128)S(1)} %get-tuple-element.36), channel_id=1, source_target_pairs={{0,8},{4,12},{8,0},{12,4},{16,24},{20,28},{24,16},{28,20},{1,9},{5... | collective-permute-start | bytes 786440 | tf_op jit(solution)/shard_map/ppermute | solution.py:483
  29.4 19.5 %collective-permute-start.2 = (f32[4,64,256]{2,1,0:T(8,128)S(1)}, f32[4,64,256]{2,1,0:T(8,128)S(1)}, u32[]{:S(2)}, u32[]{:S(2)}) collective-permute-start(f32[4,64,256]{2,1,0:T(8,128)S(1)} %get-tuple-element.37), channel_id=1, source_target_pairs={{0,12},{4,8},{8,4},{12,0},{16,28},{20,24},{24,20},{28,16},{1,13},{... | collective-permute-start | bytes 786440 | tf_op jit(solution)/shard_map/ppermute | solution.py:483
  29.8 4.3 %collective-permute-start.9 = (f32[16,4,256]{2,1,0:T(4,128)S(1)}, f32[16,4,256]{2,1,0:T(4,128)S(1)}, u32[]{:S(2)}, u32[]{:S(2)}) collective-permute-start(f32[16,4,256]{2,1,0:T(4,128)S(1)} %get-tuple-element.44.refs_0_), channel_id=1, source_target_pairs={{0,3},{1,2},{2,1},{3,0},{4,7},{5,6},{6,5},{7,4},{8,11},{9,10},{10,... | collective-permute-start | bytes 196616 | tf_op jit(solution)/shard_map/ppermute | solution.py:483
  34.2 4.3 %collective-permute-start.8 = (f32[16,4,256]{2,1,0:T(4,128)S(1)}, f32[16,4,256]{2,1,0:T(4,128)S(1)}, u32[]{:S(2)}, u32[]{:S(2)}) collective-permute-start(f32[16,4,256]{2,1,0:T(4,128)S(1)} %get-tuple-element.44.refs_0_), channel_id=1, source_target_pairs={{0,2},{1,3},{2,0},{3,1},{4,6},{5,7},{6,4},{7,5},{8,10},{9,11},{10,... | collective-permute-start | bytes 196616 | tf_op jit(solution)/shard_map/ppermute | solution.py:483
  38.4 1.3 %collective-permute-start.7 = (f32[16,4,256]{2,1,0:T(4,128)S(1)}, f32[16,4,256]{2,1,0:T(4,128)S(1)}, u32[]{:S(2)}, u32[]{:S(2)}) collective-permute-start(f32[16,4,256]{2,1,0:T(4,128)S(1)} %get-tuple-element.44.refs_0_), channel_id=1, source_target_pairs={{0,1},{1,0},{2,3},{3,2},{4,5},{5,4},{6,7},{7,6},{8,9},{9,8},{10,11... | collective-permute-start | bytes 196616 | tf_op jit(solution)/shard_map/ppermute | solution.py:483
  40.6 10.9 %collective-permute-start.10 = (f32[16,4,256]{2,1,0:T(4,128)S(1)}, f32[16,4,256]{2,1,0:T(4,128)S(1)}, u32[]{:S(2)}, u32[]{:S(2)}) collective-permute-start(f32[16,4,256]{2,1,0:T(4,128)S(1)} %shard_map.132.refs_5_), channel_id=1, source_target_pairs={{0,16},{4,20},{8,24},{12,28},{16,0},{20,4},{24,8},{28,12},{1,17},{... | collective-permute-start | bytes 196616 | tf_op jit(solution)/shard_map/ppermute | solution.py:483
  51.5 26.4 %collective-permute-start.11 = (f32[2,4,64,256]{3,2,1,0:T(8,128)S(1)}, f32[2,4,64,256]{3,2,1,0:T(8,128)S(1)}, u32[]{:S(2)}, u32[]{:S(2)}) collective-permute-start(f32[2,4,64,256]{3,2,1,0:T(8,128)S(1)} %get-tuple-element.45), channel_id=1, source_target_pairs={{0,16},{4,20},{8,24},{12,28},{16,0},{20,4},{24,8},{28,12},{1,17},{... | collective-permute-start | bytes 1572872 | tf_op jit(solution)/shard_map/ppermute | solution.py:483
  53.3 30.1 %copy-start = (bf16[2,2,256,256]{3,2,1,0:T(8,128)(2,1)S(1)}, bf16[2,2,256,256]{3,2,1,0:T(8,128)(2,1)}, u32[]{:S(2)}) copy-start(bf16[2,2,256,256]{3,2,1,0:T(8,128)(2,1)} %constant.48.both) | copy-start | bytes 1572868
  53.3 6.7 %collective-permute-start.14 = (f32[16,4,256]{2,1,0:T(4,128)S(1)}, f32[16,4,256]{2,1,0:T(4,128)S(1)}, u32[]{:S(2)}, u32[]{:S(2)}) collective-permute-start(f32[16,4,256]{2,1,0:T(4,128)S(1)} %get-tuple-element.46.refs_0_), channel_id=1, source_target_pairs={{0,3},{1,2},{2,1},{3,0},{4,7},{5,6},{6,5},{7,4},{8,11},{9,10},{10,... | collective-permute-start | bytes 196616 | tf_op jit(solution)/shard_map/ppermute | solution.py:483
  53.3 7.2 %collective-permute-start.13 = (f32[16,4,256]{2,1,0:T(4,128)S(1)}, f32[16,4,256]{2,1,0:T(4,128)S(1)}, u32[]{:S(2)}, u32[]{:S(2)}) collective-permute-start(f32[16,4,256]{2,1,0:T(4,128)S(1)} %get-tuple-element.46.refs_0_), channel_id=1, source_target_pairs={{0,2},{1,3},{2,0},{3,1},{4,6},{5,7},{6,4},{7,5},{8,10},{9,11},{10,... | collective-permute-start | bytes 196616 | tf_op jit(solution)/shard_map/ppermute | solution.py:483
  56.5 26.9 %collective-permute-start.19 = (f32[4,64,256]{2,1,0:T(8,128)S(1)}, f32[4,64,256]{2,1,0:T(8,128)S(1)}, u32[]{:S(2)}, u32[]{:S(2)}) collective-permute-start(f32[4,64,256]{2,1,0:T(8,128)S(1)} %get-tuple-element.52), channel_id=1, source_target_pairs={{0,4},{4,0},{8,12},{12,8},{16,20},{20,16},{24,28},{28,24},{1,5},{5... | collective-permute-start | bytes 786440 | tf_op jit(solution)/shard_map/ppermute | solution.py:483
  57.5 25.9 %collective-permute-start.20 = (f32[4,64,256]{2,1,0:T(8,128)S(1)}, f32[4,64,256]{2,1,0:T(8,128)S(1)}, u32[]{:S(2)}, u32[]{:S(2)}) collective-permute-start(f32[4,64,256]{2,1,0:T(8,128)S(1)} %get-tuple-element.53), channel_id=1, source_target_pairs={{0,8},{4,12},{8,0},{12,4},{16,24},{20,28},{24,16},{28,20},{1,9},{5... | collective-permute-start | bytes 786440 | tf_op jit(solution)/shard_map/ppermute | solution.py:483
  60.0 23.4 %collective-permute-start.21 = (f32[4,64,256]{2,1,0:T(8,128)S(1)}, f32[4,64,256]{2,1,0:T(8,128)S(1)}, u32[]{:S(2)}, u32[]{:S(2)}) collective-permute-start(f32[4,64,256]{2,1,0:T(8,128)S(1)} %get-tuple-element.54), channel_id=1, source_target_pairs={{0,12},{4,8},{8,4},{12,0},{16,28},{20,24},{24,20},{28,16},{1,13},{... | collective-permute-start | bytes 786440 | tf_op jit(solution)/shard_map/ppermute | solution.py:483
  60.5 1.3 %collective-permute-start.12 = (f32[16,4,256]{2,1,0:T(4,128)S(1)}, f32[16,4,256]{2,1,0:T(4,128)S(1)}, u32[]{:S(2)}, u32[]{:S(2)}) collective-permute-start(f32[16,4,256]{2,1,0:T(4,128)S(1)} %get-tuple-element.46.refs_0_), channel_id=1, source_target_pairs={{0,1},{1,0},{2,3},{3,2},{4,5},{5,4},{6,7},{7,6},{8,9},{9,8},{10,11... | collective-permute-start | bytes 196616 | tf_op jit(solution)/shard_map/ppermute | solution.py:483
  62.7 15.2 %collective-permute-start.15 = (f32[16,4,256]{2,1,0:T(4,128)S(1)}, f32[16,4,256]{2,1,0:T(4,128)S(1)}, u32[]{:S(2)}, u32[]{:S(2)}) collective-permute-start(f32[16,4,256]{2,1,0:T(4,128)S(1)} %shard_map.133.refs_5_), channel_id=1, source_target_pairs={{0,16},{4,20},{8,24},{12,28},{16,0},{20,4},{24,8},{28,12},{1,17},{... | collective-permute-start | bytes 196616 | tf_op jit(solution)/shard_map/ppermute | solution.py:483
  79.7 9.3 %collective-permute-start.16 = (f32[4,64,256]{2,1,0:T(8,128)S(1)}, f32[4,64,256]{2,1,0:T(8,128)S(1)}, u32[]{:S(2)}, u32[]{:S(2)}) collective-permute-start(f32[4,64,256]{2,1,0:T(8,128)S(1)} %get-tuple-element.48), channel_id=1, source_target_pairs={{0,4},{4,0},{8,12},{12,8},{16,20},{20,16},{24,28},{28,24},{1,5},{5... | collective-permute-start | bytes 786440 | tf_op jit(solution)/shard_map/ppermute | solution.py:483
  80.3 10.3 %collective-permute-start.17 = (f32[4,64,256]{2,1,0:T(8,128)S(1)}, f32[4,64,256]{2,1,0:T(8,128)S(1)}, u32[]{:S(2)}, u32[]{:S(2)}) collective-permute-start(f32[4,64,256]{2,1,0:T(8,128)S(1)} %get-tuple-element.49), channel_id=1, source_target_pairs={{0,8},{4,12},{8,0},{12,4},{16,24},{20,28},{24,16},{28,20},{1,9},{5... | collective-permute-start | bytes 786440 | tf_op jit(solution)/shard_map/ppermute | solution.py:483
  83.4 10.7 %collective-permute-start.18 = (f32[4,64,256]{2,1,0:T(8,128)S(1)}, f32[4,64,256]{2,1,0:T(8,128)S(1)}, u32[]{:S(2)}, u32[]{:S(2)}) collective-permute-start(f32[4,64,256]{2,1,0:T(8,128)S(1)} %get-tuple-element.50), channel_id=1, source_target_pairs={{0,12},{4,8},{8,4},{12,0},{16,28},{20,24},{24,20},{28,16},{1,13},{... | collective-permute-start | bytes 786440 | tf_op jit(solution)/shard_map/ppermute | solution.py:483
  (1 other events, 1.0 us)
